TPU v7x, 32 devices: a whole 2x2x4 slice. The times are simulated.
32 devices in a mesh: clip: 8 (over z, x), win: 4 (over y, core).
Axes of the slice: x: 2, y: 2, z: 4, core: 2. Of those that a mesh axis runs over, the one named last changes fastest.
Arguments:
- tokens: bfloat16 [8, 20, 256, 1024], P('clip', 'win'), may hold values from -6 to 6
- condition: bfloat16 [8, 1024], P('clip'), may hold values from -6 to 6
- slot_order: int32 [8, 20], P('clip'), may hold values from 0 to 19, each once within a row
- rel_index: int32 [320, 320], replicated, may hold values from 0 to 2047
- w_qkv: bfloat16 [1024, 3072], replicated, may hold values from -0.1875 to 0.1875
- b_query: bfloat16 [1024], replicated, may hold values from -4 to 4
- b_value: bfloat16 [1024], replicated, may hold values from -3 to 3
- w_out: bfloat16 [1024, 1024], replicated, may hold values from -0.75 to 0.75
- b_out: bfloat16 [1024], replicated, may hold values from -3 to 3
- w_up: bfloat16 [1024, 4096], replicated, may hold values from -0.1875 to 0.1875
- b_up: bfloat16 [4096], replicated, may hold values from -3 to 3
- w_down: bfloat16 [4096, 1024], replicated, may hold values from -0.09375 to 0.09375
- b_down: bfloat16 [1024], replicated, may hold values from -3 to 3
- w_ada: bfloat16 [1024, 6144], replicated, may hold values from -0.1875 to 0.1875
- b_ada: bfloat16 [6144], replicated, may hold values from -3 to 3
- rel_table: float32 [2048, 16], replicated, may hold values from -5 to 5
- grad_out: bfloat16 [8, 20, 256, 1024], P('clip', 'win'), may hold values from -6 to 6
Outputs:
- block_out: bfloat16 [8, 20, 256, 1024], P('clip', 'win')
- grad_tokens: bfloat16 [8, 20, 256, 1024], P('clip', 'win')
- grad_w_qkv: float32 [1024, 3072], P('clip')
- grad_b_query: float32 [1024], P('clip')
- grad_b_value: float32 [1024], P('clip')
- grad_w_out: float32 [1024, 1024], P('clip')
- grad_b_out: float32 [1024], P('clip')
- grad_w_up: float32 [1024, 4096], P('clip')
- grad_b_up: float32 [4096], P('clip')
- grad_w_down: float32 [4096, 1024], P('clip')
- grad_b_down: float32 [1024], P('clip')
- grad_w_ada: float32 [1024, 6144], P('clip')
- grad_b_ada: float32 [6144], P('clip')
- grad_rel_table: float32 [2048, 16], P('clip')
Inputs may be any that keep to these rules, and one draw needn't show every extreme that they name: Each row of slot_order is a permutation of 0 to 19.
All inputs are finite; a program needn't handle non-finite values.
Results may differ from a plain program's by a relative error of at most 0.015.
Values may be sent and summed in bfloat16 or wider, within the bound.
No kernel may reach another device: no remote copies, remote signals or barrier semaphores. Data moves between devices by JAX's collectives and lax.ppermute only.
A program may use at most 320 MiB of HBM per device.

v0:
```python
import math

import jax
import jax.numpy as jnp
from jax import lax
from jax.sharding import PartitionSpec as P

HEAD = 64
FRAMES = 5
WST = 8


def normalize(values):
    average = jnp.mean(values, axis=-1, keepdims=True)
    centered = values - average
    variance = jnp.mean(centered * centered, axis=-1, keepdims=True)
    inv_std = lax.rsqrt(variance + 1e-06)
    return (centered * inv_std, inv_std)


def norm_back(grad_hat, hat_rows, inv_std):
    first_mean = jnp.mean(grad_hat, axis=-1, keepdims=True)
    second_mean = jnp.mean(grad_hat * hat_rows, axis=-1, keepdims=True)
    return inv_std * (grad_hat - first_mean - hat_rows * second_mean)


def gelu_tanh(values):
    return jax.nn.gelu(values, approximate=True)


def permute_rows(stacked, selector):
    moved = jnp.einsum("ij,jpc->ipc", selector, stacked, preferred_element_type=jnp.float32)
    return moved.astype(stacked.dtype)


def to_quadrants(slot_rows):
    local_slots = slot_rows.shape[0]
    channels = slot_rows.shape[-1]
    arranged = slot_rows.reshape(local_slots, 2, WST, 2, WST, channels).transpose(1, 3, 0, 2, 4, 5)
    return arranged.reshape(4, local_slots, WST * WST, channels)


def from_quadrants(received):
    local_slots = received.shape[1]
    channels = received.shape[-1]
    arranged = received.reshape(2, 2, local_slots, WST, WST, channels).transpose(2, 0, 3, 1, 4, 5)
    return arranged.reshape(local_slots, 4 * WST * WST, channels)


def windows_from_slots(received, gather_sel):
    piece_rows = received.shape[2]
    channels = received.shape[-1]
    arranged = permute_rows(received.reshape(-1, piece_rows, channels), gather_sel)
    arranged = arranged.reshape(FRAMES, -1, piece_rows, channels).transpose(1, 0, 2, 3)
    return arranged.reshape(-1, FRAMES * piece_rows, channels)


def slots_from_windows(window_rows, scatter_sel, local_slots):
    sw_count = window_rows.shape[0]
    channels = window_rows.shape[-1]
    arranged = window_rows.reshape(sw_count, FRAMES, -1, channels).transpose(1, 0, 2, 3)
    piece_rows = arranged.shape[2]
    arranged = permute_rows(arranged.reshape(FRAMES * sw_count, piece_rows, channels), scatter_sel)
    return arranged.reshape(-1, local_slots, piece_rows, channels)


def bucket_sums(score_sums, rel_index, bucket_count):
    head_count = score_sums.shape[0]
    win_tokens = rel_index.shape[0]
    block_rows = math.gcd(win_tokens, 32)
    block_count = win_tokens // block_rows
    upper = score_sums.astype(jnp.bfloat16)
    lower = (score_sums - upper.astype(jnp.float32)).astype(jnp.bfloat16)
    both = jnp.concatenate([upper, lower], axis=0).reshape(
        2 * head_count, block_count, block_rows * win_tokens
    )
    both = both.transpose(1, 0, 2)
    index_blocks = rel_index.reshape(block_count, block_rows * win_tokens)
    buckets = jnp.arange(bucket_count, dtype=jnp.int32)

    def add_block(total, inputs):
        piece, index_row = inputs
        onehot = (index_row[:, None] == buckets[None, :]).astype(jnp.bfloat16)
        return (total + jnp.dot(piece, onehot, preferred_element_type=jnp.float32), None)

    init = jnp.zeros((2 * head_count, bucket_count), jnp.float32)
    total, unused = lax.scan(add_block, init, (both, index_blocks))
    return (total[:head_count] + total[head_count:]).T


def own_block(whole, clip_count):
    block_rows = whole.shape[0] // clip_count
    return lax.dynamic_slice_in_dim(whole, lax.axis_index("clip") * block_rows, block_rows, 0)


def local(
    tokens,
    condition,
    slot_order,
    rel_index,
    w_qkv,
    b_query,
    b_value,
    w_out,
    b_out,
    w_up,
    b_up,
    w_down,
    b_down,
    w_ada,
    b_ada,
    rel_table,
    grad_out,
):
    local_slots = tokens.shape[1]
    features = tokens.shape[-1]
    head_count = features // HEAD
    scale_factor = 1.0 / math.sqrt(HEAD)
    order_row = slot_order[0]
    slot_count = order_row.shape[0]
    positions = jnp.arange(slot_count, dtype=jnp.int32)
    scatter_sel = (order_row[:, None] == positions[None, :]).astype(jnp.bfloat16)
    gather_sel = scatter_sel.T
    lifted = jax.nn.silu(condition.astype(jnp.float32)).astype(jnp.bfloat16)
    modulation = jnp.dot(lifted, w_ada, preferred_element_type=jnp.float32)[0] + b_ada
    shift_one, scale_one, gate_one, shift_two, scale_two, gate_two = jnp.split(modulation, 6)
    inputs_flat = tokens[0].astype(jnp.float32).reshape(-1, features)
    hat_one, inv_one = normalize(inputs_flat)
    normed = (hat_one * (1.0 + scale_one) + shift_one).astype(jnp.bfloat16)
    quadrants = to_quadrants(normed.reshape(local_slots, -1, features))
    joined = jnp.dot(quadrants, w_qkv, preferred_element_type=jnp.float32)
    queries = (joined[..., :features] + b_query).astype(jnp.bfloat16)
    keys_all = joined[..., features : 2 * features].astype(jnp.bfloat16)
    values = (joined[..., 2 * features :] + b_value).astype(jnp.bfloat16)
    queries, keys_all, values = (queries, keys_all, values)
    queries, keys_all, values = (
        lax.all_to_all(queries, "win", split_axis=0, concat_axis=0, tiled=True),
        lax.all_to_all(keys_all, "win", split_axis=0, concat_axis=0, tiled=True),
        lax.all_to_all(values, "win", split_axis=0, concat_axis=0, tiled=True),
    )
    queries = windows_from_slots(queries, gather_sel)
    keys_all = windows_from_slots(keys_all, gather_sel)
    values = windows_from_slots(values, gather_sel)
    sw_count = queries.shape[0]
    win_tokens = queries.shape[1]
    head_shape = (sw_count, win_tokens, head_count, HEAD)
    query_heads = queries.reshape(head_shape)
    key_heads = keys_all.reshape(head_shape)
    value_heads = values.reshape(head_shape)
    pos_bias = jnp.transpose(rel_table[rel_index], (2, 0, 1))
    scores = (
        jnp.einsum("wqhe,wkhe->whqk", query_heads, key_heads, preferred_element_type=jnp.float32)
        * scale_factor
    )
    weights_soft = jax.nn.softmax(scores + pos_bias[None], axis=-1)
    probs_low = weights_soft.astype(jnp.bfloat16)
    attended = jnp.einsum(
        "whqk,wkhe->wqhe", probs_low, value_heads, preferred_element_type=jnp.float32
    )
    attended = attended.reshape(sw_count, win_tokens, features).astype(jnp.bfloat16)
    outgoing = slots_from_windows(attended, scatter_sel, local_slots)
    returned = from_quadrants(
        lax.all_to_all(outgoing, "win", split_axis=0, concat_axis=0, tiled=True)
    ).reshape(-1, features)
    branch = jnp.dot(returned, w_out, preferred_element_type=jnp.float32) + b_out
    residual_one = inputs_flat + gate_one * branch
    hat_two, inv_two = normalize(residual_one)
    normed_two = (hat_two * (1.0 + scale_two) + shift_two).astype(jnp.bfloat16)
    hidden = jnp.dot(normed_two, w_up, preferred_element_type=jnp.float32) + b_up
    activated_f, gelu_pull = jax.vjp(gelu_tanh, hidden)
    activated = activated_f.astype(jnp.bfloat16)
    mixed_out = jnp.dot(activated, w_down, preferred_element_type=jnp.float32) + b_down
    block_out = (residual_one + gate_two * mixed_out).astype(jnp.bfloat16).reshape(tokens.shape)
    upstream = grad_out[0].astype(jnp.float32).reshape(-1, features)
    grad_mixed = (gate_two * upstream).astype(jnp.bfloat16)
    grad_gate_two = jnp.sum(upstream * mixed_out, axis=0)
    grad_b_down = jnp.sum(grad_mixed.astype(jnp.float32), axis=0)
    grad_w_down = jnp.dot(activated.T, grad_mixed, preferred_element_type=jnp.float32)
    grad_act = jnp.dot(grad_mixed, w_down.T, preferred_element_type=jnp.float32)
    grad_hidden = gelu_pull(grad_act)[0].astype(jnp.bfloat16)
    grad_b_up = jnp.sum(grad_hidden.astype(jnp.float32), axis=0)
    grad_w_up = jnp.dot(normed_two.T, grad_hidden, preferred_element_type=jnp.float32)
    grad_normed_two = jnp.dot(grad_hidden, w_up.T, preferred_element_type=jnp.float32)
    grad_scale_two = jnp.sum(grad_normed_two * hat_two, axis=0)
    grad_shift_two = jnp.sum(grad_normed_two, axis=0)
    grad_residual = upstream + norm_back(grad_normed_two * (1.0 + scale_two), hat_two, inv_two)
    grad_branch = (gate_one * grad_residual).astype(jnp.bfloat16)
    grad_gate_one = jnp.sum(grad_residual * branch, axis=0)
    grad_b_out = jnp.sum(grad_branch.astype(jnp.float32), axis=0)
    grad_w_out = jnp.dot(returned.T, grad_branch, preferred_element_type=jnp.float32)
    grad_returned = jnp.dot(grad_branch, w_out.T, preferred_element_type=jnp.float32).astype(
        jnp.bfloat16
    )
    grad_quadrants = to_quadrants(grad_returned.reshape(local_slots, -1, features))
    grad_attended = windows_from_slots(
        lax.all_to_all(grad_quadrants, "win", split_axis=0, concat_axis=0, tiled=True), gather_sel
    )
    grad_att_heads = grad_attended.reshape(head_shape)
    grad_values = jnp.einsum(
        "whqk,wqhe->wkhe", probs_low, grad_att_heads, preferred_element_type=jnp.float32
    )
    grad_probs = jnp.einsum(
        "wqhe,wkhe->whqk", grad_att_heads, value_heads, preferred_element_type=jnp.float32
    )
    row_totals = jnp.sum(weights_soft * grad_probs, axis=-1, keepdims=True)
    grad_scores = (weights_soft * (grad_probs - row_totals)).astype(jnp.bfloat16)
    grad_queries = (
        jnp.einsum("whqk,wkhe->wqhe", grad_scores, key_heads, preferred_element_type=jnp.float32)
        * scale_factor
    )
    grad_keys = (
        jnp.einsum("whqk,wqhe->wkhe", grad_scores, query_heads, preferred_element_type=jnp.float32)
        * scale_factor
    )
    win_shape = (sw_count, win_tokens, features)
    grad_queries = grad_queries.reshape(win_shape).astype(jnp.bfloat16)
    grad_keys = grad_keys.reshape(win_shape).astype(jnp.bfloat16)
    grad_values = grad_values.reshape(win_shape).astype(jnp.bfloat16)
    score_sums = jnp.sum(grad_scores.astype(jnp.float32), axis=0).reshape(head_count, -1)
    grad_rel_table = bucket_sums(score_sums, rel_index, rel_table.shape[0])
    back_q = slots_from_windows(grad_queries, scatter_sel, local_slots)
    back_k = slots_from_windows(grad_keys, scatter_sel, local_slots)
    back_v = slots_from_windows(grad_values, scatter_sel, local_slots)
    back_q, back_k, back_v = (
        lax.all_to_all(back_q, "win", split_axis=0, concat_axis=0, tiled=True),
        lax.all_to_all(back_k, "win", split_axis=0, concat_axis=0, tiled=True),
        lax.all_to_all(back_v, "win", split_axis=0, concat_axis=0, tiled=True),
    )
    grad_q_rows = from_quadrants(back_q).reshape(-1, features)
    grad_k_rows = from_quadrants(back_k).reshape(-1, features)
    grad_v_rows = from_quadrants(back_v).reshape(-1, features)
    grad_w_qkv = jnp.concatenate(
        [
            jnp.dot(normed.T, grad_q_rows, preferred_element_type=jnp.float32),
            jnp.dot(normed.T, grad_k_rows, preferred_element_type=jnp.float32),
            jnp.dot(normed.T, grad_v_rows, preferred_element_type=jnp.float32),
        ],
        axis=1,
    )
    grad_b_query = jnp.sum(grad_q_rows.astype(jnp.float32), axis=0)
    grad_b_value = jnp.sum(grad_v_rows.astype(jnp.float32), axis=0)
    grad_normed = jnp.dot(grad_q_rows, w_qkv[:, :features].T, preferred_element_type=jnp.float32)
    grad_normed = grad_normed + jnp.dot(
        grad_k_rows, w_qkv[:, features : 2 * features].T, preferred_element_type=jnp.float32
    )
    grad_normed = grad_normed + jnp.dot(
        grad_v_rows, w_qkv[:, 2 * features :].T, preferred_element_type=jnp.float32
    )
    grad_normed = grad_normed.astype(jnp.bfloat16)
    grad_norm_in = grad_normed.astype(jnp.float32)
    grad_scale_one = jnp.sum(grad_norm_in * hat_one, axis=0)
    grad_shift_one = jnp.sum(grad_norm_in, axis=0)
    grad_tokens = grad_residual + norm_back(grad_norm_in * (1.0 + scale_one), hat_one, inv_one)
    grad_tokens = grad_tokens.astype(jnp.bfloat16).reshape(tokens.shape)
    grad_mod_terms = jnp.concatenate(
        [
            grad_shift_one,
            grad_scale_one,
            grad_gate_one,
            grad_shift_two,
            grad_scale_two,
            grad_gate_two,
        ]
    )
    clip_count = lax.axis_size("clip")
    all_lifted, all_terms = (
        lax.all_gather(lifted.astype(jnp.float32), ("clip", "win"), axis=0, tiled=True).astype(
            lifted.dtype
        ),
        lax.all_gather(grad_mod_terms[None, :], ("clip", "win"), axis=0, tiled=True),
    )
    ada_rows = features // clip_count
    lifted_rows = lax.dynamic_slice_in_dim(
        all_lifted, lax.axis_index("clip") * ada_rows, ada_rows, 1
    ).astype(jnp.float32)
    grad_w_ada = jnp.dot(lifted_rows.T, all_terms, precision=lax.Precision.HIGHEST)
    grad_b_ada = own_block(jnp.sum(all_terms, axis=0), clip_count)
    shares = (
        lax.psum_scatter(grad_w_qkv, "clip", scatter_dimension=0, tiled=True),
        lax.psum_scatter(grad_b_query, "clip", scatter_dimension=0, tiled=True),
        lax.psum_scatter(grad_b_value, "clip", scatter_dimension=0, tiled=True),
        lax.psum_scatter(grad_w_out, "clip", scatter_dimension=0, tiled=True),
        lax.psum_scatter(grad_b_out, "clip", scatter_dimension=0, tiled=True),
        lax.psum_scatter(grad_w_up, "clip", scatter_dimension=0, tiled=True),
        lax.psum_scatter(grad_b_up, "clip", scatter_dimension=0, tiled=True),
        lax.psum_scatter(grad_w_down, "clip", scatter_dimension=0, tiled=True),
        lax.psum_scatter(grad_b_down, "clip", scatter_dimension=0, tiled=True),
        lax.psum_scatter(grad_rel_table, "clip", scatter_dimension=0, tiled=True),
    )
    summed = (
        lax.psum(shares[0].astype(jnp.bfloat16), "win").astype(jnp.float32),
        lax.psum(shares[1].astype(jnp.bfloat16), "win").astype(jnp.float32),
        lax.psum(shares[2].astype(jnp.bfloat16), "win").astype(jnp.float32),
        lax.psum(shares[3].astype(jnp.bfloat16), "win").astype(jnp.float32),
        lax.psum(shares[4].astype(jnp.bfloat16), "win").astype(jnp.float32),
        lax.psum(shares[5].astype(jnp.bfloat16), "win").astype(jnp.float32),
        lax.psum(shares[6].astype(jnp.bfloat16), "win").astype(jnp.float32),
        lax.psum(shares[7].astype(jnp.bfloat16), "win").astype(jnp.float32),
        lax.psum(shares[8].astype(jnp.bfloat16), "win").astype(jnp.float32),
        lax.psum(shares[9].astype(jnp.bfloat16), "win").astype(jnp.float32),
    )
    sum_qkv, sum_bq, sum_bv, sum_wo, sum_bo, sum_wu, sum_bu, sum_wd, sum_bd, sum_rel = summed
    return (
        block_out,
        grad_tokens,
        sum_qkv,
        sum_bq,
        sum_bv,
        sum_wo,
        sum_bo,
        sum_wu,
        sum_bu,
        sum_wd,
        sum_bd,
        grad_w_ada,
        grad_b_ada,
        sum_rel,
    )


def solution(mesh):
    placed = (
        P("clip", "win", None, None),
        P("clip", None),
        P("clip", None),
        P(),
        P(),
        P(),
        P(),
        P(),
        P(),
        P(),
        P(),
        P(),
        P(),
        P(),
        P(),
        P(),
        P("clip", "win", None, None),
    )
    return jax.shard_map(
        local,
        mesh=mesh,
        in_specs=placed,
        out_specs=(
            P("clip", "win", None, None),
            P("clip", "win", None, None),
            P("clip", None),
            P("clip"),
            P("clip"),
            P("clip", None),
            P("clip"),
            P("clip", None),
            P("clip"),
            P("clip", None),
            P("clip"),
            P("clip", None),
            P("clip"),
            P("clip", None),
        ),
        check_vma=False,
    )
```

profile of v0, /device:TPU:0, one launch (start us, length us, event | category | flops | bytes accessed | tf_op | source)
XLA Modules:
  0.0 2206.6 jit_solution(5973291048416034124)
XLA Ops:
  22.3 10.5 fusion.26
  49.0 27.5 %all-to-all-done = bf16[4,5,64,1024]{3,2,1,0:T(8,128)(2,1)} async-done(((bf16[4,5,64,1024]{3,2,1,0:T(8,128)(2,1)}), bf16[4,5,64,1024]{3,2,1,0:T(8,128)(2,1)}, u32[]{:S(2)}, u32[]{:S(2)}) %all-to-all-start) | async-done | bytes 2621472 | tf_op jit(solution)/shard_map/all_to_all | solution.py:139
  81.3 31.0 %all-to-all-done.2 = bf16[4,5,64,1024]{3,2,1,0:T(8,128)(2,1)} async-done(((bf16[4,5,64,1024]{3,2,1,0:T(8,128)(2,1)}), bf16[4,5,64,1024]{3,2,1,0:T(8,128)(2,1)}, u32[]{:S(2)}, u32[]{:S(2)}) %all-to-all-start.2) | async-done | bytes 2621472 | tf_op jit(solution)/shard_map/all_to_all | solution.py:138
  118.2 336.4 %gather_fusion = f32[102400,16]{1,0:T(8,128)} fusion(f32[2048,16]{1,0:T(8,128)S(1)} %copy.179, s32[102400]{0:T(1024)S(1)} %broadcast_clamp_fusion), kind=kCustom, calls=%fused_computation | custom fusion | bytes 13516800 | tf_op jit(solution)/shard_map/gather | solution.py:150
  454.6 34.4 %copy.180 = f32[320,320,16]{0,1,2:T(8,128)} copy(f32[320,320,16]{2,1,0:T(8,128)} %bitcast.190) | data formatting | bytes 13107200 | tf_op jit(solution)/shard_map/gather | solution.py:150
  519.9 10.7 reshape.386
  530.5 9.9 copy.233
  540.5 10.7 reshape.385
  560.6 10.7 reshape.387
  571.3 18.6 fusion.130
  589.9 14.2 convert_bitcast_fusion.1
  635.8 27.3 %all-to-all-done.3 = bf16[4,5,64,1024]{3,2,1,0:T(8,128)(2,1)} async-done(((bf16[4,5,64,1024]{3,2,1,0:T(8,128)(2,1)}), bf16[4,5,64,1024]{3,2,1,0:T(8,128)(2,1)}, u32[]{:S(2)}, u32[]{:S(2)}) %all-to-all-start.3) | async-done | bytes 2621472 | tf_op jit(solution)/shard_map/all_to_all | solution.py:163
  672.7 19.0 fusion.126
  691.7 32.1 %convert_reduce_fusion.1 = (f32[4096]{0:T(1024)}, bf16[1280,4096]{1,0:T(8,128)(2,1)}, bf16[1280,4096]{1,0:T(8,128)(2,1)}) fusion(f32[1280,4096]{1,0:T(8,128)} %fusion.126, f32[4096]{0:T(1024)S(1)} %convert_element_type.301, bf16[1280,1024]{1,0:T(8,128)(2,1)S(1)} %copy-done.14, bf16[4096,1024]{1,0:T(8,128)(2,1)} %param.30), kind=kOutput, calls=%fused_computation.26 | convolution fusion | flops 10868486144 | bytes 52985856 | tf_op jit(solution)/shard_map/dot_general | solution.py:179
  723.7 20.0 multiply_reduce_fusion.1
  743.8 25.9 %fusion.38 = (f32[1024]{0:T(1024)}, bf16[1280,1024]{1,0:T(8,128)(2,1)}, f32[1024]{0:T(1024)}, f32[1280,1024]{1,0:T(8,128)}) fusion(bf16[1,5,256,1024]{3,2,1,0:T(8,128)(2,1)S(1)} %copy-done.5, f32[1024]{0:T(1024)S(1)} %convert_element_type.303, f32[1280,1024]{1,0:T(8,128)} %copy-done.6, f32[1024]{0:T(1024)S(1)} %copy-done.26, ...), kind=kOutput, calls=%fused_computation.65 | convolution fusion | flops 10761009152 | bytes 45133824 | tf_op jit(solution)/shard_map/dot_general | solution.py:172
  783.8 31.1 %all-to-all-done.4 = bf16[4,5,64,1024]{3,2,1,0:T(8,128)(2,1)} async-done(((bf16[4,5,64,1024]{3,2,1,0:T(8,128)(2,1)}), bf16[4,5,64,1024]{3,2,1,0:T(8,128)(2,1)}, u32[]{:S(2)}, u32[]{:S(2)}) %all-to-all-start.4) | async-done | bytes 2621472 | tf_op jit(solution)/shard_map/all_to_all | solution.py:196
  831.4 10.7 reshape.388
  842.1 15.2 convert_bitcast_fusion
  857.3 26.0 %multiply_reduce_fusion = (f32[4,16,320]{2,1,0:T(8,128)S(1)}, f32[4,16,320,320]{2,3,1,0:T(8,128)}) fusion(f32[4,16,320,320]{2,3,1,0:T(8,128)} %get-tuple-element.184, f32[4,16,320]{2,1,0:T(8,128)S(1)} %copy-done.19, bf16[4,320,16,64]{1,3,2,0:T(8,128)(2,1)} %reshape.388, bf16[4,320,16,64]{1,3,2,0:T(8,128)(2,1)} %reshape.385), kind=kOutput, calls=%fused_computation.13 | convolution fusion | flops 858501120 | bytes 57835520 | tf_op jit(solution)/shard_map/wqhe,wkhe->whqk/dot_general | solution.py:202
  911.3 29.7 %convert_reduce_fusion = (f32[16,320,320]{1,2,0:T(8,128)}, bf16[4,16,320,320]{2,3,1,0:T(8,128)(2,1)}) fusion(f32[4,16,320,320]{2,3,1,0:T(8,128)} %get-tuple-element.188, f32[4,16,320]{2,1,0:T(8,128)S(1)} %get-tuple-element.187, f32[4,16,320,320]{2,3,1,0:T(8,128)} %get-tuple-element.184, f32[4,16,320]{2,1,0:T(8,128)S(1)} %copy-done.19), kind=kLoop, calls=%fused_computation.11 | loop fusion | flops 37683200 | bytes 72253440 | tf_op jit(solution)/shard_map/reduce_sum | solution.py:219
  949.6 10.5 reshape.351
  960.1 13.5 subtract_convert_fusion
  983.6 10.2 copy.218
  993.8 183.3 %while.11 = (s32[]{:T(128)}, f32[32,2048]{1,0:T(8,128)S(1)}, bf16[10,32,10240]{2,1,0:T(8,128)(2,1)}, s32[10,10240]{1,0:T(8,128)S(1)}, s32[]{:T(128)}, /*index=5*/s32[]{:T(128)}) while((s32[]{:T(128)}, f32[32,2048]{1,0:T(8,128)S(1)}, bf16[10,32,10240]{2,1,0:T(8,128)(2,1)}, s32[10,10240]{1,0:T(8,128)S(1)}, s32[]{:T(128)}, ...), condition=%wide.region_43.44_spmd.clone, body=%wide.region_42.43_spmd.clone.sunk | while | flops 1363279872 | bytes 1302623 | solution.py:87
  993.8 18.3 fusion.179
  1012.2 18.3 fusion.179
  1030.5 18.3 fusion.179
  1048.8 18.3 fusion.179
  1067.2 18.3 fusion.179
  1085.5 18.3 fusion.179
  1103.8 18.3 fusion.179
  1122.2 18.3 fusion.179
  1140.5 18.3 fusion.179
  1158.8 18.3 fusion.179
  1185.5 11.1 fusion.49
  1224.3 10.1 fusion.50
  1273.2 20.2 all-to-all-done.6
  1314.4 19.1 fusion.125
  1333.7 17.9 fusion.135
  1354.1 44.9 %all-gather.1 = bf16[32,1,1024]{2,1,0:T(2,128)(2,1)S(1)} all-gather(bf16[1,1,1024]{2,1,0:T(2,128)(2,1)S(1)} %bitcast_convert_fusion), channel_id=1, replica_groups=mesh['clip'=8,'win'=4] {'clip','win'}, dimensions={0}, use_global_device_ids=true | all-gather | bytes 67584 | tf_op jit(solution)/shard_map/all_gather | solution.py:267
  1406.9 35.4 %all-reduce.5 = (bf16[1024]{0:T(1024)(128)(2,1)S(1)}, bf16[1024]{0:T(1024)(128)(2,1)S(1)}, bf16[1024]{0:T(1024)(128)(2,1)S(1)}, bf16[4096]{0:T(1024)(128)(2,1)S(1)}, bf16[1024]{0:T(1024)(128)(2,1)S(1)}) all-reduce(f32[1024]{0:T(1024)S(1)} %convert_reduce_fusion.7, ...), channel_id=4, replica_groups=mesh['clip'=8,'win'=4] {'clip'}, use_global_device_ids=true, to_apply=%region_14.15.clone | all-reduce | flops 8192 | bytes 49152
  1442.7 10.9 all-reduce.6
  1475.2 41.3 %all-gather = f32[196608]{0:T(1024)S(1)} all-gather(f32[6144]{0:T(1024)S(1)} %constant_dynamic-update-slice_fusion), channel_id=2, replica_groups=mesh['clip'=8,'win'=4] {'clip','win'}, dimensions={0}, use_global_device_ids=true | all-gather | bytes 811008 | tf_op jit(solution)/shard_map/all_gather | solution.py:270
  1519.2 27.2 %reduce-scatter.6.cloned.1.call-done = f32[128,3072]{0,1:T(8,128)} async-done(((f32[1024,3072]{0,1:T(8,128)}), f32[128,3072]{0,1:T(8,128)}) %reduce-scatter.6.cloned.1.call-update) | async-done | bytes 1572880 | tf_op jit(solution)/shard_map/reduce_scatter | solution.py:279
  1548.8 284.6 %reduce-scatter.10.cloned.1.call-done = f32[128,4096]{1,0:T(8,128)} async-done(((f32[1024,4096]{1,0:T(8,128)}), f32[128,4096]{1,0:T(8,128)}) %reduce-scatter.10.cloned.1.call-update) | async-done | bytes 2097168 | tf_op jit(solution)/shard_map/reduce_scatter | solution.py:284
  1836.1 282.7 %reduce-scatter.12.cloned.1.call-done = f32[512,1024]{1,0:T(8,128)} async-done(((f32[4096,1024]{1,0:T(8,128)}), f32[512,1024]{1,0:T(8,128)}) %reduce-scatter.12.cloned.1.call-update) | async-done | bytes 2097168 | tf_op jit(solution)/shard_map/reduce_scatter | solution.py:286
  2132.7 57.9 %all-reduce.10.cloned.1.call-done = (bf16[128,3072]{0,1:T(8,128)(2,1)}, bf16[128,1024]{1,0:T(8,128)(2,1)}, bf16[128,4096]{1,0:T(8,128)(2,1)}, bf16[512,1024]{1,0:T(8,128)(2,1)}) async-done(((bf16[128,3072]{0,1:T(8,128)(2,1)}, bf16[128,1024]{1,0:T(8,128)(2,1)}, bf16[128,4096]{1,0:T(8,128)(2,1)}, bf16[512,1024]{1,0:T(8,128)(2,1)}), (bf16[128,3072]{0,1:T(8,128)(2,1)}, bf16[128,1024]{1,0:T(8,128)(2,1)}, ...) | async-done | bytes 3145744 | tf_op jit(solution)/shard_map/psum | solution.py:291
  (266 shorter events, 357.7 us)
Async XLA Ops:
  7.2 658.1 %copy-start = (bf16[1024,1024]{1,0:T(8,128)(2,1)S(1)}, bf16[1024,1024]{1,0:T(8,128)(2,1)}, u32[]{:S(2)}) copy-start(bf16[1024,1024]{1,0:T(8,128)(2,1)} %param.26) | copy-start | bytes 6291460
  9.5 9.2 copy-start.20
  12.4 7.0 copy-start.22
  32.8 7.1 copy-start.4
  39.9 36.6 %all-to-all-start = ((bf16[4,5,64,1024]{3,2,1,0:T(8,128)(2,1)}), bf16[4,5,64,1024]{3,2,1,0:T(8,128)(2,1)}, u32[]{:S(2)}, u32[]{:S(2)}) async-start(bf16[4,5,64,1024]{3,2,1,0:T(8,128)(2,1)} %get-tuple-element.172), calls=%async_computation | async-start | bytes 5242880 | tf_op jit(solution)/shard_map/all_to_all | solution.py:139
  44.5 36.5 %copy-start.15 = (s32[320,320]{1,0:T(8,128)S(1)}, s32[320,320]{1,0:T(8,128)}, u32[]{:S(2)}) copy-start(s32[320,320]{1,0:T(8,128)} %param.22) | copy-start | bytes 1228804
  76.5 35.9 %all-to-all-start.2 = ((bf16[4,5,64,1024]{3,2,1,0:T(8,128)(2,1)}), bf16[4,5,64,1024]{3,2,1,0:T(8,128)(2,1)}, u32[]{:S(2)}, u32[]{:S(2)}) async-start(bf16[4,5,64,1024]{3,2,1,0:T(8,128)(2,1)} %slice.53), calls=%async_computation.2 | async-start | bytes 5242880 | tf_op jit(solution)/shard_map/all_to_all | solution.py:138
  112.4 390.9 %all-to-all-start.1 = ((bf16[4,5,64,1024]{3,2,1,0:T(8,128)(2,1)}), bf16[4,5,64,1024]{3,2,1,0:T(8,128)(2,1)}, u32[]{:S(2)}, u32[]{:S(2)}) async-start(bf16[4,5,64,1024]{3,2,1,0:T(8,128)(2,1)} %get-tuple-element.171), calls=%async_computation.1 | async-start | bytes 5242880 | tf_op jit(solution)/shard_map/all_to_all | solution.py:137
  454.6 34.4 %copy-start.30 = (s32[1,20]{1,0:T(1,128)S(1)}, s32[1,20]{1,0:T(1,128)}, u32[]{:S(2)}) copy-start(s32[1,20]{1,0:T(1,128)} %param.21) | copy-start | bytes 244
  589.9 14.2 copy-start.18
  624.1 7.7 copy-start.52
  624.1 7.7 copy-start.53
  624.1 7.7 copy-start.39
  624.1 7.7 copy-start.26
  627.0 36.1 %all-to-all-start.3 = ((bf16[4,5,64,1024]{3,2,1,0:T(8,128)(2,1)}), bf16[4,5,64,1024]{3,2,1,0:T(8,128)(2,1)}, u32[]{:S(2)}, u32[]{:S(2)}) async-start(bf16[4,5,64,1024]{3,2,1,0:T(8,128)(2,1)} %bitcast.200), calls=%async_computation.3 | async-start | bytes 5242880 | tf_op jit(solution)/shard_map/all_to_all | solution.py:163
  631.8 33.5 %copy-start.35 = (f32[1024]{0:T(1024)S(1)}, f32[1024]{0:T(1024)}, u32[]{:S(2)}) copy-start(f32[1024]{0:T(1024)} %get-tuple-element.182) | copy-start | bytes 12292
  665.3 6.6 copy-start.9
  672.0 19.7 copy-start.6
  672.0 71.8 %copy-start.31 = (f32[1280]{0:T(1024)}, f32[1280]{0:T(1024)S(1)}, u32[]{:S(2)}) copy-start(f32[1280]{0:T(1024)S(1)} %broadcast_multiply_fusion.4) | copy-start | bytes 15364
  672.7 71.1 %copy-start.40 = (f32[1280]{0:T(1024)}, f32[1280]{0:T(1024)S(1)}, u32[]{:S(2)}) copy-start(f32[1280]{0:T(1024)S(1)} %add_rsqrt_fusion) | copy-start | bytes 15364
  672.7 19.0 copy-start.14
  723.7 20.1 copy-start.5
  776.9 6.6 copy-start.16
  778.8 36.1 %all-to-all-start.4 = ((bf16[4,5,64,1024]{3,2,1,0:T(8,128)(2,1)}), bf16[4,5,64,1024]{3,2,1,0:T(8,128)(2,1)}, u32[]{:S(2)}, u32[]{:S(2)}) async-start(bf16[4,5,64,1024]{3,2,1,0:T(8,128)(2,1)} %bitcast.201), calls=%async_computation.4 | async-start | bytes 5242880 | tf_op jit(solution)/shard_map/all_to_all | solution.py:196
  831.4 10.7 copy-start.19
  906.7 312.8 %all-to-all-start.7 = ((bf16[4,5,64,1024]{3,2,1,0:T(8,128)(2,1)}), bf16[4,5,64,1024]{3,2,1,0:T(8,128)(2,1)}, u32[]{:S(2)}, u32[]{:S(2)}) async-start(bf16[4,5,64,1024]{3,2,1,0:T(8,128)(2,1)} %bitcast.197), calls=%async_computation.7 | async-start | bytes 5242880 | tf_op jit(solution)/shard_map/all_to_all | solution.py:227
  911.3 490.5 %reduce-scatter.14.cloned.1.call-start = ((), (), s32[]{:S(2)}) async-start(), calls=%async_computation.17 | async-start | bytes 147456 | tf_op jit(solution)/shard_map/reduce_scatter | solution.py:288
  1177.8 339.6 %reduce-scatter.8.cloned.1.call-start = ((), (), s32[]{:S(2)}) async-start(), calls=%async_computation.14 | async-start | bytes 4718592 | tf_op jit(solution)/shard_map/reduce_scatter | solution.py:282
  1219.5 37.9 %all-to-all-start.5 = ((bf16[4,5,64,1024]{3,2,1,0:T(8,128)(2,1)}), bf16[4,5,64,1024]{3,2,1,0:T(8,128)(2,1)}, u32[]{:S(2)}, u32[]{:S(2)}) async-start(bf16[4,5,64,1024]{3,2,1,0:T(8,128)(2,1)} %bitcast.198), calls=%async_computation.5 | async-start | bytes 5242880 | tf_op jit(solution)/shard_map/all_to_all | solution.py:225
  1254.4 8.0 copy-start.21
  1254.4 8.0 copy-start.23
  1254.5 8.0 copy-start.25
  1254.5 8.0 copy-start.29
  1257.4 36.0 %all-to-all-start.6 = ((bf16[4,5,64,1024]{3,2,1,0:T(8,128)(2,1)}), bf16[4,5,64,1024]{3,2,1,0:T(8,128)(2,1)}, u32[]{:S(2)}, u32[]{:S(2)}) async-start(bf16[4,5,64,1024]{3,2,1,0:T(8,128)(2,1)} %bitcast.199), calls=%async_computation.6 | async-start | bytes 5242880 | tf_op jit(solution)/shard_map/all_to_all | solution.py:226
  1262.0 284.5 %reduce-scatter.6.cloned.1.call-start = ((), (), s32[]{:S(2)}) async-start(), calls=%async_computation.13 | async-start | bytes 14155776 | tf_op jit(solution)/shard_map/reduce_scatter | solution.py:279
  1295.5 6.6 copy-start.10
  1313.7 519.7 %reduce-scatter.10.cloned.1.call-start = ((), (), s32[]{:S(2)}) async-start(), calls=%async_computation.15 | async-start | bytes 18874368 | tf_op jit(solution)/shard_map/reduce_scatter | solution.py:284
  1333.6 785.1 %reduce-scatter.12.cloned.1.call-start = ((), (), s32[]{:S(2)}) async-start(), calls=%async_computation.16 | async-start | bytes 18874368 | tf_op jit(solution)/shard_map/reduce_scatter | solution.py:286
  1351.5 47.5 %copy-start.27 = (f32[1024]{0:T(1024)S(1)}, f32[1024]{0:T(1024)}, u32[]{:S(2)}) copy-start(f32[1024]{0:T(1024)} %get-tuple-element.177) | copy-start | bytes 12292
  1351.6 55.3 %copy-start.36 = (f32[1024]{0:T(1024)S(1)}, f32[1024]{0:T(1024)}, u32[]{:S(2)}) copy-start(f32[1024]{0:T(1024)} %get-tuple-element.166) | copy-start | bytes 12292
  1351.6 55.3 %copy-start.37 = (f32[4096]{0:T(1024)S(1)}, f32[4096]{0:T(1024)}, u32[]{:S(2)}) copy-start(f32[4096]{0:T(1024)} %get-tuple-element.164) | copy-start | bytes 49156
  1351.6 839.0 %all-reduce.10.cloned.1.call-start = ((), (), s32[]{:S(2)}) async-start(), calls=%async_computation.18 | async-start | bytes 6291456 | tf_op jit(solution)/shard_map/psum | solution.py:291
  1467.3 7.8 copy-start.49
  1467.3 7.8 copy-start.47
  1467.3 7.8 copy-start.46
  1467.4 7.8 copy-start.48
  2124.6 74.7 %copy-start.1 = (bf16[1024,1024]{1,0:T(8,128)(2,1)S(1)}, bf16[1024,1024]{1,0:T(8,128)(2,1)}, u32[]{:S(2)}) copy-start(bf16[1024,1024]{1,0:T(8,128)(2,1)} %param.26) | copy-start | bytes 6291460
  2190.6 7.2 copy-start.17
  (21 other events, 65.8 us)
Sparse Core Ops, SparseCore 0:
  1177.9 63.7 reduce-scatter.13
  1245.4 87.1 reduce-scatter.7
  1336.6 209.7 reduce-scatter.5
  1550.5 282.8 reduce-scatter.9
  1837.0 281.6 reduce-scatter.11
  2122.5 67.9 all-reduce.9
where the time goes:
time: 2220 us; the launch traced here: 2210 us
  waiting for transfers between devices  790 us (36%)
  local copies, waits for them, and re-layouts  605 us (27%)
  matrix products  505 us (23%)
  blocking collectives  133 us (6%)
  other arithmetic  119 us (5%)
  starting transfers between devices  38 us (2%)
    gather x2, local copies, waits for them, and re-layouts, local(): pos_bias = jnp.transpose(rel_table[rel_index], (2, 0, 1))  371 us
    reduce_scatter x1, waiting for transfers between devices, local(): lax.psum_scatter(grad_w_up, 'clip', scatter_dimension=0, tiled=True)  285 us
    reduce_scatter x1, waiting for transfers between devices, local(): lax.psum_scatter(grad_w_down, 'clip', scatter_dimension=0, tiled=True)  283 us
    dot_general x10, matrix products, add_block(): jnp.dot(piece, onehot, preferred_element_type=jnp.float32)  183 us
    psum x1, waiting for transfers between devices, local(): lax.psum(shares[0].astype(jnp.bfloat16), 'win').astype(jnp.float32)  57.9 us
    all_gather x1, blocking collectives, local(): lax.all_gather(lifted.astype(jnp.float32), ('clip', 'win'), axis=0, tiled...  44.9 us
  transfers between devices with their start and end apart: 14, of which 9 were waited for; matrix products, arithmetic and copies ran while one was open for 39% of the time, Pallas kernels for 0%

commit v1 on v0

v1 whole, which is shorter than its diff:
```python
import functools
import math

import jax
import jax.numpy as jnp
from jax import lax
from jax.experimental import pallas as pl
from jax.experimental.pallas import tpu as pltpu
from jax.sharding import PartitionSpec as P

HEAD = 64
FRAMES = 5
WST = 8
PIECE = WST * WST
UNIT = 256
LANES = 128
VMEM_LIMIT = 60 * 1024 * 1024
f32 = jnp.float32
bf16 = jnp.bfloat16
GELU_C = math.sqrt(2.0 / math.pi)
GELU_A = 0.044715


def dot_nn(a, b):
    return jnp.dot(a, b, preferred_element_type=f32)


def dot_nt(a, b):
    return lax.dot_general(a, b, (((1,), (1,)), ((), ())), preferred_element_type=f32)


def dot_tn(a, b):
    return lax.dot_general(a, b, (((0,), (0,)), ((), ())), preferred_element_type=f32)


def params():
    return pltpu.CompilerParams(vmem_limit_bytes=VMEM_LIMIT)


def cost(micros):
    return pl.CostEstimate(
        flops=int(micros * 1.0e9), bytes_accessed=int(micros * 2.0e6), transcendentals=0
    )


def hat_of(rows):
    average = jnp.mean(rows, axis=-1, keepdims=True)
    centered = rows - average
    variance = jnp.mean(centered * centered, axis=-1, keepdims=True)
    inv_std = lax.rsqrt(variance + 1e-06)
    return centered * inv_std, inv_std


def norm_back(grad_hat, hat_rows, inv_std):
    first_mean = jnp.mean(grad_hat, axis=-1, keepdims=True)
    second_mean = jnp.mean(grad_hat * hat_rows, axis=-1, keepdims=True)
    return inv_std * (grad_hat - first_mean - hat_rows * second_mean)


def whole(shape):
    zeros = (0,) * len(shape)
    return pl.BlockSpec(shape, lambda *unused: zeros, pipeline_mode=pl.Buffered(1))


def bias_kernel(idx_ref, tab_ref, out_ref, scr_ref):
    lows = lax.broadcasted_iota(jnp.int32, (256, idx_ref.shape[1]), 0)
    tab = tab_ref[...]
    half = tab.shape[0] // 2
    heads = 16
    tiles = idx_ref.shape[1] // LANES
    win = out_ref.shape[2] // 2
    for i in range(8):
        idx = idx_ref[pl.ds(i, 1), :]
        low = idx & 255
        high = idx >> 8
        onehot = jnp.where(lows == low, 1.0, 0.0).astype(bf16)
        got = dot_nn(tab, onehot)
        got = got[:half] + got[half:]
        acc = got[:heads]
        for c in range(1, half // heads):
            acc = jnp.where(high == c, got[c * heads : (c + 1) * heads], acc)
        for t in range(tiles):
            scr_ref[t, pl.ds(i, heads, stride=8), :] = acc[:, t * LANES : (t + 1) * LANES]
    for pair in range(heads // 2):
        rows = []
        for h in range(2):
            at = (2 * pair + h) * 8
            rows.append(
                jnp.concatenate([scr_ref[t, at : at + 8, :] for t in range(tiles)], axis=1)[:, :win]
            )
        out_ref[pair] = jnp.concatenate(rows, axis=1)


def bias_gather(idx, table):
    rows, win = idx.shape
    padded = -(-win // LANES) * LANES
    buckets, heads = table.shape
    upper_f = lax.reduce_precision(table, 8, 7)
    lower = (table - upper_f).astype(bf16)

    def arrange(t):
        return t.reshape(-1, 256, heads).transpose(0, 2, 1).reshape(-1, 256)

    tab = jnp.concatenate([arrange(upper_f.astype(bf16)), arrange(lower)], axis=0)
    idx = jnp.pad(idx, ((0, 0), (0, padded - win)))
    return pl.pallas_call(
        bias_kernel,
        grid=(rows // 8,),
        in_specs=[pl.BlockSpec((8, padded), lambda i: (i, 0)), whole(tab.shape)],
        out_specs=pl.BlockSpec((heads // 2, 8, 2 * win), lambda i: (0, i, 0)),
        out_shape=jax.ShapeDtypeStruct((heads // 2, rows, 2 * win), f32),
        scratch_shapes=[pltpu.VMEM((padded // LANES, 8 * heads, LANES), f32)],
        name="bias_gather",
        compiler_params=params(),
        cost_estimate=cost(18),
    )(idx, tab)


def bucket_kernel(idx_ref, ss_ref, out_ref, acc_ref, scr_ref):
    @pl.when(pl.program_id(0) == 0)
    def _():
        acc_ref[...] = jnp.zeros_like(acc_ref)

    padded = idx_ref.shape[1]
    tiles = padded // LANES
    pairs = ss_ref.shape[0]
    heads = 2 * pairs
    win = ss_ref.shape[2] // 2
    lows = lax.broadcasted_iota(jnp.int32, (256, padded), 0)
    zero = jnp.zeros((8, padded - win), f32)
    for pair in range(pairs):
        sums = ss_ref[pair]
        for h in range(2):
            part = jnp.concatenate([sums[:, h * win : (h + 1) * win], zero], axis=1)
            at = (2 * pair + h) * 8
            for t in range(tiles):
                scr_ref[t, at : at + 8, :] = part[:, t * LANES : (t + 1) * LANES]
    total = acc_ref[...]
    for i in range(8):
        idx = idx_ref[pl.ds(i, 1), :]
        low = idx & 255
        high = idx >> 8
        onehot = jnp.where(lows == low, 1.0, 0.0).astype(bf16)
        sums = jnp.concatenate(
            [scr_ref[t, pl.ds(i, heads, stride=8), :] for t in range(tiles)], axis=1
        )
        spread = jnp.concatenate(
            [jnp.where(high == c, sums, 0.0) for c in range(acc_ref.shape[0] // heads)], axis=0
        )
        total += dot_nt(spread.astype(bf16), onehot)
    acc_ref[...] = total
    out_ref[...] = total


def bucket_sums(idx, sums, buckets):
    rows, win = idx.shape
    padded = -(-win // LANES) * LANES
    heads = 2 * sums.shape[0]
    idx = jnp.pad(idx, ((0, 0), (0, padded - win)))
    out_rows = buckets // 256 * heads
    out = pl.pallas_call(
        bucket_kernel,
        grid=(rows // 8,),
        in_specs=[
            pl.BlockSpec((8, padded), lambda i: (i, 0)),
            pl.BlockSpec((heads // 2, 8, 2 * win), lambda i: (0, i, 0)),
        ],
        out_specs=pl.BlockSpec((out_rows, 256), lambda i: (0, 0)),
        out_shape=jax.ShapeDtypeStruct((out_rows, 256), f32),
        scratch_shapes=[
            pltpu.VMEM((out_rows, 256), f32),
            pltpu.VMEM((padded // LANES, 8 * heads, LANES), f32),
        ],
        name="bucket_sums",
        compiler_params=params(),
        cost_estimate=cost(18),
    )(idx, sums)
    return out.reshape(-1, heads, 256)


def qkv_kernel(src_ref, a_ref, b_ref, c_ref, d_ref, mod_ref, bias_ref, w_ref, x_ref, n_ref, o_ref):
    rows = jnp.concatenate([r[0] for r in (a_ref, b_ref, c_ref, d_ref)], axis=0)
    x_ref[...] = rows
    hat_rows, unused = hat_of(rows.astype(f32))
    normed = (hat_rows * (1.0 + mod_ref[1:2, :]) + mod_ref[0:1, :]).astype(bf16)
    n_ref[...] = normed
    features = rows.shape[1]
    for j in range(w_ref.shape[1] // 512):
        cols = slice(j * 512, (j + 1) * 512)
        got = dot_nn(normed, w_ref[:, cols]) + bias_ref[0:1, cols]
        if (j + 1) * 512 <= features:
            got = got.astype(bf16).astype(f32) * (1.0 / math.sqrt(HEAD))
        o_ref[:, cols] = got.astype(bf16)


def slot_spec(features, t):
    return pl.BlockSpec((1, PIECE, features), lambda i, src, t=t: (src[4 * i + t], 0, 0))


def qkv_call(src, pieces, mod, qkv_bias, w_qkv):
    count, unused, features = pieces.shape
    rows = count * PIECE
    wide = w_qkv.shape[1]
    block = 4 * PIECE
    return pl.pallas_call(
        qkv_kernel,
        grid_spec=pltpu.PrefetchScalarGridSpec(
            num_scalar_prefetch=1,
            grid=(count // 4,),
            in_specs=[slot_spec(features, t) for t in range(4)]
            + [whole(mod.shape), whole(qkv_bias.shape), whole(w_qkv.shape)],
            out_specs=[
                pl.BlockSpec((block, features), lambda i, src: (i, 0)),
                pl.BlockSpec((block, features), lambda i, src: (i, 0)),
                pl.BlockSpec((block, wide), lambda i, src: (i, 0)),
            ],
        ),
        out_shape=[
            jax.ShapeDtypeStruct((rows, features), bf16),
            jax.ShapeDtypeStruct((rows, features), bf16),
            jax.ShapeDtypeStruct((rows, wide), bf16),
        ],
        name="norm_qkv",
        compiler_params=params(),
        cost_estimate=cost(12),
    )(src, pieces, pieces, pieces, pieces, mod, qkv_bias, w_qkv)


def split_pair(x, left):
    zero = jnp.zeros_like(x)
    return jnp.concatenate([jnp.where(left, x, zero), jnp.where(left, zero, x)], axis=0)


def values_ones(v, left):
    one = jnp.ones_like(v)
    zero = jnp.zeros_like(v)
    marks = jnp.concatenate([jnp.where(left, one, zero), jnp.where(left, zero, one)], axis=0)
    return jnp.concatenate([split_pair(v, left), marks], axis=1)


def attn_kernel(windows, core_ref, q_ref, k_ref, v_ref, mine_ref, other_ref, o_ref, p_ref, r_ref, b_ref):
    win = q_ref.shape[0] // windows
    half = win // 2
    left = lax.broadcasted_iota(jnp.int32, (win, LANES), 1) < HEAD
    first = core_ref[0] == 0
    b_ref[:half] = jnp.where(first, mine_ref[0], other_ref[0])
    b_ref[half:] = jnp.where(first, other_ref[0], mine_ref[0])
    lowest = jnp.float32(-jnp.inf)
    whole_tiles = win // LANES * LANES
    for u in range(windows):
        rows = slice(u * win, (u + 1) * win)
        keys = split_pair(k_ref[rows], left)
        vals = values_ones(v_ref[rows], left)
        s = dot_nt(q_ref[rows], keys) + b_ref[...]
        lo = s[:, :whole_tiles]
        mid = s[:, whole_tiles : whole_tiles + LANES]
        hi = s[:, whole_tiles + LANES :]
        top_lo = jnp.where(left, mid, lowest)
        top_hi = jnp.where(left, lowest, mid)
        for t in range(whole_tiles // LANES):
            cols = slice(t * LANES, (t + 1) * LANES)
            top_lo = jnp.maximum(top_lo, lo[:, cols])
            top_hi = jnp.maximum(top_hi, hi[:, cols])
        top_lo = jnp.max(top_lo, axis=1, keepdims=True)
        top_hi = jnp.max(top_hi, axis=1, keepdims=True)
        e = jnp.concatenate(
            [
                jnp.exp(lo - top_lo),
                jnp.exp(mid - jnp.where(left, top_lo, top_hi)),
                jnp.exp(hi - top_hi),
            ],
            axis=1,
        ).astype(bf16)
        p_ref[0, u] = e
        got = dot_nn(e, vals)
        r = 1.0 / got[:, LANES:]
        r_ref[rows] = r
        o_ref[rows] = (got[:, :LANES] * r).astype(bf16)


def attn_forward(core, qkv, bias_mine, bias_other, windows):
    rows = qkv.shape[0]
    win = rows // windows
    pairs = bias_mine.shape[0]
    features = qkv.shape[1] // 3

    def col(part):
        return pl.BlockSpec((rows, LANES), lambda h, c, part=part: (0, part * pairs + h))

    half_spec = pl.BlockSpec((1, win // 2, 2 * win), lambda h, c: (h, 0, 0))
    return pl.pallas_call(
        functools.partial(attn_kernel, windows),
        grid_spec=pltpu.PrefetchScalarGridSpec(
            num_scalar_prefetch=1,
            grid=(pairs,),
            in_specs=[col(0), col(1), col(2), half_spec, half_spec],
            out_specs=[
                col(0),
                pl.BlockSpec((1, windows, win, 2 * win), lambda h, c: (h, 0, 0, 0)),
                col(0),
            ],
            scratch_shapes=[pltpu.VMEM((win, 2 * win), f32)],
        ),
        out_shape=[
            jax.ShapeDtypeStruct((rows, features), bf16),
            jax.ShapeDtypeStruct((pairs, windows, win, 2 * win), bf16),
            jax.ShapeDtypeStruct((rows, features), f32),
        ],
        name="attn_forward",
        compiler_params=params(),
        cost_estimate=cost(18),
    )(core, qkv, qkv, qkv, bias_mine, bias_other)


def fold_delta(dx, lane):
    lower_half = (lane & 32) == 0
    dx = dx + jnp.where(lower_half, pltpu.roll(dx, LANES - 32, 1), pltpu.roll(dx, 32, 1))
    upper = dx.astype(bf16)
    lower = (dx - upper.astype(f32)).astype(bf16)
    return jnp.where(lower_half, upper, lower)


def attn_back_kernel(windows, q_ref, k_ref, v_ref, o_ref, do_ref, p_ref, r_ref, dq_ref, dk_ref, dv_ref, ss_ref):
    win = q_ref.shape[0] // windows
    lane = lax.broadcasted_iota(jnp.int32, (win, LANES), 1)
    left = lane < HEAD
    sums = None
    for u in range(windows):
        rows = slice(u * win, (u + 1) * win)
        keys = split_pair(k_ref[rows], left)
        vals = values_ones(v_ref[rows], left)
        up = (do_ref[rows].astype(f32) * r_ref[rows]).astype(bf16)
        delta = fold_delta(-(up.astype(f32) * o_ref[rows].astype(f32)), lane)
        d = dot_nt(jnp.concatenate([up, delta], axis=1), vals)
        p = p_ref[0, u]
        ds = p.astype(f32) * d
        sums = ds if sums is None else sums + ds
        low = ds.astype(bf16)
        dq_ref[rows] = (dot_nn(low, keys) * (1.0 / math.sqrt(HEAD))).astype(bf16)
        dk = dot_tn(low, q_ref[rows])
        dk_ref[rows] = jnp.where(left, dk[:win], dk[win:]).astype(bf16)
        dv = dot_tn(p, up)
        dv_ref[rows] = jnp.where(left, dv[:win], dv[win:]).astype(bf16)
    ss_ref[0] = sums


def attn_backward(qkv, attended, grad_att, probs, recips, windows, first, count):
    rows = qkv.shape[0]
    win = rows // windows
    pairs = probs.shape[0]

    def col(part):
        return pl.BlockSpec((rows, LANES), lambda h, part=part: (0, part * pairs + first + h))

    own = pl.BlockSpec((rows, LANES), lambda h: (0, h))
    grad_shape = jax.ShapeDtypeStruct((rows, count * LANES), bf16)
    return pl.pallas_call(
        functools.partial(attn_back_kernel, windows),
        grid=(count,),
        in_specs=[
            col(0),
            col(1),
            col(2),
            col(0),
            col(0),
            pl.BlockSpec((1, windows, win, 2 * win), lambda h: (first + h, 0, 0, 0)),
            col(0),
        ],
        out_specs=[own, own, own, pl.BlockSpec((1, win, 2 * win), lambda h: (h, 0, 0))],
        out_shape=[
            grad_shape,
            grad_shape,
            grad_shape,
            jax.ShapeDtypeStruct((count, win, 2 * win), f32),
        ],
        name="attn_backward",
        compiler_params=params(),
        cost_estimate=cost(3 * count),
    )(qkv, qkv, qkv, attended, grad_att, probs, recips)


def out_kernel(src_ref, a_ref, b_ref, c_ref, d_ref, att_ref, x_ref, mod_ref, bo_ref, w_ref, branch_ref, n_ref, gm_ref):
    branch = (dot_nn(att_ref[...], w_ref[...]) + bo_ref[...]).astype(bf16)
    branch_ref[...] = branch
    residual = x_ref[...].astype(f32) + mod_ref[2:3, :] * branch.astype(f32)
    hat_rows, unused = hat_of(residual)
    n_ref[...] = (hat_rows * (1.0 + mod_ref[4:5, :]) + mod_ref[3:4, :]).astype(bf16)
    up = jnp.concatenate([r[0] for r in (a_ref, b_ref, c_ref, d_ref)], axis=0)
    gm_ref[...] = (mod_ref[5:6, :] * up.astype(f32)).astype(bf16)


def out_call(src, pieces, attended, x_rows, mod, b_out, w_out):
    count, unused, features = pieces.shape
    rows = count * PIECE
    block = 4 * PIECE
    rows_spec = pl.BlockSpec((block, features), lambda i, src: (i, 0))
    sds = jax.ShapeDtypeStruct((rows, features), bf16)
    return pl.pallas_call(
        out_kernel,
        grid_spec=pltpu.PrefetchScalarGridSpec(
            num_scalar_prefetch=1,
            grid=(count // 4,),
            in_specs=[slot_spec(features, t) for t in range(4)]
            + [rows_spec, rows_spec, whole(mod.shape), whole(b_out.shape), whole(w_out.shape)],
            out_specs=[rows_spec, rows_spec, rows_spec],
        ),
        out_shape=[sds, sds, sds],
        name="out_norm",
        compiler_params=params(),
        cost_estimate=cost(6),
    )(src, pieces, pieces, pieces, pieces, attended, x_rows, mod, b_out, w_out)


def turn_kernel(order_ref, swap_ref, x_ref, out_ref):
    turned = x_ref[...].T
    half = turned.shape[0] // 2
    swap = swap_ref[0] == 1
    upper, lower = turned[:half], turned[half:]
    out_ref[0] = jnp.where(swap, lower, upper)
    out_ref[1] = jnp.where(swap, upper, lower)


def turn(order, swap, rows):
    count, features = rows.shape
    out = pl.pallas_call(
        turn_kernel,
        grid_spec=pltpu.PrefetchScalarGridSpec(
            num_scalar_prefetch=2,
            grid=(features // LANES,),
            in_specs=[pl.BlockSpec((count, LANES), lambda i, order, swap: (0, order[i]))],
            out_specs=pl.BlockSpec((2, LANES // 2, count), lambda i, order, swap: (0, i, 0)),
        ),
        out_shape=jax.ShapeDtypeStruct((2, features // 2, count), bf16),
        name="turn",
        compiler_params=params(),
        cost_estimate=cost(4),
    )(order, swap, rows)
    return out.reshape(features, count)


def ff_step(n_ref, gm_ref, nt_ref, gt_ref, wu_ref, bu_ref, wd_ref, up_refs, down_refs, bsum_ref, mixed_ref, back_ref, act_ref, gh_ref, first):
    rows = n_ref.shape[0]
    block = UNIT
    sums = None
    for c in range(rows // block):
        part = slice(c * block, (c + 1) * block)
        v = dot_nn(n_ref[part], wu_ref[...]) + bu_ref[0]
        v2 = v * v
        t = jnp.tanh(v * (GELU_C + (GELU_C * GELU_A) * v2))
        h = 0.5 + 0.5 * t
        act = (v * h).astype(bf16)
        slope = h + (0.5 * v) * (1.0 - t * t) * (GELU_C + (3.0 * GELU_C * GELU_A) * v2)
        gh = (dot_nt(gm_ref[part], wd_ref[...]) * slope).astype(bf16)
        act_ref[part] = act
        gh_ref[part] = gh
        piece = jnp.sum(gh.astype(f32), axis=0, keepdims=True)
        sums = piece if sums is None else sums + piece
        mixed = dot_nn(act, wd_ref[...])
        back = dot_nt(gh, wu_ref[...])

        @pl.when(first)
        def _():
            mixed_ref[part] = mixed
            back_ref[part] = back

        @pl.when(jnp.logical_not(first))
        def _():
            mixed_ref[part] += mixed
            back_ref[part] += back

    bsum_ref[0] = sums
    half = nt_ref.shape[0] // 2
    for k in range(2):
        part = slice(k * half, (k + 1) * half)
        up_refs[k][...] = dot_nn(nt_ref[part], gh_ref[...]).astype(bf16)
        down_refs[k][0] = dot_nn(gt_ref[part], act_ref[...]).astype(bf16)


def ff_first_kernel(fo_ref, co_ref, n_ref, gm_ref, nt_ref, gt_ref, wu_ref, bu_ref, wd_ref, u0, u1, d0, d1, bsum_ref, pm_ref, pb_ref, mixed_ref, back_ref, act_ref, gh_ref):
    step = pl.program_id(0)
    ff_step(n_ref, gm_ref, nt_ref, gt_ref, wu_ref, bu_ref, wd_ref, (u0, u1), (d0, d1), bsum_ref, mixed_ref, back_ref, act_ref, gh_ref, step == 0)

    @pl.when(step == pl.num_programs(0) - 1)
    def _():
        pm_ref[...] = mixed_ref[...].astype(bf16)
        pb_ref[...] = back_ref[...].astype(bf16)


def ff_specs(units, rows, features, fast):
    def clamp(i):
        return jnp.minimum(i, units - 1)

    ins = [
        whole((rows, features)),
        whole((rows, features)),
        whole((features, rows)),
        whole((features, rows)),
        pl.BlockSpec((features, UNIT), lambda i, fo, co, *more: (0, fo[clamp(i)])),
        pl.BlockSpec((1, 1, UNIT), lambda i, fo, co, *more: (fo[clamp(i)], 0, 0)),
        pl.BlockSpec((UNIT, features), lambda i, fo, co, *more: (fo[clamp(i)], 0)),
    ]
    up = pl.BlockSpec((features // 2, UNIT), lambda i, fo, co, *more: (0, co[clamp(i)]))
    down = pl.BlockSpec((1, features // 2, UNIT), lambda i, fo, co, *more: (clamp(i), 0, 0))
    outs = [up, up, down, down, pl.BlockSpec((1, 1, UNIT), lambda i, fo, co, *more: (co[clamp(i)], 0, 0))]
    shapes = [
        jax.ShapeDtypeStruct((features // 2, units * UNIT), bf16),
        jax.ShapeDtypeStruct((features // 2, units * UNIT), bf16),
        jax.ShapeDtypeStruct((units, features // 2, UNIT), bf16),
        jax.ShapeDtypeStruct((units, features // 2, UNIT), bf16),
        jax.ShapeDtypeStruct((units, 1, UNIT), f32),
    ]
    scratch = [
        pltpu.VMEM((rows, features), f32),
        pltpu.VMEM((rows, features), f32),
        pltpu.VMEM((rows, UNIT), bf16),
        pltpu.VMEM((rows, UNIT), bf16),
    ]
    return ins, outs, shapes, scratch


def ff_first(fo, co, normed, grad_mixed, normed_t, grad_t, w_up, b_up, w_down):
    units = fo.shape[0]
    rows, features = normed.shape
    ins, outs, shapes, scratch = ff_specs(units, rows, features, True)
    once = pl.BlockSpec((rows, features), lambda i, fo, co: (0, 0), pipeline_mode=pl.Buffered(1))
    return pl.pallas_call(
        ff_first_kernel,
        grid_spec=pltpu.PrefetchScalarGridSpec(
            num_scalar_prefetch=2,
            grid=(units,),
            in_specs=ins,
            out_specs=outs + [once, once],
            scratch_shapes=scratch,
        ),
        out_shape=shapes + [jax.ShapeDtypeStruct((rows, features), bf16)] * 2,
        name="ff_first",
        compiler_params=params(),
        cost_estimate=cost(40),
    )(fo, co, normed, grad_mixed, normed_t, grad_t, w_up, b_up, w_down)


def ff_second_kernel(units, fo_ref, co_ref, src_ref, n_ref, gm_ref, nt_ref, gt_ref, wu_ref, bu_ref, wd_ref, a_ref, b_ref, c_ref, d_ref, x_ref, branch_ref, pm_ref, pb_ref, mod_ref, bd_ref, u0, u1, d0, d1, bsum_ref, gres_ref, vec_ref, out_ref, mixed_ref, back_ref, act_ref, gh_ref, stage_ref, sem_ref):
    step = pl.program_id(0)

    @pl.when(step < units)
    def _():
        ff_step(n_ref, gm_ref, nt_ref, gt_ref, wu_ref, bu_ref, wd_ref, (u0, u1), (d0, d1), bsum_ref, mixed_ref, back_ref, act_ref, gh_ref, step == 0)

    @pl.when(step >= units)
    def _():
        e = step - units
        block = 4 * PIECE
        part = pl.ds(pl.multiple_of(e * block, block), block)
        mixed = mixed_ref[part] + pm_ref[...].astype(f32) + bd_ref[...]
        back = back_ref[part] + pb_ref[...].astype(f32)
        branch = branch_ref[...].astype(f32)
        gate_one = mod_ref[2:3, :]
        gate_two = mod_ref[5:6, :]
        residual = x_ref[...].astype(f32) + gate_one * branch
        hat_rows, inv_std = hat_of(residual)
        up = jnp.concatenate([r[0] for r in (a_ref, b_ref, c_ref, d_ref)], axis=0).astype(f32)
        block_out = (residual + gate_two * mixed).astype(bf16)
        stage_ref[part] = block_out
        for t in range(4):
            pltpu.make_async_copy(
                stage_ref.at[pl.ds(pl.multiple_of(e * block + t * PIECE, PIECE), PIECE)],
                out_ref.at[src_ref[4 * e + t]],
                sem_ref.at[4 * e + t],
            ).start()
        gres = up + norm_back(back * (1.0 + mod_ref[4:5, :]), hat_rows, inv_std)
        low = gres.astype(bf16)
        gres_ref[...] = low
        grad_branch = (gate_one * low.astype(f32)).astype(bf16).astype(f32)
        grad_mixed = (gate_two * up).astype(bf16).astype(f32)

        def total(values):
            return jnp.sum(values, axis=0, keepdims=True)

        pieces = jnp.concatenate(
            [
                total(gres * branch),
                total(back),
                total(back * hat_rows),
                total(up * mixed),
                total(grad_branch),
                total(grad_mixed),
                jnp.zeros((2, gate_one.shape[1]), f32),
            ],
            axis=0,
        )

        @pl.when(e == 0)
        def _():
            vec_ref[...] = pieces

        @pl.when(e > 0)
        def _():
            vec_ref[...] += pieces

    @pl.when(step == pl.num_programs(0) - 1)
    def _():
        for k in range(sem_ref.shape[0]):
            pltpu.make_async_copy(
                stage_ref.at[pl.ds(k * PIECE, PIECE)], out_ref.at[src_ref[k]], sem_ref.at[k]
            ).wait()


def ff_second(fo, co, src, normed, grad_mixed, normed_t, grad_t, w_up, b_up, w_down, pieces, x_rows, branch, part_mixed, part_back, mod, b_down):
    units = fo.shape[0]
    rows, features = normed.shape
    ins, outs, shapes, scratch = ff_specs(units, rows, features, True)
    block = 4 * PIECE

    def late(i):
        return jnp.maximum(i - units, 0)

    rows_spec = pl.BlockSpec((block, features), lambda i, *more: (late(i), 0))
    slots = [
        pl.BlockSpec((1, PIECE, features), lambda i, fo, co, src, t=t: (src[4 * late(i) + t], 0, 0))
        for t in range(4)
    ]
    return pl.pallas_call(
        functools.partial(ff_second_kernel, units),
        grid_spec=pltpu.PrefetchScalarGridSpec(
            num_scalar_prefetch=3,
            grid=(units + rows // block,),
            in_specs=ins
            + slots
            + [rows_spec, rows_spec, rows_spec, rows_spec, whole(mod.shape), whole(b_down.shape)],
            out_specs=outs
            + [
                rows_spec,
                pl.BlockSpec((8, features), lambda i, *more: (0, 0)),
                pl.BlockSpec(memory_space=pl.ANY),
            ],
            scratch_shapes=scratch
            + [pltpu.VMEM((rows, features), bf16), pltpu.SemaphoreType.DMA((rows // PIECE,))],
        ),
        out_shape=shapes
        + [
            jax.ShapeDtypeStruct((rows, features), bf16),
            jax.ShapeDtypeStruct((8, features), f32),
            jax.ShapeDtypeStruct(pieces.shape, bf16),
        ],
        name="ff_second",
        compiler_params=params(),
        cost_estimate=cost(50),
    )(fo, co, src, normed, grad_mixed, normed_t, grad_t, w_up, b_up, w_down, pieces, pieces, pieces, pieces, x_rows, branch, part_mixed, part_back, mod, b_down)


def out_back_kernel(blocks, gres_ref, mod_ref, w_ref, at_ref, do_ref, g0, g1, gb_ref):
    step = pl.program_id(0)

    @pl.when(step < blocks)
    def _():
        block = gres_ref.shape[0]
        low = (mod_ref[2:3, :] * gres_ref[...].astype(f32)).astype(bf16)
        gb_ref[pl.ds(pl.multiple_of(step * block, block), block)] = low
        do_ref[...] = dot_nt(low, w_ref[...]).astype(bf16)

    @pl.when(step >= blocks)
    def _():
        width = g0.shape[1]
        cols = pl.ds(pl.multiple_of((step - blocks) * width, width), width)
        half = g0.shape[0]
        right = gb_ref[:, cols]
        g0[...] = dot_nn(at_ref[:half], right).astype(bf16)
        g1[...] = dot_nn(at_ref[half:], right).astype(bf16)


def out_backward(gres, mod, w_out, attended_t):
    rows, features = gres.shape
    block = 4 * PIECE
    blocks = rows // block
    rows_spec = pl.BlockSpec((block, features), lambda i: (jnp.minimum(i, blocks - 1), 0))
    col_spec = pl.BlockSpec((features // 2, UNIT), lambda i: (0, jnp.maximum(i - blocks, 0)))
    grad = jax.ShapeDtypeStruct((features // 2, features), bf16)
    return pl.pallas_call(
        functools.partial(out_back_kernel, blocks),
        grid=(blocks + features // UNIT,),
        in_specs=[rows_spec, whole(mod.shape), whole(w_out.shape), whole(attended_t.shape)],
        out_specs=[rows_spec, col_spec, col_spec],
        out_shape=[jax.ShapeDtypeStruct((rows, features), bf16), grad, grad],
        scratch_shapes=[pltpu.VMEM((rows, features), bf16)],
        name="out_backward",
        compiler_params=params(),
        cost_estimate=cost(8),
    )(gres, mod, w_out, attended_t)


def qkv_weight_kernel(per, nt_ref, q_ref, k_ref, v_ref, g0, g1):
    step = pl.program_id(0)
    half = g0.shape[0]
    for part, ref in enumerate((q_ref, k_ref, v_ref)):

        @pl.when(step // per == part)
        def _(ref=ref):
            g0[...] = dot_nn(nt_ref[:half], ref[...]).astype(bf16)
            g1[...] = dot_nn(nt_ref[half:], ref[...]).astype(bf16)


def qkv_weight(normed_t, dq, dk, dv):
    features, rows = normed_t.shape
    wide = dq.shape[1]
    per = wide // UNIT

    def col(part):
        return pl.BlockSpec((rows, UNIT), lambda i: (0, jnp.clip(i - part * per, 0, per - 1)))

    out_spec = pl.BlockSpec((features // 2, UNIT), lambda i: (0, i))
    grad = jax.ShapeDtypeStruct((features // 2, 3 * wide), bf16)
    return pl.pallas_call(
        functools.partial(qkv_weight_kernel, per),
        grid=(3 * per,),
        in_specs=[whole(normed_t.shape), col(0), col(1), col(2)],
        out_specs=[out_spec, out_spec],
        out_shape=[grad, grad],
        name="qkv_weight",
        compiler_params=params(),
        cost_estimate=cost(5),
    )(normed_t, dq, dk, dv)


def qkv_back_kernel(src_ref, *refs):
    count = (len(refs) - 8) // 3
    grads = refs[: 3 * count]
    w_ref, x_ref, gres_ref, mod_ref, out_ref, vec_ref, stage_ref, sem_ref = refs[3 * count :]
    step = pl.program_id(0)
    block = x_ref.shape[0]
    features = x_ref.shape[1]
    back = None
    bias = []
    for part in range(3):
        pieces = [grads[part * count + k][...] for k in range(count)]
        joined = jnp.concatenate(pieces, axis=1)
        bias.append(jnp.sum(joined.astype(f32), axis=0, keepdims=True))
        got = dot_nt(joined, w_ref[:, part * features : (part + 1) * features])
        back = got if back is None else back + got
    back = back.astype(bf16).astype(f32)
    hat_rows, inv_std = hat_of(x_ref[...].astype(f32))
    grad = gres_ref[...].astype(f32) + norm_back(back * (1.0 + mod_ref[1:2, :]), hat_rows, inv_std)
    stage_ref[pl.ds(pl.multiple_of(step * block, block), block)] = grad.astype(bf16)
    for t in range(4):
        pltpu.make_async_copy(
            stage_ref.at[pl.ds(pl.multiple_of(step * block + t * PIECE, PIECE), PIECE)],
            out_ref.at[src_ref[4 * step + t]],
            sem_ref.at[4 * step + t],
        ).start()
    pieces = jnp.concatenate(
        [
            jnp.sum(back, axis=0, keepdims=True),
            jnp.sum(back * hat_rows, axis=0, keepdims=True),
            bias[0],
            bias[2],
            jnp.zeros((4, features), f32),
        ],
        axis=0,
    )

    @pl.when(step == 0)
    def _():
        vec_ref[...] = pieces

    @pl.when(step > 0)
    def _():
        vec_ref[...] += pieces

    @pl.when(step == pl.num_programs(0) - 1)
    def _():
        for k in range(sem_ref.shape[0]):
            pltpu.make_async_copy(
                stage_ref.at[pl.ds(k * PIECE, PIECE)], out_ref.at[src_ref[k]], sem_ref.at[k]
            ).wait()


def qkv_backward(src, grads, w_qkv, x_rows, gres, mod):
    rows, features = x_rows.shape
    block = 4 * PIECE
    rows_spec = pl.BlockSpec((block, features), lambda i, src: (i, 0))
    grad_specs = [
        pl.BlockSpec((block, g.shape[1]), lambda i, src: (i, 0)) for part in grads for g in part
    ]
    flat = [g for part in grads for g in part]
    return pl.pallas_call(
        qkv_back_kernel,
        grid_spec=pltpu.PrefetchScalarGridSpec(
            num_scalar_prefetch=1,
            grid=(rows // block,),
            in_specs=grad_specs + [whole(w_qkv.shape), rows_spec, rows_spec, whole(mod.shape)],
            out_specs=[
                pl.BlockSpec(memory_space=pl.ANY),
                pl.BlockSpec((8, features), lambda i, src: (0, 0)),
            ],
            scratch_shapes=[
                pltpu.VMEM((rows, features), bf16),
                pltpu.SemaphoreType.DMA((rows // PIECE,)),
            ],
        ),
        out_shape=[
            jax.ShapeDtypeStruct((rows // PIECE, PIECE, features), bf16),
            jax.ShapeDtypeStruct((8, features), f32),
        ],
        name="qkv_backward",
        compiler_params=params(),
        cost_estimate=cost(12),
    )(src, *flat, w_qkv, x_rows, gres, mod)


def flip(axis, bit):
    size = lax.axis_size(axis)
    return [(i, i ^ (1 << bit)) for i in range(size)]


def trade(array, axis, bit):
    return lax.ppermute(array, axis, flip(axis, bit))


def add_low(a, b):
    return (a.astype(f32) + b.astype(f32)).astype(bf16)


def reduce_relative(own, partner, clip_bits):
    got = trade(partner, "win", 0)
    half = own.shape[0] // 2
    for bit in range(clip_bits):
        keep = add_low(own[:half], got[:half])
        send = add_low(own[half:], got[half:])
        got = trade(send, "clip", bit)
        own = keep
        half //= 2
    own = add_low(own, got)
    got = trade(own, "win", 1)
    own = lax.reduce_precision(own.astype(f32) + got.astype(f32), 8, 7).astype(bf16)
    own = lax.optimization_barrier(own)
    other = trade(own, "win", 0)
    return own[0], other[0]


def ordered(core, own, other, axis):
    first = jnp.where(core == 0, own, other)
    second = jnp.where(core == 0, other, own)
    return jnp.stack([first, second], axis=axis).astype(f32)


def sum_over_win(vector):
    bits = lax.axis_size("win").bit_length() - 1
    for bit in range(bits):
        vector = vector + trade(vector, "win", bit)
    return vector


def gather_clip(vector):
    bits = lax.axis_size("clip").bit_length() - 1
    me = lax.axis_index("clip")
    rows = vector[None]
    for bit in range(bits):
        got = trade(rows, "clip", bit)
        upper = (me >> bit) & 1 == 1
        rows = jnp.where(upper, jnp.concatenate([got, rows]), jnp.concatenate([rows, got]))
    return rows


def to_quadrants(slot_rows):
    local_slots = slot_rows.shape[0]
    channels = slot_rows.shape[-1]
    arranged = slot_rows.reshape(local_slots, 2, WST, 2, WST, channels).transpose(1, 3, 0, 2, 4, 5)
    return arranged.reshape(4, local_slots, PIECE, channels)


def from_quadrants(received):
    local_slots = received.shape[1]
    channels = received.shape[-1]
    arranged = received.reshape(2, 2, local_slots, WST, WST, channels).transpose(2, 0, 3, 1, 4, 5)
    return arranged.reshape(local_slots, 4 * PIECE, channels)


def exchange(quadrants):
    return lax.all_to_all(quadrants, "win", split_axis=0, concat_axis=0, tiled=True)


def local(
    tokens,
    condition,
    slot_order,
    rel_index,
    w_qkv,
    b_query,
    b_value,
    w_out,
    b_out,
    w_up,
    b_up,
    w_down,
    b_down,
    w_ada,
    b_ada,
    rel_table,
    grad_out,
):
    features = tokens.shape[-1]
    clips = lax.axis_size("clip")
    clip_bits = clips.bit_length() - 1
    me = lax.axis_index("clip")
    core = lax.axis_index("win") & 1
    ff = w_up.shape[1]
    fast = features // clips == LANES and ff // clips == 2 * UNIT

    pieces = exchange(to_quadrants(tokens[0])).reshape(-1, PIECE, features)
    grad_pieces = exchange(to_quadrants(grad_out[0])).reshape(-1, PIECE, features)
    slots = pieces.shape[0]
    per_frame = slots // FRAMES
    order_row = slot_order[0]
    window_place = jnp.arange(slots, dtype=jnp.int32)
    wanted = (window_place % FRAMES) * per_frame + window_place // FRAMES
    src = jnp.sum(
        jnp.where(order_row[None, :] == wanted[:, None], window_place[None, :], 0), axis=1
    ).astype(jnp.int32)
    windows = per_frame
    win = FRAMES * PIECE

    half = win // 2
    idx_mine = lax.dynamic_slice_in_dim(rel_index, core * half, half, 0)
    bias_mine = bias_gather(idx_mine, rel_table)
    bias_other = trade(bias_mine, "win", 0)

    lifted = jax.nn.silu(condition.astype(f32)).astype(bf16)
    modulation = jnp.dot(lifted, w_ada, preferred_element_type=f32)[0] + b_ada
    mod = jnp.concatenate([modulation.reshape(6, features), jnp.zeros((2, features), f32)])

    qkv_bias = jnp.concatenate([b_query, jnp.zeros_like(b_query), b_value]).astype(f32)[None]
    x_rows, normed, qkv = qkv_call(src, pieces, mod, qkv_bias, w_qkv)
    core_arr = core.astype(jnp.int32)[None]
    attended, probs, recips = attn_forward(core_arr, qkv, bias_mine, bias_other, windows)
    branch, normed_two, grad_mixed = out_call(
        src, grad_pieces, attended, x_rows, mod, b_out.astype(f32)[None], w_out
    )

    places = jnp.arange(clips, dtype=jnp.int32)
    units = ff // (2 * UNIT)
    unit_places = jnp.arange(units, dtype=jnp.int32)
    identity = jnp.arange(features // LANES, dtype=jnp.int32)
    if fast:
        reverse = jnp.zeros_like(places)
        for bit in range(clip_bits):
            reverse = reverse | (((places >> (clip_bits - 1 - bit)) & 1) << bit)
        relative = me ^ reverse
        fo_first, fo_second = 2 * relative, 2 * relative + 1
        co_first = co_second = relative
        turn_rel = functools.partial(turn, relative, core_arr)
        turn_abs = functools.partial(turn, identity, core_arr)
    else:
        fo_first, fo_second = unit_places, unit_places + units
        co_first = co_second = unit_places
        turn_rel = turn_abs = lambda rows: rows.T
    normed_t = turn_rel(normed)
    attended_t = turn_rel(attended)
    normed_two_t = turn_rel(normed_two)
    grad_mixed_t = turn_abs(grad_mixed)
    b_up_rows = b_up.astype(f32).reshape(-1, 1, UNIT)
    up_a0, up_a1, down_a0, down_a1, bsum_a, part_mixed, part_back = ff_first(
        fo_first, co_first, normed_two, grad_mixed, normed_two_t, grad_mixed_t, w_up, b_up_rows, w_down
    )
    up_b0, up_b1, down_b0, down_b1, bsum_b, gres, early, out_pieces = ff_second(
        fo_second, co_second, src, normed_two, grad_mixed, normed_two_t, grad_mixed_t,
        w_up, b_up_rows, w_down, grad_pieces, x_rows, branch, part_mixed, part_back,
        mod, b_down.astype(f32)[None],
    )
    local_slots = tokens.shape[1]
    piece_shape = (-1, local_slots, PIECE, features)
    block_out = from_quadrants(exchange(out_pieces.reshape(piece_shape))).reshape(tokens.shape)

    grad_att, out_g0, out_g1 = out_backward(gres, mod, w_out, attended_t)
    pairs = probs.shape[0]
    dq_a, dk_a, dv_a, ss_a = attn_backward(qkv, attended, grad_att, probs, recips, windows, 0, pairs // 2)
    qkv_a0, qkv_a1 = qkv_weight(normed_t, dq_a, dk_a, dv_a)
    dq_b, dk_b, dv_b, ss_b = attn_backward(
        qkv, attended, grad_att, probs, recips, windows, pairs // 2, pairs // 2
    )
    qkv_b0, qkv_b1 = qkv_weight(normed_t, dq_b, dk_b, dv_b)
    token_pieces, late = qkv_backward(
        src, ((dq_a, dq_b), (dk_a, dk_b), (dv_a, dv_b)), w_qkv, x_rows, gres, mod
    )
    grad_tokens = from_quadrants(exchange(token_pieces.reshape(piece_shape))).reshape(tokens.shape)

    scores = jnp.concatenate([ss_a, ss_b], axis=0)
    send_scores = lax.dynamic_slice_in_dim(scores, (1 - core) * half, half, 1)
    keep_scores = lax.dynamic_slice_in_dim(scores, core * half, half, 1)
    keep_scores = keep_scores + trade(send_scores, "win", 0)
    buckets = rel_table.shape[0]
    rel_sums = sum_over_win(bucket_sums(idx_mine, keep_scores, buckets))
    heads = rel_sums.shape[1]
    rel_rows = buckets // clips
    rel_sums = rel_sums.transpose(0, 2, 1).reshape(clips, rel_rows, heads)
    for bit in reversed(range(clip_bits)):
        side = (me >> bit) & 1
        parts = rel_sums.reshape(2, -1, rel_rows, heads)
        keep = lax.dynamic_index_in_dim(parts, side, 0, keepdims=False)
        send = lax.dynamic_index_in_dim(parts, 1 - side, 0, keepdims=False)
        rel_sums = keep + trade(send, "clip", bit)
    sum_rel = rel_sums[0]

    grad_b_up = jnp.stack([bsum_a.reshape(-1, UNIT), bsum_b.reshape(-1, UNIT)], axis=1 if fast else 0).reshape(-1)
    early_vec = sum_over_win(jnp.concatenate([early[:6].reshape(-1), grad_b_up]))
    late_vec = sum_over_win(late[:4].reshape(-1))
    early_all = gather_clip(jnp.concatenate([early_vec, lifted[0].astype(f32)]))
    late_all = gather_clip(late_vec)
    d = features
    all_terms = jnp.concatenate([late_all[:, : 2 * d], early_all[:, : 4 * d]], axis=1)
    all_lifted = early_all[:, 6 * d + ff :]

    def own_block(vector):
        size = vector.shape[0] // clips
        return lax.dynamic_slice_in_dim(vector, me * size, size, 0)

    early_sum = jnp.sum(early_all[:, 4 * d : 6 * d + ff], axis=0)
    late_sum = jnp.sum(late_all[:, 2 * d :], axis=0)
    sum_bo, sum_bd, sum_bu = own_block(early_sum[:d]), own_block(early_sum[d : 2 * d]), own_block(early_sum[2 * d :])
    sum_bq, sum_bv = own_block(late_sum[:d]), own_block(late_sum[d:])
    ada_rows = d // clips
    lifted_rows = lax.dynamic_slice_in_dim(all_lifted, me * ada_rows, ada_rows, 1)
    grad_w_ada = jnp.dot(lifted_rows.T, all_terms, precision=lax.Precision.HIGHEST)
    grad_b_ada = own_block(jnp.sum(all_terms, axis=0))

    if fast:

        def rows_of(a, b):
            shape = (clips, d // clips // 2, -1)
            own, other = reduce_relative(a.reshape(shape), b.reshape(shape), clip_bits)
            return ordered(core, own, other, 0).reshape(d // clips, -1)

        def turned(a, b):
            own, other = reduce_relative(a, b, clip_bits)
            both = ordered(core, own.reshape(d // LANES, LANES // 2, UNIT), other.reshape(d // LANES, LANES // 2, UNIT), 1)
            return both.reshape(d, UNIT).T

        up_a = rows_of(up_a0, up_a1)
        down_a = turned(down_a0, down_a1)
        up_b = rows_of(up_b0, up_b1)
        down_b = turned(down_b0, down_b1)
        sum_wo = rows_of(out_g0, out_g1)
        qkv_a = rows_of(qkv_a0, qkv_a1)
        qkv_b = rows_of(qkv_b0, qkv_b1)
        rows = d // clips
        sum_wu = jnp.stack([up_a.reshape(rows, -1, UNIT), up_b.reshape(rows, -1, UNIT)], axis=2).reshape(rows, ff)
        sum_wd = jnp.concatenate([down_a, down_b], axis=0)
        sum_qkv = jnp.stack(
            [qkv_a.reshape(rows, 3, d // 2), qkv_b.reshape(rows, 3, d // 2)], axis=2
        ).reshape(rows, 3 * d)
    else:

        def share(whole_grad):
            part = lax.psum_scatter(whole_grad.astype(f32), "clip", scatter_dimension=0, tiled=True)
            return lax.psum(part, "win")

        def natural(a, b):
            return jnp.concatenate([a, b], axis=0)

        def down_natural(a, b):
            return jnp.concatenate([a, b], axis=1).transpose(0, 2, 1).reshape(-1, d)

        sum_wu = share(jnp.concatenate([natural(up_a0, up_a1), natural(up_b0, up_b1)], axis=1))
        sum_wd = share(jnp.concatenate([down_natural(down_a0, down_a1), down_natural(down_b0, down_b1)], axis=0))
        sum_wo = share(natural(out_g0, out_g1))
        qkv_a = natural(qkv_a0, qkv_a1).reshape(d, 3, d // 2)
        qkv_b = natural(qkv_b0, qkv_b1).reshape(d, 3, d // 2)
        sum_qkv = share(jnp.stack([qkv_a, qkv_b], axis=2).reshape(d, 3 * d))
    return (
        block_out,
        grad_tokens,
        sum_qkv,
        sum_bq,
        sum_bv,
        sum_wo,
        sum_bo,
        sum_wu,
        sum_bu,
        sum_wd,
        sum_bd,
        grad_w_ada,
        grad_b_ada,
        sum_rel,
    )


def solution(mesh):
    placed = (
        P("clip", "win", None, None),
        P("clip", None),
        P("clip", None),
    ) + (P(),) * 13 + (P("clip", "win", None, None),)
    return jax.shard_map(
        local,
        mesh=mesh,
        in_specs=placed,
        out_specs=(
            P("clip", "win", None, None),
            P("clip", "win", None, None),
            P("clip", None),
            P("clip"),
            P("clip"),
            P("clip", None),
            P("clip"),
            P("clip", None),
            P("clip"),
            P("clip", None),
            P("clip"),
            P("clip", None),
            P("clip"),
            P("clip", None),
        ),
        check_vma=False,
    )
```

time: 2220 us -> 738 us (0.33)
  waiting for transfers between devices: 790 us -> 218 us
  local copies, waits for them, and re-layouts: 605 us -> 50.6 us
  matrix products: 505 us -> 10.8 us
  Pallas kernels: 0 us -> 324 us
  blocking collectives: 133 us -> 0 us
  other arithmetic: 119 us -> 49.7 us
  starting transfers between devices: 38 us -> 73.4 us
    reduce_scatter x5 -> x0, waiting for transfers between devices: 594 us -> none  [the longest x1 285 us: local(): lax.psum_scatter(grad_w_up, 'clip', scatter_dimension=0, tiled=True)]
    dot_general x40 -> x1, matrix products: 484 us -> 6.46 us  [local(): modulation = jnp.dot(lifted, w_ada, preferred_element_type=f32)[0] + b_ada]
    gather x2 -> x0, local copies, waits for them, and re-layouts: 371 us -> none  [local(): pos_bias = jnp.transpose(rel_table[rel_index], (2, 0, 1))]
    pallas_call x0 -> x17, Pallas kernels: none -> 324 us  [the longest x1 74.6 us: ff_second(): pl.pallas_call(functools.partial(ff_second_kernel, units), grid_spec=pltp...]
    ppermute x0 -> x59, waiting for transfers between devices: none -> 212 us  [trade(): return lax.ppermute(array, axis, flip(axis, bit))]
    all_to_all x8 -> x4, waiting for transfers between devices: 137 us -> 5.94 us  [exchange(): lax.all_to_all(quadrants, 'win', split_axis=0, concat_axis=0, tiled=True)]
    all_gather x2 -> x0, blocking collectives: 86.2 us -> none  [the longest x1 44.9 us: local(): lax.all_gather(lifted.astype(jnp.float32), ('clip', 'win'), axis=0, tiled...]
    another operation x9 -> x0, local copies, waits for them, and re-layouts: 83 us -> none  [the longest x2 20.6 us: local(): value_heads = values.reshape(head_shape)]
  transfers between devices with their start and end apart: 14 -> 63, of which waited for: 9 -> 29; matrix products, arithmetic and copies ran while one was open for 39% -> 13% of each run, Pallas kernels for 0% -> 12%
where the time goes in v1:
time: 738 us; the launch traced here: 728 us
  Pallas kernels  324 us (44%)
  waiting for transfers between devices  218 us (30%)
  starting transfers between devices  73.4 us (10%)
  local copies, waits for them, and re-layouts  50.6 us (7%)
  other arithmetic  49.7 us (7%)
  matrix products  10.8 us (1%)
    ppermute x59, waiting for transfers between devices, trade(): return lax.ppermute(array, axis, flip(axis, bit))  212 us
    pallas_call x1, Pallas kernels, ff_second(): pl.pallas_call(functools.partial(ff_second_kernel, units), grid_spec=pltp...  74.6 us
    pallas_call x1, Pallas kernels, ff_first(): pl.pallas_call(ff_first_kernel, grid_spec=pltpu.PrefetchScalarGridSpec(nu...  64.1 us
    ppermute x59, starting transfers between devices, trade(): return lax.ppermute(array, axis, flip(axis, bit))  56.3 us
    convert_element_type x28, other arithmetic, add_low(): return (a.astype(f32) + b.astype(f32)).astype(bf16)  33.6 us
    pallas_call x4, Pallas kernels, turn(): pl.pallas_call(turn_kernel, grid_spec=pltpu.PrefetchScalarGridSpec(num_sc...  28.2 us
    pallas_call x2, Pallas kernels, attn_backward(): pl.pallas_call(functools.partial(attn_back_kernel, windows), grid=(count,...  26.9 us
    pallas_call x1, Pallas kernels, bias_gather(): pl.pallas_call(bias_kernel, grid=(rows // 8,), in_specs=[pl.BlockSpec((8,...  19.1 us
  transfers between devices with their start and end apart: 63, of which 29 were waited for; matrix products, arithmetic and copies ran while one was open for 13% of the time, Pallas kernels for 12%

profile of v1, /device:TPU:0, one launch (start us, length us, event | category | flops | bytes accessed | tf_op | source)
XLA Modules:
  0.0 728.3 jit_solution(16600177308765825665)
XLA Ops:
  4.3 4.7 all-to-all-start.1
  10.5 19.1 %bias_gather.1.mine_ref = f32[8,160,640]{2,1,0:T(8,128)} custom-call(s32[160,384]{1,0:T(8,128)} %pad.6.idx_ref, bf16[256,256]{1,0:T(8,128)(2,1)} %pad_maximum_fusion.9.tab_ref), custom_call_target="tpu_custom_call" | custom-call | flops 17999998976 | bytes 36000000 | tf_op jit(solution)/shard_map/bias_gather/pallas_call | solution.py:106
  30.1 6.5 fusion.15
  44.0 3.9 all-to-all-start
  47.8 16.0 %norm_qkv.1 = (bf16[1280,1024]{1,0:T(8,128)(2,1)}, bf16[1280,1024]{1,0:T(8,128)(2,1)}, bf16[1280,3072]{1,0:T(8,128)(2,1)}) custom-call(s32[20]{0:T(128)} %select_reduce_fusion.src_ref, bf16[20,64,1024]{2,1,0:T(8,128)(2,1)} %bitcast.9.a_ref.b_ref.c_ref.d_ref, bf16[20,64,1024]{2,1,0:T(8,128)(2,1)} %bitcast.9.a_ref.b_ref.c_ref.d_ref, ...), custom_call_target="tpu_custom_call" | custom-call | flops 12000000000 | bytes 24000000 | tf_op jit(solution)/shard_map/norm_qkv/pallas_call | solution.py:205
  63.9 7.1 turn.7
  70.9 17.7 %attn_forward.1 = (bf16[1280,1024]{1,0:T(8,128)(2,1)}, bf16[8,4,320,640]{3,2,1,0:T(8,128)(2,1)}, f32[1280,1024]{1,0:T(8,128)}) custom-call(s32[1]{0:T(128)} %bitcast.5.core_ref.swap_ref, bf16[1280,3072]{1,0:T(8,128)(2,1)} %get-tuple-element.55.q_ref.k_ref.v_ref, bf16[1280,3072]{1,0:T(8,128)(2,1)} %get-tuple-element.55.q_ref.k_ref.v_ref, ...), custom_call_target="tpu_custom_call" | custom-call | flops 17999998976 | bytes 36000000 | tf_op jit(solution)/shard_map/attn_forward/pallas_call | solution.py:291
  88.7 7.1 turn.6
  97.2 10.8 %out_norm.1 = (bf16[1280,1024]{1,0:T(8,128)(2,1)}, bf16[1280,1024]{1,0:T(8,128)(2,1)}, bf16[1280,1024]{1,0:T(8,128)(2,1)}) custom-call(s32[20]{0:T(128)} %select_reduce_fusion.src_ref, bf16[20,64,1024]{2,1,0:T(8,128)(2,1)} %bitcast.141, bf16[20,64,1024]{2,1,0:T(8,128)(2,1)} %bitcast.142, bf16[20,64,1024]{2,1,0:T(8,128)(2,1)} %bitcast.143, ...), custom_call_target="tpu_custom_call" | custom-call | flops 6000000000 | bytes 12000000 | tf_op jit(solution)/shard_map/out_norm/pallas_call | solution.py:398
  108.0 7.0 turn.4
  115.6 7.1 turn.5
  122.6 64.1 %ff_first.1 = (bf16[512,2048]{1,0:T(8,128)(2,1)}, bf16[512,2048]{1,0:T(8,128)(2,1)}, bf16[8,512,256]{2,1,0:T(8,128)(2,1)}, bf16[8,512,256]{2,1,0:T(8,128)(2,1)},...) custom-call(s32[8]{0:T(128)} %get-tuple-element.213.fo_ref, ...), custom_call_target="tpu_custom_call" | custom-call | flops 40000000000 | bytes 80000000 | tf_op jit(solution)/shard_map/ff_first/pallas_call | solution.py:526
  186.8 74.6 %ff_second.1 = (bf16[512,2048]{1,0:T(8,128)(2,1)}, bf16[512,2048]{1,0:T(8,128)(2,1)}, bf16[8,512,256]{2,1,0:T(8,128)(2,1)}, bf16[8,512,256]{2,1,0:T(8,128)(2,1)}...) custom-call(s32[8]{0:T(128)} %broadcast_add_fusion.fo_ref, ...), custom_call_target="tpu_custom_call" | custom-call | flops 49999998976 | bytes 100000000 | tf_op jit(solution)/shard_map/ff_second/pallas_call | solution.py:622
  261.4 12.0 %out_backward.1 = (bf16[1280,1024]{1,0:T(8,128)(2,1)}, bf16[512,1024]{1,0:T(8,128)(2,1)}, bf16[512,1024]{1,0:T(8,128)(2,1)}) custom-call(bf16[1280,1024]{1,0:T(8,128)(2,1)} %get-tuple-element.64.gres_ref.refs_8_, f32[8,1024]{1,0:T(8,128)} %concatenate.74.mod_ref.refs_9_, bf16[1024,1024]{1,0:T(8,128)(2,1)} %w_ref.5, bf16[1024,1280]{1,0:T(8,128)(2,1)} %bitcast.182), custom_call_target="tpu_custom_call" | custom-call | flops 8000000000 | bytes 16000000 | tf_op jit(solution)/shard_map/out_backward/pallas_call | solution.py:678
  273.4 13.6 %attn_backward.3 = (bf16[1280,512]{1,0:T(8,128)(2,1)}, bf16[1280,512]{1,0:T(8,128)(2,1)}, bf16[1280,512]{1,0:T(8,128)(2,1)}, f32[4,320,640]{2,1,0:T(8,128)}) custom-call(bf16[1280,3072]{1,0:T(8,128)(2,1)} %get-tuple-element.55.q_ref.k_ref.v_ref, bf16[1280,3072]{1,0:T(8,128)(2,1)} %get-tuple-element.55.q_ref.k_ref.v_ref, ...), custom_call_target="tpu_custom_call" | custom-call | flops 12000000000 | bytes 24000000 | tf_op jit(solution)/shard_map/attn_backward/pallas_call | solution.py:357
  286.9 13.4 %attn_backward.2 = (bf16[1280,512]{1,0:T(8,128)(2,1)}, bf16[1280,512]{1,0:T(8,128)(2,1)}, bf16[1280,512]{1,0:T(8,128)(2,1)}, f32[4,320,640]{2,1,0:T(8,128)}) custom-call(bf16[1280,3072]{1,0:T(8,128)(2,1)} %get-tuple-element.55.q_ref.k_ref.v_ref, bf16[1280,3072]{1,0:T(8,128)(2,1)} %get-tuple-element.55.q_ref.k_ref.v_ref, ...), custom_call_target="tpu_custom_call" | custom-call | flops 12000000000 | bytes 24000000 | tf_op jit(solution)/shard_map/attn_backward/pallas_call | solution.py:357
  300.3 9.2 %qkv_weight.2 = (bf16[512,1536]{1,0:T(8,128)(2,1)}, bf16[512,1536]{1,0:T(8,128)(2,1)}) custom-call(bf16[1024,1280]{1,0:T(8,128)(2,1)} %bitcast.180, bf16[1280,512]{1,0:T(8,128)(2,1)} %get-tuple-element.68.refs_0_.q_ref, bf16[1280,512]{1,0:T(8,128)(2,1)} %get-tuple-element.70.refs_2_.k_ref, bf16[1280,512]{1,0:T(8,128)(2,1)} %get-tuple-element.72.refs_4_.v_ref), custom_call_target="tpu_custom_call" | custom-call | flops 5000000000 | bytes 10000000 | tf_op jit(solution)/shard_map/qkv_weight/pallas_call | solution.py:712
  309.6 18.4 %qkv_backward.1 = (bf16[20,64,1024]{2,1,0:T(8,128)(2,1)}, f32[8,1024]{1,0:T(8,128)}) custom-call(s32[20]{0:T(128)} %select_reduce_fusion.src_ref, bf16[1280,512]{1,0:T(8,128)(2,1)} %get-tuple-element.68.refs_0_.q_ref, bf16[1280,512]{1,0:T(8,128)(2,1)} %get-tuple-element.69.refs_1_.q_ref, bf16[1280,512]{1,0:T(8,128)(2,1)} %get-tuple-element.70.refs_2_.k_ref, ...), custom_call_target="tpu_custom_call" | custom-call | flops 12000000000 | bytes 24000000 | tf_op jit(solution)/shard_map/qkv_backward/pallas_call | solution.py:784
  328.0 9.3 %qkv_weight.3 = (bf16[512,1536]{1,0:T(8,128)(2,1)}, bf16[512,1536]{1,0:T(8,128)(2,1)}) custom-call(bf16[1024,1280]{1,0:T(8,128)(2,1)} %bitcast.181, bf16[1280,512]{1,0:T(8,128)(2,1)} %get-tuple-element.69.refs_1_.q_ref, bf16[1280,512]{1,0:T(8,128)(2,1)} %get-tuple-element.71.refs_3_.k_ref, bf16[1280,512]{1,0:T(8,128)(2,1)} %get-tuple-element.73.refs_5_.v_ref), custom_call_target="tpu_custom_call" | custom-call | flops 5000000000 | bytes 10000000 | tf_op jit(solution)/shard_map/qkv_weight/pallas_call | solution.py:712
  349.2 3.9 all-to-all-start.3
  355.4 3.9 constant_dynamic-update-slice_fusion.1
  359.3 25.5 %collective-permute-done.14 = f32[4096]{0:T(1024)S(1)} collective-permute-done((f32[4096]{0:T(1024)S(1)}, f32[4096]{0:T(1024)S(1)}, u32[]{:S(2)}, u32[]{:S(2)}) %collective-permute-start.14) | collective-permute-done | bytes 16416 | tf_op jit(solution)/shard_map/ppermute | solution.py:815
  387.4 3.9 constant_dynamic-slice_fusion
  399.5 3.9 collective-permute-done.26
  417.7 7.5 %collective-permute-done.28 = f32[4,11264]{1,0:T(4,128)S(1)} collective-permute-done((f32[4,11264]{1,0:T(4,128)S(1)}, f32[4,11264]{1,0:T(4,128)S(1)}, u32[]{:S(2)}, u32[]{:S(2)}) %collective-permute-start.28) | collective-permute-done | bytes 180256 | tf_op jit(solution)/shard_map/ppermute | solution.py:815
  425.9 13.0 %collective-permute-done.19 = bf16[4,64,1024]{2,1,0:T(8,128)(2,1)S(1)} collective-permute-done((bf16[4,64,1024]{2,1,0:T(8,128)(2,1)S(1)}, bf16[4,64,1024]{2,1,0:T(8,128)(2,1)S(1)}, u32[]{:S(2)}, u32[]{:S(2)}) %collective-permute-start.19) | collective-permute-done | bytes 524320 | tf_op jit(solution)/shard_map/ppermute | solution.py:815
  440.7 4.6 all-to-all-start.2
  447.9 4.3 fusion.11
  471.2 5.9 all-to-all-done.2
  477.2 3.7 copy.90
  495.7 5.9 collective-permute-done.2
  502.2 16.2 %collective-permute-done.8 = bf16[4,64,1536]{2,1,0:T(8,128)(2,1)S(1)} collective-permute-done((bf16[4,64,1536]{2,1,0:T(8,128)(2,1)S(1)}, bf16[4,64,1536]{2,1,0:T(8,128)(2,1)S(1)}, u32[]{:S(2)}, u32[]{:S(2)}) %collective-permute-start.8) | collective-permute-done | bytes 786464 | tf_op jit(solution)/shard_map/ppermute | solution.py:815
  519.7 9.1 %collective-permute-done.3 = bf16[2,64,1536]{2,1,0:T(8,128)(2,1)S(1)} collective-permute-done((bf16[2,64,1536]{2,1,0:T(8,128)(2,1)S(1)}, bf16[2,64,1536]{2,1,0:T(8,128)(2,1)S(1)}, u32[]{:S(2)}, u32[]{:S(2)}) %collective-permute-start.3) | collective-permute-done | bytes 393248 | tf_op jit(solution)/shard_map/ppermute | solution.py:815
  529.9 8.3 %collective-permute-done.9 = bf16[2,64,1536]{2,1,0:T(8,128)(2,1)S(1)} collective-permute-done((bf16[2,64,1536]{2,1,0:T(8,128)(2,1)S(1)}, bf16[2,64,1536]{2,1,0:T(8,128)(2,1)S(1)}, u32[]{:S(2)}, u32[]{:S(2)}) %collective-permute-start.9) | collective-permute-done | bytes 393248 | tf_op jit(solution)/shard_map/ppermute | solution.py:815
  538.2 4.1 collective-permute-start.4
  542.4 6.0 collective-permute-done.4
  549.0 10.0 %collective-permute-done.10 = bf16[1,64,1536]{2,1,0:T(8,128)(2,1)S(1)} collective-permute-done((bf16[1,64,1536]{2,1,0:T(8,128)(2,1)S(1)}, bf16[1,64,1536]{2,1,0:T(8,128)(2,1)S(1)}, u32[]{:S(2)}, u32[]{:S(2)}) %collective-permute-start.10) | collective-permute-done | bytes 196640 | tf_op jit(solution)/shard_map/ppermute | solution.py:815
  560.9 25.0 %collective-permute-done.30 = bf16[4,64,2048]{2,1,0:T(8,128)(2,1)S(1)} collective-permute-done((bf16[4,64,2048]{2,1,0:T(8,128)(2,1)S(1)}, bf16[4,64,2048]{2,1,0:T(8,128)(2,1)S(1)}, u32[]{:S(2)}, u32[]{:S(2)}) %collective-permute-start.30) | collective-permute-done | bytes 1048608 | tf_op jit(solution)/shard_map/ppermute | solution.py:815
  593.1 14.8 %collective-permute-done.36 = bf16[4,64,2048]{2,1,0:T(8,128)(2,1)S(1)} collective-permute-done((bf16[4,64,2048]{2,1,0:T(8,128)(2,1)S(1)}, bf16[4,64,2048]{2,1,0:T(8,128)(2,1)S(1)}, u32[]{:S(2)}, u32[]{:S(2)}) %collective-permute-start.36) | collective-permute-done | bytes 1048608 | tf_op jit(solution)/shard_map/ppermute | solution.py:815
  611.9 17.6 %bucket_sums.1 = f32[128,256]{1,0:T(8,128)} custom-call(s32[160,384]{1,0:T(8,128)} %pad.6.idx_ref, f32[8,160,640]{2,1,0:T(8,128)} %dynamic-slice_add_fusion.ss_ref), custom_call_target="tpu_custom_call" | custom-call | flops 17999998976 | bytes 36000000 | tf_op jit(solution)/shard_map/bucket_sums/pallas_call | solution.py:161
  633.3 5.1 collective-permute-done.55
  641.2 4.1 collective-permute-done.56
  645.3 4.9 collective-permute-start.57
  668.3 21.7 %collective-permute-done.44 = bf16[1,512,256]{2,1,0:T(8,128)(2,1)S(1)} collective-permute-done((bf16[1,512,256]{2,1,0:T(8,128)(2,1)S(1)}, bf16[1,512,256]{2,1,0:T(8,128)(2,1)S(1)}, u32[]{:S(2)}, u32[]{:S(2)}) %collective-permute-start.44) | collective-permute-done | bytes 262176 | tf_op jit(solution)/shard_map/ppermute | solution.py:815
  691.2 4.4 collective-permute-done.50
  696.8 4.4 collective-permute-done.32
  709.5 4.8 collective-permute-done.39
  721.2 4.0 maximum_convert_fusion
  (326 shorter events, 154.2 us)
Async XLA Ops:
  4.3 39.7 %all-to-all-start.1 = ((bf16[4,5,64,1024]{3,2,1,0:T(8,128)(2,1)}), bf16[4,5,64,1024]{3,2,1,0:T(8,128)(2,1)}, u32[]{:S(2)}, u32[]{:S(2)}) async-start(bf16[4,5,64,1024]{3,2,1,0:T(8,128)(2,1)} %bitcast.8), calls=%async_computation.1 | async-start | bytes 5242880 | tf_op jit(solution)/shard_map/all_to_all | solution.py:878
  29.6 41.3 %collective-permute-start = (f32[8,160,640]{2,1,0:T(8,128)}, f32[8,160,640]{2,1,0:T(8,128)}, u32[]{:S(2)}, u32[]{:S(2)}) collective-permute-start(f32[8,160,640]{2,1,0:T(8,128)} %bias_gather.1.mine_ref), channel_id=1, source_target_pairs={{0,1},{1,0},{2,3},{3,2},{4,5},{5,4},{6,7},{7,6},{8,9},{9,8},{10,11... | collective-permute-start | bytes 9830408 | tf_op jit(solution)/shard_map/ppermute | solution.py:815
  44.0 51.8 %all-to-all-start = ((bf16[4,5,64,1024]{3,2,1,0:T(8,128)(2,1)}), bf16[4,5,64,1024]{3,2,1,0:T(8,128)(2,1)S(1)}, u32[]{:S(2)}, u32[]{:S(2)}) async-start(bf16[4,5,64,1024]{3,2,1,0:T(8,128)(2,1)} %bitcast.3), calls=%async_computation | async-start | bytes 5242880 | tf_op jit(solution)/shard_map/all_to_all | solution.py:878
  337.5 53.9 %collective-permute-start.24 = (f32[10240]{0:T(1024)S(1)}, f32[10240]{0:T(1024)S(1)}, u32[]{:S(2)}, u32[]{:S(2)}) collective-permute-start(f32[10240]{0:T(1024)S(1)} %constant_dynamic-update-slice_fusion.3), channel_id=1, source_target_pairs={{0,1},{1,0},{2,3},{3,2},{4,5},{5,4},{6,7},{7,6},{8,9},{9,8},{10,11... | collective-permute-start | bytes 122888 | tf_op jit(solution)/shard_map/ppermute | solution.py:815
  338.1 15.0 %collective-permute-start.13 = (f32[4096]{0:T(1024)S(1)}, f32[4096]{0:T(1024)S(1)}, u32[]{:S(2)}, u32[]{:S(2)}) collective-permute-start(f32[4096]{0:T(1024)S(1)} %bitcast.176), channel_id=1, source_target_pairs={{0,1},{1,0},{2,3},{3,2},{4,5},{5,4},{6,7},{7,6},{8,9},{9,8},{10,11... | collective-permute-start | bytes 49160 | tf_op jit(solution)/shard_map/ppermute | solution.py:815
  338.2 142.8 %collective-permute-start.41 = (bf16[8,512,256]{2,1,0:T(8,128)(2,1)}, bf16[8,512,256]{2,1,0:T(8,128)(2,1)}, u32[]{:S(2)}, u32[]{:S(2)}) collective-permute-start(bf16[8,512,256]{2,1,0:T(8,128)(2,1)} %get-tuple-element.91), channel_id=1, source_target_pairs={{0,1},{1,0},{2,3},{3,2},{4,5},{5,4},{6,7},{7,6},{8,9},{9,8},{10,11... | collective-permute-start | bytes 6291464 | tf_op jit(solution)/shard_map/ppermute | solution.py:815
  340.1 143.7 %collective-permute-start.29 = (bf16[8,64,2048]{2,1,0:T(8,128)(2,1)}, bf16[8,64,2048]{2,1,0:T(8,128)(2,1)}, u32[]{:S(2)}, u32[]{:S(2)}) collective-permute-start(bf16[8,64,2048]{2,1,0:T(8,128)(2,1)} %bitcast.44), channel_id=1, source_target_pairs={{0,1},{1,0},{2,3},{3,2},{4,5},{5,4},{6,7},{7,6},{8,9},{9,8},{10,11... | collective-permute-start | bytes 6291464 | tf_op jit(solution)/shard_map/ppermute | solution.py:815
  342.5 70.8 %collective-permute-start.18 = (bf16[8,64,1024]{2,1,0:T(8,128)(2,1)}, bf16[8,64,1024]{2,1,0:T(8,128)(2,1)}, u32[]{:S(2)}, u32[]{:S(2)}) collective-permute-start(bf16[8,64,1024]{2,1,0:T(8,128)(2,1)} %bitcast.39), channel_id=1, source_target_pairs={{0,1},{1,0},{2,3},{3,2},{4,5},{5,4},{6,7},{7,6},{8,9},{9,8},{10,11... | collective-permute-start | bytes 3145736 | tf_op jit(solution)/shard_map/ppermute | solution.py:815
  349.2 91.6 %all-to-all-start.3 = ((bf16[4,5,64,1024]{3,2,1,0:T(8,128)(2,1)}), bf16[4,5,64,1024]{3,2,1,0:T(8,128)(2,1)S(1)}, u32[]{:S(2)}, u32[]{:S(2)}) async-start(bf16[4,5,64,1024]{3,2,1,0:T(8,128)(2,1)} %bitcast.140), calls=%async_computation.3 | async-start | bytes 5242880 | tf_op jit(solution)/shard_map/all_to_all | solution.py:878
  353.1 31.7 %collective-permute-start.14 = (f32[4096]{0:T(1024)S(1)}, f32[4096]{0:T(1024)S(1)}, u32[]{:S(2)}, u32[]{:S(2)}) collective-permute-start(f32[4096]{0:T(1024)S(1)} %fusion.32), channel_id=1, source_target_pairs={{0,2},{1,3},{2,0},{3,1},{4,6},{5,7},{6,4},{7,5},{8,10},{9,11},{10,... | collective-permute-start | bytes 49160 | tf_op jit(solution)/shard_map/ppermute | solution.py:815
  391.3 62.3 %collective-permute-start.1 = (bf16[8,64,1536]{2,1,0:T(8,128)(2,1)}, bf16[8,64,1536]{2,1,0:T(8,128)(2,1)}, u32[]{:S(2)}, u32[]{:S(2)}) collective-permute-start(bf16[8,64,1536]{2,1,0:T(8,128)(2,1)} %bitcast.31), channel_id=1, source_target_pairs={{0,1},{1,0},{2,3},{3,2},{4,5},{5,4},{6,7},{7,6},{8,9},{9,8},{10,11... | collective-permute-start | bytes 4718600 | tf_op jit(solution)/shard_map/ppermute | solution.py:815
  413.2 51.2 %collective-permute-start.7 = (bf16[8,64,1536]{2,1,0:T(8,128)(2,1)}, bf16[8,64,1536]{2,1,0:T(8,128)(2,1)}, u32[]{:S(2)}, u32[]{:S(2)}) collective-permute-start(bf16[8,64,1536]{2,1,0:T(8,128)(2,1)} %bitcast.34), channel_id=1, source_target_pairs={{0,1},{1,0},{2,3},{3,2},{4,5},{5,4},{6,7},{7,6},{8,9},{9,8},{10,11... | collective-permute-start | bytes 4718600 | tf_op jit(solution)/shard_map/ppermute | solution.py:815
  413.3 11.9 %collective-permute-start.28 = (f32[4,11264]{1,0:T(4,128)S(1)}, f32[4,11264]{1,0:T(4,128)S(1)}, u32[]{:S(2)}, u32[]{:S(2)}) collective-permute-start(f32[4,11264]{1,0:T(4,128)S(1)} %maximum_select_fusion.1), channel_id=1, source_target_pairs={{0,16},{4,20},{8,24},{12,28},{16,0},{20,4},{24,8},{28,12},{1,17},{... | collective-permute-start | bytes 540680 | tf_op jit(solution)/shard_map/ppermute | solution.py:815
  425.2 13.6 %collective-permute-start.19 = (bf16[4,64,1024]{2,1,0:T(8,128)(2,1)S(1)}, bf16[4,64,1024]{2,1,0:T(8,128)(2,1)S(1)}, u32[]{:S(2)}, u32[]{:S(2)}) collective-permute-start(bf16[4,64,1024]{2,1,0:T(8,128)(2,1)S(1)} %get-tuple-element.187), channel_id=1, source_target_pairs={{0,4},{4,0},{8,12},{12,8},{16,20},{20,16},{24,28},{28,24},{1,5},{5... | collective-permute-start | bytes 1572872 | tf_op jit(solution)/shard_map/ppermute | solution.py:815
  439.8 12.5 %collective-permute-start.20 = (bf16[2,64,1024]{2,1,0:T(8,128)(2,1)}, bf16[2,64,1024]{2,1,0:T(8,128)(2,1)}, u32[]{:S(2)}, u32[]{:S(2)}) collective-permute-start(bf16[2,64,1024]{2,1,0:T(8,128)(2,1)} %get-tuple-element.185), channel_id=1, source_target_pairs={{0,8},{4,12},{8,0},{12,4},{16,24},{20,28},{24,16},{28,20},{1,9},{5... | collective-permute-start | bytes 786440 | tf_op jit(solution)/shard_map/ppermute | solution.py:815
  440.7 36.4 %all-to-all-start.2 = ((bf16[4,5,64,1024]{3,2,1,0:T(8,128)(2,1)}), bf16[4,5,64,1024]{3,2,1,0:T(8,128)(2,1)}, u32[]{:S(2)}, u32[]{:S(2)}) async-start(bf16[4,5,64,1024]{3,2,1,0:T(8,128)(2,1)} %bitcast.139), calls=%async_computation.2 | async-start | bytes 5242880 | tf_op jit(solution)/shard_map/all_to_all | solution.py:878
  452.2 35.6 %collective-permute-start.35 = (bf16[8,64,2048]{2,1,0:T(8,128)(2,1)}, bf16[8,64,2048]{2,1,0:T(8,128)(2,1)}, u32[]{:S(2)}, u32[]{:S(2)}) collective-permute-start(bf16[8,64,2048]{2,1,0:T(8,128)(2,1)} %bitcast.47), channel_id=1, source_target_pairs={{0,1},{1,0},{2,3},{3,2},{4,5},{5,4},{6,7},{7,6},{8,9},{9,8},{10,11... | collective-permute-start | bytes 6291464 | tf_op jit(solution)/shard_map/ppermute | solution.py:815
  453.6 9.7 %collective-permute-start.21 = (bf16[1,64,1024]{2,1,0:T(8,128)(2,1)S(1)}, bf16[1,64,1024]{2,1,0:T(8,128)(2,1)S(1)}, u32[]{:S(2)}, u32[]{:S(2)}) collective-permute-start(bf16[1,64,1024]{2,1,0:T(8,128)(2,1)S(1)} %add_convert_fusion.37), channel_id=1, source_target_pairs={{0,16},{4,20},{8,24},{12,28},{16,0},{20,4},{24,8},{28,12},{1,17},{... | collective-permute-start | bytes 393224 | tf_op jit(solution)/shard_map/ppermute | solution.py:815
  463.4 27.5 %collective-permute-start.47 = (bf16[8,512,256]{2,1,0:T(8,128)(2,1)}, bf16[8,512,256]{2,1,0:T(8,128)(2,1)}, u32[]{:S(2)}, u32[]{:S(2)}) collective-permute-start(bf16[8,512,256]{2,1,0:T(8,128)(2,1)} %get-tuple-element.93), channel_id=1, source_target_pairs={{0,1},{1,0},{2,3},{3,2},{4,5},{5,4},{6,7},{7,6},{8,9},{9,8},{10,11... | collective-permute-start | bytes 6291464 | tf_op jit(solution)/shard_map/ppermute | solution.py:815
  464.4 16.5 %collective-permute-start.22 = (bf16[1,64,1024]{2,1,0:T(8,128)(2,1)S(1)}, bf16[1,64,1024]{2,1,0:T(8,128)(2,1)S(1)}, u32[]{:S(2)}, u32[]{:S(2)}) collective-permute-start(bf16[1,64,1024]{2,1,0:T(8,128)(2,1)S(1)} %add_convert_fusion.36), channel_id=1, source_target_pairs={{0,2},{1,3},{2,0},{3,1},{4,6},{5,7},{6,4},{7,5},{8,10},{9,11},{10,... | collective-permute-start | bytes 393224 | tf_op jit(solution)/shard_map/ppermute | solution.py:815
  480.9 128.4 %collective-permute-start.53 = (f32[8,160,640]{2,1,0:T(8,128)S(1)}, f32[8,160,640]{2,1,0:T(8,128)S(1)}, u32[]{:S(2)}, u32[]{:S(2)}) collective-permute-start(f32[8,160,640]{2,1,0:T(8,128)S(1)} %copy-done.7), channel_id=1, source_target_pairs={{0,1},{1,0},{2,3},{3,2},{4,5},{5,4},{6,7},{7,6},{8,9},{9,8},{10,11... | collective-permute-start | bytes 9830408 | tf_op jit(solution)/shard_map/ppermute | solution.py:815
  481.0 20.6 %collective-permute-start.2 = (bf16[4,64,1536]{2,1,0:T(8,128)(2,1)}, bf16[4,64,1536]{2,1,0:T(8,128)(2,1)S(1)}, u32[]{:S(2)}, u32[]{:S(2)}) collective-permute-start(bf16[4,64,1536]{2,1,0:T(8,128)(2,1)} %get-tuple-element.175), channel_id=1, source_target_pairs={{0,4},{4,0},{8,12},{12,8},{16,20},{20,16},{24,28},{28,24},{1,5},{5... | collective-permute-start | bytes 2359304 | tf_op jit(solution)/shard_map/ppermute | solution.py:815
  483.8 34.6 %collective-permute-start.8 = (bf16[4,64,1536]{2,1,0:T(8,128)(2,1)S(1)}, bf16[4,64,1536]{2,1,0:T(8,128)(2,1)S(1)}, u32[]{:S(2)}, u32[]{:S(2)}) collective-permute-start(bf16[4,64,1536]{2,1,0:T(8,128)(2,1)S(1)} %copy-done.27), channel_id=1, source_target_pairs={{0,4},{4,0},{8,12},{12,8},{16,20},{20,16},{24,28},{28,24},{1,5},{5... | collective-permute-start | bytes 2359304 | tf_op jit(solution)/shard_map/ppermute | solution.py:815
  487.9 71.7 %collective-permute-start.42 = (bf16[4,512,256]{2,1,0:T(8,128)(2,1)S(1)}, bf16[4,512,256]{2,1,0:T(8,128)(2,1)S(1)}, u32[]{:S(2)}, u32[]{:S(2)}) collective-permute-start(bf16[4,512,256]{2,1,0:T(8,128)(2,1)S(1)} %get-tuple-element.153), channel_id=1, source_target_pairs={{0,4},{4,0},{8,12},{12,8},{16,20},{20,16},{24,28},{28,24},{1,5},{5... | collective-permute-start | bytes 3145736 | tf_op jit(solution)/shard_map/ppermute | solution.py:815
  493.1 94.0 %collective-permute-start.48 = (bf16[4,512,256]{2,1,0:T(8,128)(2,1)S(1)}, bf16[4,512,256]{2,1,0:T(8,128)(2,1)S(1)}, u32[]{:S(2)}, u32[]{:S(2)}) collective-permute-start(bf16[4,512,256]{2,1,0:T(8,128)(2,1)S(1)} %get-tuple-element.155), channel_id=1, source_target_pairs={{0,4},{4,0},{8,12},{12,8},{16,20},{20,16},{24,28},{28,24},{1,5},{5... | collective-permute-start | bytes 3145736 | tf_op jit(solution)/shard_map/ppermute | solution.py:815
  501.6 84.3 %collective-permute-start.30 = (bf16[4,64,2048]{2,1,0:T(8,128)(2,1)S(1)}, bf16[4,64,2048]{2,1,0:T(8,128)(2,1)S(1)}, u32[]{:S(2)}, u32[]{:S(2)}) collective-permute-start(bf16[4,64,2048]{2,1,0:T(8,128)(2,1)S(1)} %get-tuple-element.163), channel_id=1, source_target_pairs={{0,4},{4,0},{8,12},{12,8},{16,20},{20,16},{24,28},{28,24},{1,5},{5... | collective-permute-start | bytes 3145736 | tf_op jit(solution)/shard_map/ppermute | solution.py:815
  518.4 10.3 %collective-permute-start.3 = (bf16[2,64,1536]{2,1,0:T(8,128)(2,1)S(1)}, bf16[2,64,1536]{2,1,0:T(8,128)(2,1)S(1)}, u32[]{:S(2)}, u32[]{:S(2)}) collective-permute-start(bf16[2,64,1536]{2,1,0:T(8,128)(2,1)S(1)} %get-tuple-element.173), channel_id=1, source_target_pairs={{0,8},{4,12},{8,0},{12,4},{16,24},{20,28},{24,16},{28,20},{1,9},{5... | collective-permute-start | bytes 1179656 | tf_op jit(solution)/shard_map/ppermute | solution.py:815
  528.8 9.4 %collective-permute-start.9 = (bf16[2,64,1536]{2,1,0:T(8,128)(2,1)S(1)}, bf16[2,64,1536]{2,1,0:T(8,128)(2,1)S(1)}, u32[]{:S(2)}, u32[]{:S(2)}) collective-permute-start(bf16[2,64,1536]{2,1,0:T(8,128)(2,1)S(1)} %get-tuple-element.179), channel_id=1, source_target_pairs={{0,8},{4,12},{8,0},{12,4},{16,24},{20,28},{24,16},{28,20},{1,9},{5... | collective-permute-start | bytes 1179656 | tf_op jit(solution)/shard_map/ppermute | solution.py:815
  538.2 10.1 %collective-permute-start.4 = (bf16[1,64,1536]{2,1,0:T(8,128)(2,1)S(1)}, bf16[1,64,1536]{2,1,0:T(8,128)(2,1)S(1)}, u32[]{:S(2)}, u32[]{:S(2)}) collective-permute-start(bf16[1,64,1536]{2,1,0:T(8,128)(2,1)S(1)} %add_convert_fusion.34), channel_id=1, source_target_pairs={{0,16},{4,20},{8,24},{12,28},{16,0},{20,4},{24,8},{28,12},{1,17},{... | collective-permute-start | bytes 589832 | tf_op jit(solution)/shard_map/ppermute | solution.py:815
  548.3 10.8 %collective-permute-start.10 = (bf16[1,64,1536]{2,1,0:T(8,128)(2,1)S(1)}, bf16[1,64,1536]{2,1,0:T(8,128)(2,1)S(1)}, u32[]{:S(2)}, u32[]{:S(2)}) collective-permute-start(bf16[1,64,1536]{2,1,0:T(8,128)(2,1)S(1)} %add_convert_fusion.31), channel_id=1, source_target_pairs={{0,16},{4,20},{8,24},{12,28},{16,0},{20,4},{24,8},{28,12},{1,17},{... | collective-permute-start | bytes 589832 | tf_op jit(solution)/shard_map/ppermute | solution.py:815
  559.1 48.8 %collective-permute-start.36 = (bf16[4,64,2048]{2,1,0:T(8,128)(2,1)S(1)}, bf16[4,64,2048]{2,1,0:T(8,128)(2,1)S(1)}, u32[]{:S(2)}, u32[]{:S(2)}) collective-permute-start(bf16[4,64,2048]{2,1,0:T(8,128)(2,1)S(1)} %get-tuple-element.169), channel_id=1, source_target_pairs={{0,4},{4,0},{8,12},{12,8},{16,20},{20,16},{24,28},{28,24},{1,5},{5... | collective-permute-start | bytes 3145736 | tf_op jit(solution)/shard_map/ppermute | solution.py:815
  559.6 29.9 %collective-permute-start.5 = (bf16[1,64,1536]{2,1,0:T(8,128)(2,1)S(1)}, bf16[1,64,1536]{2,1,0:T(8,128)(2,1)S(1)}, u32[]{:S(2)}, u32[]{:S(2)}) collective-permute-start(bf16[1,64,1536]{2,1,0:T(8,128)(2,1)S(1)} %add_convert_fusion.33), channel_id=1, source_target_pairs={{0,2},{1,3},{2,0},{3,1},{4,6},{5,7},{6,4},{7,5},{8,10},{9,11},{10,... | collective-permute-start | bytes 589832 | tf_op jit(solution)/shard_map/ppermute | solution.py:815
  587.1 71.0 %collective-permute-start.43 = (bf16[2,512,256]{2,1,0:T(8,128)(2,1)}, bf16[2,512,256]{2,1,0:T(8,128)(2,1)}, u32[]{:S(2)}, u32[]{:S(2)}) collective-permute-start(bf16[2,512,256]{2,1,0:T(8,128)(2,1)} %get-tuple-element.157), channel_id=1, source_target_pairs={{0,8},{4,12},{8,0},{12,4},{16,24},{20,28},{24,16},{28,20},{1,9},{5... | collective-permute-start | bytes 1572872 | tf_op jit(solution)/shard_map/ppermute | solution.py:815
  589.5 70.4 %collective-permute-start.49 = (bf16[2,512,256]{2,1,0:T(8,128)(2,1)}, bf16[2,512,256]{2,1,0:T(8,128)(2,1)}, u32[]{:S(2)}, u32[]{:S(2)}) collective-permute-start(bf16[2,512,256]{2,1,0:T(8,128)(2,1)} %get-tuple-element.159), channel_id=1, source_target_pairs={{0,8},{4,12},{8,0},{12,4},{16,24},{20,28},{24,16},{28,20},{1,9},{5... | collective-permute-start | bytes 1572872 | tf_op jit(solution)/shard_map/ppermute | solution.py:815
  592.0 71.2 %collective-permute-start.31 = (bf16[2,64,2048]{2,1,0:T(8,128)(2,1)}, bf16[2,64,2048]{2,1,0:T(8,128)(2,1)}, u32[]{:S(2)}, u32[]{:S(2)}) collective-permute-start(bf16[2,64,2048]{2,1,0:T(8,128)(2,1)} %get-tuple-element.161), channel_id=1, source_target_pairs={{0,8},{4,12},{8,0},{12,4},{16,24},{20,28},{24,16},{28,20},{1,9},{5... | collective-permute-start | bytes 1572872 | tf_op jit(solution)/shard_map/ppermute | solution.py:815
  607.9 21.6 %collective-permute-start.6 = (bf16[1,64,1536]{2,1,0:T(8,128)(2,1)S(1)}, bf16[1,64,1536]{2,1,0:T(8,128)(2,1)S(1)}, u32[]{:S(2)}, u32[]{:S(2)}) collective-permute-start(bf16[1,64,1536]{2,1,0:T(8,128)(2,1)S(1)} %reduce-precision_convert_fusion.5), channel_id=1, source_target_pairs={{0,1},{1,0},{2,3},{3,2},{4,5},{5,4},{6,7},{7,6},{8,9},{9,8},{10,11... | collective-permute-start | bytes 589832 | tf_op jit(solution)/shard_map/ppermute | solution.py:815
  609.3 23.8 %collective-permute-start.12 = (bf16[1,64,1536]{2,1,0:T(8,128)(2,1)S(1)}, bf16[1,64,1536]{2,1,0:T(8,128)(2,1)S(1)}, u32[]{:S(2)}, u32[]{:S(2)}) collective-permute-start(bf16[1,64,1536]{2,1,0:T(8,128)(2,1)S(1)} %reduce-precision_convert_fusion.4), channel_id=1, source_target_pairs={{0,1},{1,0},{2,3},{3,2},{4,5},{5,4},{6,7},{7,6},{8,9},{9,8},{10,11... | collective-permute-start | bytes 589832 | tf_op jit(solution)/shard_map/ppermute | solution.py:815
  631.1 33.8 %collective-permute-start.37 = (bf16[2,64,2048]{2,1,0:T(8,128)(2,1)}, bf16[2,64,2048]{2,1,0:T(8,128)(2,1)}, u32[]{:S(2)}, u32[]{:S(2)}) collective-permute-start(bf16[2,64,2048]{2,1,0:T(8,128)(2,1)} %get-tuple-element.167), channel_id=1, source_target_pairs={{0,8},{4,12},{8,0},{12,4},{16,24},{20,28},{24,16},{28,20},{1,9},{5... | collective-permute-start | bytes 1572872 | tf_op jit(solution)/shard_map/ppermute | solution.py:815
  659.1 30.9 %collective-permute-start.44 = (bf16[1,512,256]{2,1,0:T(8,128)(2,1)S(1)}, bf16[1,512,256]{2,1,0:T(8,128)(2,1)S(1)}, u32[]{:S(2)}, u32[]{:S(2)}) collective-permute-start(bf16[1,512,256]{2,1,0:T(8,128)(2,1)S(1)} %add_convert_fusion.20), channel_id=1, source_target_pairs={{0,16},{4,20},{8,24},{12,28},{16,0},{20,4},{24,8},{28,12},{1,17},{... | collective-permute-start | bytes 786440 | tf_op jit(solution)/shard_map/ppermute | solution.py:815
  660.9 34.7 %collective-permute-start.50 = (bf16[1,512,256]{2,1,0:T(8,128)(2,1)S(1)}, bf16[1,512,256]{2,1,0:T(8,128)(2,1)S(1)}, u32[]{:S(2)}, u32[]{:S(2)}) collective-permute-start(bf16[1,512,256]{2,1,0:T(8,128)(2,1)S(1)} %add_convert_fusion.17), channel_id=1, source_target_pairs={{0,16},{4,20},{8,24},{12,28},{16,0},{20,4},{24,8},{28,12},{1,17},{... | collective-permute-start | bytes 786440 | tf_op jit(solution)/shard_map/ppermute | solution.py:815
  664.2 37.0 %collective-permute-start.32 = (bf16[1,64,2048]{2,1,0:T(8,128)(2,1)S(1)}, bf16[1,64,2048]{2,1,0:T(8,128)(2,1)S(1)}, u32[]{:S(2)}, u32[]{:S(2)}) collective-permute-start(bf16[1,64,2048]{2,1,0:T(8,128)(2,1)S(1)} %add_convert_fusion.26), channel_id=1, source_target_pairs={{0,16},{4,20},{8,24},{12,28},{16,0},{20,4},{24,8},{28,12},{1,17},{... | collective-permute-start | bytes 786440 | tf_op jit(solution)/shard_map/ppermute | solution.py:815
  666.0 39.5 %collective-permute-start.38 = (bf16[1,64,2048]{2,1,0:T(8,128)(2,1)S(1)}, bf16[1,64,2048]{2,1,0:T(8,128)(2,1)S(1)}, u32[]{:S(2)}, u32[]{:S(2)}) collective-permute-start(bf16[1,64,2048]{2,1,0:T(8,128)(2,1)S(1)} %add_convert_fusion.23), channel_id=1, source_target_pairs={{0,16},{4,20},{8,24},{12,28},{16,0},{20,4},{24,8},{28,12},{1,17},{... | collective-permute-start | bytes 786440 | tf_op jit(solution)/shard_map/ppermute | solution.py:815
  691.0 15.7 %collective-permute-start.45 = (bf16[1,512,256]{2,1,0:T(8,128)(2,1)S(1)}, bf16[1,512,256]{2,1,0:T(8,128)(2,1)S(1)}, u32[]{:S(2)}, u32[]{:S(2)}) collective-permute-start(bf16[1,512,256]{2,1,0:T(8,128)(2,1)S(1)} %add_convert_fusion.19), channel_id=1, source_target_pairs={{0,2},{1,3},{2,0},{3,1},{4,6},{5,7},{6,4},{7,5},{8,10},{9,11},{10,... | collective-permute-start | bytes 786440 | tf_op jit(solution)/shard_map/ppermute | solution.py:815
  696.7 10.2 %collective-permute-start.51 = (bf16[1,512,256]{2,1,0:T(8,128)(2,1)S(1)}, bf16[1,512,256]{2,1,0:T(8,128)(2,1)S(1)}, u32[]{:S(2)}, u32[]{:S(2)}) collective-permute-start(bf16[1,512,256]{2,1,0:T(8,128)(2,1)S(1)} %add_convert_fusion.16), channel_id=1, source_target_pairs={{0,2},{1,3},{2,0},{3,1},{4,6},{5,7},{6,4},{7,5},{8,10},{9,11},{10,... | collective-permute-start | bytes 786440 | tf_op jit(solution)/shard_map/ppermute | solution.py:815
  702.3 7.1 collective-permute-start.33
  706.5 7.8 %collective-permute-start.39 = (bf16[1,64,2048]{2,1,0:T(8,128)(2,1)S(1)}, bf16[1,64,2048]{2,1,0:T(8,128)(2,1)S(1)}, u32[]{:S(2)}, u32[]{:S(2)}) collective-permute-start(bf16[1,64,2048]{2,1,0:T(8,128)(2,1)S(1)} %add_convert_fusion.22), channel_id=1, source_target_pairs={{0,2},{1,3},{2,0},{3,1},{4,6},{5,7},{6,4},{7,5},{8,10},{9,11},{10,... | collective-permute-start | bytes 786440 | tf_op jit(solution)/shard_map/ppermute | solution.py:815
  706.8 7.7 %collective-permute-start.46 = (bf16[1,512,256]{2,1,0:T(8,128)(2,1)S(1)}, bf16[1,512,256]{2,1,0:T(8,128)(2,1)S(1)}, u32[]{:S(2)}, u32[]{:S(2)}) collective-permute-start(bf16[1,512,256]{2,1,0:T(8,128)(2,1)S(1)} %reduce-precision_convert_fusion.1), channel_id=1, source_target_pairs={{0,1},{1,0},{2,3},{3,2},{4,5},{5,4},{6,7},{7,6},{8,9},{9,8},{10,11... | collective-permute-start | bytes 786440 | tf_op jit(solution)/shard_map/ppermute | solution.py:815
  707.0 7.6 %collective-permute-start.52 = (bf16[1,512,256]{2,1,0:T(8,128)(2,1)S(1)}, bf16[1,512,256]{2,1,0:T(8,128)(2,1)S(1)}, u32[]{:S(2)}, u32[]{:S(2)}) collective-permute-start(bf16[1,512,256]{2,1,0:T(8,128)(2,1)S(1)} %reduce-precision_convert_fusion), channel_id=1, source_target_pairs={{0,1},{1,0},{2,3},{3,2},{4,5},{5,4},{6,7},{7,6},{8,9},{9,8},{10,11... | collective-permute-start | bytes 786440 | tf_op jit(solution)/shard_map/ppermute | solution.py:815
  (59 other events, 493.5 us)

commit v2 on v1

v2 whole, which is shorter than its diff:
```python
import functools
import math

import jax
import jax.numpy as jnp
from jax import lax
from jax.experimental import pallas as pl
from jax.experimental.pallas import tpu as pltpu
from jax.sharding import PartitionSpec as P

HEAD = 64
FRAMES = 5
WST = 8
PIECE = WST * WST
UNIT = 256
FF_PARTS = 4
FF_UNITS = 4
FF_BLOCKS = 2
FIRST_PAIRS = 6
LANES = 128
VMEM_LIMIT = 60 * 1024 * 1024
f32 = jnp.float32
bf16 = jnp.bfloat16
GELU_C = math.sqrt(2.0 / math.pi)
GELU_A = 0.044715


def dot_nn(a, b):
    return jnp.dot(a, b, preferred_element_type=f32)


def dot_nt(a, b):
    return lax.dot_general(a, b, (((1,), (1,)), ((), ())), preferred_element_type=f32)


def dot_tn(a, b):
    return lax.dot_general(a, b, (((0,), (0,)), ((), ())), preferred_element_type=f32)


def params():
    return pltpu.CompilerParams(vmem_limit_bytes=VMEM_LIMIT)


def cost(micros):
    return pl.CostEstimate(
        flops=int(micros * 5.0e7), bytes_accessed=int(micros * 1.0e5), transcendentals=0
    )


def pick(swap, first, second):
    return jnp.where(swap, second, first), jnp.where(swap, first, second)


def hat_of(rows):
    average = jnp.mean(rows, axis=-1, keepdims=True)
    centered = rows - average
    variance = jnp.mean(centered * centered, axis=-1, keepdims=True)
    inv_std = lax.rsqrt(variance + 1e-06)
    return centered * inv_std, inv_std


def norm_back(grad_hat, hat_rows, inv_std):
    first_mean = jnp.mean(grad_hat, axis=-1, keepdims=True)
    second_mean = jnp.mean(grad_hat * hat_rows, axis=-1, keepdims=True)
    return inv_std * (grad_hat - first_mean - hat_rows * second_mean)


def whole(shape):
    zeros = (0,) * len(shape)
    return pl.BlockSpec(shape, lambda *unused: zeros, pipeline_mode=pl.Buffered(1))


def bias_kernel(idx_ref, tab_ref, out_ref, scr_ref):
    lows = lax.broadcasted_iota(jnp.int32, (256, idx_ref.shape[1]), 0)
    tab = tab_ref[...]
    half = tab.shape[0] // 2
    heads = 16
    tiles = idx_ref.shape[1] // LANES
    win = out_ref.shape[2] // 2
    for i in range(8):
        idx = idx_ref[pl.ds(i, 1), :]
        low = idx & 255
        high = idx >> 8
        onehot = jnp.where(lows == low, 1.0, 0.0).astype(bf16)
        got = dot_nn(tab, onehot)
        got = got[:half] + got[half:]
        acc = got[:heads]
        for c in range(1, half // heads):
            acc = jnp.where(high == c, got[c * heads : (c + 1) * heads], acc)
        for t in range(tiles):
            scr_ref[t, pl.ds(i, heads, stride=8), :] = acc[:, t * LANES : (t + 1) * LANES]
    for pair in range(heads // 2):
        rows = []
        for h in range(2):
            at = (2 * pair + h) * 8
            rows.append(
                jnp.concatenate([scr_ref[t, at : at + 8, :] for t in range(tiles)], axis=1)[:, :win]
            )
        out_ref[pair] = jnp.concatenate(rows, axis=1)


def bias_gather(idx, table):
    rows, win = idx.shape
    padded = -(-win // LANES) * LANES
    buckets, heads = table.shape
    upper_f = lax.reduce_precision(table, 8, 7)
    lower = (table - upper_f).astype(bf16)

    def arrange(t):
        return t.reshape(-1, 256, heads).transpose(0, 2, 1).reshape(-1, 256)

    tab = jnp.concatenate([arrange(upper_f.astype(bf16)), arrange(lower)], axis=0)
    idx = jnp.pad(idx, ((0, 0), (0, padded - win)))
    return pl.pallas_call(
        bias_kernel,
        grid=(rows // 8,),
        in_specs=[pl.BlockSpec((8, padded), lambda i: (i, 0)), whole(tab.shape)],
        out_specs=pl.BlockSpec((heads // 2, 8, 2 * win), lambda i: (0, i, 0)),
        out_shape=jax.ShapeDtypeStruct((heads // 2, rows, 2 * win), f32),
        scratch_shapes=[pltpu.VMEM((padded // LANES, 8 * heads, LANES), f32)],
        name="bias_gather",
        compiler_params=params(),
        cost_estimate=cost(18),
    )(idx, tab)


def bucket_kernel(inv_ref, idx_ref, *refs):
    out_ref, acc_ref, scr_ref = refs[-3:]
    keep_refs = refs[: (len(refs) - 3) // 2]
    got_refs = refs[(len(refs) - 3) // 2 : -3]

    @pl.when(pl.program_id(0) == 0)
    def _():
        acc_ref[...] = jnp.zeros_like(acc_ref)

    padded = idx_ref.shape[1]
    tiles = padded // LANES
    keeps = [(r, k) for r in keep_refs for k in range(r.shape[0])]
    gots = [(r, k) for r in got_refs for k in range(r.shape[0])]
    pairs = len(keeps)
    heads = 2 * pairs
    win = keep_refs[0].shape[2] // 2
    step_rows = idx_ref.shape[0]
    lows = lax.broadcasted_iota(jnp.int32, (256, padded), 0)
    zero = jnp.zeros((step_rows, padded - win), f32)
    for pair in range(pairs):
        (keep_ref, k), (got_ref, unused) = keeps[pair], gots[pair]
        sums = keep_ref[k].astype(f32) + got_ref[k].astype(f32)
        for h in range(2):
            part = jnp.concatenate([sums[:, h * win : (h + 1) * win], zero], axis=1)
            at = (2 * pair + h) * step_rows
            for t in range(tiles):
                scr_ref[t, at : at + step_rows, :] = part[:, t * LANES : (t + 1) * LANES]
    total = acc_ref[...]
    for i in range(step_rows):
        idx = idx_ref[pl.ds(i, 1), :]
        low = idx & 255
        high = idx >> 8
        onehot = jnp.where(lows == low, 1.0, 0.0).astype(bf16)
        sums = jnp.concatenate(
            [scr_ref[t, pl.ds(i, heads, stride=step_rows), :] for t in range(tiles)], axis=1
        )
        spread = jnp.concatenate(
            [jnp.where(high == c, sums, 0.0) for c in range(acc_ref.shape[0] // heads)], axis=0
        )
        total += dot_nt(spread.astype(bf16), onehot)
    acc_ref[...] = total

    @pl.when(pl.program_id(0) == pl.num_programs(0) - 1)
    def _():
        for k in range(out_ref.shape[0]):
            out_ref[inv_ref[k]] = total[k * heads : (k + 1) * heads]


def bucket_sums(inv, idx, keeps, gots, buckets):
    rows, win = idx.shape
    padded = -(-win // LANES) * LANES
    heads = 2 * sum(k.shape[0] for k in keeps)
    step_rows = 16
    idx = jnp.pad(idx, ((0, 0), (0, padded - win)))
    out_rows = buckets // 256
    sum_specs = [
        pl.BlockSpec((k.shape[0], step_rows, 2 * win), lambda i, inv: (0, i, 0)) for k in keeps
    ]
    return pl.pallas_call(
        bucket_kernel,
        grid_spec=pltpu.PrefetchScalarGridSpec(
            num_scalar_prefetch=1,
            grid=(rows // step_rows,),
            in_specs=[pl.BlockSpec((step_rows, padded), lambda i, inv: (i, 0))] + sum_specs + sum_specs,
            out_specs=pl.BlockSpec((out_rows, heads, 256), lambda i, inv: (0, 0, 0)),
            scratch_shapes=[
                pltpu.VMEM((out_rows * heads, 256), f32),
                pltpu.VMEM((padded // LANES, step_rows * heads, LANES), f32),
            ],
        ),
        out_shape=jax.ShapeDtypeStruct((out_rows, heads, 256), f32),
        name="bucket_sums",
        compiler_params=params(),
        cost_estimate=cost(14),
    )(inv, idx, *keeps, *gots)


def qkv_kernel(src_ref, a_ref, b_ref, c_ref, d_ref, mod_ref, bias_ref, w_ref, x_ref, n_ref, o_ref):
    rows = jnp.concatenate([r[0] for r in (a_ref, b_ref, c_ref, d_ref)], axis=0)
    x_ref[...] = rows
    hat_rows, unused = hat_of(rows.astype(f32))
    normed = (hat_rows * (1.0 + mod_ref[1:2, :]) + mod_ref[0:1, :]).astype(bf16)
    n_ref[...] = normed
    features = rows.shape[1]
    for j in range(w_ref.shape[1] // 512):
        cols = slice(j * 512, (j + 1) * 512)
        got = dot_nn(normed, w_ref[:, cols]) + bias_ref[0:1, cols]
        if (j + 1) * 512 <= features:
            got = got.astype(bf16).astype(f32) * (1.0 / math.sqrt(HEAD))
        o_ref[:, cols] = got.astype(bf16)


def slot_spec(features, t):
    return pl.BlockSpec((1, PIECE, features), lambda i, src, t=t: (src[4 * i + t], 0, 0))


def qkv_call(src, pieces, mod, qkv_bias, w_qkv):
    count, unused, features = pieces.shape
    rows = count * PIECE
    wide = w_qkv.shape[1]
    block = 4 * PIECE
    return pl.pallas_call(
        qkv_kernel,
        grid_spec=pltpu.PrefetchScalarGridSpec(
            num_scalar_prefetch=1,
            grid=(count // 4,),
            in_specs=[slot_spec(features, t) for t in range(4)]
            + [whole(mod.shape), whole(qkv_bias.shape), whole(w_qkv.shape)],
            out_specs=[
                pl.BlockSpec((block, features), lambda i, src: (i, 0)),
                pl.BlockSpec((block, features), lambda i, src: (i, 0)),
                pl.BlockSpec((block, wide), lambda i, src: (i, 0)),
            ],
        ),
        out_shape=[
            jax.ShapeDtypeStruct((rows, features), bf16),
            jax.ShapeDtypeStruct((rows, features), bf16),
            jax.ShapeDtypeStruct((rows, wide), bf16),
        ],
        name="norm_qkv",
        compiler_params=params(),
        cost_estimate=cost(12),
    )(src, pieces, pieces, pieces, pieces, mod, qkv_bias, w_qkv)


def split_pair(x, left):
    zero = jnp.zeros_like(x)
    return jnp.concatenate([jnp.where(left, x, zero), jnp.where(left, zero, x)], axis=0)


def values_ones(v, left):
    one = jnp.ones_like(v)
    zero = jnp.zeros_like(v)
    marks = jnp.concatenate([jnp.where(left, one, zero), jnp.where(left, zero, one)], axis=0)
    return jnp.concatenate([split_pair(v, left), marks], axis=1)


def attn_kernel(windows, core_ref, q_ref, k_ref, v_ref, mine_ref, other_ref, o_ref, p_ref, r_ref, b_ref):
    win = q_ref.shape[0] // windows
    half = win // 2
    left = lax.broadcasted_iota(jnp.int32, (win, LANES), 1) < HEAD
    first = core_ref[0] == 0
    b_ref[:half] = jnp.where(first, mine_ref[0], other_ref[0])
    b_ref[half:] = jnp.where(first, other_ref[0], mine_ref[0])
    lowest = jnp.float32(-jnp.inf)
    whole_tiles = win // LANES * LANES
    for u in range(windows):
        rows = slice(u * win, (u + 1) * win)
        keys = split_pair(k_ref[rows], left)
        vals = values_ones(v_ref[rows], left)
        s = dot_nt(q_ref[rows], keys) + b_ref[...]
        lo = s[:, :whole_tiles]
        mid = s[:, whole_tiles : whole_tiles + LANES]
        hi = s[:, whole_tiles + LANES :]
        top_lo = jnp.where(left, mid, lowest)
        top_hi = jnp.where(left, lowest, mid)
        for t in range(whole_tiles // LANES):
            cols = slice(t * LANES, (t + 1) * LANES)
            top_lo = jnp.maximum(top_lo, lo[:, cols])
            top_hi = jnp.maximum(top_hi, hi[:, cols])
        top_lo = jnp.max(top_lo, axis=1, keepdims=True)
        top_hi = jnp.max(top_hi, axis=1, keepdims=True)
        e = jnp.concatenate(
            [
                jnp.exp(lo - top_lo),
                jnp.exp(mid - jnp.where(left, top_lo, top_hi)),
                jnp.exp(hi - top_hi),
            ],
            axis=1,
        ).astype(bf16)
        p_ref[0, u] = e
        got = dot_nn(e, vals)
        r = 1.0 / got[:, LANES:]
        r_ref[rows] = r
        o_ref[rows] = (got[:, :LANES] * r).astype(bf16)


def attn_forward(core, qkv, bias_mine, bias_other, windows):
    rows = qkv.shape[0]
    win = rows // windows
    pairs = bias_mine.shape[0]
    features = qkv.shape[1] // 3

    def col(part):
        return pl.BlockSpec((rows, LANES), lambda h, c, part=part: (0, part * pairs + h))

    half_spec = pl.BlockSpec((1, win // 2, 2 * win), lambda h, c: (h, 0, 0))
    return pl.pallas_call(
        functools.partial(attn_kernel, windows),
        grid_spec=pltpu.PrefetchScalarGridSpec(
            num_scalar_prefetch=1,
            grid=(pairs,),
            in_specs=[col(0), col(1), col(2), half_spec, half_spec],
            out_specs=[
                col(0),
                pl.BlockSpec((1, windows, win, 2 * win), lambda h, c: (h, 0, 0, 0)),
                col(0),
            ],
            scratch_shapes=[pltpu.VMEM((win, 2 * win), f32)],
        ),
        out_shape=[
            jax.ShapeDtypeStruct((rows, features), bf16),
            jax.ShapeDtypeStruct((pairs, windows, win, 2 * win), bf16),
            jax.ShapeDtypeStruct((rows, features), f32),
        ],
        name="attn_forward",
        compiler_params=params(),
        cost_estimate=cost(18),
    )(core, qkv, qkv, qkv, bias_mine, bias_other)


def fold_delta(dx, lane):
    lower_half = (lane & 32) == 0
    dx = dx + jnp.where(lower_half, pltpu.roll(dx, LANES - 32, 1), pltpu.roll(dx, 32, 1))
    upper = dx.astype(bf16)
    lower = (dx - upper.astype(f32)).astype(bf16)
    return jnp.where(lower_half, upper, lower)


def attn_back_kernel(windows, core_ref, q_ref, k_ref, v_ref, o_ref, do_ref, p_ref, r_ref, g_ref, mine_ref, other_ref):
    win = q_ref.shape[0] // windows
    lane = lax.broadcasted_iota(jnp.int32, (win, LANES), 1)
    left = lane < HEAD
    sums = None
    for u in range(windows):
        rows = slice(u * win, (u + 1) * win)
        keys = split_pair(k_ref[rows], left)
        vals = values_ones(v_ref[rows], left)
        up = (do_ref[rows].astype(f32) * r_ref[rows]).astype(bf16)
        delta = fold_delta(-(up.astype(f32) * o_ref[rows].astype(f32)), lane)
        d = dot_nt(jnp.concatenate([up, delta], axis=1), vals)
        p = p_ref[0, u]
        ds = p.astype(f32) * d
        sums = ds if sums is None else sums + ds
        low = ds.astype(bf16)
        g_ref[0, rows] = (dot_nn(low, keys) * (1.0 / math.sqrt(HEAD))).astype(bf16)
        dk = dot_tn(low, q_ref[rows])
        g_ref[1, rows] = jnp.where(left, dk[:win], dk[win:]).astype(bf16)
        dv = dot_tn(p, up)
        g_ref[2, rows] = jnp.where(left, dv[:win], dv[win:]).astype(bf16)
    half = win // 2
    first, second = sums[:half].astype(bf16), sums[half:].astype(bf16)
    mine_ref[0], other_ref[0] = pick(core_ref[0] == 1, first, second)


def attn_backward(core, qkv, attended, grad_att, probs, recips, windows, first, count):
    rows = qkv.shape[0]
    win = rows // windows
    pairs = probs.shape[0]

    def col(part):
        return pl.BlockSpec((rows, LANES), lambda h, core, part=part: (0, part * pairs + first + h))

    half_spec = pl.BlockSpec((1, win // 2, 2 * win), lambda h, core: (h, 0, 0))
    half_shape = jax.ShapeDtypeStruct((count, win // 2, 2 * win), bf16)
    return pl.pallas_call(
        functools.partial(attn_back_kernel, windows),
        grid_spec=pltpu.PrefetchScalarGridSpec(
            num_scalar_prefetch=1,
            grid=(count,),
            in_specs=[
                col(0),
                col(1),
                col(2),
                col(0),
                col(0),
                pl.BlockSpec((1, windows, win, 2 * win), lambda h, core: (first + h, 0, 0, 0)),
                col(0),
            ],
            out_specs=[
                pl.BlockSpec((3, rows, LANES), lambda h, core: (0, 0, h)),
                half_spec,
                half_spec,
            ],
        ),
        out_shape=[jax.ShapeDtypeStruct((3, rows, count * LANES), bf16), half_shape, half_shape],
        name="attn_backward",
        compiler_params=params(),
        cost_estimate=cost(3 * count),
    )(core, qkv, qkv, qkv, attended, grad_att, probs, recips)


def out_kernel(src_ref, a_ref, b_ref, c_ref, d_ref, att_ref, x_ref, mod_ref, bo_ref, w_ref, branch_ref, n_ref, gm_ref):
    branch = (dot_nn(att_ref[...], w_ref[...]) + bo_ref[...]).astype(bf16)
    branch_ref[...] = branch
    residual = x_ref[...].astype(f32) + mod_ref[2:3, :] * branch.astype(f32)
    hat_rows, unused = hat_of(residual)
    n_ref[...] = (hat_rows * (1.0 + mod_ref[4:5, :]) + mod_ref[3:4, :]).astype(bf16)
    up = jnp.concatenate([r[0] for r in (a_ref, b_ref, c_ref, d_ref)], axis=0)
    gm_ref[...] = (mod_ref[5:6, :] * up.astype(f32)).astype(bf16)


def out_call(src, pieces, attended, x_rows, mod, b_out, w_out):
    count, unused, features = pieces.shape
    rows = count * PIECE
    block = 4 * PIECE
    rows_spec = pl.BlockSpec((block, features), lambda i, src: (i, 0))
    sds = jax.ShapeDtypeStruct((rows, features), bf16)
    return pl.pallas_call(
        out_kernel,
        grid_spec=pltpu.PrefetchScalarGridSpec(
            num_scalar_prefetch=1,
            grid=(count // 4,),
            in_specs=[slot_spec(features, t) for t in range(4)]
            + [rows_spec, rows_spec, whole(mod.shape), whole(b_out.shape), whole(w_out.shape)],
            out_specs=[rows_spec, rows_spec, rows_spec],
        ),
        out_shape=[sds, sds, sds],
        name="out_norm",
        compiler_params=params(),
        cost_estimate=cost(6),
    )(src, pieces, pieces, pieces, pieces, attended, x_rows, mod, b_out, w_out)


def place_rows(inv_ref, out_ref, values):
    for k in range(out_ref.shape[0]):
        at = inv_ref[k]
        for m in range(out_ref.shape[1]):
            out_ref[at, m] = values[k * LANES : (k + 1) * LANES, m * LANES : (m + 1) * LANES]


def ff_part_kernel(count, fo_ref, co_ref, inv_ref, flag_ref, n_ref, gm_ref, *refs):
    ups = refs[:count]
    biases = refs[count : 2 * count]
    downs = refs[2 * count : 3 * count]
    act_ref, gh_ref, own_ref, other_ref, sum_ref = refs[-5:]
    step = pl.program_id(0)
    rows = n_ref.shape[0]
    block = rows // FF_BLOCKS
    wu = jnp.concatenate([r[...] for r in ups], axis=1)
    wd = jnp.concatenate([r[...] for r in downs], axis=0)
    bias = jnp.concatenate([r[0] for r in biases], axis=1)
    sums = None
    for c in range(FF_BLOCKS):
        part = slice(c * block, (c + 1) * block)
        v = dot_nn(n_ref[part], wu) + bias
        v2 = v * v
        t = jnp.tanh(v * (GELU_C + (GELU_C * GELU_A) * v2))
        h = 0.5 + 0.5 * t
        slope = h + (0.5 * v) * (1.0 - t * t) * (GELU_C + (3.0 * GELU_C * GELU_A) * v2)
        gh = (dot_nt(gm_ref[part], wd) * slope).astype(bf16)
        act_ref[0, part] = (v * h).astype(bf16)
        gh_ref[0, part] = gh
        piece = jnp.sum(gh.astype(f32), axis=0, keepdims=True)
        sums = piece if sums is None else sums + piece
    sum_ref[0] = sums
    up = dot_tn(n_ref[...], gh_ref[0]).astype(bf16)
    down = dot_tn(act_ref[0], gm_ref[...]).astype(bf16)
    half = down.shape[1] // 2
    blocks = half // LANES
    for p in range(count // 2):
        left = up[:, 2 * p * LANES : (2 * p + 1) * LANES]
        right = up[:, (2 * p + 1) * LANES : (2 * p + 2) * LANES]
        own, other = pick(flag_ref[1] == 1, left, right)
        col = co_ref[step * (count // 2) + p]
        for k in range(own_ref.shape[0]):
            at = inv_ref[k]
            own_ref[at, col] = own[k * LANES : (k + 1) * LANES]
            other_ref[at, col] = other[k * LANES : (k + 1) * LANES]
    own, other = pick(flag_ref[0] == 1, down[:, :half], down[:, half:])
    first = own_ref.shape[1] - blocks
    for k in range(count):
        for m in range(blocks):
            tile = (slice(k * LANES, (k + 1) * LANES), slice(m * LANES, (m + 1) * LANES))
            own_ref[step * count + k, first + m] = own[tile]
            other_ref[step * count + k, first + m] = other[tile]


def ff_part(j, fo, co, inv, flags, normed, grad_mixed, w_up, b_up, w_down, before):
    units = fo.shape[0]
    count = FF_UNITS
    steps = units // count
    rows, features = normed.shape

    def up(k):
        return pl.BlockSpec((features, LANES), lambda i, fo, *more: (0, fo[count * i + k]))

    def bias(k):
        return pl.BlockSpec((1, 1, LANES), lambda i, fo, *more: (fo[count * i + k], 0, 0))

    def down(k):
        return pl.BlockSpec((LANES, features), lambda i, fo, *more: (fo[count * i + k], 0))

    cols = pl.BlockSpec((1, rows, count * LANES), lambda i, *more: (j, 0, i))
    hidden = jax.ShapeDtypeStruct((FF_PARTS, rows, units * LANES), bf16)
    blocks = units // 2 + features // 2 // LANES
    grad = jax.ShapeDtypeStruct((units, blocks, LANES, LANES), bf16)
    ks = range(count)
    at = 4 + 2 + 3 * count
    return pl.pallas_call(
        functools.partial(ff_part_kernel, count),
        grid_spec=pltpu.PrefetchScalarGridSpec(
            num_scalar_prefetch=4,
            grid=(steps,),
            in_specs=[whole(normed.shape), whole(normed.shape)]
            + [up(k) for k in ks]
            + [bias(k) for k in ks]
            + [down(k) for k in ks]
            + [pl.BlockSpec(memory_space=pl.ANY)] * len(before),
            out_specs=[cols, cols, whole(grad.shape), whole(grad.shape)]
            + [pl.BlockSpec((1, 1, count * LANES), lambda i, *more: (i, 0, 0))],
        ),
        out_shape=[hidden, hidden, grad, grad, jax.ShapeDtypeStruct((steps, 1, count * LANES), f32)],
        input_output_aliases={at: 0, at + 1: 1} if before else {},
        name="ff_part",
        compiler_params=params(),
        cost_estimate=cost(20),
    )(fo, co, inv, flags, normed, grad_mixed, *[w_up] * count, *[b_up] * count, *[w_down] * count, *before)


def ff_join_kernel(parts, blocks, units, *refs):
    fo_ref, src_ref, inv_ref, flag_ref, act_ref, gh_ref = refs[:6]
    up_refs = refs[6 : 6 + units]
    down_refs = refs[6 + units : 6 + 2 * units]
    at = 6 + 2 * units
    a_ref, b_ref, c_ref, d_ref, x_ref, branch_ref, mod_ref, bd_ref, wo_ref, att_ref = refs[at : at + 10]
    gres_ref, vec_ref, do_ref, own_ref, other_ref, out_ref = refs[at + 10 : at + 16]
    mixed_ref, back_ref, stage_ref, gb_ref, sem_ref = refs[at + 16 :]
    step = pl.program_id(0)

    @pl.when(step == 0)
    def _():
        mixed_ref[...] = jnp.zeros_like(mixed_ref)
        back_ref[...] = jnp.zeros_like(back_ref)

    @pl.when(step < parts)
    def _():
        wd = jnp.concatenate([r[...] for r in down_refs], axis=0)
        wu = jnp.concatenate([r[...] for r in up_refs], axis=1)
        half = mixed_ref.shape[0] // 2
        for k in range(2):
            part = slice(k * half, (k + 1) * half)
            mixed_ref[part] += dot_nn(act_ref[0, part], wd)
            back_ref[part] += dot_nt(gh_ref[0, part], wu)

    @pl.when(jnp.logical_and(step >= parts, step < parts + blocks))
    def _():
        e = step - parts
        block = 4 * PIECE
        part = pl.ds(pl.multiple_of(e * block, block), block)
        mixed = mixed_ref[part] + bd_ref[...]
        back = back_ref[part]
        branch = branch_ref[...].astype(f32)
        gate_one = mod_ref[2:3, :]
        gate_two = mod_ref[5:6, :]
        residual = x_ref[...].astype(f32) + gate_one * branch
        hat_rows, inv_std = hat_of(residual)
        up = jnp.concatenate([r[0] for r in (a_ref, b_ref, c_ref, d_ref)], axis=0).astype(f32)
        stage_ref[part] = (residual + gate_two * mixed).astype(bf16)
        for t in range(4):
            pltpu.make_async_copy(
                stage_ref.at[pl.ds(pl.multiple_of(e * block + t * PIECE, PIECE), PIECE)],
                out_ref.at[src_ref[4 * e + t]],
                sem_ref.at[4 * e + t],
            ).start()
        gres = up + norm_back(back * (1.0 + mod_ref[4:5, :]), hat_rows, inv_std)
        gres_ref[...] = gres.astype(bf16)
        low = (gate_one * gres).astype(bf16)
        gb_ref[part] = low
        do_ref[...] = dot_nt(low, wo_ref[...]).astype(bf16)
        grad_mixed = (gate_two * up).astype(bf16).astype(f32)

        def total(values):
            return jnp.sum(values, axis=0, keepdims=True)

        pieces = jnp.concatenate(
            [
                total(gres * branch),
                total(back),
                total(back * hat_rows),
                total(up * mixed),
                total(low.astype(f32)),
                total(grad_mixed),
                jnp.zeros((2, gate_one.shape[1]), f32),
            ],
            axis=0,
        )

        @pl.when(e == 0)
        def _():
            vec_ref[...] = pieces

        @pl.when(e > 0)
        def _():
            vec_ref[...] += pieces

    @pl.when(step >= parts + blocks)
    def _():
        width = own_ref.shape[1] * LANES
        half = gb_ref.shape[1] // 2
        flag = flag_ref[0]
        for grad_ref, side in ((own_ref, flag), (other_ref, 1 - flag)):
            start = pl.multiple_of(side * half + (step - parts - blocks) * width, width)
            got = dot_tn(att_ref[...], gb_ref[:, pl.ds(start, width)])
            place_rows(inv_ref, grad_ref, got.astype(bf16))

    @pl.when(step == pl.num_programs(0) - 1)
    def _():
        for k in range(sem_ref.shape[0]):
            pltpu.make_async_copy(
                stage_ref.at[pl.ds(k * PIECE, PIECE)], out_ref.at[src_ref[k]], sem_ref.at[k]
            ).wait()


def ff_join(fo, src, inv, flags, act, gh, w_up, w_down, pieces, x_rows, branch, mod, b_down, w_out, attended):
    parts, rows, wide = act.shape
    units = wide // LANES
    features = x_rows.shape[1]
    shards = features // LANES
    block = 4 * PIECE
    blocks = rows // block
    ends = features // 2 // UNIT

    def late(i):
        return jnp.clip(i - parts, 0, blocks - 1)

    def early(i):
        return jnp.minimum(i, parts - 1)

    rows_spec = pl.BlockSpec((block, features), lambda i, *more: (late(i), 0))
    slots = [
        pl.BlockSpec((1, PIECE, features), lambda i, fo, src, *more, t=t: (src[4 * late(i) + t], 0, 0))
        for t in range(4)
    ]
    ups = [
        pl.BlockSpec((features, LANES), lambda i, fo, *more, u=u: (0, fo[early(i) * units + u]))
        for u in range(units)
    ]
    downs = [
        pl.BlockSpec((LANES, features), lambda i, fo, *more, u=u: (fo[early(i) * units + u], 0))
        for u in range(units)
    ]
    hidden = pl.BlockSpec((1, rows, wide), lambda i, *more: (early(i), 0, 0))
    grad_spec = pl.BlockSpec(
        (shards, UNIT // LANES, LANES, LANES),
        lambda i, *more: (0, jnp.maximum(i - parts - blocks, 0), 0, 0),
    )
    grad = jax.ShapeDtypeStruct((shards, features // 2 // LANES, LANES, LANES), bf16)
    rows_shape = jax.ShapeDtypeStruct((rows, features), bf16)
    return pl.pallas_call(
        functools.partial(ff_join_kernel, parts, blocks, units),
        grid_spec=pltpu.PrefetchScalarGridSpec(
            num_scalar_prefetch=4,
            grid=(parts + blocks + ends,),
            in_specs=[hidden, hidden]
            + ups
            + downs
            + slots
            + [rows_spec, rows_spec, whole(mod.shape), whole(b_down.shape)]
            + [whole(w_out.shape), whole(attended.shape)],
            out_specs=[
                rows_spec,
                pl.BlockSpec((8, features), lambda i, *more: (0, 0)),
                rows_spec,
                grad_spec,
                grad_spec,
                pl.BlockSpec(memory_space=pl.ANY),
            ],
            scratch_shapes=[
                pltpu.VMEM((rows, features), f32),
                pltpu.VMEM((rows, features), f32),
                pltpu.VMEM((rows, features), bf16),
                pltpu.VMEM((rows, features), bf16),
                pltpu.SemaphoreType.DMA((rows // PIECE,)),
            ],
        ),
        out_shape=[
            rows_shape,
            jax.ShapeDtypeStruct((8, features), f32),
            rows_shape,
            grad,
            grad,
            jax.ShapeDtypeStruct(pieces.shape, bf16),
        ],
        name="ff_join",
        compiler_params=params(),
        cost_estimate=cost(45),
    )(
        fo, src, inv, flags, act, gh, *([w_up] * units), *([w_down] * units), *([pieces] * 4),
        x_rows, branch, mod, b_down, w_out, attended,
    )


def qkv_weight_kernel(inv_ref, flag_ref, n_ref, a_ref, b_ref, g0_ref, g1_ref):
    for out_ref, ref in ((g0_ref, a_ref), (g1_ref, b_ref)):
        place_rows(inv_ref, out_ref, dot_tn(n_ref[...], ref[0]).astype(bf16))


def qkv_weight(inv, flags, normed, grads):
    rows, features = normed.shape
    parts, unused, wide = grads.shape
    half = wide // 2
    shards = features // LANES
    tiles = half // LANES
    out_spec = pl.BlockSpec((shards, tiles, LANES, LANES), lambda i, *more: (0, i, 0, 0))
    grad = jax.ShapeDtypeStruct((shards, parts * tiles, LANES, LANES), bf16)
    return pl.pallas_call(
        qkv_weight_kernel,
        grid_spec=pltpu.PrefetchScalarGridSpec(
            num_scalar_prefetch=2,
            grid=(parts,),
            in_specs=[
                whole(normed.shape),
                pl.BlockSpec((1, rows, half), lambda i, inv, flags: (i, 0, flags[0])),
                pl.BlockSpec((1, rows, half), lambda i, inv, flags: (i, 0, 1 - flags[0])),
            ],
            out_specs=[out_spec, out_spec],
        ),
        out_shape=[grad, grad],
        name="qkv_weight",
        compiler_params=params(),
        cost_estimate=cost(6),
    )(inv, flags, normed, grads, grads)


def qkv_back_kernel(src_ref, *refs):
    count = len(refs) - 8
    grads = refs[:count]
    w_ref, x_ref, gres_ref, mod_ref, out_ref, vec_ref, stage_ref, sem_ref = refs[count:]
    step = pl.program_id(0)
    block = x_ref.shape[0]
    features = x_ref.shape[1]
    back = None
    bias = []
    for part in range(3):
        joined = jnp.concatenate([g[part] for g in grads], axis=1)
        bias.append(jnp.sum(joined.astype(f32), axis=0, keepdims=True))
        got = dot_nt(joined, w_ref[:, part * features : (part + 1) * features])
        back = got if back is None else back + got
    back = back.astype(bf16).astype(f32)
    hat_rows, inv_std = hat_of(x_ref[...].astype(f32))
    grad = gres_ref[...].astype(f32) + norm_back(back * (1.0 + mod_ref[1:2, :]), hat_rows, inv_std)
    stage_ref[pl.ds(pl.multiple_of(step * block, block), block)] = grad.astype(bf16)
    for t in range(4):
        pltpu.make_async_copy(
            stage_ref.at[pl.ds(pl.multiple_of(step * block + t * PIECE, PIECE), PIECE)],
            out_ref.at[src_ref[4 * step + t]],
            sem_ref.at[4 * step + t],
        ).start()
    pieces = jnp.concatenate(
        [
            jnp.sum(back, axis=0, keepdims=True),
            jnp.sum(back * hat_rows, axis=0, keepdims=True),
            bias[0],
            bias[2],
            jnp.zeros((4, features), f32),
        ],
        axis=0,
    )

    @pl.when(step == 0)
    def _():
        vec_ref[...] = pieces

    @pl.when(step > 0)
    def _():
        vec_ref[...] += pieces

    @pl.when(step == pl.num_programs(0) - 1)
    def _():
        for k in range(sem_ref.shape[0]):
            pltpu.make_async_copy(
                stage_ref.at[pl.ds(k * PIECE, PIECE)], out_ref.at[src_ref[k]], sem_ref.at[k]
            ).wait()


def qkv_backward(src, grads, w_qkv, x_rows, gres, mod):
    rows, features = x_rows.shape
    block = 4 * PIECE
    rows_spec = pl.BlockSpec((block, features), lambda i, src: (i, 0))
    grad_specs = [pl.BlockSpec((3, block, g.shape[2]), lambda i, src: (0, i, 0)) for g in grads]
    return pl.pallas_call(
        qkv_back_kernel,
        grid_spec=pltpu.PrefetchScalarGridSpec(
            num_scalar_prefetch=1,
            grid=(rows // block,),
            in_specs=grad_specs + [whole(w_qkv.shape), rows_spec, rows_spec, whole(mod.shape)],
            out_specs=[
                pl.BlockSpec(memory_space=pl.ANY),
                pl.BlockSpec((8, features), lambda i, src: (0, 0)),
            ],
            scratch_shapes=[
                pltpu.VMEM((rows, features), bf16),
                pltpu.SemaphoreType.DMA((rows // PIECE,)),
            ],
        ),
        out_shape=[
            jax.ShapeDtypeStruct((rows // PIECE, PIECE, features), bf16),
            jax.ShapeDtypeStruct((8, features), f32),
        ],
        name="qkv_backward",
        compiler_params=params(),
        cost_estimate=cost(14),
    )(src, *grads, w_qkv, x_rows, gres, mod)


def assemble_kernel(places, counts, core_ref, *refs):
    ins = refs[: 2 * len(counts)]
    outs = refs[2 * len(counts) :]
    swap = core_ref[0] == 1
    at = 0
    for k, count in enumerate(counts):
        for m in range(count):
            pair = pick(swap, ins[2 * k][m], ins[2 * k + 1][m])
            for tile, (out, row, col) in zip(pair, places[at]):
                outs[out][row * LANES : (row + 1) * LANES, col * LANES : (col + 1) * LANES] = tile.astype(f32)
            at += 1


def assemble(core, pairs, places, shapes):
    flat = [array for pair in pairs for array in pair]
    return pl.pallas_call(
        functools.partial(assemble_kernel, places, [own.shape[0] for own, unused in pairs]),
        grid_spec=pltpu.PrefetchScalarGridSpec(
            num_scalar_prefetch=1,
            grid=(1,),
            in_specs=[whole(array.shape) for array in flat],
            out_specs=[whole(shape) for shape in shapes],
        ),
        out_shape=[jax.ShapeDtypeStruct(shape, f32) for shape in shapes],
        name="assemble",
        compiler_params=params(),
        cost_estimate=cost(5),
    )(core, *flat)


def flip(axis, bit):
    size = lax.axis_size(axis)
    return [(i, i ^ (1 << bit)) for i in range(size)]


def trade(array, axis, bit):
    return lax.ppermute(array, axis, flip(axis, bit))


def add_low(a, b):
    return (a.astype(f32) + b.astype(f32)).astype(bf16)


class Chain:
    def __init__(self, clip_bits, own, sends, stage=0):
        self.clip_bits = clip_bits
        self.own = own
        self.sends = sends
        self.stage = stage
        self.got = None

    def launch(self):
        if self.stage == 0 or self.stage == self.clip_bits + 2:
            axis, bit = "win", 0
        elif self.stage == self.clip_bits + 1:
            axis, bit = "win", 1
        else:
            axis, bit = "clip", self.stage - 1
        self.got = [trade(send, axis, bit) for send in self.sends]

    def prepare(self):
        self.stage += 1
        both = list(zip(self.own, self.got))
        if self.stage <= self.clip_bits:
            half = self.own[0].shape[0] // 2
            self.sends = [joined([add_low(o[half:], g[half:]) for o, g in both])]
            self.own = [joined([add_low(o[:half], g[:half]) for o, g in both])]
        elif self.stage == self.clip_bits + 1:
            self.own = self.sends = [joined([add_low(o, g) for o, g in both])]
        else:
            exact = [o.astype(f32) + g.astype(f32) for o, g in both]
            self.own = self.sends = [
                joined([lax.reduce_precision(e, 8, 7).astype(bf16) for e in exact])
            ]

    def finish(self):
        while self.stage < self.clip_bits + 2:
            boundary((), [self], [])
        return self.own[0][0], self.got[0][0]


class Vectors:
    def __init__(self, clip_bits, me, rows, vectors):
        self.clip_bits = clip_bits
        self.me = me
        self.rows = rows
        self.gathered = vectors
        self.stage = 0
        self.sends = [jnp.concatenate([rows, vectors])]
        self.own = None
        self.got = None

    def launch(self):
        axis, bit = ("win", self.stage) if self.stage < 2 else ("clip", self.stage - 2)
        self.got = [trade(self.sends[0], axis, bit)]

    def prepare(self):
        got = self.got[0]
        count = got.shape[0] - self.gathered.shape[0]
        if self.stage < 2:
            both = self.sends[0] + got
            self.rows, self.gathered = both[:count], both[count:]
        else:
            self.rows = self.rows[:count] + got[:count]
            upper = (self.me >> (self.stage - 2)) & 1 == 1
            self.gathered = jnp.concatenate(pick(upper, self.gathered, got[count:]))
        self.stage += 1
        if self.stage < 2:
            self.sends = [both]
        else:
            self.sends = [jnp.concatenate([self.rows[self.rows.shape[0] // 2 :], self.gathered])]

    def finish(self):
        while self.stage < self.clip_bits + 1:
            boundary((), [self], [])
        self.prepare()
        return self.rows[0], self.gathered


def joined(arrays):
    return arrays[0] if len(arrays) == 1 else jnp.concatenate(arrays, axis=1)


def unite(*chains):
    first = chains[0]
    united = Chain(first.clip_bits, None, None, first.stage)
    united.own = [o for c in chains for o in c.own]
    united.got = [g for c in chains for g in c.got]
    return united


def boundary(inputs, moved, fresh):
    got = [c.got for c in moved]
    inputs, got = lax.optimization_barrier((inputs, got))
    for c, g in zip(moved, got):
        c.got = g
        c.prepare()
    chains = moved + fresh
    inputs, sends = lax.optimization_barrier((inputs, [c.sends for c in chains]))
    for c, sent in zip(chains, sends):
        c.sends = sent
        if c.own is not None and c.stage >= c.clip_bits + 1:
            c.own = sent
        c.launch()
    return inputs


def to_quadrants(slot_rows):
    local_slots = slot_rows.shape[0]
    channels = slot_rows.shape[-1]
    arranged = slot_rows.reshape(local_slots, 2, WST, 2, WST, channels).transpose(1, 3, 0, 2, 4, 5)
    return arranged.reshape(4, local_slots, PIECE, channels)


def from_quadrants(received):
    local_slots = received.shape[1]
    channels = received.shape[-1]
    arranged = received.reshape(2, 2, local_slots, WST, WST, channels).transpose(2, 0, 3, 1, 4, 5)
    return arranged.reshape(local_slots, 4 * PIECE, channels)


def exchange(quadrants):
    return lax.all_to_all(quadrants, "win", split_axis=0, concat_axis=0, tiled=True)


def local(
    tokens,
    condition,
    slot_order,
    rel_index,
    w_qkv,
    b_query,
    b_value,
    w_out,
    b_out,
    w_up,
    b_up,
    w_down,
    b_down,
    w_ada,
    b_ada,
    rel_table,
    grad_out,
):
    features = tokens.shape[-1]
    clips = lax.axis_size("clip")
    clip_bits = clips.bit_length() - 1
    me = lax.axis_index("clip")
    core = lax.axis_index("win") & 1
    ff = w_up.shape[1]
    fast = features // clips == LANES and ff // clips == FF_PARTS * LANES

    quadrants, rel_index = lax.optimization_barrier((to_quadrants(tokens[0]), rel_index))
    pieces = exchange(quadrants).reshape(-1, PIECE, features)
    grad_quadrants = to_quadrants(grad_out[0])
    slots = pieces.shape[0]
    per_frame = slots // FRAMES
    order_row = slot_order[0]
    window_place = jnp.arange(slots, dtype=jnp.int32)
    wanted = (window_place % FRAMES) * per_frame + window_place // FRAMES
    src = jnp.sum(
        jnp.where(order_row[None, :] == wanted[:, None], window_place[None, :], 0), axis=1
    ).astype(jnp.int32)
    windows = per_frame
    win = FRAMES * PIECE

    half = win // 2
    idx_mine = lax.dynamic_slice_in_dim(rel_index, core * half, half, 0)
    bias_mine = bias_gather(idx_mine, rel_table)
    grad_quadrants, bias_mine, w_ada = lax.optimization_barrier((grad_quadrants, bias_mine, w_ada))
    grad_pieces = exchange(grad_quadrants).reshape(-1, PIECE, features)
    bias_other = trade(bias_mine, "win", 0)

    lifted = jax.nn.silu(condition.astype(f32)).astype(bf16)
    modulation = jnp.dot(lifted, w_ada, preferred_element_type=f32)[0] + b_ada
    mod = jnp.concatenate([modulation.reshape(6, features), jnp.zeros((2, features), f32)])

    qkv_bias = jnp.concatenate([b_query, jnp.zeros_like(b_query), b_value]).astype(f32)[None]
    x_rows, normed, qkv = qkv_call(src, pieces, mod, qkv_bias, w_qkv)
    core_arr = core.astype(jnp.int32)[None]
    attended, probs, recips = attn_forward(core_arr, qkv, bias_mine, bias_other, windows)
    branch, normed_two, grad_mixed = out_call(
        src, grad_pieces, attended, x_rows, mod, b_out.astype(f32)[None], w_out
    )

    shards = features // LANES
    natural = jnp.arange(shards, dtype=jnp.int32)
    if fast:
        places = jnp.zeros_like(natural)
        for bit in range(clip_bits):
            places = places | (((natural >> (clip_bits - 1 - bit)) & 1) << bit)
        order = me ^ places
        inv = jnp.zeros_like(natural)
        for bit in range(clip_bits):
            inv = inv | ((((natural ^ me) >> (clip_bits - 1 - bit)) & 1) << bit)
        per_shard = ff // clips // LANES
        fos = [order * per_shard + j for j in range(FF_PARTS)]
        co = order[::2] & (clips // 2 - 1)
        upper = me >> (clip_bits - 1)
        flags = jnp.stack([core, (upper != core).astype(jnp.int32)]).astype(jnp.int32)
    else:
        inv = natural
        per_part = ff // LANES // FF_PARTS
        fos = [jnp.arange(per_part, dtype=jnp.int32) + j * per_part for j in range(FF_PARTS)]
        co = jnp.arange(per_part // 2, dtype=jnp.int32)
        flags = jnp.zeros((2,), jnp.int32)

    def chain(own, sends):
        return Chain(clip_bits, [own], [sends]) if fast else (own, sends)

    def meet(inputs, moved, fresh=()):
        return boundary(inputs, list(moved), list(fresh)) if fast else inputs

    def merge(*chains):
        return unite(*chains) if fast else chains

    b_up_rows = b_up.astype(f32).reshape(-1, 1, LANES)
    before, up_sums, ffs = [], [], []
    steps = [((), ()), ((), (0,)), ((0,), (1,)), ((0, 1), (2,))]
    for j in range(FF_PARTS):
        moved, fresh = steps[j]
        if j:
            normed_two, grad_mixed = meet(
                (normed_two, grad_mixed), [ffs[k] for k in moved], [ffs[k] for k in fresh]
            )
        act, gh, own, other, sums = ff_part(
            j, fos[j], co, inv, flags, normed_two, grad_mixed, w_up, b_up_rows, w_down, before
        )
        before = [act, gh]
        up_sums.append(sums.reshape(-1, LANES))
        ffs.append(chain(own, other))
    act, gh = meet((act, gh), ffs[:3], [ffs[3]])
    gres, early, grad_att, out_own, out_other, out_pieces = ff_join(
        jnp.concatenate(fos), src, inv, flags, act, gh, w_up, w_down, grad_pieces, x_rows, branch, mod,
        b_down.astype(f32)[None], w_out, attended,
    )
    local_slots = tokens.shape[1]
    piece_shape = (-1, local_slots, PIECE, features)
    out_pieces = exchange(out_pieces.reshape(piece_shape))
    wos = chain(out_own, out_other)
    grad_att = meet(grad_att, ffs[1:], [wos])
    pairs = probs.shape[0]
    grads_a, mine_a, others_a = attn_backward(core_arr, qkv, attended, grad_att, probs, recips, windows, 0, FIRST_PAIRS)
    grads_a = meet(grads_a, [ffs[2], ffs[3], wos])
    qa_own, qa_other = qkv_weight(inv, flags, normed, grads_a)
    qas = chain(qa_own, qa_other)
    front = merge(*ffs[:3])
    grad_att, unused, out_pieces = meet((grad_att, qa_own, out_pieces), [front, ffs[3], wos], [qas])
    others_a = trade(others_a, "win", 0)
    grads_b, mine_b, others_b = attn_backward(
        core_arr, qkv, attended, grad_att, probs, recips, windows, FIRST_PAIRS, pairs - FIRST_PAIRS
    )
    grads_b = meet(grads_b, [qas, wos])
    qb_own, qb_other = qkv_weight(inv, flags, normed, grads_b)
    qbs = chain(qb_own, qb_other)

    rear = merge(ffs[3], wos)
    gres_late, unused, others_a, others_b = meet((gres, qb_own, others_a, others_b), [front, rear], [qbs])
    others_b = trade(others_b, "win", 0)
    token_pieces, late = qkv_backward(src, (grads_a, grads_b), w_qkv, x_rows, gres_late, mod)
    token_pieces = exchange(token_pieces.reshape(piece_shape))
    late, others_b = meet((late, others_b), [qbs, qas, rear])
    rel_sums = bucket_sums(inv, idx_mine, [mine_a, mine_b], [others_a, others_b], rel_table.shape[0])

    if fast:
        here = natural[:, None] == order[None, :]
        up_sums = [jnp.sum(jnp.where(here[:, :, None], u[None], 0.0), axis=1) for u in up_sums]
    grad_b_up = jnp.stack(up_sums, axis=1 if fast else 0)
    d = features
    tile_rows = d // LANES
    lifted_row = lifted[0].astype(f32).reshape(1, tile_rows, LANES)
    early_rows = early[:6].reshape(6, tile_rows, LANES)
    late_rows = late[:4].reshape(4, tile_rows, LANES)
    vectors = jnp.concatenate(
        [early_rows, lifted_row, jnp.zeros_like(lifted_row), grad_b_up.reshape(-1, tile_rows, LANES), late_rows]
    )
    buckets = rel_table.shape[0]
    heads = rel_sums.shape[1]
    rel_rows = buckets // clips
    if fast:
        own_rows = rel_rows * heads // LANES
        chain_v = Vectors(
            clip_bits, me, rel_sums.reshape(shards, own_rows, LANES), vectors.reshape(-1, own_rows, LANES)
        )
        boundary(rel_sums, [qbs, qas], [chain_v])
        boundary((), [qbs, chain_v], [])
        last = merge(qas, qbs)
        token_pieces = boundary(token_pieces, [last, chain_v], [])
        boundary((), [last, chain_v], [])
        rel, vectors_all = chain_v.finish()
        sum_rel = rel.reshape(heads, rel_rows).T
        vectors_all = vectors_all.reshape(clips, -1, d)
    else:
        vectors_all = lax.psum(lax.all_gather(vectors.reshape(-1, d), "clip", axis=0), "win")
        rel = lax.psum(rel_sums.transpose(0, 2, 1).reshape(buckets, heads), "win")
        sum_rel = lax.psum_scatter(rel, "clip", scatter_dimension=0, tiled=True)
    late_all = vectors_all[:, -4:].reshape(clips, 4 * d)
    early_all = vectors_all[:, :-4]
    all_lifted = early_all[:, 6] * (1.0 / lax.axis_size("win"))
    all_terms = jnp.concatenate([late_all[:, : 2 * d], early_all[:, :4].reshape(clips, 4 * d)], axis=1)

    def own_block(vector):
        size = vector.shape[0] // clips
        return lax.dynamic_slice_in_dim(vector, me * size, size, 0)

    early_sum = jnp.sum(jnp.concatenate([early_all[:, 4:6], early_all[:, 8:]], axis=1), axis=0).reshape(-1)
    late_sum = jnp.sum(late_all[:, 2 * d :], axis=0)
    sum_bo, sum_bd, sum_bu = own_block(early_sum[:d]), own_block(early_sum[d : 2 * d]), own_block(early_sum[2 * d :])
    sum_bq, sum_bv = own_block(late_sum[:d]), own_block(late_sum[d:])
    ada_rows = d // clips
    lifted_rows = lax.dynamic_slice_in_dim(all_lifted, me * ada_rows, ada_rows, 1)
    grad_w_ada = jnp.dot(lifted_rows.T, all_terms, precision=lax.Precision.HIGHEST)
    grad_b_ada = own_block(jnp.sum(all_terms, axis=0))

    rows = d // clips
    block_out = from_quadrants(out_pieces).reshape(tokens.shape)
    if fast:
        side = shards // 2
        places = []
        for j in range(FF_PARTS):
            places += [[(0, 0, (c * side + m) * FF_PARTS + j) for c in range(2)] for m in range(side)]
            places += [[(1, j, c * side + m) for c in range(2)] for m in range(side)]
        places += [[(2, 0, c * side + m) for c in range(2)] for m in range(side)]
        sum_wu, sum_wd, sum_wo = assemble(
            core_arr, [front.finish(), rear.finish()], places, [(rows, ff), (ff // clips, d), (rows, d)]
        )
        places, first = [], 0
        for count in (FIRST_PAIRS // 2, (pairs - FIRST_PAIRS) // 2):
            for part in range(3):
                places += [
                    [(0, 0, part * shards + first + c * count + m) for c in range(2)] for m in range(count)
                ]
            first += 2 * count
        (sum_qkv,) = assemble(core_arr, [last.finish()], places, [(rows, 3 * d)])
    else:

        def share(whole_grad):
            part = lax.psum_scatter(whole_grad.astype(f32), "clip", scatter_dimension=0, tiled=True)
            return lax.psum(part, "win")

        def flat_rows(blocks):
            return blocks.transpose(0, 2, 1, 3).reshape(d, -1, LANES)

        halves = len(ffs[0][0][0]) // 2
        ups = [jnp.stack([flat_rows(g[:, :halves]) for g in f], axis=2).reshape(d, -1) for f in ffs]
        sum_wu = share(jnp.concatenate(ups, axis=1))
        downs = [jnp.concatenate([flat_rows(g[:, halves:]).reshape(d, -1) for g in f], axis=1) for f in ffs]
        sum_wd = share(jnp.concatenate(downs, axis=0))
        sum_wo = share(jnp.concatenate([flat_rows(g).reshape(d, -1) for g in wos], axis=1))
        parts = [
            jnp.concatenate([flat_rows(g).reshape(d, 3, -1) for g in q], axis=2) for q in (qas, qbs)
        ]
        sum_qkv = share(jnp.concatenate(parts, axis=2).reshape(d, 3 * d))
    grad_tokens = from_quadrants(token_pieces).reshape(tokens.shape)
    return (
        block_out,
        grad_tokens,
        sum_qkv,
        sum_bq,
        sum_bv,
        sum_wo,
        sum_bo,
        sum_wu,
        sum_bu,
        sum_wd,
        sum_bd,
        grad_w_ada,
        grad_b_ada,
        sum_rel,
    )


def solution(mesh):
    placed = (
        P("clip", "win", None, None),
        P("clip", None),
        P("clip", None),
    ) + (P(),) * 13 + (P("clip", "win", None, None),)
    return jax.shard_map(
        local,
        mesh=mesh,
        in_specs=placed,
        out_specs=(
            P("clip", "win", None, None),
            P("clip", "win", None, None),
            P("clip", None),
            P("clip"),
            P("clip"),
            P("clip", None),
            P("clip"),
            P("clip", None),
            P("clip"),
            P("clip", None),
            P("clip"),
            P("clip", None),
            P("clip"),
            P("clip", None),
        ),
        check_vma=False,
    )
```

time: 738 us -> 518 us (0.70)
  waiting for transfers between devices: 218 us -> 64.1 us
  Pallas kernels: 324 us -> 279 us
  local copies, waits for them, and re-layouts: 50.6 us -> 27.5 us
  other arithmetic: 49.7 us -> 72 us
  starting transfers between devices: 73.4 us -> 54.3 us
    ppermute x59 -> x42, waiting for transfers between devices: 212 us -> 58.1 us  [trade(): return lax.ppermute(array, axis, flip(axis, bit))]
    pallas_call x12, Pallas kernels: 242 us -> 197 us  [the longest x4 78.3 us: ff_part(): pl.pallas_call(functools.partial(ff_part_kernel, count), grid_spec=pltpu....]
    ppermute x59 -> x42, starting transfers between devices: 56.3 us -> 38 us  [trade(): return lax.ppermute(array, axis, flip(axis, bit))]
    convert_element_type x28, other arithmetic: 33.6 us -> 49.9 us  [add_low(): return (a.astype(f32) + b.astype(f32)).astype(bf16)]
  transfers between devices with their start and end apart: 63 -> 46, of which waited for: 29 -> 13; matrix products, arithmetic and copies ran while one was open for 13% -> 11% of each run, Pallas kernels for 12% -> 49%
where the time goes in v2:
time: 518 us; the launch traced here: 509 us
  Pallas kernels  279 us (54%)
  other arithmetic  72 us (14%)
  waiting for transfers between devices  64.1 us (12%)
  starting transfers between devices  54.3 us (10%)
  local copies, waits for them, and re-layouts  27.5 us (5%)
  matrix products  10.6 us (2%)
    pallas_call x4, Pallas kernels, ff_part(): pl.pallas_call(functools.partial(ff_part_kernel, count), grid_spec=pltpu....  78.3 us
    ppermute x42, waiting for transfers between devices, trade(): return lax.ppermute(array, axis, flip(axis, bit))  58.1 us
    convert_element_type x28, other arithmetic, add_low(): return (a.astype(f32) + b.astype(f32)).astype(bf16)  49.9 us
    pallas_call x1, Pallas kernels, ff_join(): pl.pallas_call(functools.partial(ff_join_kernel, parts, blocks, units), g...  49.8 us
    ppermute x42, starting transfers between devices, trade(): return lax.ppermute(array, axis, flip(axis, bit))  38 us
    pallas_call x2, Pallas kernels, attn_backward(): pl.pallas_call(functools.partial(attn_back_kernel, windows), grid_spec=pl...  26.7 us
    pallas_call x2, Pallas kernels, qkv_weight(): pl.pallas_call(qkv_weight_kernel, grid_spec=pltpu.PrefetchScalarGridSpec(...  21.6 us
    pallas_call x1, Pallas kernels, bias_gather(): pl.pallas_call(bias_kernel, grid=(rows // 8,), in_specs=[pl.BlockSpec((8,...  19.1 us
  transfers between devices with their start and end apart: 46, of which 13 were waited for; matrix products, arithmetic and copies ran while one was open for 11% of the time, Pallas kernels for 49%

profile of v2, /device:TPU:0, one launch (start us, length us, event | category | flops | bytes accessed | tf_op | source)
XLA Modules:
  0.0 509.2 jit_solution(11053560001180062927)
XLA Ops:
  0.7 3.6 copy.50
  4.3 4.2 all-to-all-start.1
  8.5 3.6 copy.49
  13.6 19.1 %bias_gather.1.mine_ref = f32[8,160,640]{2,1,0:T(8,128)} custom-call(s32[160,384]{1,0:T(8,128)} %pad.6.idx_ref, bf16[256,256]{1,0:T(8,128)(2,1)} %pad_maximum_fusion.10.tab_ref), custom_call_target="tpu_custom_call" | custom-call | flops 900000000 | bytes 1800000 | tf_op jit(solution)/shard_map/bias_gather/pallas_call | solution.py:114
  33.9 6.0 %all-to-all-done.1 = bf16[4,5,64,1024]{3,2,1,0:T(8,128)(2,1)S(1)} async-done(((bf16[4,5,64,1024]{3,2,1,0:T(8,128)(2,1)}), bf16[4,5,64,1024]{3,2,1,0:T(8,128)(2,1)S(1)}, u32[]{:S(2)}, u32[]{:S(2)}) %all-to-all-start.1) | async-done | bytes 2621472 | tf_op jit(solution)/shard_map/all_to_all | solution.py:985
  41.4 3.7 all-to-all-start
  45.1 6.3 %fusion.5 = f32[1,6144]{1,0:T(1,128)S(1)} fusion(bf16[1024,6144]{1,0:T(8,128)(2,1)} %param.30, bf16[1,1024]{1,0:T(2,128)(2,1)S(1)} %copy-done.31), kind=kOutput, calls=%fused_computation.104 | convolution fusion | flops 12589056 | bytes 12609536 | tf_op jit(solution)/shard_map/dot_general | solution.py:1037
  56.4 15.9 %norm_qkv.1 = (bf16[1280,1024]{1,0:T(8,128)(2,1)}, bf16[1280,1024]{1,0:T(8,128)(2,1)}, bf16[1280,3072]{1,0:T(8,128)(2,1)}) custom-call(s32[20]{0:T(128)} %select_reduce_fusion.4.src_ref.refs_1_, bf16[20,64,1024]{2,1,0:T(8,128)(2,1)} %bitcast.98, bf16[20,64,1024]{2,1,0:T(8,128)(2,1)} %bitcast.99, bf16[20,64,1024]{2,1,0:T(8,128)(2,1)} %bitcast.100, ...), custom_call_target="tpu_custom_call" | custom-call | flops 600000000 | bytes 1200000 | tf_op jit(solution)/shard_map/norm_qkv/pallas_call | solution.py:228
  72.4 17.7 %attn_forward.1 = (bf16[1280,1024]{1,0:T(8,128)(2,1)}, bf16[8,4,320,640]{3,2,1,0:T(8,128)(2,1)}, f32[1280,1024]{1,0:T(8,128)}) custom-call(s32[1]{0:T(128)} %bitcast.1.core_ref, bf16[1280,3072]{1,0:T(8,128)(2,1)} %get-tuple-element.183.q_ref.k_ref.v_ref, bf16[1280,3072]{1,0:T(8,128)(2,1)} %get-tuple-element.183.q_ref.k_ref.v_ref, ...), custom_call_target="tpu_custom_call" | custom-call | flops 900000000 | bytes 1800000 | tf_op jit(solution)/shard_map/attn_forward/pallas_call | solution.py:314
  91.6 10.7 %out_norm.1 = (bf16[1280,1024]{1,0:T(8,128)(2,1)}, bf16[1280,1024]{1,0:T(8,128)(2,1)}, bf16[1280,1024]{1,0:T(8,128)(2,1)}) custom-call(s32[20]{0:T(128)} %select_reduce_fusion.4.src_ref.refs_1_, bf16[20,64,1024]{2,1,0:T(8,128)(2,1)} %bitcast.90, bf16[20,64,1024]{2,1,0:T(8,128)(2,1)} %bitcast.91, bf16[20,64,1024]{2,1,0:T(8,128)(2,1)} %bitcast.92, ...), custom_call_target="tpu_custom_call" | custom-call | flops 300000000 | bytes 600000 | tf_op jit(solution)/shard_map/out_norm/pallas_call | solution.py:425
  102.3 19.6 %ff_part.4 = (bf16[4,1280,1024]{2,1,0:T(8,128)(2,1)}, bf16[4,1280,1024]{2,1,0:T(8,128)(2,1)}, bf16[8,8,128,128]{3,2,1,0:T(8,128)(2,1)}, bf16[8,8,128,128]{3,2,1,0:T(8,128)(2,1)}, f32[2,1,512]{2,1,0:T(1,128)}) custom-call(s32[8]{0:T(128)} %broadcast_multiply_fusion.fo_ref, s32[4]{0:T(128)} %broadcast_and_fusion.co_ref, s32[8]{0:T(128)} %get-tuple-element.395.inv_ref.refs_2_, ...), custom_call_target="tpu_custom_call" | custom-call | flops 1000000000 | bytes 2000000 | tf_op jit(solution)/shard_map/ff_part/pallas_call | solution.py:516
  123.0 19.5 %ff_part.5 = (bf16[4,1280,1024]{2,1,0:T(8,128)(2,1)}, bf16[4,1280,1024]{2,1,0:T(8,128)(2,1)}, bf16[8,8,128,128]{3,2,1,0:T(8,128)(2,1)}, bf16[8,8,128,128]{3,2,1,0:T(8,128)(2,1)}, f32[2,1,512]{2,1,0:T(1,128)}) custom-call(s32[8]{0:T(128)} %get-tuple-element.397.fo_ref, s32[4]{0:T(128)} %broadcast_and_fusion.co_ref, ...), custom_call_target="tpu_custom_call", output_to_operand_aliasing={{0}: (18, {}), {1}: (19, {})} | custom-call | flops 1000000000 | bytes 2000000 | tf_op jit(solution)/shard_map/ff_part/pallas_call | solution.py:516
  142.5 3.6 add_convert_fusion.8
  149.0 19.8 %ff_part.6 = (bf16[4,1280,1024]{2,1,0:T(8,128)(2,1)}, bf16[4,1280,1024]{2,1,0:T(8,128)(2,1)}, bf16[8,8,128,128]{3,2,1,0:T(8,128)(2,1)}, bf16[8,8,128,128]{3,2,1,0:T(8,128)(2,1)}, f32[2,1,512]{2,1,0:T(1,128)}) custom-call(s32[8]{0:T(128)} %broadcast_add_fusion.2.fo_ref, s32[4]{0:T(128)} %broadcast_and_fusion.co_ref, ...), custom_call_target="tpu_custom_call", output_to_operand_aliasing={{0}: (18, {}), {1}: (19, {})} | custom-call | flops 1000000000 | bytes 2000000 | tf_op jit(solution)/shard_map/ff_part/pallas_call | solution.py:516
  168.8 3.8 collective-permute-done.2
  172.5 2.6 add_convert_fusion.20
  180.3 19.5 %ff_part.7 = (bf16[4,1280,1024]{2,1,0:T(8,128)(2,1)}, bf16[4,1280,1024]{2,1,0:T(8,128)(2,1)}, bf16[8,8,128,128]{3,2,1,0:T(8,128)(2,1)}, bf16[8,8,128,128]{3,2,1,0:T(8,128)(2,1)}, f32[2,1,512]{2,1,0:T(1,128)}) custom-call(s32[8]{0:T(128)} %get-tuple-element.396.fo_ref, s32[4]{0:T(128)} %broadcast_and_fusion.co_ref, ...), custom_call_target="tpu_custom_call", output_to_operand_aliasing={{0}: (18, {}), {1}: (19, {})} | custom-call | flops 1000000000 | bytes 2000000 | tf_op jit(solution)/shard_map/ff_part/pallas_call | solution.py:516
  199.8 3.1 collective-permute-done.5
  204.0 2.6 add_convert_fusion.18
  213.0 49.8 %ff_join.1 = (bf16[1280,1024]{1,0:T(8,128)(2,1)}, f32[8,1024]{1,0:T(8,128)}, bf16[1280,1024]{1,0:T(8,128)(2,1)}, bf16[8,4,128,128]{3,2,1,0:T(8,128)(2,1)}, bf16[...) custom-call(s32[32]{0:T(128)} %pad_add_fusion.refs_0_, s32[20]{0:T(128)} %select_reduce_fusion.4.src_ref.refs_1_, ...), custom_call_target="tpu_custom_call" | custom-call | flops 2249999872 | bytes 4500000 | tf_op jit(solution)/shard_map/ff_join/pallas_call | solution.py:666
  264.1 2.6 add_convert_fusion.16
  269.4 3.9 all-to-all-start.2
  273.6 18.6 %attn_backward.2 = (bf16[3,1280,768]{2,1,0:T(8,128)(2,1)}, bf16[6,160,640]{2,1,0:T(8,128)(2,1)}, bf16[6,160,640]{2,1,0:T(8,128)(2,1)}) custom-call(s32[1]{0:T(128)} %bitcast.1.core_ref, bf16[1280,3072]{1,0:T(8,128)(2,1)} %get-tuple-element.183.q_ref.k_ref.v_ref, bf16[1280,3072]{1,0:T(8,128)(2,1)} %get-tuple-element.183.q_ref.k_ref.v_ref, ...), custom_call_target="tpu_custom_call" | custom-call | flops 900000000 | bytes 1800000 | tf_op jit(solution)/shard_map/attn_backward/pallas_call | solution.py:382
  295.9 2.9 add_convert_fusion.13
  298.9 2.6 add_convert_fusion.12
  302.8 2.6 collective-permute-start.13
  305.8 2.6 collective-permute-start.15
  308.3 13.0 %qkv_weight.2 = (bf16[8,9,128,128]{3,2,1,0:T(8,128)(2,1)}, bf16[8,9,128,128]{3,2,1,0:T(8,128)(2,1)}) custom-call(s32[8]{0:T(128)} %get-tuple-element.395.inv_ref.refs_2_, s32[2]{0:T(128)} %pad_add_fusion.1.flag_ref.refs_3_, bf16[1280,1024]{1,0:T(8,128)(2,1)} %get-tuple-element.244.n_ref, bf16[3,1280,768]{2,1,0:T(8,128)(2,1)} %get-tuple-element.256.a_ref.b_ref.refs_0_, ...), custom_call_target="tpu_custom_call" | custom-call | flops 300000000 | bytes 600000 | tf_op jit(solution)/shard_map/qkv_weight/pallas_call | solution.py:723
  321.4 14.1 %collective-permute-done.14 = bf16[1,8,128,128]{3,2,1,0:T(8,128)(2,1)} collective-permute-done((bf16[1,8,128,128]{3,2,1,0:T(8,128)(2,1)S(1)}, bf16[1,8,128,128]{3,2,1,0:T(8,128)(2,1)}, u32[]{:S(2)}, u32[]{:S(2)}) %collective-permute-start.14) | collective-permute-done | bytes 262176 | tf_op jit(solution)/shard_map/ppermute | solution.py:859
  335.5 4.3 collective-permute-done.15
  349.5 3.0 collective-permute-start.22
  352.6 8.2 %attn_backward.3 = (bf16[3,1280,256]{2,1,0:T(8,128)(2,1)}, bf16[2,160,640]{2,1,0:T(8,128)(2,1)}, bf16[2,160,640]{2,1,0:T(8,128)(2,1)}) custom-call(s32[1]{0:T(128)} %bitcast.1.core_ref, bf16[1280,3072]{1,0:T(8,128)(2,1)} %get-tuple-element.183.q_ref.k_ref.v_ref, bf16[1280,3072]{1,0:T(8,128)(2,1)} %get-tuple-element.183.q_ref.k_ref.v_ref, ...), custom_call_target="tpu_custom_call" | custom-call | flops 300000000 | bytes 600000 | tf_op jit(solution)/shard_map/attn_backward/pallas_call | solution.py:382
  360.8 5.1 %add_convert_fusion = (bf16[4,9,128,128]{3,2,1,0:T(8,128)(2,1)}, bf16[4,9,128,128]{3,2,1,0:T(8,128)(2,1)}) fusion(bf16[8,9,128,128]{3,2,1,0:T(8,128)(2,1)} %collective-permute-done.18, bf16[8,9,128,128]{3,2,1,0:T(8,128)(2,1)} %get-tuple-element.257), kind=kLoop, calls=%fused_computation | loop fusion | flops 4718592 | bytes 7077888 | tf_op jit(solution)/shard_map/convert_element_type | solution.py:863
  367.4 8.6 %qkv_weight.3 = (bf16[8,3,128,128]{3,2,1,0:T(8,128)(2,1)}, bf16[8,3,128,128]{3,2,1,0:T(8,128)(2,1)}) custom-call(s32[8]{0:T(128)} %get-tuple-element.395.inv_ref.refs_2_, s32[2]{0:T(128)} %pad_add_fusion.1.flag_ref.refs_3_, bf16[1280,1024]{1,0:T(8,128)(2,1)} %get-tuple-element.244.n_ref, bf16[3,1280,256]{2,1,0:T(8,128)(2,1)} %get-tuple-element.280.a_ref.b_ref.refs_1_, ...), custom_call_target="tpu_custom_call" | custom-call | flops 300000000 | bytes 600000 | tf_op jit(solution)/shard_map/qkv_weight/pallas_call | solution.py:723
  378.2 2.7 reduce-precision_convert_fusion
  382.7 18.1 %qkv_backward.1 = (bf16[20,64,1024]{2,1,0:T(8,128)(2,1)}, f32[8,1024]{1,0:T(8,128)}) custom-call(s32[20]{0:T(128)} %select_reduce_fusion.4.src_ref.refs_1_, bf16[3,1280,768]{2,1,0:T(8,128)(2,1)} %get-tuple-element.256.a_ref.b_ref.refs_0_, bf16[3,1280,256]{2,1,0:T(8,128)(2,1)} %get-tuple-element.280.a_ref.b_ref.refs_1_, bf16[1024,3072]{1,0:T(8,128)(2,1)} %refs_2_.9, ...), custom_call_target="tpu_custom_call" | custom-call | flops 700000000 | bytes 1400000 | tf_op jit(solution)/shard_map/qkv_backward/pallas_call | solution.py:798
  400.8 4.5 all-to-all-start.3
  408.5 2.7 add_convert_fusion.10
  415.8 13.9 %bucket_sums.1 = f32[8,16,256]{2,1,0:T(8,128)} custom-call(s32[8]{0:T(128)} %get-tuple-element.395.inv_ref.refs_2_, s32[160,384]{1,0:T(8,128)} %pad.6.idx_ref, bf16[6,160,640]{2,1,0:T(8,128)(2,1)} %get-tuple-element.303.refs_0_, bf16[2,160,640]{2,1,0:T(8,128)(2,1)} %get-tuple-element.304.refs_1_, bf16[6,160,640]{2,1,0:T(8,128)(2,1)} %collective-permute-done.20.refs_2_, ...), custom_call_target="tpu_custom_call" | custom-call | flops 700000000 | bytes 1400000 | tf_op jit(solution)/shard_map/bucket_sums/pallas_call | solution.py:185
  434.7 2.9 collective-permute-start.30
  437.6 6.8 %collective-permute-done.31 = bf16[2,3,128,128]{3,2,1,0:T(8,128)(2,1)S(1)} collective-permute-done((bf16[2,3,128,128]{3,2,1,0:T(8,128)(2,1)S(1)}, bf16[2,3,128,128]{3,2,1,0:T(8,128)(2,1)S(1)}, u32[]{:S(2)}, u32[]{:S(2)}) %collective-permute-start.31) | collective-permute-done | bytes 196640 | tf_op jit(solution)/shard_map/ppermute | solution.py:859
  445.9 8.1 %collective-permute-done.30 = bf16[1,9,128,128]{3,2,1,0:T(8,128)(2,1)S(1)} collective-permute-done((bf16[1,9,128,128]{3,2,1,0:T(8,128)(2,1)S(1)}, bf16[1,9,128,128]{3,2,1,0:T(8,128)(2,1)S(1)}, u32[]{:S(2)}, u32[]{:S(2)}) %collective-permute-start.30) | collective-permute-done | bytes 294944 | tf_op jit(solution)/shard_map/ppermute | solution.py:859
  463.7 4.7 collective-permute-done.36
  468.4 3.9 collective-permute-done.35
  476.6 5.0 collective-permute-done.38
  486.6 4.2 assemble.3
  490.9 3.6 copy.55
  501.8 4.3 fusion.1
  (278 shorter events, 94.6 us)
Async XLA Ops:
  4.3 35.6 %all-to-all-start.1 = ((bf16[4,5,64,1024]{3,2,1,0:T(8,128)(2,1)}), bf16[4,5,64,1024]{3,2,1,0:T(8,128)(2,1)S(1)}, u32[]{:S(2)}, u32[]{:S(2)}) async-start(bf16[4,5,64,1024]{3,2,1,0:T(8,128)(2,1)} %bitcast.104), calls=%async_computation.1 | async-start | bytes 5242880 | tf_op jit(solution)/shard_map/all_to_all | solution.py:985
  32.7 39.6 %collective-permute-start = (f32[8,160,640]{2,1,0:T(8,128)}, f32[8,160,640]{2,1,0:T(8,128)}, u32[]{:S(2)}, u32[]{:S(2)}) collective-permute-start(f32[8,160,640]{2,1,0:T(8,128)} %bias_gather.1.mine_ref), channel_id=1, source_target_pairs={{0,1},{1,0},{2,3},{3,2},{4,5},{5,4},{6,7},{7,6},{8,9},{9,8},{10,11... | collective-permute-start | bytes 9830408 | tf_op jit(solution)/shard_map/ppermute | solution.py:859
  41.4 48.7 %all-to-all-start = ((bf16[4,5,64,1024]{3,2,1,0:T(8,128)(2,1)}), bf16[4,5,64,1024]{3,2,1,0:T(8,128)(2,1)S(1)}, u32[]{:S(2)}, u32[]{:S(2)}) async-start(bf16[4,5,64,1024]{3,2,1,0:T(8,128)(2,1)} %bitcast.103), calls=%async_computation | async-start | bytes 5242880 | tf_op jit(solution)/shard_map/all_to_all | solution.py:985
  121.9 20.5 %collective-permute-start.1 = (bf16[8,8,128,128]{3,2,1,0:T(8,128)(2,1)}, bf16[8,8,128,128]{3,2,1,0:T(8,128)(2,1)}, u32[]{:S(2)}, u32[]{:S(2)}) collective-permute-start(bf16[8,8,128,128]{3,2,1,0:T(8,128)(2,1)} %get-tuple-element.194), channel_id=1, source_target_pairs={{0,1},{1,0},{2,3},{3,2},{4,5},{5,4},{6,7},{7,6},{8,9},{9,8},{10,11... | collective-permute-start | bytes 6291464 | tf_op jit(solution)/shard_map/ppermute | solution.py:859
  146.1 26.5 %collective-permute-start.3 = (bf16[8,8,128,128]{3,2,1,0:T(8,128)(2,1)}, bf16[8,8,128,128]{3,2,1,0:T(8,128)(2,1)S(1)}, u32[]{:S(2)}, u32[]{:S(2)}) collective-permute-start(bf16[8,8,128,128]{3,2,1,0:T(8,128)(2,1)} %get-tuple-element.205), channel_id=1, source_target_pairs={{0,1},{1,0},{2,3},{3,2},{4,5},{5,4},{6,7},{7,6},{8,9},{9,8},{10,11... | collective-permute-start | bytes 6291464 | tf_op jit(solution)/shard_map/ppermute | solution.py:859
  146.1 26.4 %collective-permute-start.2 = (bf16[4,8,128,128]{3,2,1,0:T(8,128)(2,1)}, bf16[4,8,128,128]{3,2,1,0:T(8,128)(2,1)}, u32[]{:S(2)}, u32[]{:S(2)}) collective-permute-start(bf16[4,8,128,128]{3,2,1,0:T(8,128)(2,1)} %get-tuple-element.204), channel_id=1, source_target_pairs={{0,4},{4,0},{8,12},{12,8},{16,20},{20,16},{24,28},{28,24},{1,5},{5... | collective-permute-start | bytes 3145736 | tf_op jit(solution)/shard_map/ppermute | solution.py:859
  177.0 25.9 %collective-permute-start.6 = (bf16[8,8,128,128]{3,2,1,0:T(8,128)(2,1)}, bf16[8,8,128,128]{3,2,1,0:T(8,128)(2,1)S(1)}, u32[]{:S(2)}, u32[]{:S(2)}) collective-permute-start(bf16[8,8,128,128]{3,2,1,0:T(8,128)(2,1)} %get-tuple-element.222), channel_id=1, source_target_pairs={{0,1},{1,0},{2,3},{3,2},{4,5},{5,4},{6,7},{7,6},{8,9},{9,8},{10,11... | collective-permute-start | bytes 6291464 | tf_op jit(solution)/shard_map/ppermute | solution.py:859
  177.0 25.9 %collective-permute-start.5 = (bf16[4,8,128,128]{3,2,1,0:T(8,128)(2,1)}, bf16[4,8,128,128]{3,2,1,0:T(8,128)(2,1)}, u32[]{:S(2)}, u32[]{:S(2)}) collective-permute-start(bf16[4,8,128,128]{3,2,1,0:T(8,128)(2,1)} %get-tuple-element.221), channel_id=1, source_target_pairs={{0,4},{4,0},{8,12},{12,8},{16,20},{20,16},{24,28},{28,24},{1,5},{5... | collective-permute-start | bytes 3145736 | tf_op jit(solution)/shard_map/ppermute | solution.py:859
  178.7 21.1 %collective-permute-start.4 = (bf16[2,8,128,128]{3,2,1,0:T(8,128)(2,1)}, bf16[2,8,128,128]{3,2,1,0:T(8,128)(2,1)}, u32[]{:S(2)}, u32[]{:S(2)}) collective-permute-start(bf16[2,8,128,128]{3,2,1,0:T(8,128)(2,1)} %get-tuple-element.220), channel_id=1, source_target_pairs={{0,8},{4,12},{8,0},{12,4},{16,24},{20,28},{24,16},{28,20},{1,9},{5... | collective-permute-start | bytes 1572872 | tf_op jit(solution)/shard_map/ppermute | solution.py:859
  208.4 54.4 %collective-permute-start.9 = (bf16[8,8,128,128]{3,2,1,0:T(8,128)(2,1)}, bf16[8,8,128,128]{3,2,1,0:T(8,128)(2,1)S(1)}, u32[]{:S(2)}, u32[]{:S(2)}) collective-permute-start(bf16[8,8,128,128]{3,2,1,0:T(8,128)(2,1)} %get-tuple-element.236), channel_id=1, source_target_pairs={{0,1},{1,0},{2,3},{3,2},{4,5},{5,4},{6,7},{7,6},{8,9},{9,8},{10,11... | collective-permute-start | bytes 6291464 | tf_op jit(solution)/shard_map/ppermute | solution.py:859
  208.5 54.4 %collective-permute-start.8 = (bf16[4,8,128,128]{3,2,1,0:T(8,128)(2,1)}, bf16[4,8,128,128]{3,2,1,0:T(8,128)(2,1)}, u32[]{:S(2)}, u32[]{:S(2)}) collective-permute-start(bf16[4,8,128,128]{3,2,1,0:T(8,128)(2,1)} %get-tuple-element.235), channel_id=1, source_target_pairs={{0,4},{4,0},{8,12},{12,8},{16,20},{20,16},{24,28},{28,24},{1,5},{5... | collective-permute-start | bytes 3145736 | tf_op jit(solution)/shard_map/ppermute | solution.py:859
  210.2 52.6 %collective-permute-start.7 = (bf16[2,8,128,128]{3,2,1,0:T(8,128)(2,1)}, bf16[2,8,128,128]{3,2,1,0:T(8,128)(2,1)}, u32[]{:S(2)}, u32[]{:S(2)}) collective-permute-start(bf16[2,8,128,128]{3,2,1,0:T(8,128)(2,1)} %get-tuple-element.234), channel_id=1, source_target_pairs={{0,8},{4,12},{8,0},{12,4},{16,24},{20,28},{24,16},{28,20},{1,9},{5... | collective-permute-start | bytes 1572872 | tf_op jit(solution)/shard_map/ppermute | solution.py:859
  268.9 25.3 %collective-permute-start.11 = (bf16[4,8,128,128]{3,2,1,0:T(8,128)(2,1)}, bf16[4,8,128,128]{3,2,1,0:T(8,128)(2,1)}, u32[]{:S(2)}, u32[]{:S(2)}) collective-permute-start(bf16[4,8,128,128]{3,2,1,0:T(8,128)(2,1)} %get-tuple-element.249), channel_id=1, source_target_pairs={{0,4},{4,0},{8,12},{12,8},{16,20},{20,16},{24,28},{28,24},{1,5},{5... | collective-permute-start | bytes 3145736 | tf_op jit(solution)/shard_map/ppermute | solution.py:859
  269.4 24.8 %collective-permute-start.12 = (bf16[8,4,128,128]{3,2,1,0:T(8,128)(2,1)}, bf16[8,4,128,128]{3,2,1,0:T(8,128)(2,1)}, u32[]{:S(2)}, u32[]{:S(2)}) collective-permute-start(bf16[8,4,128,128]{3,2,1,0:T(8,128)(2,1)} %get-tuple-element.250), channel_id=1, source_target_pairs={{0,1},{1,0},{2,3},{3,2},{4,5},{5,4},{6,7},{7,6},{8,9},{9,8},{10,11... | collective-permute-start | bytes 3145736 | tf_op jit(solution)/shard_map/ppermute | solution.py:859
  269.4 52.0 %all-to-all-start.2 = ((bf16[4,5,64,1024]{3,2,1,0:T(8,128)(2,1)}), bf16[4,5,64,1024]{3,2,1,0:T(8,128)(2,1)S(1)}, u32[]{:S(2)}, u32[]{:S(2)}) async-start(bf16[4,5,64,1024]{3,2,1,0:T(8,128)(2,1)} %bitcast.126), calls=%async_computation.2 | async-start | bytes 5242880 | tf_op jit(solution)/shard_map/all_to_all | solution.py:985
  273.3 18.9 %collective-permute-start.10 = (bf16[2,8,128,128]{3,2,1,0:T(8,128)(2,1)}, bf16[2,8,128,128]{3,2,1,0:T(8,128)(2,1)}, u32[]{:S(2)}, u32[]{:S(2)}) collective-permute-start(bf16[2,8,128,128]{3,2,1,0:T(8,128)(2,1)} %get-tuple-element.248), channel_id=1, source_target_pairs={{0,8},{4,12},{8,0},{12,4},{16,24},{20,28},{24,16},{28,20},{1,9},{5... | collective-permute-start | bytes 1572872 | tf_op jit(solution)/shard_map/ppermute | solution.py:859
  301.5 38.4 %collective-permute-start.16 = (bf16[2,8,128,128]{3,2,1,0:T(8,128)(2,1)}, bf16[2,8,128,128]{3,2,1,0:T(8,128)(2,1)}, u32[]{:S(2)}, u32[]{:S(2)}) collective-permute-start(bf16[2,8,128,128]{3,2,1,0:T(8,128)(2,1)} %get-tuple-element.262), channel_id=1, source_target_pairs={{0,8},{4,12},{8,0},{12,4},{16,24},{20,28},{24,16},{28,20},{1,9},{5... | collective-permute-start | bytes 1572872 | tf_op jit(solution)/shard_map/ppermute | solution.py:859
  301.9 37.9 %collective-permute-start.17 = (bf16[4,4,128,128]{3,2,1,0:T(8,128)(2,1)}, bf16[4,4,128,128]{3,2,1,0:T(8,128)(2,1)}, u32[]{:S(2)}, u32[]{:S(2)}) collective-permute-start(bf16[4,4,128,128]{3,2,1,0:T(8,128)(2,1)} %get-tuple-element.263), channel_id=1, source_target_pairs={{0,4},{4,0},{8,12},{12,8},{16,20},{20,16},{24,28},{28,24},{1,5},{5... | collective-permute-start | bytes 1572872 | tf_op jit(solution)/shard_map/ppermute | solution.py:859
  302.8 18.5 %collective-permute-start.13 = (bf16[1,8,128,128]{3,2,1,0:T(8,128)(2,1)S(1)}, bf16[1,8,128,128]{3,2,1,0:T(8,128)(2,1)}, u32[]{:S(2)}, u32[]{:S(2)}) collective-permute-start(bf16[1,8,128,128]{3,2,1,0:T(8,128)(2,1)S(1)} %add_convert_fusion.40), channel_id=1, source_target_pairs={{0,16},{4,20},{8,24},{12,28},{16,0},{20,4},{24,8},{28,12},{1,17},{... | collective-permute-start | bytes 786440 | tf_op jit(solution)/shard_map/ppermute | solution.py:859
  305.4 30.1 %collective-permute-start.14 = (bf16[1,8,128,128]{3,2,1,0:T(8,128)(2,1)S(1)}, bf16[1,8,128,128]{3,2,1,0:T(8,128)(2,1)}, u32[]{:S(2)}, u32[]{:S(2)}) collective-permute-start(bf16[1,8,128,128]{3,2,1,0:T(8,128)(2,1)S(1)} %add_convert_fusion.39), channel_id=1, source_target_pairs={{0,16},{4,20},{8,24},{12,28},{16,0},{20,4},{24,8},{28,12},{1,17},{... | collective-permute-start | bytes 786440 | tf_op jit(solution)/shard_map/ppermute | solution.py:859
  305.8 34.1 %collective-permute-start.15 = (bf16[1,8,128,128]{3,2,1,0:T(8,128)(2,1)}, bf16[1,8,128,128]{3,2,1,0:T(8,128)(2,1)}, u32[]{:S(2)}, u32[]{:S(2)}) collective-permute-start(bf16[1,8,128,128]{3,2,1,0:T(8,128)(2,1)} %add_convert_fusion.38), channel_id=1, source_target_pairs={{0,16},{4,20},{8,24},{12,28},{16,0},{20,4},{24,8},{28,12},{1,17},{... | collective-permute-start | bytes 786440 | tf_op jit(solution)/shard_map/ppermute | solution.py:859
  347.0 13.8 %collective-permute-start.18 = (bf16[8,9,128,128]{3,2,1,0:T(8,128)(2,1)}, bf16[8,9,128,128]{3,2,1,0:T(8,128)(2,1)}, u32[]{:S(2)}, u32[]{:S(2)}) collective-permute-start(bf16[8,9,128,128]{3,2,1,0:T(8,128)(2,1)} %get-tuple-element.275), channel_id=1, source_target_pairs={{0,1},{1,0},{2,3},{3,2},{4,5},{5,4},{6,7},{7,6},{8,9},{9,8},{10,11... | collective-permute-start | bytes 7077896 | tf_op jit(solution)/shard_map/ppermute | solution.py:859
  347.0 28.9 %collective-permute-start.20 = (bf16[6,160,640]{2,1,0:T(8,128)(2,1)}, bf16[6,160,640]{2,1,0:T(8,128)(2,1)}, u32[]{:S(2)}, u32[]{:S(2)}) collective-permute-start(bf16[6,160,640]{2,1,0:T(8,128)(2,1)} %get-tuple-element.283), channel_id=1, source_target_pairs={{0,1},{1,0},{2,3},{3,2},{4,5},{5,4},{6,7},{7,6},{8,9},{9,8},{10,11... | collective-permute-start | bytes 3686408 | tf_op jit(solution)/shard_map/ppermute | solution.py:859
  347.6 13.2 %collective-permute-start.19 = (bf16[2,4,128,128]{3,2,1,0:T(8,128)(2,1)S(1)}, bf16[2,4,128,128]{3,2,1,0:T(8,128)(2,1)S(1)}, u32[]{:S(2)}, u32[]{:S(2)}) collective-permute-start(bf16[2,4,128,128]{3,2,1,0:T(8,128)(2,1)S(1)} %get-tuple-element.276), channel_id=1, source_target_pairs={{0,8},{4,12},{8,0},{12,4},{16,24},{20,28},{24,16},{28,20},{1,9},{5... | collective-permute-start | bytes 786440 | tf_op jit(solution)/shard_map/ppermute | solution.py:859
  347.7 28.3 %collective-permute-start.21 = (bf16[1,24,128,128]{3,2,1,0:T(8,128)(2,1)}, bf16[1,24,128,128]{3,2,1,0:T(8,128)(2,1)}, u32[]{:S(2)}, u32[]{:S(2)}) collective-permute-start(bf16[1,24,128,128]{3,2,1,0:T(8,128)(2,1)} %pad_maximum_fusion), channel_id=1, source_target_pairs={{0,2},{1,3},{2,0},{3,1},{4,6},{5,7},{6,4},{7,5},{8,10},{9,11},{10,... | collective-permute-start | bytes 2359304 | tf_op jit(solution)/shard_map/ppermute | solution.py:859
  349.5 26.4 %collective-permute-start.22 = (bf16[1,8,128,128]{3,2,1,0:T(8,128)(2,1)S(1)}, bf16[1,8,128,128]{3,2,1,0:T(8,128)(2,1)}, u32[]{:S(2)}, u32[]{:S(2)}) collective-permute-start(bf16[1,8,128,128]{3,2,1,0:T(8,128)(2,1)S(1)} %add_convert_fusion.31), channel_id=1, source_target_pairs={{0,16},{4,20},{8,24},{12,28},{16,0},{20,4},{24,8},{28,12},{1,17},{... | collective-permute-start | bytes 786440 | tf_op jit(solution)/shard_map/ppermute | solution.py:859
  366.0 10.0 %collective-permute-start.23 = (bf16[1,4,128,128]{3,2,1,0:T(8,128)(2,1)S(1)}, bf16[1,4,128,128]{3,2,1,0:T(8,128)(2,1)S(1)}, u32[]{:S(2)}, u32[]{:S(2)}) collective-permute-start(bf16[1,4,128,128]{3,2,1,0:T(8,128)(2,1)S(1)} %add_convert_fusion.45), channel_id=1, source_target_pairs={{0,16},{4,20},{8,24},{12,28},{16,0},{20,4},{24,8},{28,12},{1,17},{... | collective-permute-start | bytes 393224 | tf_op jit(solution)/shard_map/ppermute | solution.py:859
  366.1 39.3 %collective-permute-start.26 = (bf16[4,9,128,128]{3,2,1,0:T(8,128)(2,1)}, bf16[4,9,128,128]{3,2,1,0:T(8,128)(2,1)}, u32[]{:S(2)}, u32[]{:S(2)}) collective-permute-start(bf16[4,9,128,128]{3,2,1,0:T(8,128)(2,1)} %get-tuple-element.300), channel_id=1, source_target_pairs={{0,4},{4,0},{8,12},{12,8},{16,20},{20,16},{24,28},{28,24},{1,5},{5... | collective-permute-start | bytes 3538952 | tf_op jit(solution)/shard_map/ppermute | solution.py:859
  378.2 22.6 %copy-start.13 = (bf16[1,12,128,128]{3,2,1,0:T(8,128)(2,1)}, bf16[1,12,128,128]{3,2,1,0:T(8,128)(2,1)S(1)}, u32[]{:S(2)}) copy-start(bf16[1,12,128,128]{3,2,1,0:T(8,128)(2,1)S(1)} %pad_maximum_fusion.2) | copy-start | bytes 1179652
  380.9 24.4 %collective-permute-start.25 = (bf16[8,3,128,128]{3,2,1,0:T(8,128)(2,1)}, bf16[8,3,128,128]{3,2,1,0:T(8,128)(2,1)}, u32[]{:S(2)}, u32[]{:S(2)}) collective-permute-start(bf16[8,3,128,128]{3,2,1,0:T(8,128)(2,1)} %get-tuple-element.299), channel_id=1, source_target_pairs={{0,1},{1,0},{2,3},{3,2},{4,5},{5,4},{6,7},{7,6},{8,9},{9,8},{10,11... | collective-permute-start | bytes 2359304 | tf_op jit(solution)/shard_map/ppermute | solution.py:859
  380.9 24.4 %collective-permute-start.24 = (bf16[2,160,640]{2,1,0:T(8,128)(2,1)}, bf16[2,160,640]{2,1,0:T(8,128)(2,1)S(1)}, u32[]{:S(2)}, u32[]{:S(2)}) collective-permute-start(bf16[2,160,640]{2,1,0:T(8,128)(2,1)} %get-tuple-element.298), channel_id=1, source_target_pairs={{0,1},{1,0},{2,3},{3,2},{4,5},{5,4},{6,7},{7,6},{8,9},{9,8},{10,11... | collective-permute-start | bytes 1228808 | tf_op jit(solution)/shard_map/ppermute | solution.py:859
  381.4 23.9 %collective-permute-start.27 = (bf16[1,12,128,128]{3,2,1,0:T(8,128)(2,1)S(1)}, bf16[1,12,128,128]{3,2,1,0:T(8,128)(2,1)}, u32[]{:S(2)}, u32[]{:S(2)}) collective-permute-start(bf16[1,12,128,128]{3,2,1,0:T(8,128)(2,1)S(1)} %pad_maximum_fusion.2), channel_id=1, source_target_pairs={{0,2},{1,3},{2,0},{3,1},{4,6},{5,7},{6,4},{7,5},{8,10},{9,11},{10,... | collective-permute-start | bytes 1179656 | tf_op jit(solution)/shard_map/ppermute | solution.py:859
  400.8 55.1 %all-to-all-start.3 = ((bf16[4,5,64,1024]{3,2,1,0:T(8,128)(2,1)}), bf16[4,5,64,1024]{3,2,1,0:T(8,128)(2,1)}, u32[]{:S(2)}, u32[]{:S(2)}) async-start(bf16[4,5,64,1024]{3,2,1,0:T(8,128)(2,1)} %bitcast.124), calls=%async_computation.3 | async-start | bytes 5242880 | tf_op jit(solution)/shard_map/all_to_all | solution.py:985
  412.3 63.6 %copy-start.11 = (bf16[1,12,128,128]{3,2,1,0:T(8,128)(2,1)}, bf16[1,12,128,128]{3,2,1,0:T(8,128)(2,1)S(1)}, u32[]{:S(2)}) copy-start(bf16[1,12,128,128]{3,2,1,0:T(8,128)(2,1)S(1)} %reduce-precision_convert_fusion.2) | copy-start | bytes 1179652
  412.3 19.8 %collective-permute-start.28 = (bf16[4,3,128,128]{3,2,1,0:T(8,128)(2,1)}, bf16[4,3,128,128]{3,2,1,0:T(8,128)(2,1)}, u32[]{:S(2)}, u32[]{:S(2)}) collective-permute-start(bf16[4,3,128,128]{3,2,1,0:T(8,128)(2,1)} %get-tuple-element.311), channel_id=1, source_target_pairs={{0,4},{4,0},{8,12},{12,8},{16,20},{20,16},{24,28},{28,24},{1,5},{5... | collective-permute-start | bytes 1179656 | tf_op jit(solution)/shard_map/ppermute | solution.py:859
  413.8 18.4 %collective-permute-start.29 = (bf16[2,9,128,128]{3,2,1,0:T(8,128)(2,1)}, bf16[2,9,128,128]{3,2,1,0:T(8,128)(2,1)}, u32[]{:S(2)}, u32[]{:S(2)}) collective-permute-start(bf16[2,9,128,128]{3,2,1,0:T(8,128)(2,1)} %get-tuple-element.312), channel_id=1, source_target_pairs={{0,8},{4,12},{8,0},{12,4},{16,24},{20,28},{24,16},{28,20},{1,9},{5... | collective-permute-start | bytes 1769480 | tf_op jit(solution)/shard_map/ppermute | solution.py:859
  434.6 9.8 %collective-permute-start.31 = (bf16[2,3,128,128]{3,2,1,0:T(8,128)(2,1)S(1)}, bf16[2,3,128,128]{3,2,1,0:T(8,128)(2,1)S(1)}, u32[]{:S(2)}, u32[]{:S(2)}) collective-permute-start(bf16[2,3,128,128]{3,2,1,0:T(8,128)(2,1)S(1)} %get-tuple-element.322), channel_id=1, source_target_pairs={{0,8},{4,12},{8,0},{12,4},{16,24},{20,28},{24,16},{28,20},{1,9},{5... | collective-permute-start | bytes 589832 | tf_op jit(solution)/shard_map/ppermute | solution.py:859
  434.7 9.7 %collective-permute-start.32 = (f32[12,32,128]{2,1,0:T(8,128)S(1)}, f32[12,32,128]{2,1,0:T(8,128)S(1)}, u32[]{:S(2)}, u32[]{:S(2)}) collective-permute-start(f32[12,32,128]{2,1,0:T(8,128)S(1)} %pad_maximum_fusion.6), channel_id=1, source_target_pairs={{0,1},{1,0},{2,3},{3,2},{4,5},{5,4},{6,7},{7,6},{8,9},{9,8},{10,11... | collective-permute-start | bytes 589832 | tf_op jit(solution)/shard_map/ppermute | solution.py:859
  434.7 19.3 %collective-permute-start.30 = (bf16[1,9,128,128]{3,2,1,0:T(8,128)(2,1)S(1)}, bf16[1,9,128,128]{3,2,1,0:T(8,128)(2,1)S(1)}, u32[]{:S(2)}, u32[]{:S(2)}) collective-permute-start(bf16[1,9,128,128]{3,2,1,0:T(8,128)(2,1)S(1)} %add_convert_fusion.26), channel_id=1, source_target_pairs={{0,16},{4,20},{8,24},{12,28},{16,0},{20,4},{24,8},{28,12},{1,17},{... | collective-permute-start | bytes 884744 | tf_op jit(solution)/shard_map/ppermute | solution.py:859
  444.5 12.0 %collective-permute-start.34 = (f32[12,32,128]{2,1,0:T(8,128)S(1)}, f32[12,32,128]{2,1,0:T(8,128)}, u32[]{:S(2)}, u32[]{:S(2)}) collective-permute-start(f32[12,32,128]{2,1,0:T(8,128)S(1)} %add.284), channel_id=1, source_target_pairs={{0,2},{1,3},{2,0},{3,1},{4,6},{5,7},{6,4},{7,5},{8,10},{9,11},{10,... | collective-permute-start | bytes 589832 | tf_op jit(solution)/shard_map/ppermute | solution.py:859
  445.9 9.9 %collective-permute-start.33 = (bf16[1,3,128,128]{3,2,1,0:T(8,128)(2,1)S(1)}, bf16[1,3,128,128]{3,2,1,0:T(8,128)(2,1)S(1)}, u32[]{:S(2)}, u32[]{:S(2)}) collective-permute-start(bf16[1,3,128,128]{3,2,1,0:T(8,128)(2,1)S(1)} %add_convert_fusion.48), channel_id=1, source_target_pairs={{0,16},{4,20},{8,24},{12,28},{16,0},{20,4},{24,8},{28,12},{1,17},{... | collective-permute-start | bytes 294920 | tf_op jit(solution)/shard_map/ppermute | solution.py:859
  461.1 11.2 %collective-permute-start.35 = (bf16[1,12,128,128]{3,2,1,0:T(8,128)(2,1)S(1)}, bf16[1,12,128,128]{3,2,1,0:T(8,128)(2,1)}, u32[]{:S(2)}, u32[]{:S(2)}) collective-permute-start(bf16[1,12,128,128]{3,2,1,0:T(8,128)(2,1)S(1)} %pad_maximum_fusion.3), channel_id=1, source_target_pairs={{0,2},{1,3},{2,0},{3,1},{4,6},{5,7},{6,4},{7,5},{8,10},{9,11},{10,... | collective-permute-start | bytes 1179656 | tf_op jit(solution)/shard_map/ppermute | solution.py:859
  463.1 5.3 %collective-permute-start.36 = (f32[8,32,128]{2,1,0:T(8,128)}, f32[8,32,128]{2,1,0:T(8,128)}, u32[]{:S(2)}, u32[]{:S(2)}) collective-permute-start(f32[8,32,128]{2,1,0:T(8,128)} %concatenate.83), channel_id=1, source_target_pairs={{0,4},{4,0},{8,12},{12,8},{16,20},{20,16},{24,28},{28,24},{1,5},{5... | collective-permute-start | bytes 393224 | tf_op jit(solution)/shard_map/ppermute | solution.py:859
  476.0 5.6 %collective-permute-start.38 = (f32[10,32,128]{2,1,0:T(8,128)}, f32[10,32,128]{2,1,0:T(8,128)}, u32[]{:S(2)}, u32[]{:S(2)}) collective-permute-start(f32[10,32,128]{2,1,0:T(8,128)} %pad_maximum_fusion.8), channel_id=1, source_target_pairs={{0,8},{4,12},{8,0},{12,4},{16,24},{20,28},{24,16},{28,20},{1,9},{5... | collective-permute-start | bytes 491528 | tf_op jit(solution)/shard_map/ppermute | solution.py:859
  476.0 10.7 %collective-permute-start.40 = (bf16[1,24,128,128]{3,2,1,0:T(8,128)(2,1)}, bf16[1,24,128,128]{3,2,1,0:T(8,128)(2,1)}, u32[]{:S(2)}, u32[]{:S(2)}) collective-permute-start(bf16[1,24,128,128]{3,2,1,0:T(8,128)(2,1)} %reduce-precision_convert_fusion), channel_id=1, source_target_pairs={{0,1},{1,0},{2,3},{3,2},{4,5},{5,4},{6,7},{7,6},{8,9},{9,8},{10,11... | collective-permute-start | bytes 2359304 | tf_op jit(solution)/shard_map/ppermute | solution.py:859
  476.0 10.7 %collective-permute-start.41 = (bf16[1,12,128,128]{3,2,1,0:T(8,128)(2,1)S(1)}, bf16[1,12,128,128]{3,2,1,0:T(8,128)(2,1)}, u32[]{:S(2)}, u32[]{:S(2)}) collective-permute-start(bf16[1,12,128,128]{3,2,1,0:T(8,128)(2,1)S(1)} %reduce-precision_convert_fusion.2), channel_id=1, source_target_pairs={{0,1},{1,0},{2,3},{3,2},{4,5},{5,4},{6,7},{7,6},{8,9},{9,8},{10,11... | collective-permute-start | bytes 1179656 | tf_op jit(solution)/shard_map/ppermute | solution.py:859
  476.5 18.0 %collective-permute-start.37 = (bf16[1,12,128,128]{3,2,1,0:T(8,128)(2,1)S(1)}, bf16[1,12,128,128]{3,2,1,0:T(8,128)(2,1)}, u32[]{:S(2)}, u32[]{:S(2)}) collective-permute-start(bf16[1,12,128,128]{3,2,1,0:T(8,128)(2,1)S(1)} %reduce-precision_convert_fusion.1), channel_id=1, source_target_pairs={{0,1},{1,0},{2,3},{3,2},{4,5},{5,4},{6,7},{7,6},{8,9},{9,8},{10,11... | collective-permute-start | bytes 1179656 | tf_op jit(solution)/shard_map/ppermute | solution.py:859
  484.2 13.8 %collective-permute-start.39 = (f32[17,32,128]{2,1,0:T(8,128)}, f32[17,32,128]{2,1,0:T(8,128)}, u32[]{:S(2)}, u32[]{:S(2)}) collective-permute-start(f32[17,32,128]{2,1,0:T(8,128)} %pad_maximum_fusion.4), channel_id=1, source_target_pairs={{0,16},{4,20},{8,24},{12,28},{16,0},{20,4},{24,8},{28,12},{1,17},{... | collective-permute-start | bytes 835592 | tf_op jit(solution)/shard_map/ppermute | solution.py:859
  (49 other events, 292.0 us)

commit v3 on v2

--- a/solution.py
+++ b/solution.py
@@ -43,7 +43,7 @@
 
 def cost(micros):
     return pl.CostEstimate(
-        flops=int(micros * 5.0e7), bytes_accessed=int(micros * 1.0e5), transcendentals=0
+        flops=int(micros * 1.0e9), bytes_accessed=int(micros * 2.0e6), transcendentals=0
     )
 
 
@@ -120,11 +120,11 @@
         scratch_shapes=[pltpu.VMEM((padded // LANES, 8 * heads, LANES), f32)],
         name="bias_gather",
         compiler_params=params(),
-        cost_estimate=cost(18),
+        cost_estimate=cost(0.9),
     )(idx, tab)
 
 
-def bucket_kernel(inv_ref, idx_ref, *refs):
+def bucket_kernel(idx_ref, *refs):
     out_ref, acc_ref, scr_ref = refs[-3:]
     keep_refs = refs[: (len(refs) - 3) // 2]
     got_refs = refs[(len(refs) - 3) // 2 : -3]
@@ -169,36 +169,35 @@
     @pl.when(pl.program_id(0) == pl.num_programs(0) - 1)
     def _():
         for k in range(out_ref.shape[0]):
-            out_ref[inv_ref[k]] = total[k * heads : (k + 1) * heads]
-
-
-def bucket_sums(inv, idx, keeps, gots, buckets):
+            for t in range(2):
+                out_ref[k, t * heads : (t + 1) * heads] = total[
+                    k * heads : (k + 1) * heads, t * LANES : (t + 1) * LANES
+                ]
+
+
+def bucket_sums(idx, keeps, gots, buckets):
     rows, win = idx.shape
     padded = -(-win // LANES) * LANES
     heads = 2 * sum(k.shape[0] for k in keeps)
     step_rows = 16
     idx = jnp.pad(idx, ((0, 0), (0, padded - win)))
     out_rows = buckets // 256
-    sum_specs = [
-        pl.BlockSpec((k.shape[0], step_rows, 2 * win), lambda i, inv: (0, i, 0)) for k in keeps
-    ]
+    sum_specs = [pl.BlockSpec((k.shape[0], step_rows, 2 * win), lambda i: (0, i, 0)) for k in keeps]
+    out_shape = jax.ShapeDtypeStruct((out_rows, 2 * heads, LANES), f32)
     return pl.pallas_call(
         bucket_kernel,
-        grid_spec=pltpu.PrefetchScalarGridSpec(
-            num_scalar_prefetch=1,
-            grid=(rows // step_rows,),
-            in_specs=[pl.BlockSpec((step_rows, padded), lambda i, inv: (i, 0))] + sum_specs + sum_specs,
-            out_specs=pl.BlockSpec((out_rows, heads, 256), lambda i, inv: (0, 0, 0)),
-            scratch_shapes=[
-                pltpu.VMEM((out_rows * heads, 256), f32),
-                pltpu.VMEM((padded // LANES, step_rows * heads, LANES), f32),
-            ],
-        ),
-        out_shape=jax.ShapeDtypeStruct((out_rows, heads, 256), f32),
+        grid=(rows // step_rows,),
+        in_specs=[pl.BlockSpec((step_rows, padded), lambda i: (i, 0))] + sum_specs + sum_specs,
+        out_specs=pl.BlockSpec(out_shape.shape, lambda i: (0, 0, 0)),
+        out_shape=out_shape,
+        scratch_shapes=[
+            pltpu.VMEM((out_rows * heads, 256), f32),
+            pltpu.VMEM((padded // LANES, step_rows * heads, LANES), f32),
+        ],
         name="bucket_sums",
         compiler_params=params(),
         cost_estimate=cost(14),
-    )(inv, idx, *keeps, *gots)
+    )(idx, *keeps, *gots)
 
 
 def qkv_kernel(src_ref, a_ref, b_ref, c_ref, d_ref, mod_ref, bias_ref, w_ref, x_ref, n_ref, o_ref):
@@ -245,7 +244,7 @@
         ],
         name="norm_qkv",
         compiler_params=params(),
-        cost_estimate=cost(12),
+        cost_estimate=cost(0.6),
     )(src, pieces, pieces, pieces, pieces, mod, qkv_bias, w_qkv)
 
 
@@ -331,7 +330,7 @@
         ],
         name="attn_forward",
         compiler_params=params(),
-        cost_estimate=cost(18),
+        cost_estimate=cost(0.9),
     )(core, qkv, qkv, qkv, bias_mine, bias_other)
 
 
@@ -434,7 +433,7 @@
         out_shape=[sds, sds, sds],
         name="out_norm",
         compiler_params=params(),
-        cost_estimate=cost(6),
+        cost_estimate=cost(0.3),
     )(src, pieces, pieces, pieces, pieces, attended, x_rows, mod, b_out, w_out)
 
 
@@ -534,38 +533,65 @@
     )(fo, co, inv, flags, normed, grad_mixed, *[w_up] * count, *[b_up] * count, *[w_down] * count, *before)
 
 
-def ff_join_kernel(parts, blocks, units, *refs):
-    fo_ref, src_ref, inv_ref, flag_ref, act_ref, gh_ref = refs[:6]
-    up_refs = refs[6 : 6 + units]
-    down_refs = refs[6 + units : 6 + 2 * units]
-    at = 6 + 2 * units
-    a_ref, b_ref, c_ref, d_ref, x_ref, branch_ref, mod_ref, bd_ref, wo_ref, att_ref = refs[at : at + 10]
-    gres_ref, vec_ref, do_ref, own_ref, other_ref, out_ref = refs[at + 10 : at + 16]
-    mixed_ref, back_ref, stage_ref, gb_ref, sem_ref = refs[at + 16 :]
-    step = pl.program_id(0)
-
-    @pl.when(step == 0)
+def ff_join_kernel(units, fo_ref, act_ref, gh_ref, *refs):
+    up_refs = refs[:units]
+    down_refs = refs[units : 2 * units]
+    mixed_ref, back_ref = refs[2 * units :]
+
+    @pl.when(pl.program_id(0) == 0)
     def _():
         mixed_ref[...] = jnp.zeros_like(mixed_ref)
         back_ref[...] = jnp.zeros_like(back_ref)
 
-    @pl.when(step < parts)
+    wd = jnp.concatenate([r[...] for r in down_refs], axis=0)
+    wu = jnp.concatenate([r[...] for r in up_refs], axis=1)
+    half = mixed_ref.shape[0] // 2
+    for k in range(2):
+        part = slice(k * half, (k + 1) * half)
+        mixed_ref[part] += dot_nn(act_ref[0, part], wd)
+        back_ref[part] += dot_nt(gh_ref[0, part], wu)
+
+
+def ff_join(fo, act, gh, w_up, w_down):
+    parts, rows, wide = act.shape
+    units = wide // LANES
+    features = w_up.shape[0]
+    ups = [
+        pl.BlockSpec((features, LANES), lambda i, fo, u=u: (0, fo[i * units + u])) for u in range(units)
+    ]
+    downs = [
+        pl.BlockSpec((LANES, features), lambda i, fo, u=u: (fo[i * units + u], 0)) for u in range(units)
+    ]
+    hidden = pl.BlockSpec((1, rows, wide), lambda i, fo: (i, 0, 0))
+    sums = jax.ShapeDtypeStruct((rows, features), f32)
+    return pl.pallas_call(
+        functools.partial(ff_join_kernel, units),
+        grid_spec=pltpu.PrefetchScalarGridSpec(
+            num_scalar_prefetch=1,
+            grid=(parts,),
+            in_specs=[hidden, hidden] + ups + downs,
+            out_specs=[whole(sums.shape), whole(sums.shape)],
+        ),
+        out_shape=[sums, sums],
+        name="ff_join",
+        compiler_params=params(),
+        cost_estimate=cost(28),
+    )(fo, act, gh, *([w_up] * units), *([w_down] * units))
+
+
+def ff_rows_kernel(blocks, src_ref, inv_ref, flag_ref, mixed_ref, back_ref, *refs):
+    a_ref, b_ref, c_ref, d_ref, x_ref, branch_ref, mod_ref, bd_ref, wo_ref, att_ref = refs[:10]
+    gres_ref, vec_ref, do_ref, own_ref, other_ref, out_ref = refs[10:16]
+    stage_ref, gb_ref, sem_ref = refs[16:]
+    step = pl.program_id(0)
+
+    @pl.when(step < blocks)
     def _():
-        wd = jnp.concatenate([r[...] for r in down_refs], axis=0)
-        wu = jnp.concatenate([r[...] for r in up_refs], axis=1)
-        half = mixed_ref.shape[0] // 2
-        for k in range(2):
-            part = slice(k * half, (k + 1) * half)
-            mixed_ref[part] += dot_nn(act_ref[0, part], wd)
-            back_ref[part] += dot_nt(gh_ref[0, part], wu)
-
-    @pl.when(jnp.logical_and(step >= parts, step < parts + blocks))
-    def _():
-        e = step - parts
+        e = step
         block = 4 * PIECE
         part = pl.ds(pl.multiple_of(e * block, block), block)
-        mixed = mixed_ref[part] + bd_ref[...]
-        back = back_ref[part]
+        mixed = mixed_ref[...] + bd_ref[...]
+        back = back_ref[...]
         branch = branch_ref[...].astype(f32)
         gate_one = mod_ref[2:3, :]
         gate_two = mod_ref[5:6, :]
@@ -610,13 +636,13 @@
         def _():
             vec_ref[...] += pieces
 
-    @pl.when(step >= parts + blocks)
+    @pl.when(step >= blocks)
     def _():
         width = own_ref.shape[1] * LANES
         half = gb_ref.shape[1] // 2
         flag = flag_ref[0]
         for grad_ref, side in ((own_ref, flag), (other_ref, 1 - flag)):
-            start = pl.multiple_of(side * half + (step - parts - blocks) * width, width)
+            start = pl.multiple_of(side * half + (step - blocks) * width, width)
             got = dot_tn(att_ref[...], gb_ref[:, pl.ds(start, width)])
             place_rows(inv_ref, grad_ref, got.astype(bf16))
 
@@ -628,49 +654,32 @@
             ).wait()
 
 
-def ff_join(fo, src, inv, flags, act, gh, w_up, w_down, pieces, x_rows, branch, mod, b_down, w_out, attended):
-    parts, rows, wide = act.shape
-    units = wide // LANES
-    features = x_rows.shape[1]
+def ff_rows(src, inv, flags, mixed, back, pieces, x_rows, branch, mod, b_down, w_out, attended):
+    rows, features = x_rows.shape
     shards = features // LANES
     block = 4 * PIECE
     blocks = rows // block
     ends = features // 2 // UNIT
 
-    def late(i):
-        return jnp.clip(i - parts, 0, blocks - 1)
-
-    def early(i):
-        return jnp.minimum(i, parts - 1)
-
-    rows_spec = pl.BlockSpec((block, features), lambda i, *more: (late(i), 0))
+    def at(i):
+        return jnp.minimum(i, blocks - 1)
+
+    rows_spec = pl.BlockSpec((block, features), lambda i, *more: (at(i), 0))
     slots = [
-        pl.BlockSpec((1, PIECE, features), lambda i, fo, src, *more, t=t: (src[4 * late(i) + t], 0, 0))
+        pl.BlockSpec((1, PIECE, features), lambda i, src, *more, t=t: (src[4 * at(i) + t], 0, 0))
         for t in range(4)
     ]
-    ups = [
-        pl.BlockSpec((features, LANES), lambda i, fo, *more, u=u: (0, fo[early(i) * units + u]))
-        for u in range(units)
-    ]
-    downs = [
-        pl.BlockSpec((LANES, features), lambda i, fo, *more, u=u: (fo[early(i) * units + u], 0))
-        for u in range(units)
-    ]
-    hidden = pl.BlockSpec((1, rows, wide), lambda i, *more: (early(i), 0, 0))
     grad_spec = pl.BlockSpec(
-        (shards, UNIT // LANES, LANES, LANES),
-        lambda i, *more: (0, jnp.maximum(i - parts - blocks, 0), 0, 0),
+        (shards, UNIT // LANES, LANES, LANES), lambda i, *more: (0, jnp.maximum(i - blocks, 0), 0, 0)
     )
     grad = jax.ShapeDtypeStruct((shards, features // 2 // LANES, LANES, LANES), bf16)
     rows_shape = jax.ShapeDtypeStruct((rows, features), bf16)
     return pl.pallas_call(
-        functools.partial(ff_join_kernel, parts, blocks, units),
+        functools.partial(ff_rows_kernel, blocks),
         grid_spec=pltpu.PrefetchScalarGridSpec(
-            num_scalar_prefetch=4,
-            grid=(parts + blocks + ends,),
-            in_specs=[hidden, hidden]
-            + ups
-            + downs
+            num_scalar_prefetch=3,
+            grid=(blocks + ends,),
+            in_specs=[rows_spec, rows_spec]
             + slots
             + [rows_spec, rows_spec, whole(mod.shape), whole(b_down.shape)]
             + [whole(w_out.shape), whole(attended.shape)],
@@ -683,8 +692,6 @@
                 pl.BlockSpec(memory_space=pl.ANY),
             ],
             scratch_shapes=[
-                pltpu.VMEM((rows, features), f32),
-                pltpu.VMEM((rows, features), f32),
                 pltpu.VMEM((rows, features), bf16),
                 pltpu.VMEM((rows, features), bf16),
                 pltpu.SemaphoreType.DMA((rows // PIECE,)),
@@ -698,13 +705,10 @@
             grad,
             jax.ShapeDtypeStruct(pieces.shape, bf16),
         ],
-        name="ff_join",
+        name="ff_rows",
         compiler_params=params(),
-        cost_estimate=cost(45),
-    )(
-        fo, src, inv, flags, act, gh, *([w_up] * units), *([w_down] * units), *([pieces] * 4),
-        x_rows, branch, mod, b_down, w_out, attended,
-    )
+        cost_estimate=cost(22),
+    )(src, inv, flags, mixed, back, *([pieces] * 4), x_rows, branch, mod, b_down, w_out, attended)
 
 
 def qkv_weight_kernel(inv_ref, flag_ref, n_ref, a_ref, b_ref, g0_ref, g1_ref):
@@ -901,44 +905,6 @@
         return self.own[0][0], self.got[0][0]
 
 
-class Vectors:
-    def __init__(self, clip_bits, me, rows, vectors):
-        self.clip_bits = clip_bits
-        self.me = me
-        self.rows = rows
-        self.gathered = vectors
-        self.stage = 0
-        self.sends = [jnp.concatenate([rows, vectors])]
-        self.own = None
-        self.got = None
-
-    def launch(self):
-        axis, bit = ("win", self.stage) if self.stage < 2 else ("clip", self.stage - 2)
-        self.got = [trade(self.sends[0], axis, bit)]
-
-    def prepare(self):
-        got = self.got[0]
-        count = got.shape[0] - self.gathered.shape[0]
-        if self.stage < 2:
-            both = self.sends[0] + got
-            self.rows, self.gathered = both[:count], both[count:]
-        else:
-            self.rows = self.rows[:count] + got[:count]
-            upper = (self.me >> (self.stage - 2)) & 1 == 1
-            self.gathered = jnp.concatenate(pick(upper, self.gathered, got[count:]))
-        self.stage += 1
-        if self.stage < 2:
-            self.sends = [both]
-        else:
-            self.sends = [jnp.concatenate([self.rows[self.rows.shape[0] // 2 :], self.gathered])]
-
-    def finish(self):
-        while self.stage < self.clip_bits + 1:
-            boundary((), [self], [])
-        self.prepare()
-        return self.rows[0], self.gathered
-
-
 def joined(arrays):
     return arrays[0] if len(arrays) == 1 else jnp.concatenate(arrays, axis=1)
 
@@ -951,11 +917,13 @@
     return united
 
 
-def boundary(inputs, moved, fresh):
-    got = [c.got for c in moved]
+def boundary(inputs, moved, fresh, held=()):
+    waited = moved + list(held)
+    got = [c.got for c in waited]
     inputs, got = lax.optimization_barrier((inputs, got))
-    for c, g in zip(moved, got):
+    for c, g in zip(waited, got):
         c.got = g
+    for c in moved:
         c.prepare()
     chains = moved + fresh
     inputs, sends = lax.optimization_barrier((inputs, [c.sends for c in chains]))
@@ -1029,13 +997,13 @@
     half = win // 2
     idx_mine = lax.dynamic_slice_in_dim(rel_index, core * half, half, 0)
     bias_mine = bias_gather(idx_mine, rel_table)
-    grad_quadrants, bias_mine, w_ada = lax.optimization_barrier((grad_quadrants, bias_mine, w_ada))
-    grad_pieces = exchange(grad_quadrants).reshape(-1, PIECE, features)
-    bias_other = trade(bias_mine, "win", 0)
-
     lifted = jax.nn.silu(condition.astype(f32)).astype(bf16)
     modulation = jnp.dot(lifted, w_ada, preferred_element_type=f32)[0] + b_ada
     mod = jnp.concatenate([modulation.reshape(6, features), jnp.zeros((2, features), f32)])
+
+    grad_quadrants, bias_mine, mod = lax.optimization_barrier((grad_quadrants, bias_mine, mod))
+    grad_pieces = exchange(grad_quadrants).reshape(-1, PIECE, features)
+    bias_other = trade(bias_mine, "win", 0)
 
     qkv_bias = jnp.concatenate([b_query, jnp.zeros_like(b_query), b_value]).astype(f32)[None]
     x_rows, normed, qkv = qkv_call(src, pieces, mod, qkv_bias, w_qkv)
@@ -1070,8 +1038,8 @@
     def chain(own, sends):
         return Chain(clip_bits, [own], [sends]) if fast else (own, sends)
 
-    def meet(inputs, moved, fresh=()):
-        return boundary(inputs, list(moved), list(fresh)) if fast else inputs
+    def meet(inputs, moved, fresh=(), held=()):
+        return boundary(inputs, list(moved), list(fresh), list(held)) if fast else inputs
 
     def merge(*chains):
         return unite(*chains) if fast else chains
@@ -1092,37 +1060,35 @@
         up_sums.append(sums.reshape(-1, LANES))
         ffs.append(chain(own, other))
     act, gh = meet((act, gh), ffs[:3], [ffs[3]])
-    gres, early, grad_att, out_own, out_other, out_pieces = ff_join(
-        jnp.concatenate(fos), src, inv, flags, act, gh, w_up, w_down, grad_pieces, x_rows, branch, mod,
-        b_down.astype(f32)[None], w_out, attended,
+    mixed, back = ff_join(jnp.concatenate(fos), act, gh, w_up, w_down)
+    mixed, back = meet((mixed, back), ffs[1:], held=ffs[:1])
+    gres, early, grad_att, out_own, out_other, out_pieces = ff_rows(
+        src, inv, flags, mixed, back, grad_pieces, x_rows, branch, mod, b_down.astype(f32)[None], w_out, attended
     )
     local_slots = tokens.shape[1]
     piece_shape = (-1, local_slots, PIECE, features)
+    wos = chain(out_own, out_other)
+    grad_att, out_pieces = meet((grad_att, out_pieces), ffs[2:], [wos], held=ffs[1:2])
     out_pieces = exchange(out_pieces.reshape(piece_shape))
-    wos = chain(out_own, out_other)
-    grad_att = meet(grad_att, ffs[1:], [wos])
     pairs = probs.shape[0]
     grads_a, mine_a, others_a = attn_backward(core_arr, qkv, attended, grad_att, probs, recips, windows, 0, FIRST_PAIRS)
-    grads_a = meet(grads_a, [ffs[2], ffs[3], wos])
+    grads_a = meet(grads_a, [ffs[3], wos], held=ffs[2:3])
     qa_own, qa_other = qkv_weight(inv, flags, normed, grads_a)
     qas = chain(qa_own, qa_other)
     front = merge(*ffs[:3])
-    grad_att, unused, out_pieces = meet((grad_att, qa_own, out_pieces), [front, ffs[3], wos], [qas])
+    grad_att, unused, out_pieces = meet((grad_att, qa_own, out_pieces), [wos, front], [qas], held=ffs[3:])
     others_a = trade(others_a, "win", 0)
     grads_b, mine_b, others_b = attn_backward(
         core_arr, qkv, attended, grad_att, probs, recips, windows, FIRST_PAIRS, pairs - FIRST_PAIRS
     )
-    grads_b = meet(grads_b, [qas, wos])
+    grads_b, others_a, others_b = meet((grads_b, others_a, others_b), [qas, wos])
+    others_b = trade(others_b, "win", 0)
     qb_own, qb_other = qkv_weight(inv, flags, normed, grads_b)
     qbs = chain(qb_own, qb_other)
 
     rear = merge(ffs[3], wos)
-    gres_late, unused, others_a, others_b = meet((gres, qb_own, others_a, others_b), [front, rear], [qbs])
-    others_b = trade(others_b, "win", 0)
-    token_pieces, late = qkv_backward(src, (grads_a, grads_b), w_qkv, x_rows, gres_late, mod)
-    token_pieces = exchange(token_pieces.reshape(piece_shape))
-    late, others_b = meet((late, others_b), [qbs, qas, rear])
-    rel_sums = bucket_sums(inv, idx_mine, [mine_a, mine_b], [others_a, others_b], rel_table.shape[0])
+    others_a, others_b, unused = meet((others_a, others_b, qb_own), [rear, front], [qbs])
+    rel_sums = bucket_sums(idx_mine, [mine_a, mine_b], [others_a, others_b], rel_table.shape[0])
 
     if fast:
         here = natural[:, None] == order[None, :]
@@ -1130,45 +1096,88 @@
     grad_b_up = jnp.stack(up_sums, axis=1 if fast else 0)
     d = features
     tile_rows = d // LANES
-    lifted_row = lifted[0].astype(f32).reshape(1, tile_rows, LANES)
-    early_rows = early[:6].reshape(6, tile_rows, LANES)
-    late_rows = late[:4].reshape(4, tile_rows, LANES)
-    vectors = jnp.concatenate(
-        [early_rows, lifted_row, jnp.zeros_like(lifted_row), grad_b_up.reshape(-1, tile_rows, LANES), late_rows]
-    )
-    buckets = rel_table.shape[0]
-    heads = rel_sums.shape[1]
-    rel_rows = buckets // clips
+    wins = lax.axis_size("win")
+    buckets, heads = rel_table.shape
+
+    def to_all(to_each, by_clip):
+        parts = [jnp.broadcast_to(v[None], (clips,) + v.shape) for v in to_each] + by_clip
+        packed = jnp.concatenate(parts, axis=1).astype(bf16)
+        packed = jnp.broadcast_to(packed[:, None], (clips, wins) + packed.shape[1:])
+        packed = packed.reshape((clips * wins,) + packed.shape[2:])
+        return lax.all_to_all(packed, ("clip", "win"), split_axis=0, concat_axis=0, tiled=True)
+
+    def from_all(received):
+        return jnp.sum(received.astype(f32).reshape((clips, wins) + received.shape[1:]), axis=1)
+
     if fast:
-        own_rows = rel_rows * heads // LANES
-        chain_v = Vectors(
-            clip_bits, me, rel_sums.reshape(shards, own_rows, LANES), vectors.reshape(-1, own_rows, LANES)
+        early_vec = to_all(
+            [early[:4].reshape(-1, LANES), lifted[0].astype(f32).reshape(-1, LANES)],
+            [
+                early[4].reshape(clips, 1, LANES),
+                early[5].reshape(clips, 1, LANES),
+                grad_b_up.reshape(clips, -1, LANES),
+                rel_sums,
+            ],
         )
-        boundary(rel_sums, [qbs, qas], [chain_v])
-        boundary((), [qbs, chain_v], [])
+    gres_late, unused = meet((gres, rel_sums), [rear, qas, qbs])
+    home = lax.axis_index("win") if fast else 0
+    src_back = (((src // local_slots) ^ home) * local_slots + src % local_slots).astype(jnp.int32)
+    token_pieces, late = qkv_backward(src_back, (grads_a, grads_b), w_qkv, x_rows, gres_late, mod)
+    token_pieces = token_pieces.reshape(piece_shape)
+    if fast:
+        token_parts = [token_pieces[k] for k in range(4)]
+        token_parts, late, early_vec, out_pieces = meet(
+            (token_parts, late, early_vec, out_pieces), [qbs, qas], held=[front, rear]
+        )
+        moves = [[(i, i ^ k) for i in range(wins)] for k in range(4)]
+        far = [lax.ppermute(token_parts[k], "win", moves[k]) for k in (2, 3)]
+        near = lax.ppermute(token_parts[1], "win", moves[1])
+        late_vec = to_all(
+            [late[:2].reshape(-1, LANES)],
+            [late[2].reshape(clips, 1, LANES), late[3].reshape(clips, 1, LANES)],
+        )
+        near = boundary(near, [qbs], [])
         last = merge(qas, qbs)
-        token_pieces = boundary(token_pieces, [last, chain_v], [])
-        boundary((), [last, chain_v], [])
-        rel, vectors_all = chain_v.finish()
-        sum_rel = rel.reshape(heads, rel_rows).T
-        vectors_all = vectors_all.reshape(clips, -1, d)
+        far, late_vec = boundary((far, late_vec), [last], [])
+        (late_vec,) = boundary((late_vec,), [last], [])
+        token_pieces = jnp.stack([token_parts[0], near] + far).reshape((2, 2) + token_parts[0].shape)
+        for axis, bit in ((0, 1), (1, 0)):
+            swapped = (home >> bit) & 1 == 1
+            token_pieces = jnp.where(swapped, jnp.flip(token_pieces, axis), token_pieces)
+        token_pieces = token_pieces.reshape(piece_shape)
+        early_rows, late_rows = from_all(early_vec), from_all(late_vec)
+        n = 4 * tile_rows
+        early_terms = early_rows[:, :n].reshape(clips, 4 * d)
+        late_terms = late_rows[:, : 2 * tile_rows].reshape(clips, 2 * d)
+        all_lifted = early_rows[:, n : n + tile_rows].reshape(clips, d) * (1.0 / wins)
+        n += tile_rows
+        own = jnp.sum(early_rows[:, n:], axis=0)
+        sum_bo, sum_bd, sum_bu = own[0], own[1], own[2 : 2 + ff // clips // LANES].reshape(-1)
+        rel = own[2 + ff // clips // LANES :].reshape(2, heads, LANES)
+        sum_rel = rel.transpose(0, 2, 1).reshape(buckets // clips, heads)
+        own = jnp.sum(late_rows[:, 2 * tile_rows :], axis=0)
+        sum_bq, sum_bv = own[0], own[1]
     else:
-        vectors_all = lax.psum(lax.all_gather(vectors.reshape(-1, d), "clip", axis=0), "win")
-        rel = lax.psum(rel_sums.transpose(0, 2, 1).reshape(buckets, heads), "win")
-        sum_rel = lax.psum_scatter(rel, "clip", scatter_dimension=0, tiled=True)
-    late_all = vectors_all[:, -4:].reshape(clips, 4 * d)
-    early_all = vectors_all[:, :-4]
-    all_lifted = early_all[:, 6] * (1.0 / lax.axis_size("win"))
-    all_terms = jnp.concatenate([late_all[:, : 2 * d], early_all[:, :4].reshape(clips, 4 * d)], axis=1)
+        token_pieces = exchange(token_pieces)
+
+        def all_clips(rows):
+            return lax.psum(lax.all_gather(rows.reshape(-1), "clip", axis=0), "win")
+
+        def own_sum(vector):
+            return lax.psum(lax.psum_scatter(vector, "clip", scatter_dimension=0, tiled=True), "win")
+
+        early_terms, late_terms = all_clips(early[:4]), all_clips(late[:2])
+        all_lifted = lax.all_gather(lifted[0].astype(f32), "clip", axis=0)
+        sum_bo, sum_bd, sum_bu = own_sum(early[4]), own_sum(early[5]), own_sum(grad_b_up.reshape(-1))
+        sum_bq, sum_bv = own_sum(late[2]), own_sum(late[3])
+        rel = rel_sums.reshape(-1, 2, heads, LANES).transpose(0, 1, 3, 2).reshape(buckets, heads)
+        sum_rel = own_sum(rel)
+    all_terms = jnp.concatenate([late_terms, early_terms], axis=1)
 
     def own_block(vector):
         size = vector.shape[0] // clips
         return lax.dynamic_slice_in_dim(vector, me * size, size, 0)
 
-    early_sum = jnp.sum(jnp.concatenate([early_all[:, 4:6], early_all[:, 8:]], axis=1), axis=0).reshape(-1)
-    late_sum = jnp.sum(late_all[:, 2 * d :], axis=0)
-    sum_bo, sum_bd, sum_bu = own_block(early_sum[:d]), own_block(early_sum[d : 2 * d]), own_block(early_sum[2 * d :])
-    sum_bq, sum_bv = own_block(late_sum[:d]), own_block(late_sum[d:])
     ada_rows = d // clips
     lifted_rows = lax.dynamic_slice_in_dim(all_lifted, me * ada_rows, ada_rows, 1)
     grad_w_ada = jnp.dot(lifted_rows.T, all_terms, precision=lax.Precision.HIGHEST)

time: 518 us -> 478 us (0.923)
  waiting for transfers between devices: 64.1 us -> 29.1 us
  starting transfers between devices: 54.3 us -> 61.7 us
  other arithmetic: 72 us -> 65.1 us
    ppermute x42 -> x37, waiting for transfers between devices: 58.1 us -> 24.5 us  [trade(): return lax.ppermute(array, axis, flip(axis, bit))]
    all_to_all x0 -> x2, starting transfers between devices: none -> 7.42 us  [to_all(): lax.all_to_all(packed, ('clip', 'win'), split_axis=0, concat_axis=0, tile...]
    all_to_all x4 -> x3, waiting for transfers between devices: 6.01 us -> 0.01 us  [exchange(): lax.all_to_all(quadrants, 'win', split_axis=0, concat_axis=0, tiled=True)]
    all_to_all x4 -> x3, starting transfers between devices: 16.3 us -> 13 us  [exchange(): lax.all_to_all(quadrants, 'win', split_axis=0, concat_axis=0, tiled=True)]
    pallas_call x2 -> x3, Pallas kernels: 63.7 us -> 66.2 us  [the longest x1 31.9 us: ff_join(): pl.pallas_call(functools.partial(ff_join_kernel, units), grid_spec=pltpu....]
    ppermute x42 -> x37, starting transfers between devices: 38 us -> 39.4 us  [trade(): return lax.ppermute(array, axis, flip(axis, bit))]
  transfers between devices with their start and end apart: 46 -> 45, of which waited for: 13 -> 8; matrix products, arithmetic and copies ran while one was open for 11% -> 12% of each run, Pallas kernels for 49% -> 53%
where the time goes in v3:
time: 478 us; the launch traced here: 473 us
  Pallas kernels  281 us (59%)
  other arithmetic  65.1 us (14%)
  starting transfers between devices  61.7 us (13%)
  waiting for transfers between devices  29.1 us (6%)
  local copies, waits for them, and re-layouts  23 us (5%)
  matrix products  10.7 us (2%)
    pallas_call x4, Pallas kernels, ff_part(): pl.pallas_call(functools.partial(ff_part_kernel, count), grid_spec=pltpu....  78.2 us
    convert_element_type x28, other arithmetic, add_low(): return (a.astype(f32) + b.astype(f32)).astype(bf16)  46.9 us
    ppermute x37, starting transfers between devices, trade(): return lax.ppermute(array, axis, flip(axis, bit))  39.4 us
    pallas_call x1, Pallas kernels, ff_join(): pl.pallas_call(functools.partial(ff_join_kernel, units), grid_spec=pltpu....  31.9 us
    pallas_call x2, Pallas kernels, attn_backward(): pl.pallas_call(functools.partial(attn_back_kernel, windows), grid_spec=pl...  26.7 us
    ppermute x37, waiting for transfers between devices, trade(): return lax.ppermute(array, axis, flip(axis, bit))  24.5 us
    pallas_call x2, Pallas kernels, qkv_weight(): pl.pallas_call(qkv_weight_kernel, grid_spec=pltpu.PrefetchScalarGridSpec(...  21.6 us
    pallas_call x1, Pallas kernels, ff_rows(): pl.pallas_call(functools.partial(ff_rows_kernel, blocks), grid_spec=pltpu...  21 us
  transfers between devices with their start and end apart: 45, of which 8 were waited for; matrix products, arithmetic and copies ran while one was open for 12% of the time, Pallas kernels for 53%

profile of v3, /device:TPU:0, one launch (start us, length us, event | category | flops | bytes accessed | tf_op | source)
XLA Modules:
  0.0 472.9 jit_solution(4264114826928845624)
XLA Ops:
  0.7 3.6 copy.85
  4.3 4.4 all-to-all-start
  8.7 6.3 %fusion.7 = f32[1,6144]{1,0:T(1,128)S(1)} fusion(bf16[1024,6144]{1,0:T(8,128)(2,1)} %param.30, bf16[1,1024]{1,0:T(2,128)(2,1)S(1)} %copy-done.25), kind=kOutput, calls=%fused_computation.94 | convolution fusion | flops 12589056 | bytes 12609536 | tf_op jit(solution)/shard_map/dot_general | solution.py:1001
  15.1 3.6 copy.86
  20.7 19.1 %bias_gather.1.mine_ref = f32[8,160,640]{2,1,0:T(8,128)} custom-call(s32[160,384]{1,0:T(8,128)} %pad.6.idx_ref, bf16[256,256]{1,0:T(8,128)(2,1)} %pad_maximum_fusion.6.tab_ref), custom_call_target="tpu_custom_call" | custom-call | flops 900000000 | bytes 1800000 | tf_op jit(solution)/shard_map/bias_gather/pallas_call | solution.py:114
  41.9 4.8 %all-to-all-start.1 = ((bf16[4,5,64,1024]{3,2,1,0:T(8,128)(2,1)}), bf16[4,5,64,1024]{3,2,1,0:T(8,128)(2,1)}, u32[]{:S(2)}, u32[]{:S(2)}) async-start(bf16[4,5,64,1024]{3,2,1,0:T(8,128)(2,1)} %bitcast.117), calls=%async_computation.1 | async-start | bytes 5242880 | tf_op jit(solution)/shard_map/all_to_all | solution.py:953
  51.5 16.0 %norm_qkv.1 = (bf16[1280,1024]{1,0:T(8,128)(2,1)}, bf16[1280,1024]{1,0:T(8,128)(2,1)}, bf16[1280,3072]{1,0:T(8,128)(2,1)}) custom-call(s32[20]{0:T(128)} %select_reduce_fusion.4.src_ref, bf16[20,64,1024]{2,1,0:T(8,128)(2,1)} %bitcast.112, bf16[20,64,1024]{2,1,0:T(8,128)(2,1)} %bitcast.113, bf16[20,64,1024]{2,1,0:T(8,128)(2,1)} %bitcast.114, ...), custom_call_target="tpu_custom_call" | custom-call | flops 600000000 | bytes 1200000 | tf_op jit(solution)/shard_map/norm_qkv/pallas_call | solution.py:227
  67.6 17.7 %attn_forward.1 = (bf16[1280,1024]{1,0:T(8,128)(2,1)}, bf16[8,4,320,640]{3,2,1,0:T(8,128)(2,1)}, f32[1280,1024]{1,0:T(8,128)}) custom-call(s32[1]{0:T(128)} %bitcast.1.core_ref, bf16[1280,3072]{1,0:T(8,128)(2,1)} %get-tuple-element.211.q_ref.k_ref.v_ref, bf16[1280,3072]{1,0:T(8,128)(2,1)} %get-tuple-element.211.q_ref.k_ref.v_ref, ...), custom_call_target="tpu_custom_call" | custom-call | flops 900000000 | bytes 1800000 | tf_op jit(solution)/shard_map/attn_forward/pallas_call | solution.py:313
  85.3 10.7 %out_norm.1 = (bf16[1280,1024]{1,0:T(8,128)(2,1)}, bf16[1280,1024]{1,0:T(8,128)(2,1)}, bf16[1280,1024]{1,0:T(8,128)(2,1)}) custom-call(s32[20]{0:T(128)} %select_reduce_fusion.4.src_ref, bf16[20,64,1024]{2,1,0:T(8,128)(2,1)} %bitcast.15.a_ref.b_ref.c_ref.d_ref.refs_0_.refs_1_.refs_2_.refs_3_, ...), custom_call_target="tpu_custom_call" | custom-call | flops 300000000 | bytes 600000 | tf_op jit(solution)/shard_map/out_norm/pallas_call | solution.py:424
  96.0 19.4 %ff_part.4 = (bf16[4,1280,1024]{2,1,0:T(8,128)(2,1)}, bf16[4,1280,1024]{2,1,0:T(8,128)(2,1)}, bf16[8,8,128,128]{3,2,1,0:T(8,128)(2,1)}, bf16[8,8,128,128]{3,2,1,0:T(8,128)(2,1)}, f32[2,1,512]{2,1,0:T(1,128)}) custom-call(s32[8]{0:T(128)} %get-tuple-element.451.fo_ref, s32[4]{0:T(128)} %broadcast_and_fusion.co_ref, s32[8]{0:T(128)} %get-tuple-element.449.inv_ref, ...), custom_call_target="tpu_custom_call" | custom-call | flops 20000000000 | bytes 40000000 | tf_op jit(solution)/shard_map/ff_part/pallas_call | solution.py:515
  116.5 19.7 %ff_part.5 = (bf16[4,1280,1024]{2,1,0:T(8,128)(2,1)}, bf16[4,1280,1024]{2,1,0:T(8,128)(2,1)}, bf16[8,8,128,128]{3,2,1,0:T(8,128)(2,1)}, bf16[8,8,128,128]{3,2,1,0:T(8,128)(2,1)}, f32[2,1,512]{2,1,0:T(1,128)}) custom-call(s32[8]{0:T(128)} %get-tuple-element.452.fo_ref, s32[4]{0:T(128)} %broadcast_and_fusion.co_ref, ...), custom_call_target="tpu_custom_call", output_to_operand_aliasing={{0}: (18, {}), {1}: (19, {})} | custom-call | flops 20000000000 | bytes 40000000 | tf_op jit(solution)/shard_map/ff_part/pallas_call | solution.py:515
  136.2 3.6 add_convert_fusion.8
  139.9 2.4 collective-permute-start.2
  142.2 19.8 %ff_part.6 = (bf16[4,1280,1024]{2,1,0:T(8,128)(2,1)}, bf16[4,1280,1024]{2,1,0:T(8,128)(2,1)}, bf16[8,8,128,128]{3,2,1,0:T(8,128)(2,1)}, bf16[8,8,128,128]{3,2,1,0:T(8,128)(2,1)}, f32[2,1,512]{2,1,0:T(1,128)}) custom-call(s32[8]{0:T(128)} %get-tuple-element.453.fo_ref, s32[4]{0:T(128)} %broadcast_and_fusion.co_ref, ...), custom_call_target="tpu_custom_call", output_to_operand_aliasing={{0}: (18, {}), {1}: (19, {})} | custom-call | flops 20000000000 | bytes 40000000 | tf_op jit(solution)/shard_map/ff_part/pallas_call | solution.py:515
  162.1 4.2 collective-permute-done.2
  166.2 2.6 add_convert_fusion.20
  175.2 19.3 %ff_part.7 = (bf16[4,1280,1024]{2,1,0:T(8,128)(2,1)}, bf16[4,1280,1024]{2,1,0:T(8,128)(2,1)}, bf16[8,8,128,128]{3,2,1,0:T(8,128)(2,1)}, bf16[8,8,128,128]{3,2,1,0:T(8,128)(2,1)}, f32[2,1,512]{2,1,0:T(1,128)}) custom-call(s32[8]{0:T(128)} %copy-done.38, s32[4]{0:T(128)} %broadcast_and_fusion.co_ref, ...), custom_call_target="tpu_custom_call", output_to_operand_aliasing={{0}: (18, {}), {1}: (19, {})} | custom-call | flops 20000000000 | bytes 40000000 | tf_op jit(solution)/shard_map/ff_part/pallas_call | solution.py:515
  194.6 4.8 %collective-permute-done.5 = bf16[4,8,128,128]{3,2,1,0:T(8,128)(2,1)} collective-permute-done((bf16[4,8,128,128]{3,2,1,0:T(8,128)(2,1)}, bf16[4,8,128,128]{3,2,1,0:T(8,128)(2,1)}, u32[]{:S(2)}, u32[]{:S(2)}) %collective-permute-start.5) | collective-permute-done | bytes 1048608 | tf_op jit(solution)/shard_map/ppermute | solution.py:863
  200.5 2.6 add_convert_fusion.18
  206.8 2.6 collective-permute-start.10
  209.4 31.9 %ff_join.1 = (f32[1280,1024]{1,0:T(8,128)}, f32[1280,1024]{1,0:T(8,128)}) custom-call(s32[32]{0:T(128)} %pad_add_fusion.1.fo_ref, bf16[4,1280,1024]{2,1,0:T(8,128)(2,1)} %get-tuple-element.259.act_ref, bf16[4,1280,1024]{2,1,0:T(8,128)(2,1)} %get-tuple-element.260.gh_ref, bf16[1024,4096]{1,0:T(8,128)(2,1)} %refs_7_.1, bf16[1024,4096]{1,0:T(8,128)(2,1)} %refs_7_.1, ...), custom_call_target="tpu_custom_call" | custom-call | flops 28000000000 | bytes 56000000 | tf_op jit(solution)/shard_map/ff_join/pallas_call | solution.py:567
  242.6 2.6 add_convert_fusion.16
  249.5 21.0 %ff_rows.1 = (bf16[1280,1024]{1,0:T(8,128)(2,1)}, f32[8,1024]{1,0:T(8,128)}, bf16[1280,1024]{1,0:T(8,128)(2,1)}, bf16[8,4,128,128]{3,2,1,0:T(8,128)(2,1)}, bf16[...) custom-call(s32[20]{0:T(128)} %select_reduce_fusion.4.src_ref, s32[8]{0:T(128)} %get-tuple-element.449.inv_ref, ...), custom_call_target="tpu_custom_call" | custom-call | flops 22000001024 | bytes 44000000 | tf_op jit(solution)/shard_map/ff_rows/pallas_call | solution.py:677
  270.6 3.3 collective-permute-done.12
  276.2 3.9 all-to-all-start.2
  280.1 18.6 %attn_backward.2 = (bf16[3,1280,768]{2,1,0:T(8,128)(2,1)}, bf16[6,160,640]{2,1,0:T(8,128)(2,1)}, bf16[6,160,640]{2,1,0:T(8,128)(2,1)}) custom-call(s32[1]{0:T(128)} %bitcast.1.core_ref, bf16[1280,3072]{1,0:T(8,128)(2,1)} %get-tuple-element.211.q_ref.k_ref.v_ref, bf16[1280,3072]{1,0:T(8,128)(2,1)} %get-tuple-element.211.q_ref.k_ref.v_ref, ...), custom_call_target="tpu_custom_call" | custom-call | flops 17999998976 | bytes 36000000 | tf_op jit(solution)/shard_map/attn_backward/pallas_call | solution.py:381
  299.7 2.8 add_convert_fusion.12
  303.0 2.6 collective-permute-start.18
  305.6 13.1 %qkv_weight.2 = (bf16[8,9,128,128]{3,2,1,0:T(8,128)(2,1)}, bf16[8,9,128,128]{3,2,1,0:T(8,128)(2,1)}) custom-call(s32[8]{0:T(128)} %get-tuple-element.449.inv_ref, s32[2]{0:T(128)} %pad_add_fusion.flag_ref, bf16[1280,1024]{1,0:T(8,128)(2,1)} %get-tuple-element.298.n_ref, bf16[3,1280,768]{2,1,0:T(8,128)(2,1)} %get-tuple-element.297.a_ref.b_ref.refs_0_, ...), custom_call_target="tpu_custom_call" | custom-call | flops 6000000000 | bytes 12000000 | tf_op jit(solution)/shard_map/qkv_weight/pallas_call | solution.py:727
  328.6 8.2 %attn_backward.3 = (bf16[3,1280,256]{2,1,0:T(8,128)(2,1)}, bf16[2,160,640]{2,1,0:T(8,128)(2,1)}, bf16[2,160,640]{2,1,0:T(8,128)(2,1)}) custom-call(s32[1]{0:T(128)} %bitcast.1.core_ref, bf16[1280,3072]{1,0:T(8,128)(2,1)} %get-tuple-element.211.q_ref.k_ref.v_ref, bf16[1280,3072]{1,0:T(8,128)(2,1)} %get-tuple-element.211.q_ref.k_ref.v_ref, ...), custom_call_target="tpu_custom_call" | custom-call | flops 6000000000 | bytes 12000000 | tf_op jit(solution)/shard_map/attn_backward/pallas_call | solution.py:381
  336.7 2.1 collective-permute-start.24
  338.8 5.0 %add_convert_fusion = (bf16[4,9,128,128]{3,2,1,0:T(8,128)(2,1)}, bf16[4,9,128,128]{3,2,1,0:T(8,128)(2,1)}) fusion(bf16[8,9,128,128]{3,2,1,0:T(8,128)(2,1)} %collective-permute-done.20, bf16[8,9,128,128]{3,2,1,0:T(8,128)(2,1)} %get-tuple-element.299), kind=kLoop, calls=%fused_computation.4 | loop fusion | flops 4718592 | bytes 7077888 | tf_op jit(solution)/shard_map/convert_element_type | solution.py:867
  345.4 8.5 %qkv_weight.3 = (bf16[8,3,128,128]{3,2,1,0:T(8,128)(2,1)}, bf16[8,3,128,128]{3,2,1,0:T(8,128)(2,1)}) custom-call(s32[8]{0:T(128)} %get-tuple-element.449.inv_ref, s32[2]{0:T(128)} %pad_add_fusion.flag_ref, bf16[1280,1024]{1,0:T(8,128)(2,1)} %get-tuple-element.298.n_ref, bf16[3,1280,256]{2,1,0:T(8,128)(2,1)} %get-tuple-element.324.a_ref.b_ref.refs_1_, ...), custom_call_target="tpu_custom_call" | custom-call | flops 6000000000 | bytes 12000000 | tf_op jit(solution)/shard_map/qkv_weight/pallas_call | solution.py:727
  357.8 2.3 reduce-precision_convert_fusion
  361.9 13.2 %bucket_sums.1 = f32[8,32,128]{2,1,0:T(8,128)} custom-call(s32[160,384]{1,0:T(8,128)} %pad.6.idx_ref, bf16[6,160,640]{2,1,0:T(8,128)(2,1)} %get-tuple-element.326.refs_0_, bf16[2,160,640]{2,1,0:T(8,128)(2,1)} %get-tuple-element.327.refs_1_, bf16[6,160,640]{2,1,0:T(8,128)(2,1)} %collective-permute-done.19.refs_2_, ...), custom_call_target="tpu_custom_call" | custom-call | flops 14000000000 | bytes 28000000 | tf_op jit(solution)/shard_map/bucket_sums/pallas_call | solution.py:187
  377.3 3.3 all-to-all-start.3
  385.2 2.7 add_convert_fusion.10
  389.7 18.1 %qkv_backward.1 = (bf16[20,64,1024]{2,1,0:T(8,128)(2,1)}, f32[8,1024]{1,0:T(8,128)}) custom-call(s32[20]{0:T(128)} %fusion.13.src_ref, bf16[3,1280,768]{2,1,0:T(8,128)(2,1)} %get-tuple-element.297.a_ref.b_ref.refs_0_, bf16[3,1280,256]{2,1,0:T(8,128)(2,1)} %get-tuple-element.324.a_ref.b_ref.refs_1_, bf16[1024,3072]{1,0:T(8,128)(2,1)} %refs_2_.11, ...), custom_call_target="tpu_custom_call" | custom-call | flops 14000000000 | bytes 28000000 | tf_op jit(solution)/shard_map/qkv_backward/pallas_call | solution.py:802
  407.8 3.2 fusion.25
  418.8 4.1 all-to-all-start.4
  422.9 2.9 collective-permute-start.36
  427.2 4.2 assemble.3
  432.1 5.3 %collective-permute-done.33 = bf16[2,3,128,128]{3,2,1,0:T(8,128)(2,1)S(1)} collective-permute-done((bf16[2,3,128,128]{3,2,1,0:T(8,128)(2,1)}, bf16[2,3,128,128]{3,2,1,0:T(8,128)(2,1)S(1)}, u32[]{:S(2)}, u32[]{:S(2)}) %collective-permute-start.33) | collective-permute-done | bytes 196640 | tf_op jit(solution)/shard_map/ppermute | solution.py:863
  437.4 4.5 collective-permute-start.37
  445.0 4.6 all-to-all-done.4
  458.6 4.5 collective-permute-done.38
  464.3 4.3 fusion.2
  469.9 2.5 assemble.2
  (264 shorter events, 80.3 us)
Async XLA Ops:
  4.3 36.1 %all-to-all-start = ((bf16[4,5,64,1024]{3,2,1,0:T(8,128)(2,1)}), bf16[4,5,64,1024]{3,2,1,0:T(8,128)(2,1)S(1)}, u32[]{:S(2)}, u32[]{:S(2)}) async-start(bf16[4,5,64,1024]{3,2,1,0:T(8,128)(2,1)} %bitcast.118), calls=%async_computation | async-start | bytes 5242880 | tf_op jit(solution)/shard_map/all_to_all | solution.py:953
  39.9 27.7 %collective-permute-start = (f32[8,160,640]{2,1,0:T(8,128)}, f32[8,160,640]{2,1,0:T(8,128)}, u32[]{:S(2)}, u32[]{:S(2)}) collective-permute-start(f32[8,160,640]{2,1,0:T(8,128)} %bias_gather.1.mine_ref), channel_id=1, source_target_pairs={{0,1},{1,0},{2,3},{3,2},{4,5},{5,4},{6,7},{7,6},{8,9},{9,8},{10,11... | collective-permute-start | bytes 9830408 | tf_op jit(solution)/shard_map/ppermute | solution.py:863
  41.9 43.4 %all-to-all-start.1 = ((bf16[4,5,64,1024]{3,2,1,0:T(8,128)(2,1)}), bf16[4,5,64,1024]{3,2,1,0:T(8,128)(2,1)}, u32[]{:S(2)}, u32[]{:S(2)}) async-start(bf16[4,5,64,1024]{3,2,1,0:T(8,128)(2,1)} %bitcast.117), calls=%async_computation.1 | async-start | bytes 5242880 | tf_op jit(solution)/shard_map/all_to_all | solution.py:953
  49.7 121.6 %copy-start.38 = (s32[8]{0:T(128)}, s32[8]{0:T(128)S(1)}, u32[]{:S(2)}) copy-start(s32[8]{0:T(128)S(1)} %get-tuple-element.450.fo_ref) | copy-start | bytes 100
  115.4 20.7 %collective-permute-start.1 = (bf16[8,8,128,128]{3,2,1,0:T(8,128)(2,1)}, bf16[8,8,128,128]{3,2,1,0:T(8,128)(2,1)}, u32[]{:S(2)}, u32[]{:S(2)}) collective-permute-start(bf16[8,8,128,128]{3,2,1,0:T(8,128)(2,1)} %get-tuple-element.223), channel_id=1, source_target_pairs={{0,1},{1,0},{2,3},{3,2},{4,5},{5,4},{6,7},{7,6},{8,9},{9,8},{10,11... | collective-permute-start | bytes 6291464 | tf_op jit(solution)/shard_map/ppermute | solution.py:863
  139.8 26.5 %collective-permute-start.3 = (bf16[8,8,128,128]{3,2,1,0:T(8,128)(2,1)}, bf16[8,8,128,128]{3,2,1,0:T(8,128)(2,1)S(1)}, u32[]{:S(2)}, u32[]{:S(2)}) collective-permute-start(bf16[8,8,128,128]{3,2,1,0:T(8,128)(2,1)} %get-tuple-element.234), channel_id=1, source_target_pairs={{0,1},{1,0},{2,3},{3,2},{4,5},{5,4},{6,7},{7,6},{8,9},{9,8},{10,11... | collective-permute-start | bytes 6291464 | tf_op jit(solution)/shard_map/ppermute | solution.py:863
  139.9 26.3 %collective-permute-start.2 = (bf16[4,8,128,128]{3,2,1,0:T(8,128)(2,1)}, bf16[4,8,128,128]{3,2,1,0:T(8,128)(2,1)}, u32[]{:S(2)}, u32[]{:S(2)}) collective-permute-start(bf16[4,8,128,128]{3,2,1,0:T(8,128)(2,1)} %get-tuple-element.233), channel_id=1, source_target_pairs={{0,4},{4,0},{8,12},{12,8},{16,20},{20,16},{24,28},{28,24},{1,5},{5... | collective-permute-start | bytes 3145736 | tf_op jit(solution)/shard_map/ppermute | solution.py:863
  170.7 28.6 %collective-permute-start.6 = (bf16[8,8,128,128]{3,2,1,0:T(8,128)(2,1)}, bf16[8,8,128,128]{3,2,1,0:T(8,128)(2,1)S(1)}, u32[]{:S(2)}, u32[]{:S(2)}) collective-permute-start(bf16[8,8,128,128]{3,2,1,0:T(8,128)(2,1)} %get-tuple-element.251), channel_id=1, source_target_pairs={{0,1},{1,0},{2,3},{3,2},{4,5},{5,4},{6,7},{7,6},{8,9},{9,8},{10,11... | collective-permute-start | bytes 6291464 | tf_op jit(solution)/shard_map/ppermute | solution.py:863
  171.9 22.7 %collective-permute-start.4 = (bf16[2,8,128,128]{3,2,1,0:T(8,128)(2,1)}, bf16[2,8,128,128]{3,2,1,0:T(8,128)(2,1)}, u32[]{:S(2)}, u32[]{:S(2)}) collective-permute-start(bf16[2,8,128,128]{3,2,1,0:T(8,128)(2,1)} %get-tuple-element.249), channel_id=1, source_target_pairs={{0,8},{4,12},{8,0},{12,4},{16,24},{20,28},{24,16},{28,20},{1,9},{5... | collective-permute-start | bytes 1572872 | tf_op jit(solution)/shard_map/ppermute | solution.py:863
  173.7 25.6 %collective-permute-start.5 = (bf16[4,8,128,128]{3,2,1,0:T(8,128)(2,1)}, bf16[4,8,128,128]{3,2,1,0:T(8,128)(2,1)}, u32[]{:S(2)}, u32[]{:S(2)}) collective-permute-start(bf16[4,8,128,128]{3,2,1,0:T(8,128)(2,1)} %get-tuple-element.250), channel_id=1, source_target_pairs={{0,4},{4,0},{8,12},{12,8},{16,20},{20,16},{24,28},{28,24},{1,5},{5... | collective-permute-start | bytes 3145736 | tf_op jit(solution)/shard_map/ppermute | solution.py:863
  204.9 36.5 %collective-permute-start.7 = (bf16[2,8,128,128]{3,2,1,0:T(8,128)(2,1)}, bf16[2,8,128,128]{3,2,1,0:T(8,128)(2,1)}, u32[]{:S(2)}, u32[]{:S(2)}) collective-permute-start(bf16[2,8,128,128]{3,2,1,0:T(8,128)(2,1)} %get-tuple-element.263), channel_id=1, source_target_pairs={{0,8},{4,12},{8,0},{12,4},{16,24},{20,28},{24,16},{28,20},{1,9},{5... | collective-permute-start | bytes 1572872 | tf_op jit(solution)/shard_map/ppermute | solution.py:863
  205.2 36.2 %collective-permute-start.8 = (bf16[4,8,128,128]{3,2,1,0:T(8,128)(2,1)}, bf16[4,8,128,128]{3,2,1,0:T(8,128)(2,1)}, u32[]{:S(2)}, u32[]{:S(2)}) collective-permute-start(bf16[4,8,128,128]{3,2,1,0:T(8,128)(2,1)} %get-tuple-element.264), channel_id=1, source_target_pairs={{0,4},{4,0},{8,12},{12,8},{16,20},{20,16},{24,28},{28,24},{1,5},{5... | collective-permute-start | bytes 3145736 | tf_op jit(solution)/shard_map/ppermute | solution.py:863
  206.8 34.6 %collective-permute-start.9 = (bf16[8,8,128,128]{3,2,1,0:T(8,128)(2,1)}, bf16[8,8,128,128]{3,2,1,0:T(8,128)(2,1)S(1)}, u32[]{:S(2)}, u32[]{:S(2)}) collective-permute-start(bf16[8,8,128,128]{3,2,1,0:T(8,128)(2,1)} %get-tuple-element.265), channel_id=1, source_target_pairs={{0,1},{1,0},{2,3},{3,2},{4,5},{5,4},{6,7},{7,6},{8,9},{9,8},{10,11... | collective-permute-start | bytes 6291464 | tf_op jit(solution)/shard_map/ppermute | solution.py:863
  206.8 34.5 %collective-permute-start.10 = (bf16[1,8,128,128]{3,2,1,0:T(8,128)(2,1)S(1)}, bf16[1,8,128,128]{3,2,1,0:T(8,128)(2,1)S(1)}, u32[]{:S(2)}, u32[]{:S(2)}) collective-permute-start(bf16[1,8,128,128]{3,2,1,0:T(8,128)(2,1)S(1)} %add_convert_fusion.40), channel_id=1, source_target_pairs={{0,16},{4,20},{8,24},{12,28},{16,0},{20,4},{24,8},{28,12},{1,17},{... | collective-permute-start | bytes 786440 | tf_op jit(solution)/shard_map/ppermute | solution.py:863
  247.1 23.5 %collective-permute-start.11 = (bf16[2,8,128,128]{3,2,1,0:T(8,128)(2,1)}, bf16[2,8,128,128]{3,2,1,0:T(8,128)(2,1)S(1)}, u32[]{:S(2)}, u32[]{:S(2)}) collective-permute-start(bf16[2,8,128,128]{3,2,1,0:T(8,128)(2,1)} %get-tuple-element.278), channel_id=1, source_target_pairs={{0,8},{4,12},{8,0},{12,4},{16,24},{20,28},{24,16},{28,20},{1,9},{5... | collective-permute-start | bytes 1572872 | tf_op jit(solution)/shard_map/ppermute | solution.py:863
  248.7 25.2 %collective-permute-start.12 = (bf16[4,8,128,128]{3,2,1,0:T(8,128)(2,1)}, bf16[4,8,128,128]{3,2,1,0:T(8,128)(2,1)S(1)}, u32[]{:S(2)}, u32[]{:S(2)}) collective-permute-start(bf16[4,8,128,128]{3,2,1,0:T(8,128)(2,1)} %get-tuple-element.279), channel_id=1, source_target_pairs={{0,4},{4,0},{8,12},{12,8},{16,20},{20,16},{24,28},{28,24},{1,5},{5... | collective-permute-start | bytes 3145736 | tf_op jit(solution)/shard_map/ppermute | solution.py:863
  249.2 21.4 %collective-permute-start.13 = (bf16[1,8,128,128]{3,2,1,0:T(8,128)(2,1)S(1)}, bf16[1,8,128,128]{3,2,1,0:T(8,128)(2,1)S(1)}, u32[]{:S(2)}, u32[]{:S(2)}) collective-permute-start(bf16[1,8,128,128]{3,2,1,0:T(8,128)(2,1)S(1)} %add_convert_fusion.39), channel_id=1, source_target_pairs={{0,16},{4,20},{8,24},{12,28},{16,0},{20,4},{24,8},{28,12},{1,17},{... | collective-permute-start | bytes 786440 | tf_op jit(solution)/shard_map/ppermute | solution.py:863
  249.5 24.4 %copy-start.12 = (bf16[2,8,128,128]{3,2,1,0:T(8,128)(2,1)S(1)}, bf16[2,8,128,128]{3,2,1,0:T(8,128)(2,1)}, u32[]{:S(2)}) copy-start(bf16[2,8,128,128]{3,2,1,0:T(8,128)(2,1)} %get-tuple-element.426) | copy-start | bytes 1572868
  275.4 23.3 %collective-permute-start.14 = (bf16[2,8,128,128]{3,2,1,0:T(8,128)(2,1)}, bf16[2,8,128,128]{3,2,1,0:T(8,128)(2,1)}, u32[]{:S(2)}, u32[]{:S(2)}) collective-permute-start(bf16[2,8,128,128]{3,2,1,0:T(8,128)(2,1)} %get-tuple-element.290), channel_id=1, source_target_pairs={{0,8},{4,12},{8,0},{12,4},{16,24},{20,28},{24,16},{28,20},{1,9},{5... | collective-permute-start | bytes 1572872 | tf_op jit(solution)/shard_map/ppermute | solution.py:863
  275.8 22.8 %collective-permute-start.15 = (bf16[8,4,128,128]{3,2,1,0:T(8,128)(2,1)}, bf16[8,4,128,128]{3,2,1,0:T(8,128)(2,1)}, u32[]{:S(2)}, u32[]{:S(2)}) collective-permute-start(bf16[8,4,128,128]{3,2,1,0:T(8,128)(2,1)} %get-tuple-element.291), channel_id=1, source_target_pairs={{0,1},{1,0},{2,3},{3,2},{4,5},{5,4},{6,7},{7,6},{8,9},{9,8},{10,11... | collective-permute-start | bytes 3145736 | tf_op jit(solution)/shard_map/ppermute | solution.py:863
  275.8 22.8 %collective-permute-start.16 = (bf16[1,8,128,128]{3,2,1,0:T(8,128)(2,1)S(1)}, bf16[1,8,128,128]{3,2,1,0:T(8,128)(2,1)}, u32[]{:S(2)}, u32[]{:S(2)}) collective-permute-start(bf16[1,8,128,128]{3,2,1,0:T(8,128)(2,1)S(1)} %add_convert_fusion.38), channel_id=1, source_target_pairs={{0,16},{4,20},{8,24},{12,28},{16,0},{20,4},{24,8},{28,12},{1,17},{... | collective-permute-start | bytes 786440 | tf_op jit(solution)/shard_map/ppermute | solution.py:863
  276.2 42.5 %all-to-all-start.2 = ((bf16[4,5,64,1024]{3,2,1,0:T(8,128)(2,1)}), bf16[4,5,64,1024]{3,2,1,0:T(8,128)(2,1)S(1)}, u32[]{:S(2)}, u32[]{:S(2)}) async-start(bf16[4,5,64,1024]{3,2,1,0:T(8,128)(2,1)} %bitcast.140), calls=%async_computation.2 | async-start | bytes 5242880 | tf_op jit(solution)/shard_map/all_to_all | solution.py:953
  302.5 16.2 %collective-permute-start.17 = (bf16[4,4,128,128]{3,2,1,0:T(8,128)(2,1)S(1)}, bf16[4,4,128,128]{3,2,1,0:T(8,128)(2,1)}, u32[]{:S(2)}, u32[]{:S(2)}) collective-permute-start(bf16[4,4,128,128]{3,2,1,0:T(8,128)(2,1)S(1)} %get-tuple-element.301), channel_id=1, source_target_pairs={{0,4},{4,0},{8,12},{12,8},{16,20},{20,16},{24,28},{28,24},{1,5},{5... | collective-permute-start | bytes 1572872 | tf_op jit(solution)/shard_map/ppermute | solution.py:863
  303.0 15.7 %collective-permute-start.18 = (bf16[1,8,128,128]{3,2,1,0:T(8,128)(2,1)S(1)}, bf16[1,8,128,128]{3,2,1,0:T(8,128)(2,1)S(1)}, u32[]{:S(2)}, u32[]{:S(2)}) collective-permute-start(bf16[1,8,128,128]{3,2,1,0:T(8,128)(2,1)S(1)} %add_convert_fusion.37), channel_id=1, source_target_pairs={{0,16},{4,20},{8,24},{12,28},{16,0},{20,4},{24,8},{28,12},{1,17},{... | collective-permute-start | bytes 786440 | tf_op jit(solution)/shard_map/ppermute | solution.py:863
  325.5 13.3 %collective-permute-start.20 = (bf16[8,9,128,128]{3,2,1,0:T(8,128)(2,1)}, bf16[8,9,128,128]{3,2,1,0:T(8,128)(2,1)}, u32[]{:S(2)}, u32[]{:S(2)}) collective-permute-start(bf16[8,9,128,128]{3,2,1,0:T(8,128)(2,1)} %get-tuple-element.317), channel_id=1, source_target_pairs={{0,1},{1,0},{2,3},{3,2},{4,5},{5,4},{6,7},{7,6},{8,9},{9,8},{10,11... | collective-permute-start | bytes 7077896 | tf_op jit(solution)/shard_map/ppermute | solution.py:863
  326.1 12.7 %collective-permute-start.19 = (bf16[6,160,640]{2,1,0:T(8,128)(2,1)}, bf16[6,160,640]{2,1,0:T(8,128)(2,1)}, u32[]{:S(2)}, u32[]{:S(2)}) collective-permute-start(bf16[6,160,640]{2,1,0:T(8,128)(2,1)} %get-tuple-element.315), channel_id=1, source_target_pairs={{0,1},{1,0},{2,3},{3,2},{4,5},{5,4},{6,7},{7,6},{8,9},{9,8},{10,11... | collective-permute-start | bytes 3686408 | tf_op jit(solution)/shard_map/ppermute | solution.py:863
  326.9 11.9 %collective-permute-start.21 = (bf16[2,4,128,128]{3,2,1,0:T(8,128)(2,1)}, bf16[2,4,128,128]{3,2,1,0:T(8,128)(2,1)S(1)}, u32[]{:S(2)}, u32[]{:S(2)}) collective-permute-start(bf16[2,4,128,128]{3,2,1,0:T(8,128)(2,1)} %get-tuple-element.318), channel_id=1, source_target_pairs={{0,8},{4,12},{8,0},{12,4},{16,24},{20,28},{24,16},{28,20},{1,9},{5... | collective-permute-start | bytes 786440 | tf_op jit(solution)/shard_map/ppermute | solution.py:863
  336.7 19.8 %collective-permute-start.24 = (bf16[1,24,128,128]{3,2,1,0:T(8,128)(2,1)}, bf16[1,24,128,128]{3,2,1,0:T(8,128)(2,1)}, u32[]{:S(2)}, u32[]{:S(2)}) collective-permute-start(bf16[1,24,128,128]{3,2,1,0:T(8,128)(2,1)} %pad_maximum_fusion.1), channel_id=1, source_target_pairs={{0,2},{1,3},{2,0},{3,1},{4,6},{5,7},{6,4},{7,5},{8,10},{9,11},{10,... | collective-permute-start | bytes 2359304 | tf_op jit(solution)/shard_map/ppermute | solution.py:863
  343.8 12.7 %collective-permute-start.22 = (bf16[2,160,640]{2,1,0:T(8,128)(2,1)}, bf16[2,160,640]{2,1,0:T(8,128)(2,1)}, u32[]{:S(2)}, u32[]{:S(2)}) collective-permute-start(bf16[2,160,640]{2,1,0:T(8,128)(2,1)} %get-tuple-element.329), channel_id=1, source_target_pairs={{0,1},{1,0},{2,3},{3,2},{4,5},{5,4},{6,7},{7,6},{8,9},{9,8},{10,11... | collective-permute-start | bytes 1228808 | tf_op jit(solution)/shard_map/ppermute | solution.py:863
  343.9 12.6 %collective-permute-start.23 = (bf16[1,4,128,128]{3,2,1,0:T(8,128)(2,1)S(1)}, bf16[1,4,128,128]{3,2,1,0:T(8,128)(2,1)S(1)}, u32[]{:S(2)}, u32[]{:S(2)}) collective-permute-start(bf16[1,4,128,128]{3,2,1,0:T(8,128)(2,1)S(1)} %add_convert_fusion.45), channel_id=1, source_target_pairs={{0,16},{4,20},{8,24},{12,28},{16,0},{20,4},{24,8},{28,12},{1,17},{... | collective-permute-start | bytes 393224 | tf_op jit(solution)/shard_map/ppermute | solution.py:863
  353.9 28.4 %collective-permute-start.26 = (bf16[4,9,128,128]{3,2,1,0:T(8,128)(2,1)}, bf16[4,9,128,128]{3,2,1,0:T(8,128)(2,1)}, u32[]{:S(2)}, u32[]{:S(2)}) collective-permute-start(bf16[4,9,128,128]{3,2,1,0:T(8,128)(2,1)} %get-tuple-element.343), channel_id=1, source_target_pairs={{0,4},{4,0},{8,12},{12,8},{16,20},{20,16},{24,28},{28,24},{1,5},{5... | collective-permute-start | bytes 3538952 | tf_op jit(solution)/shard_map/ppermute | solution.py:863
  360.1 20.9 %collective-permute-start.25 = (bf16[1,12,128,128]{3,2,1,0:T(8,128)(2,1)S(1)}, bf16[1,12,128,128]{3,2,1,0:T(8,128)(2,1)}, u32[]{:S(2)}, u32[]{:S(2)}) collective-permute-start(bf16[1,12,128,128]{3,2,1,0:T(8,128)(2,1)S(1)} %pad_maximum_fusion.2), channel_id=1, source_target_pairs={{0,2},{1,3},{2,0},{3,1},{4,6},{5,7},{6,4},{7,5},{8,10},{9,11},{10,... | collective-permute-start | bytes 1179656 | tf_op jit(solution)/shard_map/ppermute | solution.py:863
  361.9 20.4 %collective-permute-start.27 = (bf16[8,3,128,128]{3,2,1,0:T(8,128)(2,1)}, bf16[8,3,128,128]{3,2,1,0:T(8,128)(2,1)}, u32[]{:S(2)}, u32[]{:S(2)}) collective-permute-start(bf16[8,3,128,128]{3,2,1,0:T(8,128)(2,1)} %get-tuple-element.344), channel_id=1, source_target_pairs={{0,1},{1,0},{2,3},{3,2},{4,5},{5,4},{6,7},{7,6},{8,9},{9,8},{10,11... | collective-permute-start | bytes 2359304 | tf_op jit(solution)/shard_map/ppermute | solution.py:863
  377.3 33.8 %all-to-all-start.3 = ((bf16[32,78,128]{2,1,0:T(8,128)(2,1)}), bf16[32,78,128]{2,1,0:T(8,128)(2,1)}, u32[]{:S(2)}, u32[]{:S(2)}) async-start(bf16[32,78,128]{2,1,0:T(8,128)(2,1)} %bitcast.142), calls=%async_computation.3 | async-start | bytes 1310720 | tf_op jit(solution)/shard_map/all_to_all | solution.py:1107
  380.7 30.4 %collective-permute-start.30 = (bf16[1,24,128,128]{3,2,1,0:T(8,128)(2,1)}, bf16[1,24,128,128]{3,2,1,0:T(8,128)(2,1)}, u32[]{:S(2)}, u32[]{:S(2)}) collective-permute-start(bf16[1,24,128,128]{3,2,1,0:T(8,128)(2,1)} %reduce-precision_convert_fusion), channel_id=1, source_target_pairs={{0,1},{1,0},{2,3},{3,2},{4,5},{5,4},{6,7},{7,6},{8,9},{9,8},{10,11... | collective-permute-start | bytes 2359304 | tf_op jit(solution)/shard_map/ppermute | solution.py:863
  387.9 23.2 %collective-permute-start.28 = (bf16[4,3,128,128]{3,2,1,0:T(8,128)(2,1)S(1)}, bf16[4,3,128,128]{3,2,1,0:T(8,128)(2,1)}, u32[]{:S(2)}, u32[]{:S(2)}) collective-permute-start(bf16[4,3,128,128]{3,2,1,0:T(8,128)(2,1)S(1)} %get-tuple-element.358), channel_id=1, source_target_pairs={{0,4},{4,0},{8,12},{12,8},{16,20},{20,16},{24,28},{28,24},{1,5},{5... | collective-permute-start | bytes 1179656 | tf_op jit(solution)/shard_map/ppermute | solution.py:863
  389.4 21.7 %collective-permute-start.29 = (bf16[2,9,128,128]{3,2,1,0:T(8,128)(2,1)}, bf16[2,9,128,128]{3,2,1,0:T(8,128)(2,1)}, u32[]{:S(2)}, u32[]{:S(2)}) collective-permute-start(bf16[2,9,128,128]{3,2,1,0:T(8,128)(2,1)} %get-tuple-element.359), channel_id=1, source_target_pairs={{0,8},{4,12},{8,0},{12,4},{16,24},{20,28},{24,16},{28,20},{1,9},{5... | collective-permute-start | bytes 1769480 | tf_op jit(solution)/shard_map/ppermute | solution.py:863
  389.7 21.4 %collective-permute-start.31 = (bf16[1,12,128,128]{3,2,1,0:T(8,128)(2,1)S(1)}, bf16[1,12,128,128]{3,2,1,0:T(8,128)(2,1)}, u32[]{:S(2)}, u32[]{:S(2)}) collective-permute-start(bf16[1,12,128,128]{3,2,1,0:T(8,128)(2,1)S(1)} %reduce-precision_convert_fusion.2), channel_id=1, source_target_pairs={{0,1},{1,0},{2,3},{3,2},{4,5},{5,4},{6,7},{7,6},{8,9},{9,8},{10,11... | collective-permute-start | bytes 1179656 | tf_op jit(solution)/shard_map/ppermute | solution.py:863
  416.0 26.4 %copy-start.13 = (f32[8,78,128]{2,1,0:T(8,128)}, f32[8,78,128]{2,1,0:T(8,128)S(1)}, u32[]{:S(2)}) copy-start(f32[8,78,128]{2,1,0:T(8,128)S(1)} %convert_reduce_fusion) | copy-start | bytes 958468
  416.1 33.5 %collective-permute-start.34 = (bf16[5,64,1024]{2,1,0:T(8,128)(2,1)}, bf16[5,64,1024]{2,1,0:T(8,128)(2,1)}, u32[]{:S(2)}, u32[]{:S(2)}) collective-permute-start(bf16[5,64,1024]{2,1,0:T(8,128)(2,1)} %get-tuple-element.378), channel_id=1, source_target_pairs={{0,2},{1,3},{2,0},{3,1},{4,6},{5,7},{6,4},{7,5},{8,10},{9,11},{10,... | collective-permute-start | bytes 1966088 | tf_op jit(solution)/shard_map/ppermute | solution.py:1133
  417.6 32.0 %collective-permute-start.35 = (bf16[5,64,1024]{2,1,0:T(8,128)(2,1)}, bf16[5,64,1024]{2,1,0:T(8,128)(2,1)}, u32[]{:S(2)}, u32[]{:S(2)}) collective-permute-start(bf16[5,64,1024]{2,1,0:T(8,128)(2,1)} %get-tuple-element.379), channel_id=1, source_target_pairs={{0,3},{1,2},{2,1},{3,0},{4,7},{5,6},{6,5},{7,4},{8,11},{9,10},{10,... | collective-permute-start | bytes 1966088 | tf_op jit(solution)/shard_map/ppermute | solution.py:1133
  418.8 30.8 %all-to-all-start.4 = ((bf16[32,18,128]{2,1,0:T(8,128)(2,1)}), bf16[32,18,128]{2,1,0:T(8,128)(2,1)S(1)}, u32[]{:S(2)}, u32[]{:S(2)}) async-start(bf16[32,18,128]{2,1,0:T(8,128)(2,1)} %bitcast.145), calls=%async_computation.4 | async-start | bytes 393216 | tf_op jit(solution)/shard_map/all_to_all | solution.py:1107
  422.9 26.7 %collective-permute-start.36 = (bf16[1,9,128,128]{3,2,1,0:T(8,128)(2,1)}, bf16[1,9,128,128]{3,2,1,0:T(8,128)(2,1)}, u32[]{:S(2)}, u32[]{:S(2)}) collective-permute-start(bf16[1,9,128,128]{3,2,1,0:T(8,128)(2,1)} %add_convert_fusion.26), channel_id=1, source_target_pairs={{0,16},{4,20},{8,24},{12,28},{16,0},{20,4},{24,8},{28,12},{1,17},{... | collective-permute-start | bytes 884744 | tf_op jit(solution)/shard_map/ppermute | solution.py:863
  425.7 11.7 %collective-permute-start.32 = (bf16[5,64,1024]{2,1,0:T(8,128)(2,1)}, bf16[5,64,1024]{2,1,0:T(8,128)(2,1)}, u32[]{:S(2)}, u32[]{:S(2)}) collective-permute-start(bf16[5,64,1024]{2,1,0:T(8,128)(2,1)} %get-tuple-element.373), channel_id=1, source_target_pairs={{0,1},{1,0},{2,3},{3,2},{4,5},{5,4},{6,7},{7,6},{8,9},{9,8},{10,11... | collective-permute-start | bytes 1966088 | tf_op jit(solution)/shard_map/ppermute | solution.py:1134
  425.7 11.7 %collective-permute-start.33 = (bf16[2,3,128,128]{3,2,1,0:T(8,128)(2,1)}, bf16[2,3,128,128]{3,2,1,0:T(8,128)(2,1)S(1)}, u32[]{:S(2)}, u32[]{:S(2)}) collective-permute-start(bf16[2,3,128,128]{3,2,1,0:T(8,128)(2,1)} %get-tuple-element.374), channel_id=1, source_target_pairs={{0,8},{4,12},{8,0},{12,4},{16,24},{20,28},{24,16},{28,20},{1,9},{5... | collective-permute-start | bytes 589832 | tf_op jit(solution)/shard_map/ppermute | solution.py:863
  437.4 12.2 %collective-permute-start.37 = (bf16[1,3,128,128]{3,2,1,0:T(8,128)(2,1)S(1)}, bf16[1,3,128,128]{3,2,1,0:T(8,128)(2,1)}, u32[]{:S(2)}, u32[]{:S(2)}) collective-permute-start(bf16[1,3,128,128]{3,2,1,0:T(8,128)(2,1)S(1)} %add_convert_fusion.48), channel_id=1, source_target_pairs={{0,16},{4,20},{8,24},{12,28},{16,0},{20,4},{24,8},{28,12},{1,17},{... | collective-permute-start | bytes 294920 | tf_op jit(solution)/shard_map/ppermute | solution.py:863
  451.9 11.2 %collective-permute-start.38 = (bf16[1,12,128,128]{3,2,1,0:T(8,128)(2,1)S(1)}, bf16[1,12,128,128]{3,2,1,0:T(8,128)(2,1)S(1)}, u32[]{:S(2)}, u32[]{:S(2)}) collective-permute-start(bf16[1,12,128,128]{3,2,1,0:T(8,128)(2,1)S(1)} %pad_maximum_fusion.3), channel_id=1, source_target_pairs={{0,2},{1,3},{2,0},{3,1},{4,6},{5,7},{6,4},{7,5},{8,10},{9,11},{10,... | collective-permute-start | bytes 1179656 | tf_op jit(solution)/shard_map/ppermute | solution.py:863
  463.5 5.7 %collective-permute-start.39 = (bf16[1,12,128,128]{3,2,1,0:T(8,128)(2,1)S(1)}, bf16[1,12,128,128]{3,2,1,0:T(8,128)(2,1)S(1)}, u32[]{:S(2)}, u32[]{:S(2)}) collective-permute-start(bf16[1,12,128,128]{3,2,1,0:T(8,128)(2,1)S(1)} %reduce-precision_convert_fusion.1), channel_id=1, source_target_pairs={{0,1},{1,0},{2,3},{3,2},{4,5},{5,4},{6,7},{7,6},{8,9},{9,8},{10,11... | collective-permute-start | bytes 1179656 | tf_op jit(solution)/shard_map/ppermute | solution.py:863
  (44 other events, 266.1 us)

commit v4 on v3

--- a/solution.py
+++ b/solution.py
@@ -196,7 +196,7 @@
         ],
         name="bucket_sums",
         compiler_params=params(),
-        cost_estimate=cost(14),
+        cost_estimate=cost(4),
     )(idx, *keeps, *gots)
 
 
@@ -711,17 +711,19 @@
     )(src, inv, flags, mixed, back, *([pieces] * 4), x_rows, branch, mod, b_down, w_out, attended)
 
 
-def qkv_weight_kernel(inv_ref, flag_ref, n_ref, a_ref, b_ref, g0_ref, g1_ref):
-    for out_ref, ref in ((g0_ref, a_ref), (g1_ref, b_ref)):
-        place_rows(inv_ref, out_ref, dot_tn(n_ref[...], ref[0]).astype(bf16))
+def qkv_weight_kernel(inv_ref, flag_ref, n_ref, grad_ref, g0_ref, g1_ref):
+    got = dot_tn(n_ref[...], grad_ref[0]).astype(bf16)
+    half = got.shape[1] // 2
+    own, other = pick(flag_ref[0] == 1, got[:, :half], got[:, half:])
+    place_rows(inv_ref, g0_ref, own)
+    place_rows(inv_ref, g1_ref, other)
 
 
 def qkv_weight(inv, flags, normed, grads):
     rows, features = normed.shape
     parts, unused, wide = grads.shape
-    half = wide // 2
     shards = features // LANES
-    tiles = half // LANES
+    tiles = wide // 2 // LANES
     out_spec = pl.BlockSpec((shards, tiles, LANES, LANES), lambda i, *more: (0, i, 0, 0))
     grad = jax.ShapeDtypeStruct((shards, parts * tiles, LANES, LANES), bf16)
     return pl.pallas_call(
@@ -731,8 +733,7 @@
             grid=(parts,),
             in_specs=[
                 whole(normed.shape),
-                pl.BlockSpec((1, rows, half), lambda i, inv, flags: (i, 0, flags[0])),
-                pl.BlockSpec((1, rows, half), lambda i, inv, flags: (i, 0, 1 - flags[0])),
+                pl.BlockSpec((1, rows, wide), lambda i, *more: (i, 0, 0)),
             ],
             out_specs=[out_spec, out_spec],
         ),
@@ -740,13 +741,16 @@
         name="qkv_weight",
         compiler_params=params(),
         cost_estimate=cost(6),
-    )(inv, flags, normed, grads, grads)
+    )(inv, flags, normed, grads)
 
 
 def qkv_back_kernel(src_ref, *refs):
-    count = len(refs) - 8
+    count = len(refs) - 11
     grads = refs[:count]
-    w_ref, x_ref, gres_ref, mod_ref, out_ref, vec_ref, stage_ref, sem_ref = refs[count:]
+    w_ref, x_ref, gres_ref, mod_ref = refs[count : count + 4]
+    out_refs = refs[count + 4 : count + 8]
+    vec_ref, stage_ref, sem_ref = refs[count + 8 :]
+    per = out_refs[0].shape[0]
     step = pl.program_id(0)
     block = x_ref.shape[0]
     features = x_ref.shape[1]
@@ -762,11 +766,16 @@
     grad = gres_ref[...].astype(f32) + norm_back(back * (1.0 + mod_ref[1:2, :]), hat_rows, inv_std)
     stage_ref[pl.ds(pl.multiple_of(step * block, block), block)] = grad.astype(bf16)
     for t in range(4):
-        pltpu.make_async_copy(
-            stage_ref.at[pl.ds(pl.multiple_of(step * block + t * PIECE, PIECE), PIECE)],
-            out_ref.at[src_ref[4 * step + t]],
-            sem_ref.at[4 * step + t],
-        ).start()
+        slot = src_ref[4 * step + t]
+        for k in range(4):
+
+            @pl.when(slot // per == k)
+            def _(k=k, t=t, slot=slot):
+                pltpu.make_async_copy(
+                    stage_ref.at[pl.ds(pl.multiple_of(step * block + t * PIECE, PIECE), PIECE)],
+                    out_refs[k].at[slot - k * per],
+                    sem_ref.at[4 * step + t],
+                ).start()
     pieces = jnp.concatenate(
         [
             jnp.sum(back, axis=0, keepdims=True),
@@ -790,7 +799,7 @@
     def _():
         for k in range(sem_ref.shape[0]):
             pltpu.make_async_copy(
-                stage_ref.at[pl.ds(k * PIECE, PIECE)], out_ref.at[src_ref[k]], sem_ref.at[k]
+                stage_ref.at[pl.ds(k * PIECE, PIECE)], out_refs[0].at[0], sem_ref.at[k]
             ).wait()
 
 
@@ -806,7 +815,7 @@
             grid=(rows // block,),
             in_specs=grad_specs + [whole(w_qkv.shape), rows_spec, rows_spec, whole(mod.shape)],
             out_specs=[
-                pl.BlockSpec(memory_space=pl.ANY),
+                *[pl.BlockSpec(memory_space=pl.ANY)] * 4,
                 pl.BlockSpec((8, features), lambda i, src: (0, 0)),
             ],
             scratch_shapes=[
@@ -815,7 +824,7 @@
             ],
         ),
         out_shape=[
-            jax.ShapeDtypeStruct((rows // PIECE, PIECE, features), bf16),
+            *[jax.ShapeDtypeStruct((rows // PIECE // 4, PIECE, features), bf16)] * 4,
             jax.ShapeDtypeStruct((8, features), f32),
         ],
         name="qkv_backward",
@@ -863,8 +872,64 @@
     return lax.ppermute(array, axis, flip(axis, bit))
 
 
-def add_low(a, b):
-    return (a.astype(f32) + b.astype(f32)).astype(bf16)
+def add_kernel(plans, *refs):
+    ins = refs[: 2 * sum(count for count, unused in plans)]
+    outs = refs[len(ins) :]
+    at = out_at = 0
+    for count, halve in plans:
+        col = 0
+        for k in range(count):
+            own_ref, got_ref = ins[at], ins[at + 1]
+            at += 2
+            n, m = own_ref.shape[:2]
+            total = (own_ref[...].astype(f32) + got_ref[...].astype(f32)).astype(bf16)
+            if halve:
+                outs[out_at][:, col : col + m] = total[: n // 2]
+                outs[out_at + 1][:, col : col + m] = total[n // 2 :]
+            else:
+                outs[out_at][:, col : col + m] = total
+            col += m
+        out_at += 2 if halve else 1
+
+
+def add_all(groups):
+    steps = 2
+    plans, ins, specs, out_shapes, out_specs = [], [], [], [], []
+
+    def spec(shape):
+        return pl.BlockSpec(shape[:2] + (shape[2] // steps, shape[3]), lambda i: (0, 0, i, 0))
+
+    for pairs, halve in groups:
+        plans.append((len(pairs), halve))
+        for own, got in pairs:
+            ins += [own, got]
+            specs += [spec(own.shape)] * 2
+        n, unused, rows, cols = pairs[0][0].shape
+        m = sum(own.shape[1] for own, unused in pairs)
+        shape = (n // 2 if halve else n, m, rows, cols)
+        out_shapes += [jax.ShapeDtypeStruct(shape, bf16)] * (2 if halve else 1)
+        out_specs += [spec(shape)] * (2 if halve else 1)
+    return pl.pallas_call(
+        functools.partial(add_kernel, plans),
+        grid=(steps,),
+        in_specs=specs,
+        out_specs=out_specs,
+        out_shape=out_shapes,
+        name="add_all",
+        compiler_params=params(),
+        cost_estimate=cost(2),
+    )(*ins)
+
+
+def prepare(chains):
+    groups = []
+    for c in chains:
+        c.stage += 1
+        groups.append((list(zip(c.own, c.got)), c.stage <= c.clip_bits))
+    sums = list(add_all(groups))
+    for c, (unused, halve) in zip(chains, groups):
+        c.own = [sums.pop(0)]
+        c.sends = [sums.pop(0)] if halve else c.own
 
 
 class Chain:
@@ -884,29 +949,10 @@
             axis, bit = "clip", self.stage - 1
         self.got = [trade(send, axis, bit) for send in self.sends]
 
-    def prepare(self):
-        self.stage += 1
-        both = list(zip(self.own, self.got))
-        if self.stage <= self.clip_bits:
-            half = self.own[0].shape[0] // 2
-            self.sends = [joined([add_low(o[half:], g[half:]) for o, g in both])]
-            self.own = [joined([add_low(o[:half], g[:half]) for o, g in both])]
-        elif self.stage == self.clip_bits + 1:
-            self.own = self.sends = [joined([add_low(o, g) for o, g in both])]
-        else:
-            exact = [o.astype(f32) + g.astype(f32) for o, g in both]
-            self.own = self.sends = [
-                joined([lax.reduce_precision(e, 8, 7).astype(bf16) for e in exact])
-            ]
-
     def finish(self):
         while self.stage < self.clip_bits + 2:
             boundary((), [self], [])
         return self.own[0][0], self.got[0][0]
-
-
-def joined(arrays):
-    return arrays[0] if len(arrays) == 1 else jnp.concatenate(arrays, axis=1)
 
 
 def unite(*chains):
@@ -923,13 +969,13 @@
     inputs, got = lax.optimization_barrier((inputs, got))
     for c, g in zip(waited, got):
         c.got = g
-    for c in moved:
-        c.prepare()
+    if moved:
+        prepare(moved)
     chains = moved + fresh
     inputs, sends = lax.optimization_barrier((inputs, [c.sends for c in chains]))
     for c, sent in zip(chains, sends):
         c.sends = sent
-        if c.own is not None and c.stage >= c.clip_bits + 1:
+        if c.stage >= c.clip_bits + 1:
             c.own = sent
         c.launch()
     return inputs
@@ -1090,75 +1136,53 @@
     others_a, others_b, unused = meet((others_a, others_b, qb_own), [rear, front], [qbs])
     rel_sums = bucket_sums(idx_mine, [mine_a, mine_b], [others_a, others_b], rel_table.shape[0])
 
-    if fast:
-        here = natural[:, None] == order[None, :]
-        up_sums = [jnp.sum(jnp.where(here[:, :, None], u[None], 0.0), axis=1) for u in up_sums]
-    grad_b_up = jnp.stack(up_sums, axis=1 if fast else 0)
     d = features
     tile_rows = d // LANES
     wins = lax.axis_size("win")
     buckets, heads = rel_table.shape
-
-    def to_all(to_each, by_clip):
+    gres_late, unused = meet((gres, rel_sums), [rear, qas, qbs])
+    home = lax.axis_index("win") if fast else 0
+    src_back = (((src // local_slots) ^ home) * local_slots + src % local_slots).astype(jnp.int32)
+    *token_parts, late = qkv_backward(src_back, (grads_a, grads_b), w_qkv, x_rows, gres_late, mod)
+    if fast:
+        token_parts, late, early, up_sums, rel_sums, out_pieces = meet(
+            (token_parts, late, early, up_sums, rel_sums, out_pieces), [qbs, qas], held=[front, rear]
+        )
+        moves = [[(i, i ^ k) for i in range(wins)] for k in range(4)]
+        far = [lax.ppermute(token_parts[k], "win", moves[k]) for k in (2, 3)]
+        near = lax.ppermute(token_parts[1], "win", moves[1])
+        near, late, early, up_sums, rel_sums = boundary((near, late, early, up_sums, rel_sums), [qbs], [])
+        here = natural[:, None] == order[None, :]
+        up_sums = [jnp.sum(jnp.where(here[:, :, None], u[None], 0.0), axis=1) for u in up_sums]
+    grad_b_up = jnp.stack(up_sums, axis=1 if fast else 0)
+    if fast:
+        to_each = [early[:4].reshape(-1, LANES), late[:2].reshape(-1, LANES), lifted[0].astype(f32).reshape(-1, LANES)]
+        by_clip = [v.reshape(clips, 1, LANES) for v in (early[4], early[5], late[2], late[3])]
+        by_clip += [grad_b_up.reshape(clips, -1, LANES), rel_sums]
         parts = [jnp.broadcast_to(v[None], (clips,) + v.shape) for v in to_each] + by_clip
         packed = jnp.concatenate(parts, axis=1).astype(bf16)
         packed = jnp.broadcast_to(packed[:, None], (clips, wins) + packed.shape[1:])
         packed = packed.reshape((clips * wins,) + packed.shape[2:])
-        return lax.all_to_all(packed, ("clip", "win"), split_axis=0, concat_axis=0, tiled=True)
-
-    def from_all(received):
-        return jnp.sum(received.astype(f32).reshape((clips, wins) + received.shape[1:]), axis=1)
-
-    if fast:
-        early_vec = to_all(
-            [early[:4].reshape(-1, LANES), lifted[0].astype(f32).reshape(-1, LANES)],
-            [
-                early[4].reshape(clips, 1, LANES),
-                early[5].reshape(clips, 1, LANES),
-                grad_b_up.reshape(clips, -1, LANES),
-                rel_sums,
-            ],
-        )
-    gres_late, unused = meet((gres, rel_sums), [rear, qas, qbs])
-    home = lax.axis_index("win") if fast else 0
-    src_back = (((src // local_slots) ^ home) * local_slots + src % local_slots).astype(jnp.int32)
-    token_pieces, late = qkv_backward(src_back, (grads_a, grads_b), w_qkv, x_rows, gres_late, mod)
-    token_pieces = token_pieces.reshape(piece_shape)
-    if fast:
-        token_parts = [token_pieces[k] for k in range(4)]
-        token_parts, late, early_vec, out_pieces = meet(
-            (token_parts, late, early_vec, out_pieces), [qbs, qas], held=[front, rear]
-        )
-        moves = [[(i, i ^ k) for i in range(wins)] for k in range(4)]
-        far = [lax.ppermute(token_parts[k], "win", moves[k]) for k in (2, 3)]
-        near = lax.ppermute(token_parts[1], "win", moves[1])
-        late_vec = to_all(
-            [late[:2].reshape(-1, LANES)],
-            [late[2].reshape(clips, 1, LANES), late[3].reshape(clips, 1, LANES)],
-        )
-        near = boundary(near, [qbs], [])
+        vectors = lax.all_to_all(packed, ("clip", "win"), split_axis=0, concat_axis=0, tiled=True)
         last = merge(qas, qbs)
-        far, late_vec = boundary((far, late_vec), [last], [])
-        (late_vec,) = boundary((late_vec,), [last], [])
+        far = boundary(far, [last], [])
+        (vectors,) = boundary((vectors,), [last], [])
         token_pieces = jnp.stack([token_parts[0], near] + far).reshape((2, 2) + token_parts[0].shape)
         for axis, bit in ((0, 1), (1, 0)):
             swapped = (home >> bit) & 1 == 1
             token_pieces = jnp.where(swapped, jnp.flip(token_pieces, axis), token_pieces)
         token_pieces = token_pieces.reshape(piece_shape)
-        early_rows, late_rows = from_all(early_vec), from_all(late_vec)
-        n = 4 * tile_rows
-        early_terms = early_rows[:, :n].reshape(clips, 4 * d)
-        late_terms = late_rows[:, : 2 * tile_rows].reshape(clips, 2 * d)
-        all_lifted = early_rows[:, n : n + tile_rows].reshape(clips, d) * (1.0 / wins)
-        n += tile_rows
-        own = jnp.sum(early_rows[:, n:], axis=0)
-        sum_bo, sum_bd, sum_bu = own[0], own[1], own[2 : 2 + ff // clips // LANES].reshape(-1)
-        rel = own[2 + ff // clips // LANES :].reshape(2, heads, LANES)
-        sum_rel = rel.transpose(0, 2, 1).reshape(buckets // clips, heads)
-        own = jnp.sum(late_rows[:, 2 * tile_rows :], axis=0)
-        sum_bq, sum_bv = own[0], own[1]
+        rows_of = jnp.sum(vectors.astype(f32).reshape((clips, wins) + vectors.shape[1:]), axis=1)
+        early_terms = rows_of[:, : 4 * tile_rows].reshape(clips, 4 * d)
+        late_terms = rows_of[:, 4 * tile_rows : 6 * tile_rows].reshape(clips, 2 * d)
+        all_lifted = rows_of[:, 6 * tile_rows : 7 * tile_rows].reshape(clips, d) * (1.0 / wins)
+        own = jnp.sum(rows_of[:, 7 * tile_rows :], axis=0)
+        sum_bo, sum_bd, sum_bq, sum_bv = own[0], own[1], own[2], own[3]
+        at = 4 + ff // clips // LANES
+        sum_bu = own[4:at].reshape(-1)
+        sum_rel = own[at:].reshape(2, heads, LANES).transpose(0, 2, 1).reshape(buckets // clips, heads)
     else:
-        token_pieces = exchange(token_pieces)
+        token_pieces = exchange(jnp.stack(token_parts))
 
         def all_clips(rows):
             return lax.psum(lax.all_gather(rows.reshape(-1), "clip", axis=0), "win")

time: 478 us -> 473 us (0.990)
  other arithmetic: 65.1 us -> 12.5 us
  Pallas kernels: 281 us -> 322 us
  waiting for transfers between devices: 29.1 us -> 40.6 us
  starting transfers between devices: 61.7 us -> 53.3 us
  local copies, waits for them, and re-layouts: 23 us -> 27.8 us
    convert_element_type x31 -> x0, other arithmetic: 50.4 us -> none  [the longest x28 46.9 us: add_low(): return (a.astype(f32) + b.astype(f32)).astype(bf16)]
    pallas_call x0 -> x14, Pallas kernels: none -> 45.5 us  [add_all(): pl.pallas_call(functools.partial(add_kernel, plans), grid=(steps,), in_sp...]
    ppermute x2, waiting for transfers between devices: 0.01 us -> 15.1 us  [local(): far = [lax.ppermute(token_parts[k], 'win', moves[k]) for k in (2, 3)]]
    unnamed x93 -> x110, local copies, waits for them, and re-layouts: 2.54 us -> 11.8 us
    ppermute x37, starting transfers between devices: 39.4 us -> 34.5 us  [trade(): return lax.ppermute(array, axis, flip(axis, bit))]
  transfers between devices with their start and end apart: 45 -> 44, of which waited for: 8 -> 8; matrix products, arithmetic and copies ran while one was open for 12% -> 7% of each run, Pallas kernels for 53% -> 56%
where the time goes in v4:
time: 473 us; the launch traced here: 469 us
  Pallas kernels  322 us (68%)
  starting transfers between devices  53.3 us (11%)
  waiting for transfers between devices  40.6 us (9%)
  local copies, waits for them, and re-layouts  27.8 us (6%)
  other arithmetic  12.5 us (3%)
  matrix products  10.7 us (2%)
    pallas_call x4, Pallas kernels, ff_part(): pl.pallas_call(functools.partial(ff_part_kernel, count), grid_spec=pltpu....  77.9 us
    pallas_call x14, Pallas kernels, add_all(): pl.pallas_call(functools.partial(add_kernel, plans), grid=(steps,), in_sp...  45.5 us
    ppermute x37, starting transfers between devices, trade(): return lax.ppermute(array, axis, flip(axis, bit))  34.5 us
    pallas_call x1, Pallas kernels, ff_join(): pl.pallas_call(functools.partial(ff_join_kernel, units), grid_spec=pltpu....  31.7 us
    pallas_call x2, Pallas kernels, attn_backward(): pl.pallas_call(functools.partial(attn_back_kernel, windows), grid_spec=pl...  26.8 us
    ppermute x37, waiting for transfers between devices, trade(): return lax.ppermute(array, axis, flip(axis, bit))  25.4 us
    pallas_call x1, Pallas kernels, ff_rows(): pl.pallas_call(functools.partial(ff_rows_kernel, blocks), grid_spec=pltpu...  20.8 us
    pallas_call x1, Pallas kernels, bias_gather(): pl.pallas_call(bias_kernel, grid=(rows // 8,), in_specs=[pl.BlockSpec((8,...  19.1 us
  transfers between devices with their start and end apart: 44, of which 8 were waited for; matrix products, arithmetic and copies ran while one was open for 7% of the time, Pallas kernels for 56%

profile of v4, /device:TPU:0, one launch (start us, length us, event | category | flops | bytes accessed | tf_op | source)
XLA Modules:
  0.0 468.7 jit_solution(508808173996967756)
XLA Ops:
  0.7 3.6 copy.59
  4.3 4.4 all-to-all-start
  8.7 6.3 %fusion.5 = f32[1,6144]{1,0:T(1,128)S(1)} fusion(bf16[1024,6144]{1,0:T(8,128)(2,1)} %param.30, bf16[1,1024]{1,0:T(2,128)(2,1)S(1)} %copy-done.8), kind=kOutput, calls=%fused_computation.36 | convolution fusion | flops 12589056 | bytes 12609536 | tf_op jit(solution)/shard_map/dot_general | solution.py:1047
  15.1 3.6 copy.60
  20.7 19.1 %bias_gather.1.mine_ref = f32[8,160,640]{2,1,0:T(8,128)} custom-call(s32[160,384]{1,0:T(8,128)} %pad.6.idx_ref, bf16[256,256]{1,0:T(8,128)(2,1)} %pad_maximum_fusion.1.tab_ref), custom_call_target="tpu_custom_call" | custom-call | flops 900000000 | bytes 1800000 | tf_op jit(solution)/shard_map/bias_gather/pallas_call | solution.py:114
  41.9 4.9 %all-to-all-start.1 = ((bf16[4,5,64,1024]{3,2,1,0:T(8,128)(2,1)}), bf16[4,5,64,1024]{3,2,1,0:T(8,128)(2,1)}, u32[]{:S(2)}, u32[]{:S(2)}) async-start(bf16[4,5,64,1024]{3,2,1,0:T(8,128)(2,1)} %bitcast.121), calls=%async_computation.1 | async-start | bytes 5242880 | tf_op jit(solution)/shard_map/all_to_all | solution.py:999
  51.7 15.9 %norm_qkv.1 = (bf16[1280,1024]{1,0:T(8,128)(2,1)}, bf16[1280,1024]{1,0:T(8,128)(2,1)}, bf16[1280,3072]{1,0:T(8,128)(2,1)}) custom-call(s32[20]{0:T(128)} %select_reduce_fusion.4.src_ref, bf16[20,64,1024]{2,1,0:T(8,128)(2,1)} %bitcast.116, bf16[20,64,1024]{2,1,0:T(8,128)(2,1)} %bitcast.117, bf16[20,64,1024]{2,1,0:T(8,128)(2,1)} %bitcast.118, ...), custom_call_target="tpu_custom_call" | custom-call | flops 600000000 | bytes 1200000 | tf_op jit(solution)/shard_map/norm_qkv/pallas_call | solution.py:227
  67.6 17.7 %attn_forward.1 = (bf16[1280,1024]{1,0:T(8,128)(2,1)}, bf16[8,4,320,640]{3,2,1,0:T(8,128)(2,1)}, f32[1280,1024]{1,0:T(8,128)}) custom-call(s32[1]{0:T(128)} %bitcast.1.core_ref, bf16[1280,3072]{1,0:T(8,128)(2,1)} %get-tuple-element.282.q_ref.k_ref.v_ref, bf16[1280,3072]{1,0:T(8,128)(2,1)} %get-tuple-element.282.q_ref.k_ref.v_ref, ...), custom_call_target="tpu_custom_call" | custom-call | flops 900000000 | bytes 1800000 | tf_op jit(solution)/shard_map/attn_forward/pallas_call | solution.py:313
  85.3 10.8 %out_norm.1 = (bf16[1280,1024]{1,0:T(8,128)(2,1)}, bf16[1280,1024]{1,0:T(8,128)(2,1)}, bf16[1280,1024]{1,0:T(8,128)(2,1)}) custom-call(s32[20]{0:T(128)} %select_reduce_fusion.4.src_ref, bf16[20,64,1024]{2,1,0:T(8,128)(2,1)} %bitcast.15.a_ref.b_ref.c_ref.d_ref.refs_0_.refs_1_.refs_2_.refs_3_, ...), custom_call_target="tpu_custom_call" | custom-call | flops 300000000 | bytes 600000 | tf_op jit(solution)/shard_map/out_norm/pallas_call | solution.py:424
  96.1 19.4 %ff_part.4 = (bf16[4,1280,1024]{2,1,0:T(8,128)(2,1)}, bf16[4,1280,1024]{2,1,0:T(8,128)(2,1)}, bf16[8,8,128,128]{3,2,1,0:T(8,128)(2,1)}, bf16[8,8,128,128]{3,2,1,0:T(8,128)(2,1)}, f32[2,1,512]{2,1,0:T(1,128)}) custom-call(s32[8]{0:T(128)} %get-tuple-element.561.fo_ref, s32[4]{0:T(128)} %broadcast_and_fusion.co_ref, s32[8]{0:T(128)} %get-tuple-element.559.inv_ref, ...), custom_call_target="tpu_custom_call" | custom-call | flops 20000000000 | bytes 40000000 | tf_op jit(solution)/shard_map/ff_part/pallas_call | solution.py:515
  116.6 19.9 %ff_part.5 = (bf16[4,1280,1024]{2,1,0:T(8,128)(2,1)}, bf16[4,1280,1024]{2,1,0:T(8,128)(2,1)}, bf16[8,8,128,128]{3,2,1,0:T(8,128)(2,1)}, bf16[8,8,128,128]{3,2,1,0:T(8,128)(2,1)}, f32[2,1,512]{2,1,0:T(1,128)}) custom-call(s32[8]{0:T(128)} %get-tuple-element.562.fo_ref, s32[4]{0:T(128)} %broadcast_and_fusion.co_ref, ...), custom_call_target="tpu_custom_call", output_to_operand_aliasing={{0}: (18, {}), {1}: (19, {})} | custom-call | flops 20000000000 | bytes 40000000 | tf_op jit(solution)/shard_map/ff_part/pallas_call | solution.py:515
  137.8 3.6 add_all.14
  141.5 2.4 collective-permute-start.2
  143.9 19.4 %ff_part.6 = (bf16[4,1280,1024]{2,1,0:T(8,128)(2,1)}, bf16[4,1280,1024]{2,1,0:T(8,128)(2,1)}, bf16[8,8,128,128]{3,2,1,0:T(8,128)(2,1)}, bf16[8,8,128,128]{3,2,1,0:T(8,128)(2,1)}, f32[2,1,512]{2,1,0:T(1,128)}) custom-call(s32[8]{0:T(128)} %get-tuple-element.563.fo_ref, s32[4]{0:T(128)} %broadcast_and_fusion.co_ref, ...), custom_call_target="tpu_custom_call", output_to_operand_aliasing={{0}: (18, {}), {1}: (19, {})} | custom-call | flops 20000000000 | bytes 40000000 | tf_op jit(solution)/shard_map/ff_part/pallas_call | solution.py:515
  163.3 4.6 collective-permute-done.2.refs_1_
  168.9 4.7 add_all.15
  178.2 19.3 %ff_part.7 = (bf16[4,1280,1024]{2,1,0:T(8,128)(2,1)}, bf16[4,1280,1024]{2,1,0:T(8,128)(2,1)}, bf16[8,8,128,128]{3,2,1,0:T(8,128)(2,1)}, bf16[8,8,128,128]{3,2,1,0:T(8,128)(2,1)}, f32[2,1,512]{2,1,0:T(1,128)}) custom-call(s32[8]{0:T(128)} %copy-done.21, s32[4]{0:T(128)} %broadcast_and_fusion.co_ref, ...), custom_call_target="tpu_custom_call", output_to_operand_aliasing={{0}: (18, {}), {1}: (19, {})} | custom-call | flops 20000000000 | bytes 40000000 | tf_op jit(solution)/shard_map/ff_part/pallas_call | solution.py:515
  197.5 4.6 collective-permute-done.5.refs_3_
  203.1 5.0 %add_all.16 = (bf16[1,8,128,128]{3,2,1,0:T(8,128)(2,1)}, bf16[1,8,128,128]{3,2,1,0:T(8,128)(2,1)}, bf16[2,8,128,128]{3,2,1,0:T(8,128)(2,1)}, bf16[2,8,128,128]{3...) custom-call(bf16[2,8,128,128]{3,2,1,0:T(8,128)(2,1)} %get-tuple-element.329.refs_0_, ...), custom_call_target="tpu_custom_call" | custom-call | flops 2000000000 | bytes 4000000 | tf_op jit(solution)/shard_map/add_all/pallas_call | solution.py:912
  210.2 2.6 collective-permute-start.10
  212.8 31.7 %ff_join.1 = (f32[1280,1024]{1,0:T(8,128)}, f32[1280,1024]{1,0:T(8,128)}) custom-call(s32[32]{0:T(128)} %pad_add_fusion.1.fo_ref, bf16[4,1280,1024]{2,1,0:T(8,128)(2,1)} %get-tuple-element.339.act_ref, bf16[4,1280,1024]{2,1,0:T(8,128)(2,1)} %get-tuple-element.340.gh_ref, bf16[1024,4096]{1,0:T(8,128)(2,1)} %refs_7_.1, bf16[1024,4096]{1,0:T(8,128)(2,1)} %refs_7_.1, ...), custom_call_target="tpu_custom_call" | custom-call | flops 28000000000 | bytes 56000000 | tf_op jit(solution)/shard_map/ff_join/pallas_call | solution.py:567
  245.6 4.9 %add_all.17 = (bf16[1,8,128,128]{3,2,1,0:T(8,128)(2,1)}, bf16[1,8,128,128]{3,2,1,0:T(8,128)(2,1)}, bf16[2,8,128,128]{3,2,1,0:T(8,128)(2,1)}, bf16[2,8,128,128]{3...) custom-call(bf16[2,8,128,128]{3,2,1,0:T(8,128)(2,1)} %get-tuple-element.349.refs_0_, ...), custom_call_target="tpu_custom_call" | custom-call | flops 2000000000 | bytes 4000000 | tf_op jit(solution)/shard_map/add_all/pallas_call | solution.py:912
  253.0 20.8 %ff_rows.1 = (bf16[1280,1024]{1,0:T(8,128)(2,1)}, f32[8,1024]{1,0:T(8,128)}, bf16[1280,1024]{1,0:T(8,128)(2,1)}, bf16[8,4,128,128]{3,2,1,0:T(8,128)(2,1)}, bf16[...) custom-call(s32[20]{0:T(128)} %select_reduce_fusion.4.src_ref, s32[8]{0:T(128)} %get-tuple-element.559.inv_ref, ...), custom_call_target="tpu_custom_call" | custom-call | flops 22000001024 | bytes 44000000 | tf_op jit(solution)/shard_map/ff_rows/pallas_call | solution.py:677
  273.9 3.4 collective-permute-done.12.refs_3_
  278.3 2.9 add_all.18
  282.0 4.1 all-to-all-start.2
  286.1 18.6 %attn_backward.2 = (bf16[3,1280,768]{2,1,0:T(8,128)(2,1)}, bf16[6,160,640]{2,1,0:T(8,128)(2,1)}, bf16[6,160,640]{2,1,0:T(8,128)(2,1)}) custom-call(s32[1]{0:T(128)} %bitcast.1.core_ref, bf16[1280,3072]{1,0:T(8,128)(2,1)} %get-tuple-element.282.q_ref.k_ref.v_ref, bf16[1280,3072]{1,0:T(8,128)(2,1)} %get-tuple-element.282.q_ref.k_ref.v_ref, ...), custom_call_target="tpu_custom_call" | custom-call | flops 17999998976 | bytes 36000000 | tf_op jit(solution)/shard_map/attn_backward/pallas_call | solution.py:381
  304.7 3.0 add_all.19
  308.3 2.6 collective-permute-start.18
  310.9 11.1 %qkv_weight.2 = (bf16[8,9,128,128]{3,2,1,0:T(8,128)(2,1)}, bf16[8,9,128,128]{3,2,1,0:T(8,128)(2,1)}) custom-call(s32[8]{0:T(128)} %get-tuple-element.559.inv_ref, s32[2]{0:T(128)} %pad_add_fusion.flag_ref, bf16[1280,1024]{1,0:T(8,128)(2,1)} %get-tuple-element.390.n_ref, bf16[3,1280,768]{2,1,0:T(8,128)(2,1)} %get-tuple-element.389.grad_ref.refs_0_), custom_call_target="tpu_custom_call" | custom-call | flops 6000000000 | bytes 12000000 | tf_op jit(solution)/shard_map/qkv_weight/pallas_call | solution.py:729
  323.4 2.8 add_all.20
  329.3 8.2 %attn_backward.3 = (bf16[3,1280,256]{2,1,0:T(8,128)(2,1)}, bf16[2,160,640]{2,1,0:T(8,128)(2,1)}, bf16[2,160,640]{2,1,0:T(8,128)(2,1)}) custom-call(s32[1]{0:T(128)} %bitcast.1.core_ref, bf16[1280,3072]{1,0:T(8,128)(2,1)} %get-tuple-element.282.q_ref.k_ref.v_ref, bf16[1280,3072]{1,0:T(8,128)(2,1)} %get-tuple-element.282.q_ref.k_ref.v_ref, ...), custom_call_target="tpu_custom_call" | custom-call | flops 6000000000 | bytes 12000000 | tf_op jit(solution)/shard_map/attn_backward/pallas_call | solution.py:381
  338.2 3.8 add_all.21
  342.2 3.3 collective-permute-start.23
  347.0 6.6 %qkv_weight.3 = (bf16[8,3,128,128]{3,2,1,0:T(8,128)(2,1)}, bf16[8,3,128,128]{3,2,1,0:T(8,128)(2,1)}) custom-call(s32[8]{0:T(128)} %get-tuple-element.559.inv_ref, s32[2]{0:T(128)} %pad_add_fusion.flag_ref, bf16[1280,1024]{1,0:T(8,128)(2,1)} %get-tuple-element.390.n_ref, bf16[3,1280,256]{2,1,0:T(8,128)(2,1)} %get-tuple-element.425.grad_ref.refs_1_), custom_call_target="tpu_custom_call" | custom-call | flops 6000000000 | bytes 12000000 | tf_op jit(solution)/shard_map/qkv_weight/pallas_call | solution.py:729
  354.3 2.7 add_all.22
  358.2 13.2 %bucket_sums.1 = f32[8,32,128]{2,1,0:T(8,128)} custom-call(s32[160,384]{1,0:T(8,128)} %pad.6.idx_ref, bf16[6,160,640]{2,1,0:T(8,128)(2,1)} %get-tuple-element.427.refs_0_, bf16[2,160,640]{2,1,0:T(8,128)(2,1)} %get-tuple-element.428.refs_1_, bf16[6,160,640]{2,1,0:T(8,128)(2,1)} %collective-permute-done.19.refs_2_, bf16[2,160,640]{2,1,0:T(8,128)(2,1)} %copy-done.34), custom_call_target="tpu_custom_call" | custom-call | flops 4000000000 | bytes 8000000 | tf_op jit(solution)/shard_map/bucket_sums/pallas_call | solution.py:187
  371.4 2.5 collective-permute-done.26.refs_3_
  373.9 3.7 add_all.23
  379.1 18.3 %qkv_backward.1 = (bf16[5,64,1024]{2,1,0:T(8,128)(2,1)}, bf16[5,64,1024]{2,1,0:T(8,128)(2,1)}, bf16[5,64,1024]{2,1,0:T(8,128)(2,1)}, bf16[5,64,1024]{2,1,0:T(8,128)(2,1)}, f32[8,1024]{1,0:T(8,128)}) custom-call(s32[20]{0:T(128)} %fusion.12.src_ref, bf16[3,1280,768]{2,1,0:T(8,128)(2,1)} %get-tuple-element.389.grad_ref.refs_0_, ...), custom_call_target="tpu_custom_call" | custom-call | flops 14000000000 | bytes 28000000 | tf_op jit(solution)/shard_map/qkv_backward/pallas_call | solution.py:811
  398.2 2.5 add_all.24
  404.9 4.2 collective-permute-done.33.refs_1_
  414.5 3.8 all-to-all-start.3
  418.3 4.2 assemble.3
  424.4 15.1 %collective-permute-done.35 = bf16[5,64,1024]{2,1,0:T(8,128)(2,1)} collective-permute-done((bf16[5,64,1024]{2,1,0:T(8,128)(2,1)}, bf16[5,64,1024]{2,1,0:T(8,128)(2,1)}, u32[]{:S(2)}, u32[]{:S(2)}) %collective-permute-start.35) | collective-permute-done | bytes 655392 | tf_op jit(solution)/shard_map/ppermute | solution.py:1152
  449.4 4.6 collective-permute-done.38.refs_1_
  461.0 4.3 fusion.7
  466.1 2.5 assemble.2
  (249 shorter events, 65.6 us)
Async XLA Ops:
  0.6 18.0 %copy-start = (s32[320,320]{1,0:T(8,128)S(1)}, s32[320,320]{1,0:T(8,128)}, u32[]{:S(2)}) copy-start(s32[320,320]{1,0:T(8,128)} %param.20) | copy-start | bytes 1228804
  4.3 36.1 %all-to-all-start = ((bf16[4,5,64,1024]{3,2,1,0:T(8,128)(2,1)}), bf16[4,5,64,1024]{3,2,1,0:T(8,128)(2,1)S(1)}, u32[]{:S(2)}, u32[]{:S(2)}) async-start(bf16[4,5,64,1024]{3,2,1,0:T(8,128)(2,1)} %bitcast.122), calls=%async_computation | async-start | bytes 5242880 | tf_op jit(solution)/shard_map/all_to_all | solution.py:999
  39.8 27.7 %collective-permute-start = (f32[8,160,640]{2,1,0:T(8,128)}, f32[8,160,640]{2,1,0:T(8,128)}, u32[]{:S(2)}, u32[]{:S(2)}) collective-permute-start(f32[8,160,640]{2,1,0:T(8,128)} %bias_gather.1.mine_ref), channel_id=1, source_target_pairs={{0,1},{1,0},{2,3},{3,2},{4,5},{5,4},{6,7},{7,6},{8,9},{9,8},{10,11... | collective-permute-start | bytes 9830408 | tf_op jit(solution)/shard_map/ppermute | solution.py:872
  41.9 43.4 %all-to-all-start.1 = ((bf16[4,5,64,1024]{3,2,1,0:T(8,128)(2,1)}), bf16[4,5,64,1024]{3,2,1,0:T(8,128)(2,1)}, u32[]{:S(2)}, u32[]{:S(2)}) async-start(bf16[4,5,64,1024]{3,2,1,0:T(8,128)(2,1)} %bitcast.121), calls=%async_computation.1 | async-start | bytes 5242880 | tf_op jit(solution)/shard_map/all_to_all | solution.py:999
  49.8 124.4 %copy-start.21 = (s32[8]{0:T(128)}, s32[8]{0:T(128)S(1)}, u32[]{:S(2)}) copy-start(s32[8]{0:T(128)S(1)} %get-tuple-element.560.fo_ref) | copy-start | bytes 100
  115.5 21.0 %collective-permute-start.1 = (bf16[8,8,128,128]{3,2,1,0:T(8,128)(2,1)}, bf16[8,8,128,128]{3,2,1,0:T(8,128)(2,1)S(1)}, u32[]{:S(2)}, u32[]{:S(2)}) collective-permute-start(bf16[8,8,128,128]{3,2,1,0:T(8,128)(2,1)} %get-tuple-element.294), channel_id=1, source_target_pairs={{0,1},{1,0},{2,3},{3,2},{4,5},{5,4},{6,7},{7,6},{8,9},{9,8},{10,11... | collective-permute-start | bytes 6291464 | tf_op jit(solution)/shard_map/ppermute | solution.py:872
  141.5 26.4 %collective-permute-start.3 = (bf16[8,8,128,128]{3,2,1,0:T(8,128)(2,1)S(1)}, bf16[8,8,128,128]{3,2,1,0:T(8,128)(2,1)}, u32[]{:S(2)}, u32[]{:S(2)}) collective-permute-start(bf16[8,8,128,128]{3,2,1,0:T(8,128)(2,1)S(1)} %copy-done.27), channel_id=1, source_target_pairs={{0,1},{1,0},{2,3},{3,2},{4,5},{5,4},{6,7},{7,6},{8,9},{9,8},{10,11... | collective-permute-start | bytes 6291464 | tf_op jit(solution)/shard_map/ppermute | solution.py:872
  141.5 26.3 %collective-permute-start.2 = (bf16[4,8,128,128]{3,2,1,0:T(8,128)(2,1)}, bf16[4,8,128,128]{3,2,1,0:T(8,128)(2,1)S(1)}, u32[]{:S(2)}, u32[]{:S(2)}) collective-permute-start(bf16[4,8,128,128]{3,2,1,0:T(8,128)(2,1)} %get-tuple-element.305), channel_id=1, source_target_pairs={{0,4},{4,0},{8,12},{12,8},{16,20},{20,16},{24,28},{28,24},{1,5},{5... | collective-permute-start | bytes 3145736 | tf_op jit(solution)/shard_map/ppermute | solution.py:872
  173.6 28.6 %collective-permute-start.6 = (bf16[8,8,128,128]{3,2,1,0:T(8,128)(2,1)S(1)}, bf16[8,8,128,128]{3,2,1,0:T(8,128)(2,1)}, u32[]{:S(2)}, u32[]{:S(2)}) collective-permute-start(bf16[8,8,128,128]{3,2,1,0:T(8,128)(2,1)S(1)} %copy-done.26), channel_id=1, source_target_pairs={{0,1},{1,0},{2,3},{3,2},{4,5},{5,4},{6,7},{7,6},{8,9},{9,8},{10,11... | collective-permute-start | bytes 6291464 | tf_op jit(solution)/shard_map/ppermute | solution.py:872
  174.9 22.7 %collective-permute-start.4 = (bf16[2,8,128,128]{3,2,1,0:T(8,128)(2,1)}, bf16[2,8,128,128]{3,2,1,0:T(8,128)(2,1)}, u32[]{:S(2)}, u32[]{:S(2)}) collective-permute-start(bf16[2,8,128,128]{3,2,1,0:T(8,128)(2,1)} %get-tuple-element.324), channel_id=1, source_target_pairs={{0,8},{4,12},{8,0},{12,4},{16,24},{20,28},{24,16},{28,20},{1,9},{5... | collective-permute-start | bytes 1572872 | tf_op jit(solution)/shard_map/ppermute | solution.py:872
  176.7 25.5 %collective-permute-start.5 = (bf16[4,8,128,128]{3,2,1,0:T(8,128)(2,1)}, bf16[4,8,128,128]{3,2,1,0:T(8,128)(2,1)S(1)}, u32[]{:S(2)}, u32[]{:S(2)}) collective-permute-start(bf16[4,8,128,128]{3,2,1,0:T(8,128)(2,1)} %get-tuple-element.325), channel_id=1, source_target_pairs={{0,4},{4,0},{8,12},{12,8},{16,20},{20,16},{24,28},{28,24},{1,5},{5... | collective-permute-start | bytes 3145736 | tf_op jit(solution)/shard_map/ppermute | solution.py:872
  208.2 36.4 %collective-permute-start.7 = (bf16[2,8,128,128]{3,2,1,0:T(8,128)(2,1)}, bf16[2,8,128,128]{3,2,1,0:T(8,128)(2,1)}, u32[]{:S(2)}, u32[]{:S(2)}) collective-permute-start(bf16[2,8,128,128]{3,2,1,0:T(8,128)(2,1)} %get-tuple-element.343), channel_id=1, source_target_pairs={{0,8},{4,12},{8,0},{12,4},{16,24},{20,28},{24,16},{28,20},{1,9},{5... | collective-permute-start | bytes 1572872 | tf_op jit(solution)/shard_map/ppermute | solution.py:872
  208.5 36.0 %collective-permute-start.8 = (bf16[4,8,128,128]{3,2,1,0:T(8,128)(2,1)}, bf16[4,8,128,128]{3,2,1,0:T(8,128)(2,1)S(1)}, u32[]{:S(2)}, u32[]{:S(2)}) collective-permute-start(bf16[4,8,128,128]{3,2,1,0:T(8,128)(2,1)} %get-tuple-element.344), channel_id=1, source_target_pairs={{0,4},{4,0},{8,12},{12,8},{16,20},{20,16},{24,28},{28,24},{1,5},{5... | collective-permute-start | bytes 3145736 | tf_op jit(solution)/shard_map/ppermute | solution.py:872
  210.2 34.4 %collective-permute-start.9 = (bf16[8,8,128,128]{3,2,1,0:T(8,128)(2,1)S(1)}, bf16[8,8,128,128]{3,2,1,0:T(8,128)(2,1)}, u32[]{:S(2)}, u32[]{:S(2)}) collective-permute-start(bf16[8,8,128,128]{3,2,1,0:T(8,128)(2,1)S(1)} %copy-done.25), channel_id=1, source_target_pairs={{0,1},{1,0},{2,3},{3,2},{4,5},{5,4},{6,7},{7,6},{8,9},{9,8},{10,11... | collective-permute-start | bytes 6291464 | tf_op jit(solution)/shard_map/ppermute | solution.py:872
  210.2 34.3 %collective-permute-start.10 = (bf16[1,8,128,128]{3,2,1,0:T(8,128)(2,1)}, bf16[1,8,128,128]{3,2,1,0:T(8,128)(2,1)S(1)}, u32[]{:S(2)}, u32[]{:S(2)}) collective-permute-start(bf16[1,8,128,128]{3,2,1,0:T(8,128)(2,1)} %get-tuple-element.346), channel_id=1, source_target_pairs={{0,16},{4,20},{8,24},{12,28},{16,0},{20,4},{24,8},{28,12},{1,17},{... | collective-permute-start | bytes 786440 | tf_op jit(solution)/shard_map/ppermute | solution.py:872
  244.5 29.3 %copy-start.42 = (bf16[1,8,128,128]{3,2,1,0:T(8,128)(2,1)}, bf16[1,8,128,128]{3,2,1,0:T(8,128)(2,1)S(1)}, u32[]{:S(2)}) copy-start(bf16[1,8,128,128]{3,2,1,0:T(8,128)(2,1)S(1)} %collective-permute-done.10.refs_3_) | copy-start | bytes 786436
  250.5 23.4 %collective-permute-start.11 = (bf16[2,8,128,128]{3,2,1,0:T(8,128)(2,1)}, bf16[2,8,128,128]{3,2,1,0:T(8,128)(2,1)S(1)}, u32[]{:S(2)}, u32[]{:S(2)}) collective-permute-start(bf16[2,8,128,128]{3,2,1,0:T(8,128)(2,1)} %get-tuple-element.363), channel_id=1, source_target_pairs={{0,8},{4,12},{8,0},{12,4},{16,24},{20,28},{24,16},{28,20},{1,9},{5... | collective-permute-start | bytes 1572872 | tf_op jit(solution)/shard_map/ppermute | solution.py:872
  252.1 25.2 %collective-permute-start.12 = (bf16[4,8,128,128]{3,2,1,0:T(8,128)(2,1)}, bf16[4,8,128,128]{3,2,1,0:T(8,128)(2,1)S(1)}, u32[]{:S(2)}, u32[]{:S(2)}) collective-permute-start(bf16[4,8,128,128]{3,2,1,0:T(8,128)(2,1)} %get-tuple-element.364), channel_id=1, source_target_pairs={{0,4},{4,0},{8,12},{12,8},{16,20},{20,16},{24,28},{28,24},{1,5},{5... | collective-permute-start | bytes 3145736 | tf_op jit(solution)/shard_map/ppermute | solution.py:872
  252.6 21.2 %collective-permute-start.13 = (bf16[1,8,128,128]{3,2,1,0:T(8,128)(2,1)}, bf16[1,8,128,128]{3,2,1,0:T(8,128)(2,1)S(1)}, u32[]{:S(2)}, u32[]{:S(2)}) collective-permute-start(bf16[1,8,128,128]{3,2,1,0:T(8,128)(2,1)} %get-tuple-element.365), channel_id=1, source_target_pairs={{0,16},{4,20},{8,24},{12,28},{16,0},{20,4},{24,8},{28,12},{1,17},{... | collective-permute-start | bytes 786440 | tf_op jit(solution)/shard_map/ppermute | solution.py:872
  281.2 23.5 %collective-permute-start.14 = (bf16[2,8,128,128]{3,2,1,0:T(8,128)(2,1)}, bf16[2,8,128,128]{3,2,1,0:T(8,128)(2,1)}, u32[]{:S(2)}, u32[]{:S(2)}) collective-permute-start(bf16[2,8,128,128]{3,2,1,0:T(8,128)(2,1)} %get-tuple-element.379), channel_id=1, source_target_pairs={{0,8},{4,12},{8,0},{12,4},{16,24},{20,28},{24,16},{28,20},{1,9},{5... | collective-permute-start | bytes 1572872 | tf_op jit(solution)/shard_map/ppermute | solution.py:872
  281.7 23.0 %collective-permute-start.15 = (bf16[8,4,128,128]{3,2,1,0:T(8,128)(2,1)}, bf16[8,4,128,128]{3,2,1,0:T(8,128)(2,1)}, u32[]{:S(2)}, u32[]{:S(2)}) collective-permute-start(bf16[8,4,128,128]{3,2,1,0:T(8,128)(2,1)} %get-tuple-element.380), channel_id=1, source_target_pairs={{0,1},{1,0},{2,3},{3,2},{4,5},{5,4},{6,7},{7,6},{8,9},{9,8},{10,11... | collective-permute-start | bytes 3145736 | tf_op jit(solution)/shard_map/ppermute | solution.py:872
  281.7 23.0 %collective-permute-start.16 = (bf16[1,8,128,128]{3,2,1,0:T(8,128)(2,1)}, bf16[1,8,128,128]{3,2,1,0:T(8,128)(2,1)S(1)}, u32[]{:S(2)}, u32[]{:S(2)}) collective-permute-start(bf16[1,8,128,128]{3,2,1,0:T(8,128)(2,1)} %get-tuple-element.381), channel_id=1, source_target_pairs={{0,16},{4,20},{8,24},{12,28},{16,0},{20,4},{24,8},{28,12},{1,17},{... | collective-permute-start | bytes 786440 | tf_op jit(solution)/shard_map/ppermute | solution.py:872
  282.0 41.4 %all-to-all-start.2 = ((bf16[4,5,64,1024]{3,2,1,0:T(8,128)(2,1)}), bf16[4,5,64,1024]{3,2,1,0:T(8,128)(2,1)S(1)}, u32[]{:S(2)}, u32[]{:S(2)}) async-start(bf16[4,5,64,1024]{3,2,1,0:T(8,128)(2,1)} %bitcast.144), calls=%async_computation.2 | async-start | bytes 5242880 | tf_op jit(solution)/shard_map/all_to_all | solution.py:999
  307.7 15.7 %collective-permute-start.17 = (bf16[4,4,128,128]{3,2,1,0:T(8,128)(2,1)}, bf16[4,4,128,128]{3,2,1,0:T(8,128)(2,1)}, u32[]{:S(2)}, u32[]{:S(2)}) collective-permute-start(bf16[4,4,128,128]{3,2,1,0:T(8,128)(2,1)} %get-tuple-element.393), channel_id=1, source_target_pairs={{0,4},{4,0},{8,12},{12,8},{16,20},{20,16},{24,28},{28,24},{1,5},{5... | collective-permute-start | bytes 1572872 | tf_op jit(solution)/shard_map/ppermute | solution.py:872
  308.3 15.1 %collective-permute-start.18 = (bf16[1,8,128,128]{3,2,1,0:T(8,128)(2,1)}, bf16[1,8,128,128]{3,2,1,0:T(8,128)(2,1)S(1)}, u32[]{:S(2)}, u32[]{:S(2)}) collective-permute-start(bf16[1,8,128,128]{3,2,1,0:T(8,128)(2,1)} %get-tuple-element.397), channel_id=1, source_target_pairs={{0,16},{4,20},{8,24},{12,28},{16,0},{20,4},{24,8},{28,12},{1,17},{... | collective-permute-start | bytes 786440 | tf_op jit(solution)/shard_map/ppermute | solution.py:872
  326.3 11.2 %collective-permute-start.20 = (bf16[8,9,128,128]{3,2,1,0:T(8,128)(2,1)}, bf16[8,9,128,128]{3,2,1,0:T(8,128)(2,1)}, u32[]{:S(2)}, u32[]{:S(2)}) collective-permute-start(bf16[8,9,128,128]{3,2,1,0:T(8,128)(2,1)} %get-tuple-element.415), channel_id=1, source_target_pairs={{0,1},{1,0},{2,3},{3,2},{4,5},{5,4},{6,7},{7,6},{8,9},{9,8},{10,11... | collective-permute-start | bytes 7077896 | tf_op jit(solution)/shard_map/ppermute | solution.py:872
  326.4 11.1 %collective-permute-start.19 = (bf16[6,160,640]{2,1,0:T(8,128)(2,1)}, bf16[6,160,640]{2,1,0:T(8,128)(2,1)}, u32[]{:S(2)}, u32[]{:S(2)}) collective-permute-start(bf16[6,160,640]{2,1,0:T(8,128)(2,1)} %get-tuple-element.413), channel_id=1, source_target_pairs={{0,1},{1,0},{2,3},{3,2},{4,5},{5,4},{6,7},{7,6},{8,9},{9,8},{10,11... | collective-permute-start | bytes 3686408 | tf_op jit(solution)/shard_map/ppermute | solution.py:872
  326.9 10.6 %collective-permute-start.21 = (bf16[2,4,128,128]{3,2,1,0:T(8,128)(2,1)}, bf16[2,4,128,128]{3,2,1,0:T(8,128)(2,1)S(1)}, u32[]{:S(2)}, u32[]{:S(2)}) collective-permute-start(bf16[2,4,128,128]{3,2,1,0:T(8,128)(2,1)} %get-tuple-element.416), channel_id=1, source_target_pairs={{0,8},{4,12},{8,0},{12,4},{16,24},{20,28},{24,16},{28,20},{1,9},{5... | collective-permute-start | bytes 786440 | tf_op jit(solution)/shard_map/ppermute | solution.py:872
  327.7 26.0 %collective-permute-start.24 = (bf16[1,24,128,128]{3,2,1,0:T(8,128)(2,1)}, bf16[1,24,128,128]{3,2,1,0:T(8,128)(2,1)}, u32[]{:S(2)}, u32[]{:S(2)}) collective-permute-start(bf16[1,24,128,128]{3,2,1,0:T(8,128)(2,1)} %get-tuple-element.434.refs_4_), channel_id=1, source_target_pairs={{0,2},{1,3},{2,0},{3,1},{4,6},{5,7},{6,4},{7,5},{8,10},{9,11},{10,... | collective-permute-start | bytes 2359304 | tf_op jit(solution)/shard_map/ppermute | solution.py:872
  342.1 11.6 %collective-permute-start.22 = (bf16[2,160,640]{2,1,0:T(8,128)(2,1)S(1)}, bf16[2,160,640]{2,1,0:T(8,128)(2,1)S(1)}, u32[]{:S(2)}, u32[]{:S(2)}) collective-permute-start(bf16[2,160,640]{2,1,0:T(8,128)(2,1)S(1)} %copy-done.35), channel_id=1, source_target_pairs={{0,1},{1,0},{2,3},{3,2},{4,5},{5,4},{6,7},{7,6},{8,9},{9,8},{10,11... | collective-permute-start | bytes 1228808 | tf_op jit(solution)/shard_map/ppermute | solution.py:872
  342.2 11.5 %collective-permute-start.23 = (bf16[1,4,128,128]{3,2,1,0:T(8,128)(2,1)}, bf16[1,4,128,128]{3,2,1,0:T(8,128)(2,1)S(1)}, u32[]{:S(2)}, u32[]{:S(2)}) collective-permute-start(bf16[1,4,128,128]{3,2,1,0:T(8,128)(2,1)} %get-tuple-element.433), channel_id=1, source_target_pairs={{0,16},{4,20},{8,24},{12,28},{16,0},{20,4},{24,8},{28,12},{1,17},{... | collective-permute-start | bytes 393224 | tf_op jit(solution)/shard_map/ppermute | solution.py:872
  345.5 28.4 %collective-permute-start.26 = (bf16[4,9,128,128]{3,2,1,0:T(8,128)(2,1)}, bf16[4,9,128,128]{3,2,1,0:T(8,128)(2,1)}, u32[]{:S(2)}, u32[]{:S(2)}) collective-permute-start(bf16[4,9,128,128]{3,2,1,0:T(8,128)(2,1)} %get-tuple-element.448), channel_id=1, source_target_pairs={{0,4},{4,0},{8,12},{12,8},{16,20},{20,16},{24,28},{28,24},{1,5},{5... | collective-permute-start | bytes 3538952 | tf_op jit(solution)/shard_map/ppermute | solution.py:872
  357.0 16.9 %collective-permute-start.27 = (bf16[8,3,128,128]{3,2,1,0:T(8,128)(2,1)}, bf16[8,3,128,128]{3,2,1,0:T(8,128)(2,1)}, u32[]{:S(2)}, u32[]{:S(2)}) collective-permute-start(bf16[8,3,128,128]{3,2,1,0:T(8,128)(2,1)} %get-tuple-element.449), channel_id=1, source_target_pairs={{0,1},{1,0},{2,3},{3,2},{4,5},{5,4},{6,7},{7,6},{8,9},{9,8},{10,11... | collective-permute-start | bytes 2359304 | tf_op jit(solution)/shard_map/ppermute | solution.py:872
  357.0 14.3 %collective-permute-start.25 = (bf16[1,12,128,128]{3,2,1,0:T(8,128)(2,1)}, bf16[1,12,128,128]{3,2,1,0:T(8,128)(2,1)S(1)}, u32[]{:S(2)}, u32[]{:S(2)}) collective-permute-start(bf16[1,12,128,128]{3,2,1,0:T(8,128)(2,1)} %get-tuple-element.447.refs_0_), channel_id=1, source_target_pairs={{0,2},{1,3},{2,0},{3,1},{4,6},{5,7},{6,4},{7,5},{8,10},{9,11},{10,... | collective-permute-start | bytes 1179656 | tf_op jit(solution)/shard_map/ppermute | solution.py:872
  358.0 39.5 %collective-permute-start.30 = (bf16[1,24,128,128]{3,2,1,0:T(8,128)(2,1)}, bf16[1,24,128,128]{3,2,1,0:T(8,128)(2,1)}, u32[]{:S(2)}, u32[]{:S(2)}) collective-permute-start(bf16[1,24,128,128]{3,2,1,0:T(8,128)(2,1)} %get-tuple-element.472), channel_id=1, source_target_pairs={{0,1},{1,0},{2,3},{3,2},{4,5},{5,4},{6,7},{7,6},{8,9},{9,8},{10,11... | collective-permute-start | bytes 2359304 | tf_op jit(solution)/shard_map/ppermute | solution.py:872
  377.6 19.9 %collective-permute-start.28 = (bf16[4,3,128,128]{3,2,1,0:T(8,128)(2,1)}, bf16[4,3,128,128]{3,2,1,0:T(8,128)(2,1)S(1)}, u32[]{:S(2)}, u32[]{:S(2)}) collective-permute-start(bf16[4,3,128,128]{3,2,1,0:T(8,128)(2,1)} %get-tuple-element.470), channel_id=1, source_target_pairs={{0,4},{4,0},{8,12},{12,8},{16,20},{20,16},{24,28},{28,24},{1,5},{5... | collective-permute-start | bytes 1179656 | tf_op jit(solution)/shard_map/ppermute | solution.py:872
  379.1 18.4 %collective-permute-start.29 = (bf16[2,9,128,128]{3,2,1,0:T(8,128)(2,1)}, bf16[2,9,128,128]{3,2,1,0:T(8,128)(2,1)}, u32[]{:S(2)}, u32[]{:S(2)}) collective-permute-start(bf16[2,9,128,128]{3,2,1,0:T(8,128)(2,1)} %get-tuple-element.471), channel_id=1, source_target_pairs={{0,8},{4,12},{8,0},{12,4},{16,24},{20,28},{24,16},{28,20},{1,9},{5... | collective-permute-start | bytes 1769480 | tf_op jit(solution)/shard_map/ppermute | solution.py:872
  379.1 18.4 %collective-permute-start.31 = (bf16[1,12,128,128]{3,2,1,0:T(8,128)(2,1)}, bf16[1,12,128,128]{3,2,1,0:T(8,128)(2,1)S(1)}, u32[]{:S(2)}, u32[]{:S(2)}) collective-permute-start(bf16[1,12,128,128]{3,2,1,0:T(8,128)(2,1)} %get-tuple-element.473), channel_id=1, source_target_pairs={{0,1},{1,0},{2,3},{3,2},{4,5},{5,4},{6,7},{7,6},{8,9},{9,8},{10,11... | collective-permute-start | bytes 1179656 | tf_op jit(solution)/shard_map/ppermute | solution.py:872
  400.7 8.3 %collective-permute-start.32 = (bf16[5,64,1024]{2,1,0:T(8,128)(2,1)}, bf16[5,64,1024]{2,1,0:T(8,128)(2,1)}, u32[]{:S(2)}, u32[]{:S(2)}) collective-permute-start(bf16[5,64,1024]{2,1,0:T(8,128)(2,1)} %get-tuple-element.494), channel_id=1, source_target_pairs={{0,1},{1,0},{2,3},{3,2},{4,5},{5,4},{6,7},{7,6},{8,9},{9,8},{10,11... | collective-permute-start | bytes 1966088 | tf_op jit(solution)/shard_map/ppermute | solution.py:1153
  401.3 7.7 %collective-permute-start.33 = (bf16[2,3,128,128]{3,2,1,0:T(8,128)(2,1)}, bf16[2,3,128,128]{3,2,1,0:T(8,128)(2,1)S(1)}, u32[]{:S(2)}, u32[]{:S(2)}) collective-permute-start(bf16[2,3,128,128]{3,2,1,0:T(8,128)(2,1)} %get-tuple-element.502), channel_id=1, source_target_pairs={{0,8},{4,12},{8,0},{12,4},{16,24},{20,28},{24,16},{28,20},{1,9},{5... | collective-permute-start | bytes 589832 | tf_op jit(solution)/shard_map/ppermute | solution.py:872
  403.4 21.0 %collective-permute-start.34 = (bf16[5,64,1024]{2,1,0:T(8,128)(2,1)}, bf16[5,64,1024]{2,1,0:T(8,128)(2,1)}, u32[]{:S(2)}, u32[]{:S(2)}) collective-permute-start(bf16[5,64,1024]{2,1,0:T(8,128)(2,1)} %get-tuple-element.515), channel_id=1, source_target_pairs={{0,2},{1,3},{2,0},{3,1},{4,6},{5,7},{6,4},{7,5},{8,10},{9,11},{10,... | collective-permute-start | bytes 1966088 | tf_op jit(solution)/shard_map/ppermute | solution.py:1152
  403.8 35.7 %collective-permute-start.35 = (bf16[5,64,1024]{2,1,0:T(8,128)(2,1)}, bf16[5,64,1024]{2,1,0:T(8,128)(2,1)}, u32[]{:S(2)}, u32[]{:S(2)}) collective-permute-start(bf16[5,64,1024]{2,1,0:T(8,128)(2,1)} %get-tuple-element.516), channel_id=1, source_target_pairs={{0,3},{1,2},{2,1},{3,0},{4,7},{5,6},{6,5},{7,4},{8,11},{9,10},{10,... | collective-permute-start | bytes 1966088 | tf_op jit(solution)/shard_map/ppermute | solution.py:1152
  404.6 19.8 %collective-permute-start.36 = (bf16[1,9,128,128]{3,2,1,0:T(8,128)(2,1)}, bf16[1,9,128,128]{3,2,1,0:T(8,128)(2,1)S(1)}, u32[]{:S(2)}, u32[]{:S(2)}) collective-permute-start(bf16[1,9,128,128]{3,2,1,0:T(8,128)(2,1)} %get-tuple-element.517), channel_id=1, source_target_pairs={{0,16},{4,20},{8,24},{12,28},{16,0},{20,4},{24,8},{28,12},{1,17},{... | collective-permute-start | bytes 884744 | tf_op jit(solution)/shard_map/ppermute | solution.py:872
  411.6 27.9 %collective-permute-start.37 = (bf16[1,3,128,128]{3,2,1,0:T(8,128)(2,1)}, bf16[1,3,128,128]{3,2,1,0:T(8,128)(2,1)S(1)}, u32[]{:S(2)}, u32[]{:S(2)}) collective-permute-start(bf16[1,3,128,128]{3,2,1,0:T(8,128)(2,1)} %get-tuple-element.518), channel_id=1, source_target_pairs={{0,16},{4,20},{8,24},{12,28},{16,0},{20,4},{24,8},{28,12},{1,17},{... | collective-permute-start | bytes 294920 | tf_op jit(solution)/shard_map/ppermute | solution.py:872
  414.5 39.4 %all-to-all-start.3 = ((bf16[32,96,128]{2,1,0:T(8,128)(2,1)}), bf16[32,96,128]{2,1,0:T(8,128)(2,1)}, u32[]{:S(2)}, u32[]{:S(2)}) async-start(bf16[32,96,128]{2,1,0:T(8,128)(2,1)} %bitcast.124), calls=%async_computation.3 | async-start | bytes 1572864 | tf_op jit(solution)/shard_map/all_to_all | solution.py:1166
  424.4 15.1 %copy-start.41 = (bf16[1,9,128,128]{3,2,1,0:T(8,128)(2,1)}, bf16[1,9,128,128]{3,2,1,0:T(8,128)(2,1)S(1)}, u32[]{:S(2)}) copy-start(bf16[1,9,128,128]{3,2,1,0:T(8,128)(2,1)S(1)} %collective-permute-done.36.refs_1_) | copy-start | bytes 884740
  442.1 11.9 %collective-permute-start.38 = (bf16[1,12,128,128]{3,2,1,0:T(8,128)(2,1)}, bf16[1,12,128,128]{3,2,1,0:T(8,128)(2,1)S(1)}, u32[]{:S(2)}, u32[]{:S(2)}) collective-permute-start(bf16[1,12,128,128]{3,2,1,0:T(8,128)(2,1)} %add_all.26.refs_0_), channel_id=1, source_target_pairs={{0,2},{1,3},{2,0},{3,1},{4,6},{5,7},{6,4},{7,5},{8,10},{9,11},{10,... | collective-permute-start | bytes 1179656 | tf_op jit(solution)/shard_map/ppermute | solution.py:872
  458.1 7.2 %collective-permute-start.39 = (bf16[1,12,128,128]{3,2,1,0:T(8,128)(2,1)}, bf16[1,12,128,128]{3,2,1,0:T(8,128)(2,1)S(1)}, u32[]{:S(2)}, u32[]{:S(2)}) collective-permute-start(bf16[1,12,128,128]{3,2,1,0:T(8,128)(2,1)} %add_all.27), channel_id=1, source_target_pairs={{0,1},{1,0},{2,3},{3,2},{4,5},{5,4},{6,7},{7,6},{8,9},{9,8},{10,11... | collective-permute-start | bytes 1179656 | tf_op jit(solution)/shard_map/ppermute | solution.py:872
  (49 other events, 173.1 us)

commit v5 on v4

--- a/solution.py
+++ b/solution.py
@@ -533,23 +533,41 @@
     )(fo, co, inv, flags, normed, grad_mixed, *[w_up] * count, *[b_up] * count, *[w_down] * count, *before)
 
 
-def ff_join_kernel(units, fo_ref, act_ref, gh_ref, *refs):
+def ff_join_kernel(units, parts, fo_ref, act_ref, gh_ref, *refs):
     up_refs = refs[:units]
     down_refs = refs[units : 2 * units]
-    mixed_ref, back_ref = refs[2 * units :]
-
-    @pl.when(pl.program_id(0) == 0)
+    mixed_ref, back_ref, mixed_sum, back_sum = refs[2 * units :]
+    step = pl.program_id(0)
+    half = mixed_ref.shape[0] // 2
+
+    def each(put):
+        wd = jnp.concatenate([r[...] for r in down_refs], axis=0)
+        wu = jnp.concatenate([r[...] for r in up_refs], axis=1)
+        for k in range(2):
+            part = slice(k * half, (k + 1) * half)
+            put(part, mixed_ref, mixed_sum, dot_nn(act_ref[0, part], wd))
+            put(part, back_ref, back_sum, dot_nt(gh_ref[0, part], wu))
+
+    def first(part, out_ref, sum_ref, got):
+        sum_ref[part] = got
+
+    def middle(part, out_ref, sum_ref, got):
+        sum_ref[part] += got
+
+    def last(part, out_ref, sum_ref, got):
+        out_ref[part] = (sum_ref[part] + got).astype(bf16)
+
+    @pl.when(step == 0)
     def _():
-        mixed_ref[...] = jnp.zeros_like(mixed_ref)
-        back_ref[...] = jnp.zeros_like(back_ref)
-
-    wd = jnp.concatenate([r[...] for r in down_refs], axis=0)
-    wu = jnp.concatenate([r[...] for r in up_refs], axis=1)
-    half = mixed_ref.shape[0] // 2
-    for k in range(2):
-        part = slice(k * half, (k + 1) * half)
-        mixed_ref[part] += dot_nn(act_ref[0, part], wd)
-        back_ref[part] += dot_nt(gh_ref[0, part], wu)
+        each(first)
+
+    @pl.when(jnp.logical_and(step > 0, step < parts - 1))
+    def _():
+        each(middle)
+
+    @pl.when(step == parts - 1)
+    def _():
+        each(last)
 
 
 def ff_join(fo, act, gh, w_up, w_down):
@@ -563,14 +581,15 @@
         pl.BlockSpec((LANES, features), lambda i, fo, u=u: (fo[i * units + u], 0)) for u in range(units)
     ]
     hidden = pl.BlockSpec((1, rows, wide), lambda i, fo: (i, 0, 0))
-    sums = jax.ShapeDtypeStruct((rows, features), f32)
+    sums = jax.ShapeDtypeStruct((rows, features), bf16)
     return pl.pallas_call(
-        functools.partial(ff_join_kernel, units),
+        functools.partial(ff_join_kernel, units, parts),
         grid_spec=pltpu.PrefetchScalarGridSpec(
             num_scalar_prefetch=1,
             grid=(parts,),
             in_specs=[hidden, hidden] + ups + downs,
             out_specs=[whole(sums.shape), whole(sums.shape)],
+            scratch_shapes=[pltpu.VMEM(sums.shape, f32), pltpu.VMEM(sums.shape, f32)],
         ),
         out_shape=[sums, sums],
         name="ff_join",
@@ -590,8 +609,8 @@
         e = step
         block = 4 * PIECE
         part = pl.ds(pl.multiple_of(e * block, block), block)
-        mixed = mixed_ref[...] + bd_ref[...]
-        back = back_ref[...]
+        mixed = mixed_ref[...].astype(f32) + bd_ref[...]
+        back = back_ref[...].astype(f32)
         branch = branch_ref[...].astype(f32)
         gate_one = mod_ref[2:3, :]
         gate_two = mod_ref[5:6, :]
@@ -1092,20 +1111,23 @@
 
     b_up_rows = b_up.astype(f32).reshape(-1, 1, LANES)
     before, up_sums, ffs = [], [], []
-    steps = [((), ()), ((), (0,)), ((0,), (1,)), ((0, 1), (2,))]
+    steps = [((), ()), ((), (0,)), ((0,), (1,)), ((1,), (2,))]
     for j in range(FF_PARTS):
         moved, fresh = steps[j]
         if j:
             normed_two, grad_mixed = meet(
                 (normed_two, grad_mixed), [ffs[k] for k in moved], [ffs[k] for k in fresh]
             )
+        if j == 3:
+            normed_two, grad_mixed = meet((normed_two, grad_mixed), ffs[:1])
         act, gh, own, other, sums = ff_part(
             j, fos[j], co, inv, flags, normed_two, grad_mixed, w_up, b_up_rows, w_down, before
         )
         before = [act, gh]
         up_sums.append(sums.reshape(-1, LANES))
         ffs.append(chain(own, other))
-    act, gh = meet((act, gh), ffs[:3], [ffs[3]])
+    act, gh = meet((act, gh), ffs[2:3], ffs[3:])
+    act, gh = meet((act, gh), ffs[:2])
     mixed, back = ff_join(jnp.concatenate(fos), act, gh, w_up, w_down)
     mixed, back = meet((mixed, back), ffs[1:], held=ffs[:1])
     gres, early, grad_att, out_own, out_other, out_pieces = ff_rows(
@@ -1114,7 +1136,8 @@
     local_slots = tokens.shape[1]
     piece_shape = (-1, local_slots, PIECE, features)
     wos = chain(out_own, out_other)
-    grad_att, out_pieces = meet((grad_att, out_pieces), ffs[2:], [wos], held=ffs[1:2])
+    grad_att, out_pieces = meet((grad_att, out_pieces), ffs[2:3], [wos], held=ffs[1:2])
+    grad_att, out_pieces = meet((grad_att, out_pieces), ffs[3:])
     out_pieces = exchange(out_pieces.reshape(piece_shape))
     pairs = probs.shape[0]
     grads_a, mine_a, others_a = attn_backward(core_arr, qkv, attended, grad_att, probs, recips, windows, 0, FIRST_PAIRS)

time: 473 us -> 463 us (0.979)
  waiting for transfers between devices: 40.6 us -> 27.8 us
    ppermute x37, waiting for transfers between devices: 25.4 us -> 14.6 us  [trade(): return lax.ppermute(array, axis, flip(axis, bit))]
    pallas_call x14 -> x17, Pallas kernels: 45.5 us -> 50.5 us  [add_all(): pl.pallas_call(functools.partial(add_kernel, plans), grid=(steps,), in_sp...]
  transfers between devices with their start and end apart: 44 -> 44, of which waited for: 8 -> 7; matrix products, arithmetic and copies ran while one was open for 7% -> 7% of each run, Pallas kernels for 56% -> 60%
where the time goes in v5:
time: 463 us; the launch traced here: 458 us
  Pallas kernels  325 us (70%)
  starting transfers between devices  53.6 us (12%)
  waiting for transfers between devices  27.8 us (6%)
  local copies, waits for them, and re-layouts  26.6 us (6%)
  other arithmetic  12.5 us (3%)
  matrix products  10.7 us (2%)
    pallas_call x4, Pallas kernels, ff_part(): pl.pallas_call(functools.partial(ff_part_kernel, count), grid_spec=pltpu....  78.1 us
    pallas_call x17, Pallas kernels, add_all(): pl.pallas_call(functools.partial(add_kernel, plans), grid=(steps,), in_sp...  50.5 us
    ppermute x37, starting transfers between devices, trade(): return lax.ppermute(array, axis, flip(axis, bit))  35.6 us
    pallas_call x1, Pallas kernels, ff_join(): pl.pallas_call(functools.partial(ff_join_kernel, units, parts), grid_spec...  30.2 us
    pallas_call x2, Pallas kernels, attn_backward(): pl.pallas_call(functools.partial(attn_back_kernel, windows), grid_spec=pl...  26.7 us
    pallas_call x1, Pallas kernels, ff_rows(): pl.pallas_call(functools.partial(ff_rows_kernel, blocks), grid_spec=pltpu...  20.3 us
    pallas_call x1, Pallas kernels, bias_gather(): pl.pallas_call(bias_kernel, grid=(rows // 8,), in_specs=[pl.BlockSpec((8,...  19.1 us
    pallas_call x1, Pallas kernels, qkv_backward(): pl.pallas_call(qkv_back_kernel, grid_spec=pltpu.PrefetchScalarGridSpec(nu...  18.3 us
  transfers between devices with their start and end apart: 44, of which 7 were waited for; matrix products, arithmetic and copies ran while one was open for 7% of the time, Pallas kernels for 60%

profile of v5, /device:TPU:0, one launch (start us, length us, event | category | flops | bytes accessed | tf_op | source)
XLA Modules:
  0.0 458.1 jit_solution(8429073083737239258)
XLA Ops:
  0.7 3.6 copy.59
  4.3 4.4 all-to-all-start
  8.7 6.3 %fusion.5 = f32[1,6144]{1,0:T(1,128)S(1)} fusion(bf16[1024,6144]{1,0:T(8,128)(2,1)} %param.30, bf16[1,1024]{1,0:T(2,128)(2,1)S(1)} %copy-done.8), kind=kOutput, calls=%fused_computation.36 | convolution fusion | flops 12589056 | bytes 12609536 | tf_op jit(solution)/shard_map/dot_general | solution.py:1066
  15.1 3.6 copy.60
  20.7 19.1 %bias_gather.1.mine_ref = f32[8,160,640]{2,1,0:T(8,128)} custom-call(s32[160,384]{1,0:T(8,128)} %pad.6.idx_ref, bf16[256,256]{1,0:T(8,128)(2,1)} %pad_maximum_fusion.1.tab_ref), custom_call_target="tpu_custom_call" | custom-call | flops 900000000 | bytes 1800000 | tf_op jit(solution)/shard_map/bias_gather/pallas_call | solution.py:114
  41.9 4.8 %all-to-all-start.1 = ((bf16[4,5,64,1024]{3,2,1,0:T(8,128)(2,1)}), bf16[4,5,64,1024]{3,2,1,0:T(8,128)(2,1)}, u32[]{:S(2)}, u32[]{:S(2)}) async-start(bf16[4,5,64,1024]{3,2,1,0:T(8,128)(2,1)} %bitcast.121), calls=%async_computation.1 | async-start | bytes 5242880 | tf_op jit(solution)/shard_map/all_to_all | solution.py:1018
  51.6 15.9 %norm_qkv.1 = (bf16[1280,1024]{1,0:T(8,128)(2,1)}, bf16[1280,1024]{1,0:T(8,128)(2,1)}, bf16[1280,3072]{1,0:T(8,128)(2,1)}) custom-call(s32[20]{0:T(128)} %select_reduce_fusion.4.src_ref, bf16[20,64,1024]{2,1,0:T(8,128)(2,1)} %bitcast.116, bf16[20,64,1024]{2,1,0:T(8,128)(2,1)} %bitcast.117, bf16[20,64,1024]{2,1,0:T(8,128)(2,1)} %bitcast.118, ...), custom_call_target="tpu_custom_call" | custom-call | flops 600000000 | bytes 1200000 | tf_op jit(solution)/shard_map/norm_qkv/pallas_call | solution.py:227
  67.5 17.7 %attn_forward.1 = (bf16[1280,1024]{1,0:T(8,128)(2,1)}, bf16[8,4,320,640]{3,2,1,0:T(8,128)(2,1)}, f32[1280,1024]{1,0:T(8,128)}) custom-call(s32[1]{0:T(128)} %bitcast.1.core_ref, bf16[1280,3072]{1,0:T(8,128)(2,1)} %get-tuple-element.294.q_ref.k_ref.v_ref, bf16[1280,3072]{1,0:T(8,128)(2,1)} %get-tuple-element.294.q_ref.k_ref.v_ref, ...), custom_call_target="tpu_custom_call" | custom-call | flops 900000000 | bytes 1800000 | tf_op jit(solution)/shard_map/attn_forward/pallas_call | solution.py:313
  85.3 10.8 %out_norm.1 = (bf16[1280,1024]{1,0:T(8,128)(2,1)}, bf16[1280,1024]{1,0:T(8,128)(2,1)}, bf16[1280,1024]{1,0:T(8,128)(2,1)}) custom-call(s32[20]{0:T(128)} %select_reduce_fusion.4.src_ref, bf16[20,64,1024]{2,1,0:T(8,128)(2,1)} %bitcast.15.a_ref.b_ref.c_ref.d_ref.refs_0_.refs_1_.refs_2_.refs_3_, ...), custom_call_target="tpu_custom_call" | custom-call | flops 300000000 | bytes 600000 | tf_op jit(solution)/shard_map/out_norm/pallas_call | solution.py:424
  96.0 19.4 %ff_part.4 = (bf16[4,1280,1024]{2,1,0:T(8,128)(2,1)}, bf16[4,1280,1024]{2,1,0:T(8,128)(2,1)}, bf16[8,8,128,128]{3,2,1,0:T(8,128)(2,1)}, bf16[8,8,128,128]{3,2,1,0:T(8,128)(2,1)}, f32[2,1,512]{2,1,0:T(1,128)}) custom-call(s32[8]{0:T(128)} %get-tuple-element.585.fo_ref, s32[4]{0:T(128)} %broadcast_and_fusion.co_ref, s32[8]{0:T(128)} %get-tuple-element.583.inv_ref, ...), custom_call_target="tpu_custom_call" | custom-call | flops 20000000000 | bytes 40000000 | tf_op jit(solution)/shard_map/ff_part/pallas_call | solution.py:515
  116.5 19.9 %ff_part.5 = (bf16[4,1280,1024]{2,1,0:T(8,128)(2,1)}, bf16[4,1280,1024]{2,1,0:T(8,128)(2,1)}, bf16[8,8,128,128]{3,2,1,0:T(8,128)(2,1)}, bf16[8,8,128,128]{3,2,1,0:T(8,128)(2,1)}, f32[2,1,512]{2,1,0:T(1,128)}) custom-call(s32[8]{0:T(128)} %get-tuple-element.586.fo_ref, s32[4]{0:T(128)} %broadcast_and_fusion.co_ref, ...), custom_call_target="tpu_custom_call", output_to_operand_aliasing={{0}: (18, {}), {1}: (19, {})} | custom-call | flops 20000000000 | bytes 40000000 | tf_op jit(solution)/shard_map/ff_part/pallas_call | solution.py:515
  137.8 3.6 add_all.17
  141.4 2.4 collective-permute-start.3
  143.8 19.4 %ff_part.6 = (bf16[4,1280,1024]{2,1,0:T(8,128)(2,1)}, bf16[4,1280,1024]{2,1,0:T(8,128)(2,1)}, bf16[8,8,128,128]{3,2,1,0:T(8,128)(2,1)}, bf16[8,8,128,128]{3,2,1,0:T(8,128)(2,1)}, f32[2,1,512]{2,1,0:T(1,128)}) custom-call(s32[8]{0:T(128)} %get-tuple-element.587.fo_ref, s32[4]{0:T(128)} %broadcast_and_fusion.co_ref, ...), custom_call_target="tpu_custom_call", output_to_operand_aliasing={{0}: (18, {}), {1}: (19, {})} | custom-call | flops 20000000000 | bytes 40000000 | tf_op jit(solution)/shard_map/ff_part/pallas_call | solution.py:515
  163.2 3.6 add_all.18
  169.2 2.7 add_all.19
  174.8 19.4 %ff_part.7 = (bf16[4,1280,1024]{2,1,0:T(8,128)(2,1)}, bf16[4,1280,1024]{2,1,0:T(8,128)(2,1)}, bf16[8,8,128,128]{3,2,1,0:T(8,128)(2,1)}, bf16[8,8,128,128]{3,2,1,0:T(8,128)(2,1)}, f32[2,1,512]{2,1,0:T(1,128)}) custom-call(s32[8]{0:T(128)} %copy-done.21, s32[4]{0:T(128)} %broadcast_and_fusion.co_ref, ...), custom_call_target="tpu_custom_call", output_to_operand_aliasing={{0}: (18, {}), {1}: (19, {})} | custom-call | flops 20000000000 | bytes 40000000 | tf_op jit(solution)/shard_map/ff_part/pallas_call | solution.py:515
  194.3 3.5 add_all.20
  198.8 3.1 add_all.21
  202.9 2.6 collective-permute-start.10
  205.5 30.2 %ff_join.1 = (bf16[1280,1024]{1,0:T(8,128)(2,1)}, bf16[1280,1024]{1,0:T(8,128)(2,1)}) custom-call(s32[32]{0:T(128)} %pad_add_fusion.1.fo_ref, bf16[4,1280,1024]{2,1,0:T(8,128)(2,1)} %get-tuple-element.359.act_ref, bf16[4,1280,1024]{2,1,0:T(8,128)(2,1)} %get-tuple-element.360.gh_ref, bf16[1024,4096]{1,0:T(8,128)(2,1)} %refs_7_.1, bf16[1024,4096]{1,0:T(8,128)(2,1)} %refs_7_.1, ...), custom_call_target="tpu_custom_call" | custom-call | flops 28000000000 | bytes 56000000 | tf_op jit(solution)/shard_map/ff_join/pallas_call | solution.py:585
  235.7 5.3 %add_all.22 = (bf16[1,8,128,128]{3,2,1,0:T(8,128)(2,1)}, bf16[1,8,128,128]{3,2,1,0:T(8,128)(2,1)}, bf16[2,8,128,128]{3,2,1,0:T(8,128)(2,1)}, bf16[2,8,128,128]{3...) custom-call(bf16[2,8,128,128]{3,2,1,0:T(8,128)(2,1)} %get-tuple-element.369.refs_0_, ...), custom_call_target="tpu_custom_call" | custom-call | flops 2000000000 | bytes 4000000 | tf_op jit(solution)/shard_map/add_all/pallas_call | solution.py:931
  244.4 20.3 %ff_rows.1 = (bf16[1280,1024]{1,0:T(8,128)(2,1)}, f32[8,1024]{1,0:T(8,128)}, bf16[1280,1024]{1,0:T(8,128)(2,1)}, bf16[8,4,128,128]{3,2,1,0:T(8,128)(2,1)}, bf16[...) custom-call(s32[20]{0:T(128)} %select_reduce_fusion.4.src_ref, s32[8]{0:T(128)} %get-tuple-element.583.inv_ref, ...), custom_call_target="tpu_custom_call" | custom-call | flops 22000001024 | bytes 44000000 | tf_op jit(solution)/shard_map/ff_rows/pallas_call | solution.py:696
  267.6 2.6 collective-permute-start.16
  271.2 2.4 add_all.24
  274.1 3.7 all-to-all-start.2
  277.7 18.6 %attn_backward.2 = (bf16[3,1280,768]{2,1,0:T(8,128)(2,1)}, bf16[6,160,640]{2,1,0:T(8,128)(2,1)}, bf16[6,160,640]{2,1,0:T(8,128)(2,1)}) custom-call(s32[1]{0:T(128)} %bitcast.1.core_ref, bf16[1280,3072]{1,0:T(8,128)(2,1)} %get-tuple-element.294.q_ref.k_ref.v_ref, bf16[1280,3072]{1,0:T(8,128)(2,1)} %get-tuple-element.294.q_ref.k_ref.v_ref, ...), custom_call_target="tpu_custom_call" | custom-call | flops 17999998976 | bytes 36000000 | tf_op jit(solution)/shard_map/attn_backward/pallas_call | solution.py:381
  296.3 3.0 add_all.25
  301.2 11.1 %qkv_weight.2 = (bf16[8,9,128,128]{3,2,1,0:T(8,128)(2,1)}, bf16[8,9,128,128]{3,2,1,0:T(8,128)(2,1)}) custom-call(s32[8]{0:T(128)} %get-tuple-element.583.inv_ref, s32[2]{0:T(128)} %pad_add_fusion.flag_ref, bf16[1280,1024]{1,0:T(8,128)(2,1)} %get-tuple-element.414.n_ref, bf16[3,1280,768]{2,1,0:T(8,128)(2,1)} %get-tuple-element.413.grad_ref.refs_0_), custom_call_target="tpu_custom_call" | custom-call | flops 6000000000 | bytes 12000000 | tf_op jit(solution)/shard_map/qkv_weight/pallas_call | solution.py:748
  312.3 2.9 collective-permute-done.18.refs_1_
  315.2 2.8 add_all.26
  320.6 8.2 %attn_backward.3 = (bf16[3,1280,256]{2,1,0:T(8,128)(2,1)}, bf16[2,160,640]{2,1,0:T(8,128)(2,1)}, bf16[2,160,640]{2,1,0:T(8,128)(2,1)}) custom-call(s32[1]{0:T(128)} %bitcast.1.core_ref, bf16[1280,3072]{1,0:T(8,128)(2,1)} %get-tuple-element.294.q_ref.k_ref.v_ref, bf16[1280,3072]{1,0:T(8,128)(2,1)} %get-tuple-element.294.q_ref.k_ref.v_ref, ...), custom_call_target="tpu_custom_call" | custom-call | flops 6000000000 | bytes 12000000 | tf_op jit(solution)/shard_map/attn_backward/pallas_call | solution.py:381
  329.5 3.9 add_all.27
  336.4 6.6 %qkv_weight.3 = (bf16[8,3,128,128]{3,2,1,0:T(8,128)(2,1)}, bf16[8,3,128,128]{3,2,1,0:T(8,128)(2,1)}) custom-call(s32[8]{0:T(128)} %get-tuple-element.583.inv_ref, s32[2]{0:T(128)} %pad_add_fusion.flag_ref, bf16[1280,1024]{1,0:T(8,128)(2,1)} %get-tuple-element.414.n_ref, bf16[3,1280,256]{2,1,0:T(8,128)(2,1)} %get-tuple-element.449.grad_ref.refs_1_), custom_call_target="tpu_custom_call" | custom-call | flops 6000000000 | bytes 12000000 | tf_op jit(solution)/shard_map/qkv_weight/pallas_call | solution.py:748
  343.9 2.7 add_all.28
  347.8 13.2 %bucket_sums.1 = f32[8,32,128]{2,1,0:T(8,128)} custom-call(s32[160,384]{1,0:T(8,128)} %pad.6.idx_ref, bf16[6,160,640]{2,1,0:T(8,128)(2,1)} %get-tuple-element.451.refs_0_, bf16[2,160,640]{2,1,0:T(8,128)(2,1)} %get-tuple-element.452.refs_1_, bf16[6,160,640]{2,1,0:T(8,128)(2,1)} %collective-permute-done.19.refs_2_, bf16[2,160,640]{2,1,0:T(8,128)(2,1)} %copy-done.34), custom_call_target="tpu_custom_call" | custom-call | flops 4000000000 | bytes 8000000 | tf_op jit(solution)/shard_map/bucket_sums/pallas_call | solution.py:187
  361.0 3.1 collective-permute-done.26.refs_3_
  364.1 3.7 add_all.29
  369.0 18.3 %qkv_backward.1 = (bf16[5,64,1024]{2,1,0:T(8,128)(2,1)}, bf16[5,64,1024]{2,1,0:T(8,128)(2,1)}, bf16[5,64,1024]{2,1,0:T(8,128)(2,1)}, bf16[5,64,1024]{2,1,0:T(8,128)(2,1)}, f32[8,1024]{1,0:T(8,128)}) custom-call(s32[20]{0:T(128)} %fusion.12.src_ref, bf16[3,1280,768]{2,1,0:T(8,128)(2,1)} %get-tuple-element.413.grad_ref.refs_0_, ...), custom_call_target="tpu_custom_call" | custom-call | flops 14000000000 | bytes 28000000 | tf_op jit(solution)/shard_map/qkv_backward/pallas_call | solution.py:830
  388.1 2.5 add_all.30
  395.4 3.0 collective-permute-done.33.refs_1_
  400.9 3.6 collective-permute-start.37
  406.0 3.4 all-to-all-start.3
  409.4 4.2 assemble.3
  415.4 13.2 %collective-permute-done.35 = bf16[5,64,1024]{2,1,0:T(8,128)(2,1)} collective-permute-done((bf16[5,64,1024]{2,1,0:T(8,128)(2,1)}, bf16[5,64,1024]{2,1,0:T(8,128)(2,1)}, u32[]{:S(2)}, u32[]{:S(2)}) %collective-permute-start.35) | collective-permute-done | bytes 655392 | tf_op jit(solution)/shard_map/ppermute | solution.py:1175
  438.8 4.3 collective-permute-done.38.refs_1_
  450.4 4.3 fusion.7
  455.5 2.5 assemble.2
  (252 shorter events, 67.2 us)
Async XLA Ops:
  0.6 18.0 %copy-start = (s32[320,320]{1,0:T(8,128)S(1)}, s32[320,320]{1,0:T(8,128)}, u32[]{:S(2)}) copy-start(s32[320,320]{1,0:T(8,128)} %param.20) | copy-start | bytes 1228804
  4.3 36.1 %all-to-all-start = ((bf16[4,5,64,1024]{3,2,1,0:T(8,128)(2,1)}), bf16[4,5,64,1024]{3,2,1,0:T(8,128)(2,1)S(1)}, u32[]{:S(2)}, u32[]{:S(2)}) async-start(bf16[4,5,64,1024]{3,2,1,0:T(8,128)(2,1)} %bitcast.122), calls=%async_computation | async-start | bytes 5242880 | tf_op jit(solution)/shard_map/all_to_all | solution.py:1018
  39.8 10.0 %copy-start.50 = (s32[1,20]{1,0:T(1,128)S(1)}, s32[1,20]{1,0:T(1,128)}, u32[]{:S(2)}) copy-start(s32[1,20]{1,0:T(1,128)} %param.19) | copy-start | bytes 244
  39.8 27.7 %collective-permute-start = (f32[8,160,640]{2,1,0:T(8,128)}, f32[8,160,640]{2,1,0:T(8,128)}, u32[]{:S(2)}, u32[]{:S(2)}) collective-permute-start(f32[8,160,640]{2,1,0:T(8,128)} %bias_gather.1.mine_ref), channel_id=1, source_target_pairs={{0,1},{1,0},{2,3},{3,2},{4,5},{5,4},{6,7},{7,6},{8,9},{9,8},{10,11... | collective-permute-start | bytes 9830408 | tf_op jit(solution)/shard_map/ppermute | solution.py:891
  41.9 43.4 %all-to-all-start.1 = ((bf16[4,5,64,1024]{3,2,1,0:T(8,128)(2,1)}), bf16[4,5,64,1024]{3,2,1,0:T(8,128)(2,1)}, u32[]{:S(2)}, u32[]{:S(2)}) async-start(bf16[4,5,64,1024]{3,2,1,0:T(8,128)(2,1)} %bitcast.121), calls=%async_computation.1 | async-start | bytes 5242880 | tf_op jit(solution)/shard_map/all_to_all | solution.py:1018
  49.8 117.2 %copy-start.21 = (s32[8]{0:T(128)}, s32[8]{0:T(128)S(1)}, u32[]{:S(2)}) copy-start(s32[8]{0:T(128)S(1)} %get-tuple-element.584.fo_ref) | copy-start | bytes 100
  115.4 21.1 %collective-permute-start.1 = (bf16[8,8,128,128]{3,2,1,0:T(8,128)(2,1)}, bf16[8,8,128,128]{3,2,1,0:T(8,128)(2,1)S(1)}, u32[]{:S(2)}, u32[]{:S(2)}) collective-permute-start(bf16[8,8,128,128]{3,2,1,0:T(8,128)(2,1)} %get-tuple-element.306), channel_id=1, source_target_pairs={{0,1},{1,0},{2,3},{3,2},{4,5},{5,4},{6,7},{7,6},{8,9},{9,8},{10,11... | collective-permute-start | bytes 6291464 | tf_op jit(solution)/shard_map/ppermute | solution.py:891
  141.4 21.8 %collective-permute-start.2 = (bf16[8,8,128,128]{3,2,1,0:T(8,128)(2,1)S(1)}, bf16[8,8,128,128]{3,2,1,0:T(8,128)(2,1)}, u32[]{:S(2)}, u32[]{:S(2)}) collective-permute-start(bf16[8,8,128,128]{3,2,1,0:T(8,128)(2,1)S(1)} %copy-done.27), channel_id=1, source_target_pairs={{0,1},{1,0},{2,3},{3,2},{4,5},{5,4},{6,7},{7,6},{8,9},{9,8},{10,11... | collective-permute-start | bytes 6291464 | tf_op jit(solution)/shard_map/ppermute | solution.py:891
  141.4 26.8 %collective-permute-start.3 = (bf16[4,8,128,128]{3,2,1,0:T(8,128)(2,1)}, bf16[4,8,128,128]{3,2,1,0:T(8,128)(2,1)S(1)}, u32[]{:S(2)}, u32[]{:S(2)}) collective-permute-start(bf16[4,8,128,128]{3,2,1,0:T(8,128)(2,1)} %get-tuple-element.328), channel_id=1, source_target_pairs={{0,4},{4,0},{8,12},{12,8},{16,20},{20,16},{24,28},{28,24},{1,5},{5... | collective-permute-start | bytes 3145736 | tf_op jit(solution)/shard_map/ppermute | solution.py:891
  166.9 27.4 %collective-permute-start.4 = (bf16[8,8,128,128]{3,2,1,0:T(8,128)(2,1)S(1)}, bf16[8,8,128,128]{3,2,1,0:T(8,128)(2,1)}, u32[]{:S(2)}, u32[]{:S(2)}) collective-permute-start(bf16[8,8,128,128]{3,2,1,0:T(8,128)(2,1)S(1)} %copy-done.26), channel_id=1, source_target_pairs={{0,1},{1,0},{2,3},{3,2},{4,5},{5,4},{6,7},{7,6},{8,9},{9,8},{10,11... | collective-permute-start | bytes 6291464 | tf_op jit(solution)/shard_map/ppermute | solution.py:891
  171.9 25.9 %collective-permute-start.5 = (bf16[2,8,128,128]{3,2,1,0:T(8,128)(2,1)}, bf16[2,8,128,128]{3,2,1,0:T(8,128)(2,1)}, u32[]{:S(2)}, u32[]{:S(2)}) collective-permute-start(bf16[2,8,128,128]{3,2,1,0:T(8,128)(2,1)} %get-tuple-element.349), channel_id=1, source_target_pairs={{0,8},{4,12},{8,0},{12,4},{16,24},{20,28},{24,16},{28,20},{1,9},{5... | collective-permute-start | bytes 1572872 | tf_op jit(solution)/shard_map/ppermute | solution.py:891
  173.5 25.2 %collective-permute-start.6 = (bf16[4,8,128,128]{3,2,1,0:T(8,128)(2,1)S(1)}, bf16[4,8,128,128]{3,2,1,0:T(8,128)(2,1)}, u32[]{:S(2)}, u32[]{:S(2)}) collective-permute-start(bf16[4,8,128,128]{3,2,1,0:T(8,128)(2,1)S(1)} %copy-done.29), channel_id=1, source_target_pairs={{0,4},{4,0},{8,12},{12,8},{16,20},{20,16},{24,28},{28,24},{1,5},{5... | collective-permute-start | bytes 3145736 | tf_op jit(solution)/shard_map/ppermute | solution.py:891
  201.9 33.8 %collective-permute-start.7 = (bf16[2,8,128,128]{3,2,1,0:T(8,128)(2,1)}, bf16[2,8,128,128]{3,2,1,0:T(8,128)(2,1)}, u32[]{:S(2)}, u32[]{:S(2)}) collective-permute-start(bf16[2,8,128,128]{3,2,1,0:T(8,128)(2,1)} %get-tuple-element.363), channel_id=1, source_target_pairs={{0,8},{4,12},{8,0},{12,4},{16,24},{20,28},{24,16},{28,20},{1,9},{5... | collective-permute-start | bytes 1572872 | tf_op jit(solution)/shard_map/ppermute | solution.py:891
  202.3 33.4 %collective-permute-start.8 = (bf16[4,8,128,128]{3,2,1,0:T(8,128)(2,1)S(1)}, bf16[4,8,128,128]{3,2,1,0:T(8,128)(2,1)}, u32[]{:S(2)}, u32[]{:S(2)}) collective-permute-start(bf16[4,8,128,128]{3,2,1,0:T(8,128)(2,1)S(1)} %copy-done.30), channel_id=1, source_target_pairs={{0,4},{4,0},{8,12},{12,8},{16,20},{20,16},{24,28},{28,24},{1,5},{5... | collective-permute-start | bytes 3145736 | tf_op jit(solution)/shard_map/ppermute | solution.py:891
  202.9 32.8 %collective-permute-start.9 = (bf16[8,8,128,128]{3,2,1,0:T(8,128)(2,1)S(1)}, bf16[8,8,128,128]{3,2,1,0:T(8,128)(2,1)}, u32[]{:S(2)}, u32[]{:S(2)}) collective-permute-start(bf16[8,8,128,128]{3,2,1,0:T(8,128)(2,1)S(1)} %copy-done.25), channel_id=1, source_target_pairs={{0,1},{1,0},{2,3},{3,2},{4,5},{5,4},{6,7},{7,6},{8,9},{9,8},{10,11... | collective-permute-start | bytes 6291464 | tf_op jit(solution)/shard_map/ppermute | solution.py:891
  202.9 32.8 %collective-permute-start.10 = (bf16[1,8,128,128]{3,2,1,0:T(8,128)(2,1)}, bf16[1,8,128,128]{3,2,1,0:T(8,128)(2,1)S(1)}, u32[]{:S(2)}, u32[]{:S(2)}) collective-permute-start(bf16[1,8,128,128]{3,2,1,0:T(8,128)(2,1)} %get-tuple-element.366), channel_id=1, source_target_pairs={{0,16},{4,20},{8,24},{12,28},{16,0},{20,4},{24,8},{28,12},{1,17},{... | collective-permute-start | bytes 786440 | tf_op jit(solution)/shard_map/ppermute | solution.py:891
  241.0 23.7 %collective-permute-start.11 = (bf16[2,8,128,128]{3,2,1,0:T(8,128)(2,1)}, bf16[2,8,128,128]{3,2,1,0:T(8,128)(2,1)S(1)}, u32[]{:S(2)}, u32[]{:S(2)}) collective-permute-start(bf16[2,8,128,128]{3,2,1,0:T(8,128)(2,1)} %get-tuple-element.383), channel_id=1, source_target_pairs={{0,8},{4,12},{8,0},{12,4},{16,24},{20,28},{24,16},{28,20},{1,9},{5... | collective-permute-start | bytes 1572872 | tf_op jit(solution)/shard_map/ppermute | solution.py:891
  242.7 22.0 %collective-permute-start.12 = (bf16[1,8,128,128]{3,2,1,0:T(8,128)(2,1)}, bf16[1,8,128,128]{3,2,1,0:T(8,128)(2,1)S(1)}, u32[]{:S(2)}, u32[]{:S(2)}) collective-permute-start(bf16[1,8,128,128]{3,2,1,0:T(8,128)(2,1)} %get-tuple-element.384), channel_id=1, source_target_pairs={{0,16},{4,20},{8,24},{12,28},{16,0},{20,4},{24,8},{28,12},{1,17},{... | collective-permute-start | bytes 786440 | tf_op jit(solution)/shard_map/ppermute | solution.py:891
  243.0 27.2 %collective-permute-start.13 = (bf16[4,8,128,128]{3,2,1,0:T(8,128)(2,1)}, bf16[4,8,128,128]{3,2,1,0:T(8,128)(2,1)S(1)}, u32[]{:S(2)}, u32[]{:S(2)}) collective-permute-start(bf16[4,8,128,128]{3,2,1,0:T(8,128)(2,1)} %get-tuple-element.393), channel_id=1, source_target_pairs={{0,4},{4,0},{8,12},{12,8},{16,20},{20,16},{24,28},{28,24},{1,5},{5... | collective-permute-start | bytes 3145736 | tf_op jit(solution)/shard_map/ppermute | solution.py:891
  267.6 28.7 %collective-permute-start.15 = (bf16[8,4,128,128]{3,2,1,0:T(8,128)(2,1)}, bf16[8,4,128,128]{3,2,1,0:T(8,128)(2,1)}, u32[]{:S(2)}, u32[]{:S(2)}) collective-permute-start(bf16[8,4,128,128]{3,2,1,0:T(8,128)(2,1)} %get-tuple-element.404), channel_id=1, source_target_pairs={{0,1},{1,0},{2,3},{3,2},{4,5},{5,4},{6,7},{7,6},{8,9},{9,8},{10,11... | collective-permute-start | bytes 3145736 | tf_op jit(solution)/shard_map/ppermute | solution.py:891
  267.6 28.7 %collective-permute-start.16 = (bf16[1,8,128,128]{3,2,1,0:T(8,128)(2,1)}, bf16[1,8,128,128]{3,2,1,0:T(8,128)(2,1)S(1)}, u32[]{:S(2)}, u32[]{:S(2)}) collective-permute-start(bf16[1,8,128,128]{3,2,1,0:T(8,128)(2,1)} %get-tuple-element.405), channel_id=1, source_target_pairs={{0,16},{4,20},{8,24},{12,28},{16,0},{20,4},{24,8},{28,12},{1,17},{... | collective-permute-start | bytes 786440 | tf_op jit(solution)/shard_map/ppermute | solution.py:891
  273.6 22.7 %collective-permute-start.14 = (bf16[2,8,128,128]{3,2,1,0:T(8,128)(2,1)}, bf16[2,8,128,128]{3,2,1,0:T(8,128)(2,1)}, u32[]{:S(2)}, u32[]{:S(2)}) collective-permute-start(bf16[2,8,128,128]{3,2,1,0:T(8,128)(2,1)} %get-tuple-element.403), channel_id=1, source_target_pairs={{0,8},{4,12},{8,0},{12,4},{16,24},{20,28},{24,16},{28,20},{1,9},{5... | collective-permute-start | bytes 1572872 | tf_op jit(solution)/shard_map/ppermute | solution.py:891
  274.1 41.1 %all-to-all-start.2 = ((bf16[4,5,64,1024]{3,2,1,0:T(8,128)(2,1)}), bf16[4,5,64,1024]{3,2,1,0:T(8,128)(2,1)S(1)}, u32[]{:S(2)}, u32[]{:S(2)}) async-start(bf16[4,5,64,1024]{3,2,1,0:T(8,128)(2,1)} %bitcast.144), calls=%async_computation.2 | async-start | bytes 5242880 | tf_op jit(solution)/shard_map/all_to_all | solution.py:1018
  299.4 15.8 %collective-permute-start.17 = (bf16[4,4,128,128]{3,2,1,0:T(8,128)(2,1)}, bf16[4,4,128,128]{3,2,1,0:T(8,128)(2,1)}, u32[]{:S(2)}, u32[]{:S(2)}) collective-permute-start(bf16[4,4,128,128]{3,2,1,0:T(8,128)(2,1)} %get-tuple-element.417), channel_id=1, source_target_pairs={{0,4},{4,0},{8,12},{12,8},{16,20},{20,16},{24,28},{28,24},{1,5},{5... | collective-permute-start | bytes 1572872 | tf_op jit(solution)/shard_map/ppermute | solution.py:891
  300.1 15.1 %collective-permute-start.18 = (bf16[1,8,128,128]{3,2,1,0:T(8,128)(2,1)}, bf16[1,8,128,128]{3,2,1,0:T(8,128)(2,1)S(1)}, u32[]{:S(2)}, u32[]{:S(2)}) collective-permute-start(bf16[1,8,128,128]{3,2,1,0:T(8,128)(2,1)} %get-tuple-element.421), channel_id=1, source_target_pairs={{0,16},{4,20},{8,24},{12,28},{16,0},{20,4},{24,8},{28,12},{1,17},{... | collective-permute-start | bytes 786440 | tf_op jit(solution)/shard_map/ppermute | solution.py:891
  318.0 10.8 %collective-permute-start.20 = (bf16[8,9,128,128]{3,2,1,0:T(8,128)(2,1)}, bf16[8,9,128,128]{3,2,1,0:T(8,128)(2,1)}, u32[]{:S(2)}, u32[]{:S(2)}) collective-permute-start(bf16[8,9,128,128]{3,2,1,0:T(8,128)(2,1)} %get-tuple-element.439), channel_id=1, source_target_pairs={{0,1},{1,0},{2,3},{3,2},{4,5},{5,4},{6,7},{7,6},{8,9},{9,8},{10,11... | collective-permute-start | bytes 7077896 | tf_op jit(solution)/shard_map/ppermute | solution.py:891
  318.1 10.7 %collective-permute-start.19 = (bf16[6,160,640]{2,1,0:T(8,128)(2,1)}, bf16[6,160,640]{2,1,0:T(8,128)(2,1)}, u32[]{:S(2)}, u32[]{:S(2)}) collective-permute-start(bf16[6,160,640]{2,1,0:T(8,128)(2,1)} %get-tuple-element.437), channel_id=1, source_target_pairs={{0,1},{1,0},{2,3},{3,2},{4,5},{5,4},{6,7},{7,6},{8,9},{9,8},{10,11... | collective-permute-start | bytes 3686408 | tf_op jit(solution)/shard_map/ppermute | solution.py:891
  318.5 10.2 %collective-permute-start.21 = (bf16[2,4,128,128]{3,2,1,0:T(8,128)(2,1)}, bf16[2,4,128,128]{3,2,1,0:T(8,128)(2,1)S(1)}, u32[]{:S(2)}, u32[]{:S(2)}) collective-permute-start(bf16[2,4,128,128]{3,2,1,0:T(8,128)(2,1)} %get-tuple-element.440), channel_id=1, source_target_pairs={{0,8},{4,12},{8,0},{12,4},{16,24},{20,28},{24,16},{28,20},{1,9},{5... | collective-permute-start | bytes 786440 | tf_op jit(solution)/shard_map/ppermute | solution.py:891
  318.9 24.0 %collective-permute-start.24 = (bf16[1,24,128,128]{3,2,1,0:T(8,128)(2,1)}, bf16[1,24,128,128]{3,2,1,0:T(8,128)(2,1)}, u32[]{:S(2)}, u32[]{:S(2)}) collective-permute-start(bf16[1,24,128,128]{3,2,1,0:T(8,128)(2,1)} %get-tuple-element.458.refs_4_), channel_id=1, source_target_pairs={{0,2},{1,3},{2,0},{3,1},{4,6},{5,7},{6,4},{7,5},{8,10},{9,11},{10,... | collective-permute-start | bytes 2359304 | tf_op jit(solution)/shard_map/ppermute | solution.py:891
  333.4 9.9 %collective-permute-start.22 = (bf16[2,160,640]{2,1,0:T(8,128)(2,1)S(1)}, bf16[2,160,640]{2,1,0:T(8,128)(2,1)S(1)}, u32[]{:S(2)}, u32[]{:S(2)}) collective-permute-start(bf16[2,160,640]{2,1,0:T(8,128)(2,1)S(1)} %copy-done.35), channel_id=1, source_target_pairs={{0,1},{1,0},{2,3},{3,2},{4,5},{5,4},{6,7},{7,6},{8,9},{9,8},{10,11... | collective-permute-start | bytes 1228808 | tf_op jit(solution)/shard_map/ppermute | solution.py:891
  333.5 9.8 %collective-permute-start.23 = (bf16[1,4,128,128]{3,2,1,0:T(8,128)(2,1)}, bf16[1,4,128,128]{3,2,1,0:T(8,128)(2,1)S(1)}, u32[]{:S(2)}, u32[]{:S(2)}) collective-permute-start(bf16[1,4,128,128]{3,2,1,0:T(8,128)(2,1)} %get-tuple-element.457), channel_id=1, source_target_pairs={{0,16},{4,20},{8,24},{12,28},{16,0},{20,4},{24,8},{28,12},{1,17},{... | collective-permute-start | bytes 393224 | tf_op jit(solution)/shard_map/ppermute | solution.py:891
  335.7 28.4 %collective-permute-start.26 = (bf16[4,9,128,128]{3,2,1,0:T(8,128)(2,1)}, bf16[4,9,128,128]{3,2,1,0:T(8,128)(2,1)}, u32[]{:S(2)}, u32[]{:S(2)}) collective-permute-start(bf16[4,9,128,128]{3,2,1,0:T(8,128)(2,1)} %get-tuple-element.472), channel_id=1, source_target_pairs={{0,4},{4,0},{8,12},{12,8},{16,20},{20,16},{24,28},{28,24},{1,5},{5... | collective-permute-start | bytes 3538952 | tf_op jit(solution)/shard_map/ppermute | solution.py:891
  346.6 17.5 %collective-permute-start.27 = (bf16[8,3,128,128]{3,2,1,0:T(8,128)(2,1)}, bf16[8,3,128,128]{3,2,1,0:T(8,128)(2,1)}, u32[]{:S(2)}, u32[]{:S(2)}) collective-permute-start(bf16[8,3,128,128]{3,2,1,0:T(8,128)(2,1)} %get-tuple-element.473), channel_id=1, source_target_pairs={{0,1},{1,0},{2,3},{3,2},{4,5},{5,4},{6,7},{7,6},{8,9},{9,8},{10,11... | collective-permute-start | bytes 2359304 | tf_op jit(solution)/shard_map/ppermute | solution.py:891
  346.7 14.3 %collective-permute-start.25 = (bf16[1,12,128,128]{3,2,1,0:T(8,128)(2,1)}, bf16[1,12,128,128]{3,2,1,0:T(8,128)(2,1)S(1)}, u32[]{:S(2)}, u32[]{:S(2)}) collective-permute-start(bf16[1,12,128,128]{3,2,1,0:T(8,128)(2,1)} %get-tuple-element.471.refs_0_), channel_id=1, source_target_pairs={{0,2},{1,3},{2,0},{3,1},{4,6},{5,7},{6,4},{7,5},{8,10},{9,11},{10,... | collective-permute-start | bytes 1179656 | tf_op jit(solution)/shard_map/ppermute | solution.py:891
  347.6 39.7 %collective-permute-start.30 = (bf16[1,24,128,128]{3,2,1,0:T(8,128)(2,1)}, bf16[1,24,128,128]{3,2,1,0:T(8,128)(2,1)}, u32[]{:S(2)}, u32[]{:S(2)}) collective-permute-start(bf16[1,24,128,128]{3,2,1,0:T(8,128)(2,1)} %get-tuple-element.496), channel_id=1, source_target_pairs={{0,1},{1,0},{2,3},{3,2},{4,5},{5,4},{6,7},{7,6},{8,9},{9,8},{10,11... | collective-permute-start | bytes 2359304 | tf_op jit(solution)/shard_map/ppermute | solution.py:891
  367.8 19.5 %collective-permute-start.28 = (bf16[4,3,128,128]{3,2,1,0:T(8,128)(2,1)}, bf16[4,3,128,128]{3,2,1,0:T(8,128)(2,1)S(1)}, u32[]{:S(2)}, u32[]{:S(2)}) collective-permute-start(bf16[4,3,128,128]{3,2,1,0:T(8,128)(2,1)} %get-tuple-element.494), channel_id=1, source_target_pairs={{0,4},{4,0},{8,12},{12,8},{16,20},{20,16},{24,28},{28,24},{1,5},{5... | collective-permute-start | bytes 1179656 | tf_op jit(solution)/shard_map/ppermute | solution.py:891
  368.5 18.9 %collective-permute-start.29 = (bf16[2,9,128,128]{3,2,1,0:T(8,128)(2,1)}, bf16[2,9,128,128]{3,2,1,0:T(8,128)(2,1)}, u32[]{:S(2)}, u32[]{:S(2)}) collective-permute-start(bf16[2,9,128,128]{3,2,1,0:T(8,128)(2,1)} %get-tuple-element.495), channel_id=1, source_target_pairs={{0,8},{4,12},{8,0},{12,4},{16,24},{20,28},{24,16},{28,20},{1,9},{5... | collective-permute-start | bytes 1769480 | tf_op jit(solution)/shard_map/ppermute | solution.py:891
  369.0 18.4 %collective-permute-start.31 = (bf16[1,12,128,128]{3,2,1,0:T(8,128)(2,1)}, bf16[1,12,128,128]{3,2,1,0:T(8,128)(2,1)S(1)}, u32[]{:S(2)}, u32[]{:S(2)}) collective-permute-start(bf16[1,12,128,128]{3,2,1,0:T(8,128)(2,1)} %get-tuple-element.497), channel_id=1, source_target_pairs={{0,1},{1,0},{2,3},{3,2},{4,5},{5,4},{6,7},{7,6},{8,9},{9,8},{10,11... | collective-permute-start | bytes 1179656 | tf_op jit(solution)/shard_map/ppermute | solution.py:891
  390.6 7.8 %collective-permute-start.32 = (bf16[5,64,1024]{2,1,0:T(8,128)(2,1)}, bf16[5,64,1024]{2,1,0:T(8,128)(2,1)}, u32[]{:S(2)}, u32[]{:S(2)}) collective-permute-start(bf16[5,64,1024]{2,1,0:T(8,128)(2,1)} %get-tuple-element.518), channel_id=1, source_target_pairs={{0,1},{1,0},{2,3},{3,2},{4,5},{5,4},{6,7},{7,6},{8,9},{9,8},{10,11... | collective-permute-start | bytes 1966088 | tf_op jit(solution)/shard_map/ppermute | solution.py:1176
  391.3 7.1 %collective-permute-start.33 = (bf16[2,3,128,128]{3,2,1,0:T(8,128)(2,1)}, bf16[2,3,128,128]{3,2,1,0:T(8,128)(2,1)S(1)}, u32[]{:S(2)}, u32[]{:S(2)}) collective-permute-start(bf16[2,3,128,128]{3,2,1,0:T(8,128)(2,1)} %get-tuple-element.526), channel_id=1, source_target_pairs={{0,8},{4,12},{8,0},{12,4},{16,24},{20,28},{24,16},{28,20},{1,9},{5... | collective-permute-start | bytes 589832 | tf_op jit(solution)/shard_map/ppermute | solution.py:891
  392.8 22.6 %collective-permute-start.34 = (bf16[5,64,1024]{2,1,0:T(8,128)(2,1)}, bf16[5,64,1024]{2,1,0:T(8,128)(2,1)}, u32[]{:S(2)}, u32[]{:S(2)}) collective-permute-start(bf16[5,64,1024]{2,1,0:T(8,128)(2,1)} %get-tuple-element.539), channel_id=1, source_target_pairs={{0,2},{1,3},{2,0},{3,1},{4,6},{5,7},{6,4},{7,5},{8,10},{9,11},{10,... | collective-permute-start | bytes 1966088 | tf_op jit(solution)/shard_map/ppermute | solution.py:1175
  393.2 35.5 %collective-permute-start.35 = (bf16[5,64,1024]{2,1,0:T(8,128)(2,1)}, bf16[5,64,1024]{2,1,0:T(8,128)(2,1)}, u32[]{:S(2)}, u32[]{:S(2)}) collective-permute-start(bf16[5,64,1024]{2,1,0:T(8,128)(2,1)} %get-tuple-element.540), channel_id=1, source_target_pairs={{0,3},{1,2},{2,1},{3,0},{4,7},{5,6},{6,5},{7,4},{8,11},{9,10},{10,... | collective-permute-start | bytes 1966088 | tf_op jit(solution)/shard_map/ppermute | solution.py:1175
  394.0 21.5 %collective-permute-start.36 = (bf16[1,9,128,128]{3,2,1,0:T(8,128)(2,1)}, bf16[1,9,128,128]{3,2,1,0:T(8,128)(2,1)S(1)}, u32[]{:S(2)}, u32[]{:S(2)}) collective-permute-start(bf16[1,9,128,128]{3,2,1,0:T(8,128)(2,1)} %get-tuple-element.541), channel_id=1, source_target_pairs={{0,16},{4,20},{8,24},{12,28},{16,0},{20,4},{24,8},{28,12},{1,17},{... | collective-permute-start | bytes 884744 | tf_op jit(solution)/shard_map/ppermute | solution.py:891
  400.9 27.8 %collective-permute-start.37 = (bf16[1,3,128,128]{3,2,1,0:T(8,128)(2,1)}, bf16[1,3,128,128]{3,2,1,0:T(8,128)(2,1)S(1)}, u32[]{:S(2)}, u32[]{:S(2)}) collective-permute-start(bf16[1,3,128,128]{3,2,1,0:T(8,128)(2,1)} %get-tuple-element.542), channel_id=1, source_target_pairs={{0,16},{4,20},{8,24},{12,28},{16,0},{20,4},{24,8},{28,12},{1,17},{... | collective-permute-start | bytes 294920 | tf_op jit(solution)/shard_map/ppermute | solution.py:891
  406.0 37.1 %all-to-all-start.3 = ((bf16[32,96,128]{2,1,0:T(8,128)(2,1)}), bf16[32,96,128]{2,1,0:T(8,128)(2,1)}, u32[]{:S(2)}, u32[]{:S(2)}) async-start(bf16[32,96,128]{2,1,0:T(8,128)(2,1)} %bitcast.124), calls=%async_computation.3 | async-start | bytes 1572864 | tf_op jit(solution)/shard_map/all_to_all | solution.py:1189
  415.4 13.3 %copy-start.41 = (bf16[1,9,128,128]{3,2,1,0:T(8,128)(2,1)}, bf16[1,9,128,128]{3,2,1,0:T(8,128)(2,1)S(1)}, u32[]{:S(2)}) copy-start(bf16[1,9,128,128]{3,2,1,0:T(8,128)(2,1)S(1)} %collective-permute-done.36.refs_1_) | copy-start | bytes 884740
  431.3 11.8 %collective-permute-start.38 = (bf16[1,12,128,128]{3,2,1,0:T(8,128)(2,1)}, bf16[1,12,128,128]{3,2,1,0:T(8,128)(2,1)S(1)}, u32[]{:S(2)}, u32[]{:S(2)}) collective-permute-start(bf16[1,12,128,128]{3,2,1,0:T(8,128)(2,1)} %add_all.32.refs_0_), channel_id=1, source_target_pairs={{0,2},{1,3},{2,0},{3,1},{4,6},{5,7},{6,4},{7,5},{8,10},{9,11},{10,... | collective-permute-start | bytes 1179656 | tf_op jit(solution)/shard_map/ppermute | solution.py:891
  447.2 7.5 %collective-permute-start.39 = (bf16[1,12,128,128]{3,2,1,0:T(8,128)(2,1)}, bf16[1,12,128,128]{3,2,1,0:T(8,128)(2,1)S(1)}, u32[]{:S(2)}, u32[]{:S(2)}) collective-permute-start(bf16[1,12,128,128]{3,2,1,0:T(8,128)(2,1)} %add_all.33), channel_id=1, source_target_pairs={{0,1},{1,0},{2,3},{3,2},{4,5},{5,4},{6,7},{7,6},{8,9},{9,8},{10,11... | collective-permute-start | bytes 1179656 | tf_op jit(solution)/shard_map/ppermute | solution.py:891
  (49 other events, 174.6 us)

commit v6 on v5

--- a/solution.py
+++ b/solution.py
@@ -1145,7 +1145,8 @@
     qa_own, qa_other = qkv_weight(inv, flags, normed, grads_a)
     qas = chain(qa_own, qa_other)
     front = merge(*ffs[:3])
-    grad_att, unused, out_pieces = meet((grad_att, qa_own, out_pieces), [wos, front], [qas], held=ffs[3:])
+    grad_att, qa_own = meet((grad_att, qa_own), [wos], [qas])
+    grad_att, unused, out_pieces = meet((grad_att, qa_own, out_pieces), [front], held=ffs[3:])
     others_a = trade(others_a, "win", 0)
     grads_b, mine_b, others_b = attn_backward(
         core_arr, qkv, attended, grad_att, probs, recips, windows, FIRST_PAIRS, pairs - FIRST_PAIRS

time: 463 us -> 477 us (1.030)
  waiting for transfers between devices: 27.8 us -> 44.2 us
    ppermute x37, waiting for transfers between devices: 14.6 us -> 29.9 us  [trade(): return lax.ppermute(array, axis, flip(axis, bit))]
    pallas_call x17 -> x18, Pallas kernels: 50.5 us -> 52 us  [add_all(): pl.pallas_call(functools.partial(add_kernel, plans), grid=(steps,), in_sp...]
    unnamed x110 -> x112, local copies, waits for them, and re-layouts: 10.6 us -> 11.4 us
  transfers between devices with their start and end apart: 44 -> 44, of which waited for: 7 -> 8; matrix products, arithmetic and copies ran while one was open for 7% -> 7% of each run, Pallas kernels for 60% -> 59%
where the time goes in v6:
time: 477 us; the launch traced here: 473 us
  Pallas kernels  327 us (69%)
  starting transfers between devices  49.5 us (10%)
  waiting for transfers between devices  44.2 us (9%)
  local copies, waits for them, and re-layouts  27.4 us (6%)
  other arithmetic  12.5 us (3%)
  matrix products  10.6 us (2%)
    pallas_call x4, Pallas kernels, ff_part(): pl.pallas_call(functools.partial(ff_part_kernel, count), grid_spec=pltpu....  78 us
    pallas_call x18, Pallas kernels, add_all(): pl.pallas_call(functools.partial(add_kernel, plans), grid=(steps,), in_sp...  52 us
    ppermute x37, starting transfers between devices, trade(): return lax.ppermute(array, axis, flip(axis, bit))  30.9 us
    pallas_call x1, Pallas kernels, ff_join(): pl.pallas_call(functools.partial(ff_join_kernel, units, parts), grid_spec...  30.2 us
    ppermute x37, waiting for transfers between devices, trade(): return lax.ppermute(array, axis, flip(axis, bit))  29.9 us
    pallas_call x2, Pallas kernels, attn_backward(): pl.pallas_call(functools.partial(attn_back_kernel, windows), grid_spec=pl...  26.7 us
    pallas_call x1, Pallas kernels, ff_rows(): pl.pallas_call(functools.partial(ff_rows_kernel, blocks), grid_spec=pltpu...  20.3 us
    pallas_call x1, Pallas kernels, bias_gather(): pl.pallas_call(bias_kernel, grid=(rows // 8,), in_specs=[pl.BlockSpec((8,...  19.1 us
  transfers between devices with their start and end apart: 44, of which 8 were waited for; matrix products, arithmetic and copies ran while one was open for 7% of the time, Pallas kernels for 59%

profile of v6, /device:TPU:0, one launch (start us, length us, event | category | flops | bytes accessed | tf_op | source)
XLA Modules:
  0.0 472.5 jit_solution(13574187696952971207)
XLA Ops:
  0.7 3.6 copy.59
  4.3 4.4 all-to-all-start
  8.7 6.3 %fusion.5 = f32[1,6144]{1,0:T(1,128)S(1)} fusion(bf16[1024,6144]{1,0:T(8,128)(2,1)} %param.30, bf16[1,1024]{1,0:T(2,128)(2,1)S(1)} %copy-done.8), kind=kOutput, calls=%fused_computation.36 | convolution fusion | flops 12589056 | bytes 12609536 | tf_op jit(solution)/shard_map/dot_general | solution.py:1066
  15.1 3.6 copy.60
  20.7 19.1 %bias_gather.1.mine_ref = f32[8,160,640]{2,1,0:T(8,128)} custom-call(s32[160,384]{1,0:T(8,128)} %pad.6.idx_ref, bf16[256,256]{1,0:T(8,128)(2,1)} %pad_maximum_fusion.1.tab_ref), custom_call_target="tpu_custom_call" | custom-call | flops 900000000 | bytes 1800000 | tf_op jit(solution)/shard_map/bias_gather/pallas_call | solution.py:114
  41.9 4.9 %all-to-all-start.1 = ((bf16[4,5,64,1024]{3,2,1,0:T(8,128)(2,1)}), bf16[4,5,64,1024]{3,2,1,0:T(8,128)(2,1)}, u32[]{:S(2)}, u32[]{:S(2)}) async-start(bf16[4,5,64,1024]{3,2,1,0:T(8,128)(2,1)} %bitcast.121), calls=%async_computation.1 | async-start | bytes 5242880 | tf_op jit(solution)/shard_map/all_to_all | solution.py:1018
  51.7 15.9 %norm_qkv.1 = (bf16[1280,1024]{1,0:T(8,128)(2,1)}, bf16[1280,1024]{1,0:T(8,128)(2,1)}, bf16[1280,3072]{1,0:T(8,128)(2,1)}) custom-call(s32[20]{0:T(128)} %select_reduce_fusion.4.src_ref, bf16[20,64,1024]{2,1,0:T(8,128)(2,1)} %bitcast.116, bf16[20,64,1024]{2,1,0:T(8,128)(2,1)} %bitcast.117, bf16[20,64,1024]{2,1,0:T(8,128)(2,1)} %bitcast.118, ...), custom_call_target="tpu_custom_call" | custom-call | flops 600000000 | bytes 1200000 | tf_op jit(solution)/shard_map/norm_qkv/pallas_call | solution.py:227
  67.6 17.7 %attn_forward.1 = (bf16[1280,1024]{1,0:T(8,128)(2,1)}, bf16[8,4,320,640]{3,2,1,0:T(8,128)(2,1)}, f32[1280,1024]{1,0:T(8,128)}) custom-call(s32[1]{0:T(128)} %bitcast.1.core_ref, bf16[1280,3072]{1,0:T(8,128)(2,1)} %get-tuple-element.295.q_ref.k_ref.v_ref, bf16[1280,3072]{1,0:T(8,128)(2,1)} %get-tuple-element.295.q_ref.k_ref.v_ref, ...), custom_call_target="tpu_custom_call" | custom-call | flops 900000000 | bytes 1800000 | tf_op jit(solution)/shard_map/attn_forward/pallas_call | solution.py:313
  85.4 10.8 %out_norm.1 = (bf16[1280,1024]{1,0:T(8,128)(2,1)}, bf16[1280,1024]{1,0:T(8,128)(2,1)}, bf16[1280,1024]{1,0:T(8,128)(2,1)}) custom-call(s32[20]{0:T(128)} %select_reduce_fusion.4.src_ref, bf16[20,64,1024]{2,1,0:T(8,128)(2,1)} %bitcast.15.a_ref.b_ref.c_ref.d_ref.refs_0_.refs_1_.refs_2_.refs_3_, ...), custom_call_target="tpu_custom_call" | custom-call | flops 300000000 | bytes 600000 | tf_op jit(solution)/shard_map/out_norm/pallas_call | solution.py:424
  96.1 19.4 %ff_part.4 = (bf16[4,1280,1024]{2,1,0:T(8,128)(2,1)}, bf16[4,1280,1024]{2,1,0:T(8,128)(2,1)}, bf16[8,8,128,128]{3,2,1,0:T(8,128)(2,1)}, bf16[8,8,128,128]{3,2,1,0:T(8,128)(2,1)}, f32[2,1,512]{2,1,0:T(1,128)}) custom-call(s32[8]{0:T(128)} %get-tuple-element.587.fo_ref, s32[4]{0:T(128)} %broadcast_and_fusion.co_ref, s32[8]{0:T(128)} %get-tuple-element.585.inv_ref, ...), custom_call_target="tpu_custom_call" | custom-call | flops 20000000000 | bytes 40000000 | tf_op jit(solution)/shard_map/ff_part/pallas_call | solution.py:515
  116.6 19.9 %ff_part.5 = (bf16[4,1280,1024]{2,1,0:T(8,128)(2,1)}, bf16[4,1280,1024]{2,1,0:T(8,128)(2,1)}, bf16[8,8,128,128]{3,2,1,0:T(8,128)(2,1)}, bf16[8,8,128,128]{3,2,1,0:T(8,128)(2,1)}, f32[2,1,512]{2,1,0:T(1,128)}) custom-call(s32[8]{0:T(128)} %get-tuple-element.588.fo_ref, s32[4]{0:T(128)} %broadcast_and_fusion.co_ref, ...), custom_call_target="tpu_custom_call", output_to_operand_aliasing={{0}: (18, {}), {1}: (19, {})} | custom-call | flops 20000000000 | bytes 40000000 | tf_op jit(solution)/shard_map/ff_part/pallas_call | solution.py:515
  137.9 3.6 add_all.18
  143.9 19.4 %ff_part.6 = (bf16[4,1280,1024]{2,1,0:T(8,128)(2,1)}, bf16[4,1280,1024]{2,1,0:T(8,128)(2,1)}, bf16[8,8,128,128]{3,2,1,0:T(8,128)(2,1)}, bf16[8,8,128,128]{3,2,1,0:T(8,128)(2,1)}, f32[2,1,512]{2,1,0:T(1,128)}) custom-call(s32[8]{0:T(128)} %get-tuple-element.589.fo_ref, s32[4]{0:T(128)} %broadcast_and_fusion.co_ref, ...), custom_call_target="tpu_custom_call", output_to_operand_aliasing={{0}: (18, {}), {1}: (19, {})} | custom-call | flops 20000000000 | bytes 40000000 | tf_op jit(solution)/shard_map/ff_part/pallas_call | solution.py:515
  163.3 3.6 add_all.19
  169.2 2.7 add_all.20
  174.9 19.4 %ff_part.7 = (bf16[4,1280,1024]{2,1,0:T(8,128)(2,1)}, bf16[4,1280,1024]{2,1,0:T(8,128)(2,1)}, bf16[8,8,128,128]{3,2,1,0:T(8,128)(2,1)}, bf16[8,8,128,128]{3,2,1,0:T(8,128)(2,1)}, f32[2,1,512]{2,1,0:T(1,128)}) custom-call(s32[8]{0:T(128)} %copy-done.21, s32[4]{0:T(128)} %broadcast_and_fusion.co_ref, ...), custom_call_target="tpu_custom_call", output_to_operand_aliasing={{0}: (18, {}), {1}: (19, {})} | custom-call | flops 20000000000 | bytes 40000000 | tf_op jit(solution)/shard_map/ff_part/pallas_call | solution.py:515
  194.3 3.5 add_all.21
  198.8 3.1 add_all.22
  203.0 2.6 collective-permute-start.10
  205.6 30.2 %ff_join.1 = (bf16[1280,1024]{1,0:T(8,128)(2,1)}, bf16[1280,1024]{1,0:T(8,128)(2,1)}) custom-call(s32[32]{0:T(128)} %pad_add_fusion.1.fo_ref, bf16[4,1280,1024]{2,1,0:T(8,128)(2,1)} %get-tuple-element.360.act_ref, bf16[4,1280,1024]{2,1,0:T(8,128)(2,1)} %get-tuple-element.361.gh_ref, bf16[1024,4096]{1,0:T(8,128)(2,1)} %refs_7_.1, bf16[1024,4096]{1,0:T(8,128)(2,1)} %refs_7_.1, ...), custom_call_target="tpu_custom_call" | custom-call | flops 28000000000 | bytes 56000000 | tf_op jit(solution)/shard_map/ff_join/pallas_call | solution.py:585
  235.8 5.3 %add_all.23 = (bf16[1,8,128,128]{3,2,1,0:T(8,128)(2,1)}, bf16[1,8,128,128]{3,2,1,0:T(8,128)(2,1)}, bf16[2,8,128,128]{3,2,1,0:T(8,128)(2,1)}, bf16[2,8,128,128]{3...) custom-call(bf16[2,8,128,128]{3,2,1,0:T(8,128)(2,1)} %get-tuple-element.370.refs_0_, ...), custom_call_target="tpu_custom_call" | custom-call | flops 2000000000 | bytes 4000000 | tf_op jit(solution)/shard_map/add_all/pallas_call | solution.py:931
  244.4 20.3 %ff_rows.1 = (bf16[1280,1024]{1,0:T(8,128)(2,1)}, f32[8,1024]{1,0:T(8,128)}, bf16[1280,1024]{1,0:T(8,128)(2,1)}, bf16[8,4,128,128]{3,2,1,0:T(8,128)(2,1)}, bf16[...) custom-call(s32[20]{0:T(128)} %select_reduce_fusion.4.src_ref, s32[8]{0:T(128)} %get-tuple-element.585.inv_ref, ...), custom_call_target="tpu_custom_call" | custom-call | flops 22000001024 | bytes 44000000 | tf_op jit(solution)/shard_map/ff_rows/pallas_call | solution.py:696
  267.5 2.6 collective-permute-start.16
  271.1 2.4 add_all.25
  274.0 3.7 all-to-all-start.2
  277.7 18.5 %attn_backward.2 = (bf16[3,1280,768]{2,1,0:T(8,128)(2,1)}, bf16[6,160,640]{2,1,0:T(8,128)(2,1)}, bf16[6,160,640]{2,1,0:T(8,128)(2,1)}) custom-call(s32[1]{0:T(128)} %bitcast.1.core_ref, bf16[1280,3072]{1,0:T(8,128)(2,1)} %get-tuple-element.295.q_ref.k_ref.v_ref, bf16[1280,3072]{1,0:T(8,128)(2,1)} %get-tuple-element.295.q_ref.k_ref.v_ref, ...), custom_call_target="tpu_custom_call" | custom-call | flops 17999998976 | bytes 36000000 | tf_op jit(solution)/shard_map/attn_backward/pallas_call | solution.py:381
  296.2 3.0 add_all.26
  299.9 11.1 %qkv_weight.2 = (bf16[8,9,128,128]{3,2,1,0:T(8,128)(2,1)}, bf16[8,9,128,128]{3,2,1,0:T(8,128)(2,1)}) custom-call(s32[8]{0:T(128)} %get-tuple-element.585.inv_ref, s32[2]{0:T(128)} %pad_add_fusion.flag_ref, bf16[1280,1024]{1,0:T(8,128)(2,1)} %get-tuple-element.415.n_ref, bf16[3,1280,768]{2,1,0:T(8,128)(2,1)} %get-tuple-element.414.grad_ref.refs_0_), custom_call_target="tpu_custom_call" | custom-call | flops 6000000000 | bytes 12000000 | tf_op jit(solution)/shard_map/qkv_weight/pallas_call | solution.py:748
  311.0 2.8 collective-permute-done.17.refs_1_
  319.1 13.0 %collective-permute-done.18.refs_1_ = bf16[1,8,128,128]{3,2,1,0:T(8,128)(2,1)S(1)} collective-permute-done((bf16[1,8,128,128]{3,2,1,0:T(8,128)(2,1)}, bf16[1,8,128,128]{3,2,1,0:T(8,128)(2,1)S(1)}, u32[]{:S(2)}, u32[]{:S(2)}) %collective-permute-start.18) | collective-permute-done | bytes 262176 | tf_op jit(solution)/shard_map/ppermute | solution.py:891
  332.1 2.4 add_all.28.refs_4_
  336.2 8.2 %attn_backward.3 = (bf16[3,1280,256]{2,1,0:T(8,128)(2,1)}, bf16[2,160,640]{2,1,0:T(8,128)(2,1)}, bf16[2,160,640]{2,1,0:T(8,128)(2,1)}) custom-call(s32[1]{0:T(128)} %bitcast.1.core_ref, bf16[1280,3072]{1,0:T(8,128)(2,1)} %get-tuple-element.295.q_ref.k_ref.v_ref, bf16[1280,3072]{1,0:T(8,128)(2,1)} %get-tuple-element.295.q_ref.k_ref.v_ref, ...), custom_call_target="tpu_custom_call" | custom-call | flops 6000000000 | bytes 12000000 | tf_op jit(solution)/shard_map/attn_backward/pallas_call | solution.py:381
  345.1 3.9 add_all.29
  349.8 6.6 %qkv_weight.3 = (bf16[8,3,128,128]{3,2,1,0:T(8,128)(2,1)}, bf16[8,3,128,128]{3,2,1,0:T(8,128)(2,1)}) custom-call(s32[8]{0:T(128)} %get-tuple-element.585.inv_ref, s32[2]{0:T(128)} %pad_add_fusion.flag_ref, bf16[1280,1024]{1,0:T(8,128)(2,1)} %get-tuple-element.415.n_ref, bf16[3,1280,256]{2,1,0:T(8,128)(2,1)} %get-tuple-element.451.grad_ref.refs_1_), custom_call_target="tpu_custom_call" | custom-call | flops 6000000000 | bytes 12000000 | tf_op jit(solution)/shard_map/qkv_weight/pallas_call | solution.py:748
  358.2 2.7 add_all.30
  362.1 13.2 %bucket_sums.1 = f32[8,32,128]{2,1,0:T(8,128)} custom-call(s32[160,384]{1,0:T(8,128)} %pad.6.idx_ref, bf16[6,160,640]{2,1,0:T(8,128)(2,1)} %get-tuple-element.453.refs_0_, bf16[2,160,640]{2,1,0:T(8,128)(2,1)} %get-tuple-element.454.refs_1_, bf16[6,160,640]{2,1,0:T(8,128)(2,1)} %collective-permute-done.19.refs_2_, bf16[2,160,640]{2,1,0:T(8,128)(2,1)} %copy-done.35), custom_call_target="tpu_custom_call" | custom-call | flops 4000000000 | bytes 8000000 | tf_op jit(solution)/shard_map/bucket_sums/pallas_call | solution.py:187
  375.3 2.4 collective-permute-done.26.refs_3_
  377.7 3.7 add_all.31
  382.1 2.5 collective-permute-start.29
  384.5 18.3 %qkv_backward.1 = (bf16[5,64,1024]{2,1,0:T(8,128)(2,1)}, bf16[5,64,1024]{2,1,0:T(8,128)(2,1)}, bf16[5,64,1024]{2,1,0:T(8,128)(2,1)}, bf16[5,64,1024]{2,1,0:T(8,128)(2,1)}, f32[8,1024]{1,0:T(8,128)}) custom-call(s32[20]{0:T(128)} %fusion.12.src_ref, bf16[3,1280,768]{2,1,0:T(8,128)(2,1)} %get-tuple-element.414.grad_ref.refs_0_, ...), custom_call_target="tpu_custom_call" | custom-call | flops 14000000000 | bytes 28000000 | tf_op jit(solution)/shard_map/qkv_backward/pallas_call | solution.py:830
  403.7 2.5 add_all.32
  410.2 5.1 %collective-permute-done.33.refs_1_ = bf16[2,3,128,128]{3,2,1,0:T(8,128)(2,1)S(1)} collective-permute-done((bf16[2,3,128,128]{3,2,1,0:T(8,128)(2,1)}, bf16[2,3,128,128]{3,2,1,0:T(8,128)(2,1)S(1)}, u32[]{:S(2)}, u32[]{:S(2)}) %collective-permute-start.33) | collective-permute-done | bytes 196640 | tf_op jit(solution)/shard_map/ppermute | solution.py:891
  419.4 3.7 all-to-all-start.3
  423.1 4.2 assemble.3
  429.2 14.3 %collective-permute-done.35 = bf16[5,64,1024]{2,1,0:T(8,128)(2,1)} collective-permute-done((bf16[5,64,1024]{2,1,0:T(8,128)(2,1)}, bf16[5,64,1024]{2,1,0:T(8,128)(2,1)}, u32[]{:S(2)}, u32[]{:S(2)}) %collective-permute-start.35) | collective-permute-done | bytes 655392 | tf_op jit(solution)/shard_map/ppermute | solution.py:1176
  453.1 4.3 collective-permute-done.38.refs_1_
  464.8 4.3 fusion.7
  469.8 2.5 assemble.2
  (255 shorter events, 69.9 us)
Async XLA Ops:
  0.6 18.0 %copy-start = (s32[320,320]{1,0:T(8,128)S(1)}, s32[320,320]{1,0:T(8,128)}, u32[]{:S(2)}) copy-start(s32[320,320]{1,0:T(8,128)} %param.20) | copy-start | bytes 1228804
  4.3 36.1 %all-to-all-start = ((bf16[4,5,64,1024]{3,2,1,0:T(8,128)(2,1)}), bf16[4,5,64,1024]{3,2,1,0:T(8,128)(2,1)S(1)}, u32[]{:S(2)}, u32[]{:S(2)}) async-start(bf16[4,5,64,1024]{3,2,1,0:T(8,128)(2,1)} %bitcast.122), calls=%async_computation | async-start | bytes 5242880 | tf_op jit(solution)/shard_map/all_to_all | solution.py:1018
  39.8 10.0 %copy-start.51 = (s32[1,20]{1,0:T(1,128)S(1)}, s32[1,20]{1,0:T(1,128)}, u32[]{:S(2)}) copy-start(s32[1,20]{1,0:T(1,128)} %param.19) | copy-start | bytes 244
  39.9 27.8 %collective-permute-start = (f32[8,160,640]{2,1,0:T(8,128)}, f32[8,160,640]{2,1,0:T(8,128)}, u32[]{:S(2)}, u32[]{:S(2)}) collective-permute-start(f32[8,160,640]{2,1,0:T(8,128)} %bias_gather.1.mine_ref), channel_id=1, source_target_pairs={{0,1},{1,0},{2,3},{3,2},{4,5},{5,4},{6,7},{7,6},{8,9},{9,8},{10,11... | collective-permute-start | bytes 9830408 | tf_op jit(solution)/shard_map/ppermute | solution.py:891
  41.9 43.4 %all-to-all-start.1 = ((bf16[4,5,64,1024]{3,2,1,0:T(8,128)(2,1)}), bf16[4,5,64,1024]{3,2,1,0:T(8,128)(2,1)}, u32[]{:S(2)}, u32[]{:S(2)}) async-start(bf16[4,5,64,1024]{3,2,1,0:T(8,128)(2,1)} %bitcast.121), calls=%async_computation.1 | async-start | bytes 5242880 | tf_op jit(solution)/shard_map/all_to_all | solution.py:1018
  49.8 117.3 %copy-start.21 = (s32[8]{0:T(128)}, s32[8]{0:T(128)S(1)}, u32[]{:S(2)}) copy-start(s32[8]{0:T(128)S(1)} %get-tuple-element.586.fo_ref) | copy-start | bytes 100
  115.5 21.1 %collective-permute-start.1 = (bf16[8,8,128,128]{3,2,1,0:T(8,128)(2,1)}, bf16[8,8,128,128]{3,2,1,0:T(8,128)(2,1)S(1)}, u32[]{:S(2)}, u32[]{:S(2)}) collective-permute-start(bf16[8,8,128,128]{3,2,1,0:T(8,128)(2,1)} %get-tuple-element.307), channel_id=1, source_target_pairs={{0,1},{1,0},{2,3},{3,2},{4,5},{5,4},{6,7},{7,6},{8,9},{9,8},{10,11... | collective-permute-start | bytes 6291464 | tf_op jit(solution)/shard_map/ppermute | solution.py:891
  141.5 21.8 %collective-permute-start.2 = (bf16[8,8,128,128]{3,2,1,0:T(8,128)(2,1)S(1)}, bf16[8,8,128,128]{3,2,1,0:T(8,128)(2,1)}, u32[]{:S(2)}, u32[]{:S(2)}) collective-permute-start(bf16[8,8,128,128]{3,2,1,0:T(8,128)(2,1)S(1)} %copy-done.27), channel_id=1, source_target_pairs={{0,1},{1,0},{2,3},{3,2},{4,5},{5,4},{6,7},{7,6},{8,9},{9,8},{10,11... | collective-permute-start | bytes 6291464 | tf_op jit(solution)/shard_map/ppermute | solution.py:891
  141.5 26.8 %collective-permute-start.3 = (bf16[4,8,128,128]{3,2,1,0:T(8,128)(2,1)}, bf16[4,8,128,128]{3,2,1,0:T(8,128)(2,1)S(1)}, u32[]{:S(2)}, u32[]{:S(2)}) collective-permute-start(bf16[4,8,128,128]{3,2,1,0:T(8,128)(2,1)} %get-tuple-element.329), channel_id=1, source_target_pairs={{0,4},{4,0},{8,12},{12,8},{16,20},{20,16},{24,28},{28,24},{1,5},{5... | collective-permute-start | bytes 3145736 | tf_op jit(solution)/shard_map/ppermute | solution.py:891
  166.9 27.4 %collective-permute-start.4 = (bf16[8,8,128,128]{3,2,1,0:T(8,128)(2,1)S(1)}, bf16[8,8,128,128]{3,2,1,0:T(8,128)(2,1)}, u32[]{:S(2)}, u32[]{:S(2)}) collective-permute-start(bf16[8,8,128,128]{3,2,1,0:T(8,128)(2,1)S(1)} %copy-done.26), channel_id=1, source_target_pairs={{0,1},{1,0},{2,3},{3,2},{4,5},{5,4},{6,7},{7,6},{8,9},{9,8},{10,11... | collective-permute-start | bytes 6291464 | tf_op jit(solution)/shard_map/ppermute | solution.py:891
  171.9 25.8 %collective-permute-start.5 = (bf16[2,8,128,128]{3,2,1,0:T(8,128)(2,1)}, bf16[2,8,128,128]{3,2,1,0:T(8,128)(2,1)}, u32[]{:S(2)}, u32[]{:S(2)}) collective-permute-start(bf16[2,8,128,128]{3,2,1,0:T(8,128)(2,1)} %get-tuple-element.350), channel_id=1, source_target_pairs={{0,8},{4,12},{8,0},{12,4},{16,24},{20,28},{24,16},{28,20},{1,9},{5... | collective-permute-start | bytes 1572872 | tf_op jit(solution)/shard_map/ppermute | solution.py:891
  173.6 25.2 %collective-permute-start.6 = (bf16[4,8,128,128]{3,2,1,0:T(8,128)(2,1)S(1)}, bf16[4,8,128,128]{3,2,1,0:T(8,128)(2,1)}, u32[]{:S(2)}, u32[]{:S(2)}) collective-permute-start(bf16[4,8,128,128]{3,2,1,0:T(8,128)(2,1)S(1)} %copy-done.29), channel_id=1, source_target_pairs={{0,4},{4,0},{8,12},{12,8},{16,20},{20,16},{24,28},{28,24},{1,5},{5... | collective-permute-start | bytes 3145736 | tf_op jit(solution)/shard_map/ppermute | solution.py:891
  201.9 33.8 %collective-permute-start.7 = (bf16[2,8,128,128]{3,2,1,0:T(8,128)(2,1)}, bf16[2,8,128,128]{3,2,1,0:T(8,128)(2,1)}, u32[]{:S(2)}, u32[]{:S(2)}) collective-permute-start(bf16[2,8,128,128]{3,2,1,0:T(8,128)(2,1)} %get-tuple-element.364), channel_id=1, source_target_pairs={{0,8},{4,12},{8,0},{12,4},{16,24},{20,28},{24,16},{28,20},{1,9},{5... | collective-permute-start | bytes 1572872 | tf_op jit(solution)/shard_map/ppermute | solution.py:891
  202.4 33.4 %collective-permute-start.8 = (bf16[4,8,128,128]{3,2,1,0:T(8,128)(2,1)S(1)}, bf16[4,8,128,128]{3,2,1,0:T(8,128)(2,1)}, u32[]{:S(2)}, u32[]{:S(2)}) collective-permute-start(bf16[4,8,128,128]{3,2,1,0:T(8,128)(2,1)S(1)} %copy-done.30), channel_id=1, source_target_pairs={{0,4},{4,0},{8,12},{12,8},{16,20},{20,16},{24,28},{28,24},{1,5},{5... | collective-permute-start | bytes 3145736 | tf_op jit(solution)/shard_map/ppermute | solution.py:891
  203.0 32.8 %collective-permute-start.9 = (bf16[8,8,128,128]{3,2,1,0:T(8,128)(2,1)S(1)}, bf16[8,8,128,128]{3,2,1,0:T(8,128)(2,1)}, u32[]{:S(2)}, u32[]{:S(2)}) collective-permute-start(bf16[8,8,128,128]{3,2,1,0:T(8,128)(2,1)S(1)} %copy-done.25), channel_id=1, source_target_pairs={{0,1},{1,0},{2,3},{3,2},{4,5},{5,4},{6,7},{7,6},{8,9},{9,8},{10,11... | collective-permute-start | bytes 6291464 | tf_op jit(solution)/shard_map/ppermute | solution.py:891
  203.0 32.7 %collective-permute-start.10 = (bf16[1,8,128,128]{3,2,1,0:T(8,128)(2,1)}, bf16[1,8,128,128]{3,2,1,0:T(8,128)(2,1)S(1)}, u32[]{:S(2)}, u32[]{:S(2)}) collective-permute-start(bf16[1,8,128,128]{3,2,1,0:T(8,128)(2,1)} %get-tuple-element.367), channel_id=1, source_target_pairs={{0,16},{4,20},{8,24},{12,28},{16,0},{20,4},{24,8},{28,12},{1,17},{... | collective-permute-start | bytes 786440 | tf_op jit(solution)/shard_map/ppermute | solution.py:891
  241.0 23.7 %collective-permute-start.11 = (bf16[2,8,128,128]{3,2,1,0:T(8,128)(2,1)}, bf16[2,8,128,128]{3,2,1,0:T(8,128)(2,1)S(1)}, u32[]{:S(2)}, u32[]{:S(2)}) collective-permute-start(bf16[2,8,128,128]{3,2,1,0:T(8,128)(2,1)} %get-tuple-element.384), channel_id=1, source_target_pairs={{0,8},{4,12},{8,0},{12,4},{16,24},{20,28},{24,16},{28,20},{1,9},{5... | collective-permute-start | bytes 1572872 | tf_op jit(solution)/shard_map/ppermute | solution.py:891
  242.7 22.0 %collective-permute-start.12 = (bf16[1,8,128,128]{3,2,1,0:T(8,128)(2,1)}, bf16[1,8,128,128]{3,2,1,0:T(8,128)(2,1)S(1)}, u32[]{:S(2)}, u32[]{:S(2)}) collective-permute-start(bf16[1,8,128,128]{3,2,1,0:T(8,128)(2,1)} %get-tuple-element.385), channel_id=1, source_target_pairs={{0,16},{4,20},{8,24},{12,28},{16,0},{20,4},{24,8},{28,12},{1,17},{... | collective-permute-start | bytes 786440 | tf_op jit(solution)/shard_map/ppermute | solution.py:891
  243.0 27.1 %collective-permute-start.13 = (bf16[4,8,128,128]{3,2,1,0:T(8,128)(2,1)}, bf16[4,8,128,128]{3,2,1,0:T(8,128)(2,1)S(1)}, u32[]{:S(2)}, u32[]{:S(2)}) collective-permute-start(bf16[4,8,128,128]{3,2,1,0:T(8,128)(2,1)} %get-tuple-element.394), channel_id=1, source_target_pairs={{0,4},{4,0},{8,12},{12,8},{16,20},{20,16},{24,28},{28,24},{1,5},{5... | collective-permute-start | bytes 3145736 | tf_op jit(solution)/shard_map/ppermute | solution.py:891
  267.5 28.7 %collective-permute-start.15 = (bf16[8,4,128,128]{3,2,1,0:T(8,128)(2,1)}, bf16[8,4,128,128]{3,2,1,0:T(8,128)(2,1)}, u32[]{:S(2)}, u32[]{:S(2)}) collective-permute-start(bf16[8,4,128,128]{3,2,1,0:T(8,128)(2,1)} %get-tuple-element.405), channel_id=1, source_target_pairs={{0,1},{1,0},{2,3},{3,2},{4,5},{5,4},{6,7},{7,6},{8,9},{9,8},{10,11... | collective-permute-start | bytes 3145736 | tf_op jit(solution)/shard_map/ppermute | solution.py:891
  267.5 28.7 %collective-permute-start.16 = (bf16[1,8,128,128]{3,2,1,0:T(8,128)(2,1)}, bf16[1,8,128,128]{3,2,1,0:T(8,128)(2,1)S(1)}, u32[]{:S(2)}, u32[]{:S(2)}) collective-permute-start(bf16[1,8,128,128]{3,2,1,0:T(8,128)(2,1)} %get-tuple-element.406), channel_id=1, source_target_pairs={{0,16},{4,20},{8,24},{12,28},{16,0},{20,4},{24,8},{28,12},{1,17},{... | collective-permute-start | bytes 786440 | tf_op jit(solution)/shard_map/ppermute | solution.py:891
  273.6 22.7 %collective-permute-start.14 = (bf16[2,8,128,128]{3,2,1,0:T(8,128)(2,1)}, bf16[2,8,128,128]{3,2,1,0:T(8,128)(2,1)}, u32[]{:S(2)}, u32[]{:S(2)}) collective-permute-start(bf16[2,8,128,128]{3,2,1,0:T(8,128)(2,1)} %get-tuple-element.404), channel_id=1, source_target_pairs={{0,8},{4,12},{8,0},{12,4},{16,24},{20,28},{24,16},{28,20},{1,9},{5... | collective-permute-start | bytes 1572872 | tf_op jit(solution)/shard_map/ppermute | solution.py:891
  274.0 58.1 %all-to-all-start.2 = ((bf16[4,5,64,1024]{3,2,1,0:T(8,128)(2,1)}), bf16[4,5,64,1024]{3,2,1,0:T(8,128)(2,1)S(1)}, u32[]{:S(2)}, u32[]{:S(2)}) async-start(bf16[4,5,64,1024]{3,2,1,0:T(8,128)(2,1)} %bitcast.144), calls=%async_computation.2 | async-start | bytes 5242880 | tf_op jit(solution)/shard_map/all_to_all | solution.py:1018
  299.3 14.5 %collective-permute-start.17 = (bf16[4,4,128,128]{3,2,1,0:T(8,128)(2,1)}, bf16[4,4,128,128]{3,2,1,0:T(8,128)(2,1)S(1)}, u32[]{:S(2)}, u32[]{:S(2)}) collective-permute-start(bf16[4,4,128,128]{3,2,1,0:T(8,128)(2,1)} %get-tuple-element.417), channel_id=1, source_target_pairs={{0,4},{4,0},{8,12},{12,8},{16,20},{20,16},{24,28},{28,24},{1,5},{5... | collective-permute-start | bytes 1572872 | tf_op jit(solution)/shard_map/ppermute | solution.py:891
  316.6 27.8 %collective-permute-start.20 = (bf16[8,9,128,128]{3,2,1,0:T(8,128)(2,1)}, bf16[8,9,128,128]{3,2,1,0:T(8,128)(2,1)}, u32[]{:S(2)}, u32[]{:S(2)}) collective-permute-start(bf16[8,9,128,128]{3,2,1,0:T(8,128)(2,1)} %get-tuple-element.441), channel_id=1, source_target_pairs={{0,1},{1,0},{2,3},{3,2},{4,5},{5,4},{6,7},{7,6},{8,9},{9,8},{10,11... | collective-permute-start | bytes 7077896 | tf_op jit(solution)/shard_map/ppermute | solution.py:891
  316.6 27.8 %collective-permute-start.19 = (bf16[6,160,640]{2,1,0:T(8,128)(2,1)}, bf16[6,160,640]{2,1,0:T(8,128)(2,1)}, u32[]{:S(2)}, u32[]{:S(2)}) collective-permute-start(bf16[6,160,640]{2,1,0:T(8,128)(2,1)} %get-tuple-element.439), channel_id=1, source_target_pairs={{0,1},{1,0},{2,3},{3,2},{4,5},{5,4},{6,7},{7,6},{8,9},{9,8},{10,11... | collective-permute-start | bytes 3686408 | tf_op jit(solution)/shard_map/ppermute | solution.py:891
  317.1 15.0 %collective-permute-start.18 = (bf16[1,8,128,128]{3,2,1,0:T(8,128)(2,1)}, bf16[1,8,128,128]{3,2,1,0:T(8,128)(2,1)S(1)}, u32[]{:S(2)}, u32[]{:S(2)}) collective-permute-start(bf16[1,8,128,128]{3,2,1,0:T(8,128)(2,1)} %get-tuple-element.428), channel_id=1, source_target_pairs={{0,16},{4,20},{8,24},{12,28},{16,0},{20,4},{24,8},{28,12},{1,17},{... | collective-permute-start | bytes 786440 | tf_op jit(solution)/shard_map/ppermute | solution.py:891
  317.5 26.9 %collective-permute-start.21 = (bf16[2,4,128,128]{3,2,1,0:T(8,128)(2,1)}, bf16[2,4,128,128]{3,2,1,0:T(8,128)(2,1)S(1)}, u32[]{:S(2)}, u32[]{:S(2)}) collective-permute-start(bf16[2,4,128,128]{3,2,1,0:T(8,128)(2,1)} %get-tuple-element.442), channel_id=1, source_target_pairs={{0,8},{4,12},{8,0},{12,4},{16,24},{20,28},{24,16},{28,20},{1,9},{5... | collective-permute-start | bytes 786440 | tf_op jit(solution)/shard_map/ppermute | solution.py:891
  334.5 21.9 %collective-permute-start.24 = (bf16[1,24,128,128]{3,2,1,0:T(8,128)(2,1)}, bf16[1,24,128,128]{3,2,1,0:T(8,128)(2,1)}, u32[]{:S(2)}, u32[]{:S(2)}) collective-permute-start(bf16[1,24,128,128]{3,2,1,0:T(8,128)(2,1)} %add_all.28.refs_4_), channel_id=1, source_target_pairs={{0,2},{1,3},{2,0},{3,1},{4,6},{5,7},{6,4},{7,5},{8,10},{9,11},{10,... | collective-permute-start | bytes 2359304 | tf_op jit(solution)/shard_map/ppermute | solution.py:891
  348.9 8.6 %collective-permute-start.22 = (bf16[2,160,640]{2,1,0:T(8,128)(2,1)S(1)}, bf16[2,160,640]{2,1,0:T(8,128)(2,1)S(1)}, u32[]{:S(2)}, u32[]{:S(2)}) collective-permute-start(bf16[2,160,640]{2,1,0:T(8,128)(2,1)S(1)} %copy-done.36), channel_id=1, source_target_pairs={{0,1},{1,0},{2,3},{3,2},{4,5},{5,4},{6,7},{7,6},{8,9},{9,8},{10,11... | collective-permute-start | bytes 1228808 | tf_op jit(solution)/shard_map/ppermute | solution.py:891
  349.0 8.5 %collective-permute-start.23 = (bf16[1,4,128,128]{3,2,1,0:T(8,128)(2,1)}, bf16[1,4,128,128]{3,2,1,0:T(8,128)(2,1)S(1)}, u32[]{:S(2)}, u32[]{:S(2)}) collective-permute-start(bf16[1,4,128,128]{3,2,1,0:T(8,128)(2,1)} %get-tuple-element.459), channel_id=1, source_target_pairs={{0,16},{4,20},{8,24},{12,28},{16,0},{20,4},{24,8},{28,12},{1,17},{... | collective-permute-start | bytes 393224 | tf_op jit(solution)/shard_map/ppermute | solution.py:891
  349.1 28.6 %collective-permute-start.26 = (bf16[4,9,128,128]{3,2,1,0:T(8,128)(2,1)}, bf16[4,9,128,128]{3,2,1,0:T(8,128)(2,1)}, u32[]{:S(2)}, u32[]{:S(2)}) collective-permute-start(bf16[4,9,128,128]{3,2,1,0:T(8,128)(2,1)} %get-tuple-element.474), channel_id=1, source_target_pairs={{0,4},{4,0},{8,12},{12,8},{16,20},{20,16},{24,28},{28,24},{1,5},{5... | collective-permute-start | bytes 3538952 | tf_op jit(solution)/shard_map/ppermute | solution.py:891
  360.9 16.8 %collective-permute-start.27 = (bf16[8,3,128,128]{3,2,1,0:T(8,128)(2,1)}, bf16[8,3,128,128]{3,2,1,0:T(8,128)(2,1)}, u32[]{:S(2)}, u32[]{:S(2)}) collective-permute-start(bf16[8,3,128,128]{3,2,1,0:T(8,128)(2,1)} %get-tuple-element.475), channel_id=1, source_target_pairs={{0,1},{1,0},{2,3},{3,2},{4,5},{5,4},{6,7},{7,6},{8,9},{9,8},{10,11... | collective-permute-start | bytes 2359304 | tf_op jit(solution)/shard_map/ppermute | solution.py:891
  361.0 14.3 %collective-permute-start.25 = (bf16[1,12,128,128]{3,2,1,0:T(8,128)(2,1)}, bf16[1,12,128,128]{3,2,1,0:T(8,128)(2,1)S(1)}, u32[]{:S(2)}, u32[]{:S(2)}) collective-permute-start(bf16[1,12,128,128]{3,2,1,0:T(8,128)(2,1)} %get-tuple-element.473.refs_0_), channel_id=1, source_target_pairs={{0,2},{1,3},{2,0},{3,1},{4,6},{5,7},{6,4},{7,5},{8,10},{9,11},{10,... | collective-permute-start | bytes 1179656 | tf_op jit(solution)/shard_map/ppermute | solution.py:891
  361.9 41.0 %collective-permute-start.30 = (bf16[1,24,128,128]{3,2,1,0:T(8,128)(2,1)}, bf16[1,24,128,128]{3,2,1,0:T(8,128)(2,1)}, u32[]{:S(2)}, u32[]{:S(2)}) collective-permute-start(bf16[1,24,128,128]{3,2,1,0:T(8,128)(2,1)} %get-tuple-element.498), channel_id=1, source_target_pairs={{0,1},{1,0},{2,3},{3,2},{4,5},{5,4},{6,7},{7,6},{8,9},{9,8},{10,11... | collective-permute-start | bytes 2359304 | tf_op jit(solution)/shard_map/ppermute | solution.py:891
  381.5 21.4 %collective-permute-start.28 = (bf16[4,3,128,128]{3,2,1,0:T(8,128)(2,1)}, bf16[4,3,128,128]{3,2,1,0:T(8,128)(2,1)S(1)}, u32[]{:S(2)}, u32[]{:S(2)}) collective-permute-start(bf16[4,3,128,128]{3,2,1,0:T(8,128)(2,1)} %get-tuple-element.496), channel_id=1, source_target_pairs={{0,4},{4,0},{8,12},{12,8},{16,20},{20,16},{24,28},{28,24},{1,5},{5... | collective-permute-start | bytes 1179656 | tf_op jit(solution)/shard_map/ppermute | solution.py:891
  382.1 20.9 %collective-permute-start.29 = (bf16[2,9,128,128]{3,2,1,0:T(8,128)(2,1)}, bf16[2,9,128,128]{3,2,1,0:T(8,128)(2,1)}, u32[]{:S(2)}, u32[]{:S(2)}) collective-permute-start(bf16[2,9,128,128]{3,2,1,0:T(8,128)(2,1)} %get-tuple-element.497), channel_id=1, source_target_pairs={{0,8},{4,12},{8,0},{12,4},{16,24},{20,28},{24,16},{28,20},{1,9},{5... | collective-permute-start | bytes 1769480 | tf_op jit(solution)/shard_map/ppermute | solution.py:891
  384.5 18.4 %collective-permute-start.31 = (bf16[1,12,128,128]{3,2,1,0:T(8,128)(2,1)}, bf16[1,12,128,128]{3,2,1,0:T(8,128)(2,1)S(1)}, u32[]{:S(2)}, u32[]{:S(2)}) collective-permute-start(bf16[1,12,128,128]{3,2,1,0:T(8,128)(2,1)} %get-tuple-element.499), channel_id=1, source_target_pairs={{0,1},{1,0},{2,3},{3,2},{4,5},{5,4},{6,7},{7,6},{8,9},{9,8},{10,11... | collective-permute-start | bytes 1179656 | tf_op jit(solution)/shard_map/ppermute | solution.py:891
  406.2 9.1 %collective-permute-start.32 = (bf16[5,64,1024]{2,1,0:T(8,128)(2,1)}, bf16[5,64,1024]{2,1,0:T(8,128)(2,1)}, u32[]{:S(2)}, u32[]{:S(2)}) collective-permute-start(bf16[5,64,1024]{2,1,0:T(8,128)(2,1)} %get-tuple-element.520), channel_id=1, source_target_pairs={{0,1},{1,0},{2,3},{3,2},{4,5},{5,4},{6,7},{7,6},{8,9},{9,8},{10,11... | collective-permute-start | bytes 1966088 | tf_op jit(solution)/shard_map/ppermute | solution.py:1177
  406.8 8.5 %collective-permute-start.33 = (bf16[2,3,128,128]{3,2,1,0:T(8,128)(2,1)}, bf16[2,3,128,128]{3,2,1,0:T(8,128)(2,1)S(1)}, u32[]{:S(2)}, u32[]{:S(2)}) collective-permute-start(bf16[2,3,128,128]{3,2,1,0:T(8,128)(2,1)} %get-tuple-element.528), channel_id=1, source_target_pairs={{0,8},{4,12},{8,0},{12,4},{16,24},{20,28},{24,16},{28,20},{1,9},{5... | collective-permute-start | bytes 589832 | tf_op jit(solution)/shard_map/ppermute | solution.py:891
  406.9 22.3 %collective-permute-start.34 = (bf16[5,64,1024]{2,1,0:T(8,128)(2,1)}, bf16[5,64,1024]{2,1,0:T(8,128)(2,1)}, u32[]{:S(2)}, u32[]{:S(2)}) collective-permute-start(bf16[5,64,1024]{2,1,0:T(8,128)(2,1)} %get-tuple-element.541), channel_id=1, source_target_pairs={{0,2},{1,3},{2,0},{3,1},{4,6},{5,7},{6,4},{7,5},{8,10},{9,11},{10,... | collective-permute-start | bytes 1966088 | tf_op jit(solution)/shard_map/ppermute | solution.py:1176
  407.3 36.1 %collective-permute-start.35 = (bf16[5,64,1024]{2,1,0:T(8,128)(2,1)}, bf16[5,64,1024]{2,1,0:T(8,128)(2,1)}, u32[]{:S(2)}, u32[]{:S(2)}) collective-permute-start(bf16[5,64,1024]{2,1,0:T(8,128)(2,1)} %get-tuple-element.542), channel_id=1, source_target_pairs={{0,3},{1,2},{2,1},{3,0},{4,7},{5,6},{6,5},{7,4},{8,11},{9,10},{10,... | collective-permute-start | bytes 1966088 | tf_op jit(solution)/shard_map/ppermute | solution.py:1176
  408.3 20.8 %collective-permute-start.36 = (bf16[1,9,128,128]{3,2,1,0:T(8,128)(2,1)}, bf16[1,9,128,128]{3,2,1,0:T(8,128)(2,1)S(1)}, u32[]{:S(2)}, u32[]{:S(2)}) collective-permute-start(bf16[1,9,128,128]{3,2,1,0:T(8,128)(2,1)} %get-tuple-element.543), channel_id=1, source_target_pairs={{0,16},{4,20},{8,24},{12,28},{16,0},{20,4},{24,8},{28,12},{1,17},{... | collective-permute-start | bytes 884744 | tf_op jit(solution)/shard_map/ppermute | solution.py:891
  417.9 25.6 %collective-permute-start.37 = (bf16[1,3,128,128]{3,2,1,0:T(8,128)(2,1)}, bf16[1,3,128,128]{3,2,1,0:T(8,128)(2,1)S(1)}, u32[]{:S(2)}, u32[]{:S(2)}) collective-permute-start(bf16[1,3,128,128]{3,2,1,0:T(8,128)(2,1)} %get-tuple-element.544), channel_id=1, source_target_pairs={{0,16},{4,20},{8,24},{12,28},{16,0},{20,4},{24,8},{28,12},{1,17},{... | collective-permute-start | bytes 294920 | tf_op jit(solution)/shard_map/ppermute | solution.py:891
  419.4 38.0 %all-to-all-start.3 = ((bf16[32,96,128]{2,1,0:T(8,128)(2,1)}), bf16[32,96,128]{2,1,0:T(8,128)(2,1)}, u32[]{:S(2)}, u32[]{:S(2)}) async-start(bf16[32,96,128]{2,1,0:T(8,128)(2,1)} %bitcast.124), calls=%async_computation.3 | async-start | bytes 1572864 | tf_op jit(solution)/shard_map/all_to_all | solution.py:1190
  429.2 14.3 %copy-start.42 = (bf16[1,9,128,128]{3,2,1,0:T(8,128)(2,1)}, bf16[1,9,128,128]{3,2,1,0:T(8,128)(2,1)S(1)}, u32[]{:S(2)}) copy-start(bf16[1,9,128,128]{3,2,1,0:T(8,128)(2,1)S(1)} %collective-permute-done.36.refs_1_) | copy-start | bytes 884740
  446.0 11.4 %collective-permute-start.38 = (bf16[1,12,128,128]{3,2,1,0:T(8,128)(2,1)}, bf16[1,12,128,128]{3,2,1,0:T(8,128)(2,1)S(1)}, u32[]{:S(2)}, u32[]{:S(2)}) collective-permute-start(bf16[1,12,128,128]{3,2,1,0:T(8,128)(2,1)} %add_all.34.refs_0_), channel_id=1, source_target_pairs={{0,2},{1,3},{2,0},{3,1},{4,6},{5,7},{6,4},{7,5},{8,10},{9,11},{10,... | collective-permute-start | bytes 1179656 | tf_op jit(solution)/shard_map/ppermute | solution.py:891
  461.5 7.6 %collective-permute-start.39 = (bf16[1,12,128,128]{3,2,1,0:T(8,128)(2,1)}, bf16[1,12,128,128]{3,2,1,0:T(8,128)(2,1)S(1)}, u32[]{:S(2)}, u32[]{:S(2)}) collective-permute-start(bf16[1,12,128,128]{3,2,1,0:T(8,128)(2,1)} %add_all.35), channel_id=1, source_target_pairs={{0,1},{1,0},{2,3},{3,2},{4,5},{5,4},{6,7},{7,6},{8,9},{9,8},{10,11... | collective-permute-start | bytes 1179656 | tf_op jit(solution)/shard_map/ppermute | solution.py:891
  (50 other events, 154.7 us)
